TPU v7x, 32 devices: a whole 2x2x4 slice. The times are simulated.
32 devices in a mesh: rep: 8 (over y, x, core), grp: 4 (over z).
Axes of the slice: x: 2, y: 2, z: 4, core: 2. Of those that a mesh axis runs over, the one named last changes fastest.
Arguments:
- grads: bfloat16 [32, 2, 320, 2048], P(('rep', 'grp')), may hold values from -6 to 6
- errors: float32 [32, 2, 320, 2048], P(('rep', 'grp')), may hold values from -4 to 4
- warm_start: float32 [2, 32, 2048], replicated, may hold values from -0.125 to 0.125
- vec_grads: float32 [32, 2, 2048], P(('rep', 'grp')), may hold values from -6 to 6
- owners: int32 [12], replicated, may hold values from 0 to 31, as said below
- mat_momentum: float32 [64, 64, 2048], P(('rep', 'grp')), may hold values from -0.3 to 0.3
- mat_weights: float32 [64, 64, 2048], P(('rep', 'grp')), may hold values from -0.3 to 0.3
- vec_momentum: float32 [64, 2048], P(('rep', 'grp')), may hold values from -0.3 to 0.3
- vec_weights: float32 [64, 2048], P(('rep', 'grp')), may hold values from 0.5 to 1.5
Outputs:
- new_errors: float32 [32, 2, 320, 2048], P(('rep', 'grp'))
- mat_momentum_out: float32 [64, 64, 2048], P(('rep', 'grp'))
- mat_weights_out: float32 [64, 64, 2048], P(('rep', 'grp'))
- vec_momentum_out: float32 [64, 2048], P(('rep', 'grp'))
- vec_weights_out: float32 [64, 2048], P(('rep', 'grp'))
Inputs may be any that keep to these rules, and one draw needn't show every extreme that they name: `owners`: no replica owns more than 2 items, and some replica owns exactly 2. Replicas 0 and 31 each own at least one item.
All inputs are finite; a program needn't handle non-finite values.
Results may differ from a plain program's by a relative error of at most 0.0003.
Values sent between devices are 32-bit elements; how exact they have to be, the bound alone decides.
No kernel may reach another device: no remote copies, remote signals or barrier semaphores. Data moves between devices by JAX's collectives and lax.ppermute only.
A program may use at most 64 MiB of HBM per device.

v0:
```python
import jax
import jax.numpy as jnp
from jax import lax
from jax.sharding import PartitionSpec as P

ROOT_ITERS = 12


high = lax.Precision.HIGHEST


def orthonormal(factor):
    gram_matrix = jnp.einsum("mkr,mks->mrs", factor, factor, precision=high)
    spread = jnp.sqrt(jnp.sum(gram_matrix * gram_matrix, axis=(1, 2)))[:, None, None]
    identity_mat = jnp.broadcast_to(
        jnp.eye(gram_matrix.shape[1], dtype=jnp.float32), gram_matrix.shape
    )
    root_left = gram_matrix / spread
    root_right = identity_mat
    for sweep in range(ROOT_ITERS):
        middle = 1.5 * identity_mat - 0.5 * jnp.einsum(
            "mrs,mst->mrt", root_right, root_left, precision=high
        )
        root_left = jnp.einsum("mrs,mst->mrt", root_left, middle, precision=high)
        root_right = jnp.einsum("mrs,mst->mrt", middle, root_right, precision=high)
    return jnp.einsum("mkr,mrs->mks", factor, root_right, precision=high) / jnp.sqrt(spread)


def replicas_total(partial_term):
    return lax.psum(partial_term, ("rep", "grp"))


def local(
    grads,
    errors,
    warm_start,
    vec_grads,
    owners,
    mat_momentum,
    mat_weights,
    vec_momentum,
    vec_weights,
):
    count = lax.axis_size("rep") * lax.axis_size("grp")
    combined = grads[0].astype(jnp.float32) + errors[0]
    first_term = jnp.einsum("mkd,mrd->mkr", combined, warm_start, precision=high)
    p_sum = lax.psum(first_term, ("rep", "grp"))
    p_hat = orthonormal(p_sum / count)
    q_factor = replicas_total(jnp.einsum("mks,mkd->msd", p_hat, combined, precision=high)) / count
    p_sum = replicas_total(jnp.einsum("mkd,mrd->mkr", combined, q_factor, precision=high))
    p_hat = orthonormal(p_sum / count)
    q_factor = replicas_total(jnp.einsum("mks,mkd->msd", p_hat, combined, precision=high)) / count
    approx = jnp.einsum("mks,msd->mkd", p_hat, q_factor, precision=high)
    new_errors = (combined - approx)[None]
    vec_sum = lax.psum(vec_grads[0], ("rep", "grp"))
    vec_avg = vec_sum / count
    device = lax.axis_index("rep") * lax.axis_size("grp") + lax.axis_index("grp")
    items = owners.shape[0]
    earlier = jnp.arange(items)[None, :] < jnp.arange(items)[:, None]
    same = owners[None, :] == owners[:, None]
    slot = jnp.sum((earlier & same).astype(jnp.int32), axis=1)
    slot_count = mat_momentum.shape[0]
    match = (owners[None, :] == device) & (slot[None, :] == jnp.arange(slot_count)[:, None])
    match = match.astype(jnp.float32)
    head_items = approx.shape[0] * (approx.shape[1] // mat_momentum.shape[1])
    mat_match = match[:, :head_items]
    vec_match = match[:, head_items:]
    blocks = approx.reshape(head_items, mat_momentum.shape[1], approx.shape[2])
    picked = jnp.einsum("si,ihd->shd", mat_match, blocks, precision=high)
    has_block = jnp.sum(mat_match, axis=1) > 0.5
    moment = 0.9 * mat_momentum + picked
    mat_momentum_out = jnp.where(has_block[:, None, None], moment, mat_momentum)
    mat_weights_out = jnp.where(has_block[:, None, None], mat_weights - 0.5 * moment, mat_weights)
    picked_vec = jnp.dot(vec_match, vec_avg, precision=high)
    has_vec = jnp.sum(vec_match, axis=1) > 0.5
    vec_moment = 0.9 * vec_momentum + picked_vec
    vec_momentum_out = jnp.where(has_vec[:, None], vec_moment, vec_momentum)
    vec_weights_out = jnp.where(has_vec[:, None], vec_weights - 0.5 * vec_moment, vec_weights)
    return (new_errors, mat_momentum_out, mat_weights_out, vec_momentum_out, vec_weights_out)


def solution(mesh):
    placed = (
        P(("rep", "grp"), None, None, None),
        P(("rep", "grp"), None, None, None),
        P(),
        P(("rep", "grp"), None, None),
        P(),
        P(("rep", "grp"), None, None),
        P(("rep", "grp"), None, None),
        P(("rep", "grp"), None),
        P(("rep", "grp"), None),
    )
    return jax.shard_map(
        local,
        mesh=mesh,
        in_specs=placed,
        out_specs=(
            P(("rep", "grp"), None, None, None),
            P(("rep", "grp"), None, None),
            P(("rep", "grp"), None, None),
            P(("rep", "grp"), None),
            P(("rep", "grp"), None),
        ),
        check_vma=False,
    )
```

profile of v0, /device:TPU:0, one launch (start us, length us, event | category | flops | bytes accessed | tf_op | source)
XLA Modules:
  0.0 587.1 jit_solution(11399507689327947429)
XLA Ops:
  7.2 1.0 copy-done
  8.2 7.8 %fusion.8 = f32[2,320,32]{1,2,0:T(8,128)} fusion(f32[2,32,2048]{2,1,0:T(8,128)S(1)} %copy-done, f32[1,2,320,2048]{3,2,1,0:T(8,128)} %param.10, bf16[1,2,320,2048]{3,2,1,0:T(8,128)(2,1)} %param.9), kind=kOutput, calls=%fused_computation.9 | convolution fusion | flops 505937920 | bytes 8470528 | tf_op jit(solution)/shard_map/mkd,mrd->mkr/dot_general | solution.py:46
  16.2 0.2 convert_reduce_fusion
  16.4 123.1 %all-reduce.5.cloned.1.call-done = f32[2,320,32]{1,2,0:T(8,128)} async-done(((f32[2,320,32]{1,2,0:T(8,128)}), f32[2,320,32]{1,2,0:T(8,128)}) %all-reduce.5.cloned.1.call-update) | async-done | bytes 81936 | tf_op jit(solution)/shard_map/psum | solution.py:47
  139.5 1.3 multiply_reduce_fusion.1
  140.8 0.2 fusion.37
  141.0 0.2 fusion.64
  141.4 0.2 fusion.36
  141.8 0.2 fusion.77
  141.9 0.2 fusion.35
  142.4 0.2 fusion.34
  142.9 0.2 fusion.33
  143.5 0.2 fusion.32
  143.6 0.2 fusion.86
  143.8 0.2 fusion.85
  144.0 0.2 fusion.31
  144.1 0.2 fusion.88
  144.3 0.2 fusion.87
  144.5 0.2 fusion.30
  144.6 0.2 fusion.90
  144.8 0.2 fusion.89
  145.0 0.2 fusion.29
  145.5 0.2 fusion.28
  146.0 0.2 fusion.27
  146.5 0.2 fusion.26
  146.8 1.6 convolution_divide_fusion
  148.4 6.8 %fusion.6 = f32[2,32,2048]{2,1,0:T(8,128)} fusion(f32[2,320,32]{2,1,0:T(8,128)S(1)} %convolution_divide_fusion, f32[1,2,320,2048]{3,2,1,0:T(8,128)} %param.10, bf16[1,2,320,2048]{3,2,1,0:T(8,128)(2,1)S(1)} %copy-done.1), kind=kOutput, calls=%fused_computation.7 | convolution fusion | flops 505937920 | bytes 8470528 | tf_op jit(solution)/shard_map/mks,mkd->msd/dot_general | solution.py:49
  155.2 0.2 all-reduce.9.cloned.1.call-start
  155.6 128.5 %all-reduce.7.cloned.1.call-done = f32[2,32,2048]{2,1,0:T(8,128)} async-done(((f32[2,32,2048]{2,1,0:T(8,128)}), f32[2,32,2048]{2,1,0:T(8,128)}) %all-reduce.7.cloned.1.call-update) | async-done | bytes 524304 | tf_op jit(solution)/shard_map/psum | solution.py:30
  284.1 8.3 %fusion.4 = f32[2,320,32]{1,2,0:T(8,128)} fusion(f32[2,32,2048]{2,1,0:T(8,128)} %all-reduce.7.cloned.1.call-done, f32[1,2,320,2048]{3,2,1,0:T(8,128)} %param.10, bf16[1,2,320,2048]{3,2,1,0:T(8,128)(2,1)S(1)} %copy-done.1), kind=kOutput, calls=%fused_computation.5 | convolution fusion | flops 506068992 | bytes 8470528 | tf_op jit(solution)/shard_map/mkd,mrd->mkr/dot_general | solution.py:50
  292.4 0.2 slice_reduce_fusion
  292.6 119.5 %all-reduce.9.cloned.1.call-done = f32[2,320,32]{1,2,0:T(8,128)} async-done(((f32[2,320,32]{1,2,0:T(8,128)}), f32[2,320,32]{1,2,0:T(8,128)}) %all-reduce.9.cloned.1.call-update) | async-done | bytes 81936 | tf_op jit(solution)/shard_map/psum | solution.py:30
  412.1 1.3 multiply_reduce_fusion
  413.4 0.2 fusion.25
  413.6 0.2 fusion.65
  414.0 0.2 fusion.24
  414.6 0.2 fusion.23
  415.1 0.2 fusion.22
  415.6 0.2 fusion.21
  416.1 0.2 fusion.20
  416.2 0.2 fusion.107
  416.4 0.2 fusion.106
  416.6 0.2 fusion.19
  416.7 0.2 fusion.109
  416.9 0.2 fusion.108
  417.1 0.2 fusion.18
  417.3 0.2 fusion.111
  417.6 0.2 fusion.17
  418.1 0.2 fusion.16
  418.6 0.2 fusion.15
  418.8 0.2 fusion.116
  419.0 0.2 fusion.117
  419.1 0.2 fusion.14
  419.3 0.2 fusion.118
  419.6 1.1 convolution_divide_fusion.1
  420.7 6.7 %fusion.2 = f32[2,32,2048]{2,1,0:T(8,128)} fusion(f32[2,320,32]{1,2,0:T(8,128)S(1)} %convolution_divide_fusion.1, f32[1,2,320,2048]{3,2,1,0:T(8,128)} %param.10, bf16[1,2,320,2048]{3,2,1,0:T(8,128)(2,1)S(1)} %copy-done.1), kind=kOutput, calls=%fused_computation.3 | convolution fusion | flops 505937920 | bytes 8470528 | tf_op jit(solution)/shard_map/mks,mkd->msd/dot_general | solution.py:52
  427.4 41.5 %psum.39 = f32[2,2048]{1,0:T(2,128)S(1)} all-reduce(f32[2,2048]{1,0:T(2,128)S(1)} %bitcast.160), channel_id=1, replica_groups=mesh['rep'=8,'grp'=4] {'rep','grp'}, use_global_device_ids=true, to_apply=%region_9.10 | all-reduce | flops 4096 | bytes 32768 | tf_op jit(solution)/shard_map/psum | solution.py:55
  468.9 0.8 subtract_select_fusion.1
  469.7 86.6 %all-reduce.11.cloned.1.call-done = f32[2,32,2048]{2,1,0:T(8,128)} async-done(((f32[2,32,2048]{2,1,0:T(8,128)}), f32[2,32,2048]{2,1,0:T(8,128)}) %all-reduce.11.cloned.1.call-update) | async-done | bytes 524304 | tf_op jit(solution)/shard_map/psum | solution.py:30
  556.3 5.3 fusion.38
  561.7 6.5 %fusion.10 = f32[1,2,320,2048]{3,2,1,0:T(8,128)} fusion(f32[2,320,2048]{2,1,0:T(8,128)S(1)} %fusion.38, f32[1,2,320,2048]{3,2,1,0:T(8,128)} %param.10, bf16[1,2,320,2048]{3,2,1,0:T(8,128)(2,1)S(1)} %copy-done.1), kind=kLoop, calls=%fused_computation.11 | loop fusion | flops 3932160 | bytes 18350080 | tf_op jit(solution)/shard_map/broadcast_in_dim | solution.py:54
  568.2 9.2 %subtract_select_fusion = (f32[2,64,2048]{2,0,1:T(2,128)S(1)}, f32[2,64,2048]{2,0,1:T(2,128)S(1)}) fusion(f32[2,64,2048]{2,1,0:T(8,128)S(1)} %copy-done.2, pred[2]{0:T(512)(128)(4,1)S(1)} %broadcast_compare_fusion.1, f32[2,64,2048]{2,1,0:T(8,128)S(1)} %copy-done.3, f32[10,64,2048]{2,1,0:T(8,128)S(1)} %bitcast.159, pred[2,12]{1,0:T(4,128)(4,1)S(1)} %get-tuple-element.16), kind=kOutput, calls=%fused_computation.15 | convolution fusion | flops 33030144 | bytes 9437210 | tf_op jit(solution)/shard_map/si,ihd->shd/dot_general | solution.py:69
  577.4 1.6 copy.27
  579.0 1.6 copy.26
  (60 shorter events, 5.1 us)
Async XLA Ops:
  7.2 1.0 copy-start
  7.2 141.3 %copy-start.1 = (bf16[1,2,320,2048]{3,2,1,0:T(8,128)(2,1)S(1)}, bf16[1,2,320,2048]{3,2,1,0:T(8,128)(2,1)}, u32[]{:S(2)}) copy-start(bf16[1,2,320,2048]{3,2,1,0:T(8,128)(2,1)} %param.9) | copy-start | bytes 7864324
  7.2 9.0 %copy-start.7 = (s32[12]{0:T(128)S(1)}, s32[12]{0:T(128)}, u32[]{:S(2)}) copy-start(s32[12]{0:T(128)} %param.13) | copy-start | bytes 148
  7.2 132.3 %all-reduce.5.cloned.1.call-start = ((), (), s32[]{:S(2)}) async-start(), calls=%async_computation | async-start | bytes 196608 | tf_op jit(solution)/shard_map/psum | solution.py:47
  16.1 268.0 %all-reduce.7.cloned.1.call-start = ((), (), s32[]{:S(2)}) async-start(), calls=%async_computation.1 | async-start | bytes 1048576 | tf_op jit(solution)/shard_map/psum | solution.py:30
  155.2 256.8 %all-reduce.9.cloned.1.call-start = ((), (), s32[]{:S(2)}) async-start(), calls=%async_computation.2 | async-start | bytes 196608 | tf_op jit(solution)/shard_map/psum | solution.py:30
  292.4 263.9 %all-reduce.11.cloned.1.call-start = ((), (), s32[]{:S(2)}) async-start(), calls=%async_computation.3 | async-start | bytes 1048576 | tf_op jit(solution)/shard_map/psum | solution.py:30
  417.6 9.8 %copy-start.4 = (f32[1,2,2048]{2,1,0:T(2,128)S(1)}, f32[1,2,2048]{2,1,0:T(2,128)}, u32[]{:S(2)}) copy-start(f32[1,2,2048]{2,1,0:T(2,128)} %param.12) | copy-start | bytes 49156
  417.8 51.1 %copy-start.5 = (f32[2,2048]{1,0:T(2,128)S(1)}, f32[2,2048]{1,0:T(2,128)}, u32[]{:S(2)}) copy-start(f32[2,2048]{1,0:T(2,128)} %param.17) | copy-start | bytes 49156
  417.8 51.1 %copy-start.6 = (f32[2,2048]{1,0:T(2,128)S(1)}, f32[2,2048]{1,0:T(2,128)}, u32[]{:S(2)}) copy-start(f32[2,2048]{1,0:T(2,128)} %param.16) | copy-start | bytes 49156
  561.7 6.5 %copy-start.2 = (f32[2,64,2048]{2,1,0:T(8,128)S(1)}, f32[2,64,2048]{2,1,0:T(8,128)}, u32[]{:S(2)}) copy-start(f32[2,64,2048]{2,1,0:T(8,128)} %param.15) | copy-start | bytes 3145732
  561.7 6.5 %copy-start.3 = (f32[2,64,2048]{2,1,0:T(8,128)S(1)}, f32[2,64,2048]{2,1,0:T(8,128)}, u32[]{:S(2)}) copy-start(f32[2,64,2048]{2,1,0:T(8,128)} %param.14) | copy-start | bytes 3145732
Sparse Core Ops, SparseCore 0:
  16.2 123.2 all-reduce.4
  155.4 128.6 all-reduce.6
  292.5 119.5 all-reduce.8
  427.5 128.8 all-reduce.10
where the time goes:
time: 588 us; the launch traced here: 587 us
  waiting for transfers between devices  458 us (78%)
  matrix products  61.9 us (11%)
  blocking collectives  41.5 us (7%)
  between operations  14.5 us (2%)
  other arithmetic  7.02 us (1%)
    psum x3, waiting for transfers between devices, replicas_total(): return lax.psum(partial_term, ('rep', 'grp'))  335 us
    psum x1, waiting for transfers between devices, local(): p_sum = lax.psum(first_term, ('rep', 'grp'))  123 us
    psum x1, blocking collectives, local(): vec_sum = lax.psum(vec_grads[0], ('rep', 'grp'))  41.5 us
    dot_general x2, matrix products, local(): jnp.einsum('mks,mkd->msd', p_hat, combined, precision=high)  13.4 us
  transfers between devices with their start and end apart: 4, of which 4 were waited for; matrix products, arithmetic and copies ran while one was open for 0% of the time, Pallas kernels for 0%

commit v1 on v0

v1 whole, which is shorter than its diff:
```python
import functools

import jax
import jax.numpy as jnp
from jax import lax
from jax.experimental import pallas as pl
from jax.experimental.pallas import tpu as pltpu
from jax.sharding import PartitionSpec as P

ROOT_ITERS = 12
f32 = jnp.float32
VMEM_LIMIT = 48 * 1024 * 1024
NN = ((1,), (0,))
NT = ((1,), (1,))
TN = ((0,), (0,))


def dot(a, b, dims=NN):
    return lax.dot_general(
        a, b, (dims, ((), ())), precision=lax.Precision.HIGHEST, preferred_element_type=f32
    )


def split3(a):
    high = a.astype(jnp.bfloat16)
    rest = a - high.astype(f32)
    middle = rest.astype(jnp.bfloat16)
    low = (rest - middle.astype(f32)).astype(jnp.bfloat16)
    return high, middle, low


def params():
    return pltpu.CompilerParams(vmem_limit_bytes=VMEM_LIMIT)


def cost(flops, nbytes):
    return pl.CostEstimate(flops=flops, bytes_accessed=nbytes, transcendentals=0)


def outgoing_kernel(place, g_ref, e_ref, o_ref):
    o_ref[0] = g_ref[0, 0].astype(f32) + e_ref[0, 0]


def outgoing(place, grads, errors, blocks, streams, stream):
    rows, cols = grads.shape[2:]
    width = cols // (blocks * streams)

    def source(p, place):
        return (0, 1 - place[0], 0, (place[1] ^ p) * streams + stream)

    return pl.pallas_call(
        outgoing_kernel,
        grid_spec=pltpu.PrefetchScalarGridSpec(
            num_scalar_prefetch=1,
            grid=(blocks,),
            in_specs=[pl.BlockSpec((1, 1, rows, width), source)] * 2,
            out_specs=pl.BlockSpec((1, rows, width), lambda p, place: (p, 0, 0)),
        ),
        out_shape=jax.ShapeDtypeStruct((blocks, rows, width), f32),
        compiler_params=params(),
        cost_estimate=cost(blocks * rows * width, blocks * rows * width * 10),
        name=f"outgoing{stream}",
    )(place, grads, errors)


def pair_kernel(place, g_ref, e_ref, r_ref, w_ref, send_ref, keep_ref, p_ref, *, half):
    step = pl.program_id(0)
    total = g_ref[0, 0].astype(f32) + e_ref[0, 0] + r_ref[0]
    term = dot(w_ref[0], total, NT)

    @pl.when(step < half)
    def _():
        send_ref[0] = total

    @pl.when(step >= half)
    def _():
        keep_ref[0] = total

    @pl.when(step == 0)
    def _():
        p_ref[...] = term

    @pl.when(step > 0)
    def _():
        p_ref[...] += term


def pair(place, grads, errors, received, warm_start, blocks, streams, stream, bit):
    rows, cols = grads.shape[2:]
    rank = warm_start.shape[1]
    width = cols // (blocks * streams)
    half = blocks // 2

    def position(i):
        goes = jnp.where(i < half, 1, 0)
        h = lax.rem(i, half)
        low = h & ((1 << bit) - 1)
        return ((h >> bit) << (bit + 1)) | (goes << bit) | low

    def column(i, place):
        return (place[1] ^ position(i)) * streams + stream

    def source(i, place):
        return (0, place[0], 0, column(i, place))

    return pl.pallas_call(
        functools.partial(pair_kernel, half=half),
        grid_spec=pltpu.PrefetchScalarGridSpec(
            num_scalar_prefetch=1,
            grid=(blocks,),
            in_specs=[
                pl.BlockSpec((1, 1, rows, width), source),
                pl.BlockSpec((1, 1, rows, width), source),
                pl.BlockSpec((1, rows, width), lambda i, place: (position(i), 0, 0)),
                pl.BlockSpec((1, rank, width), lambda i, place: (place[0], 0, column(i, place))),
            ],
            out_specs=[
                pl.BlockSpec((1, rows, width), lambda i, place: (jnp.minimum(i, half - 1), 0, 0)),
                pl.BlockSpec((1, rows, width), lambda i, place: (jnp.maximum(i - half, 0), 0, 0)),
                pl.BlockSpec((rank, rows), lambda i, place: (0, 0)),
            ],
        ),
        out_shape=[
            jax.ShapeDtypeStruct((half, rows, width), f32),
            jax.ShapeDtypeStruct((half, rows, width), f32),
            jax.ShapeDtypeStruct((rank, rows), f32),
        ],
        compiler_params=params(),
        cost_estimate=cost(12 * rank * rows * cols // streams, blocks * rows * width * 14),
        name=f"pair{stream}",
    )(place, grads, errors, received, warm_start)


def whole_call(kernel, shapes, name, flops, *operands):
    nbytes = 4 * sum(o.size for o in operands)
    return pl.pallas_call(
        kernel,
        out_shape=[jax.ShapeDtypeStruct(s, f32) for s in shapes],
        compiler_params=params(),
        cost_estimate=cost(flops, nbytes),
        name=name,
    )(*operands)


def project_kernel(*refs, streams, count):
    x_ref, parts, (s_ref, v_ref) = refs[0], refs[1 : 1 + 2 * streams], refs[1 + 2 * streams :]
    rows = s_ref.shape[0]
    width = s_ref.shape[1] // streams
    factor = x_ref[:, :rows] / count
    for s in range(streams):
        block = parts[2 * s][...] + parts[2 * s + 1][...]
        where = slice(s * width, (s + 1) * width)
        s_ref[:, where] = block
        v_ref[:, where] = dot(factor, block) / count


def lift_kernel(v_ref, s_ref, u_ref, *, count):
    u_ref[...] = dot(v_ref[...], s_ref[...], NT) / count


def lower_kernel(u_ref, s_ref, v_ref, *, count):
    v_ref[...] = dot(u_ref[...], s_ref[...]) / count


def inverse_root(gram):
    rank = gram.shape[0]
    eye = (
        lax.broadcasted_iota(jnp.int32, (rank, rank), 0)
        == lax.broadcasted_iota(jnp.int32, (rank, rank), 1)
    ).astype(f32)
    spread = jnp.sqrt(jnp.sum(gram * gram, keepdims=True))
    left = gram / spread
    right = eye
    for sweep in range(ROOT_ITERS):
        if sweep == 0:
            middle = 1.5 * eye - 0.5 * left
            right = middle
        else:
            middle = 1.5 * eye - 0.5 * dot(right, left)
            right = dot(middle, right)
        if sweep + 1 < ROOT_ITERS:
            left = dot(left, middle)
    return right / jnp.sqrt(spread)


def first_root_kernel(x_ref, a_ref, *, rows, count):
    factor = x_ref[:, :rows] / count
    a_ref[...] = inverse_root(dot(factor, factor, NT))


def second_root_kernel(a_ref, u_ref, f_ref):
    a = a_ref[...]
    u = u_ref[...]
    rank, rows = u.shape
    gram = dot(a, dot(dot(u, u, NT), a), TN)
    both = dot(a, inverse_root(gram))
    f_ref[...] = jnp.zeros(f_ref.shape, f32)
    f_ref[:, :rows] = dot(both, u, TN)
    f_ref[:, rows : rows + rank] = both


def final_kernel(place, g_ref, e_ref, v0_ref, v1_ref, f0_ref, f1_ref, mm_ref, mw_ref,
                 n_ref, mo_ref, wo_ref, approx, left, *, head):
    rows, width = g_ref.shape[2:]
    rank = f0_ref.shape[0]

    @pl.when(pl.program_id(0) == 0)
    def _():
        for i, f_ref in enumerate((f0_ref, f1_ref)):
            high, middle, low = split3(f_ref[:, :rows].T)
            left[i] = jnp.concatenate([high, high, middle, high, low, middle], axis=1)

    for i, (v_ref, f_ref) in enumerate(((v0_ref, f0_ref), (v1_ref, f1_ref))):
        m = place[0] if i == 0 else 1 - place[0]
        q = dot(f_ref[:, rows : rows + rank], v_ref[0], TN)
        high, middle, low = split3(q)
        right = jnp.concatenate([high, middle, high, low, high, middle], axis=0)
        product = jnp.dot(left[i], right, preferred_element_type=f32)
        approx[pl.ds(m * rows, rows), :] = product
        n_ref[0, m] = g_ref[0, m].astype(f32) + e_ref[0, m] - product
    for slot in range(mm_ref.shape[0]):
        item = place[2 + slot]

        @pl.when(item >= 0)
        def _():
            block = approx[pl.ds(jnp.maximum(item, 0) * head, head), :]
            moment = 0.9 * mm_ref[slot] + block
            mo_ref[slot] = moment
            wo_ref[slot] = mw_ref[slot] - 0.5 * moment

        @pl.when(item < 0)
        def _():
            mo_ref[slot] = mm_ref[slot]
            wo_ref[slot] = mw_ref[slot]


def final(place, grads, errors, own_v, other_v, own_f, other_f, mat_momentum, mat_weights):
    blocks, rank, width = own_v.shape
    matrices, rows, cols = grads.shape[1:]
    slots, head = mat_momentum.shape[:2]

    def here(b, place):
        return (0, 0, 0, b)

    def there(b, place):
        return (place[1] ^ b, 0, 0)

    def whole(b, place):
        return (0, 0)

    def bank(b, place):
        return (0, 0, b)

    big = pl.BlockSpec((1, matrices, rows, width), here)
    small = pl.BlockSpec((slots, head, width), bank)
    return pl.pallas_call(
        functools.partial(final_kernel, head=head),
        grid_spec=pltpu.PrefetchScalarGridSpec(
            num_scalar_prefetch=1,
            grid=(blocks,),
            in_specs=[
                big,
                big,
                pl.BlockSpec((1, rank, width), there),
                pl.BlockSpec((1, rank, width), there),
                pl.BlockSpec(own_f.shape, whole),
                pl.BlockSpec(other_f.shape, whole),
                small,
                small,
            ],
            out_specs=[big, small, small],
            scratch_shapes=[
                pltpu.VMEM((matrices * rows, width), f32),
                pltpu.VMEM((matrices, rows, 6 * rank), jnp.bfloat16),
            ],
        ),
        out_shape=[
            jax.ShapeDtypeStruct(errors.shape, f32),
            jax.ShapeDtypeStruct(mat_momentum.shape, f32),
            jax.ShapeDtypeStruct(mat_weights.shape, f32),
        ],
        compiler_params=params(),
        cost_estimate=cost(2 * matrices * rows * cols * 6 * rank, 18_000_000),
        name="final",
    )(place, grads, errors, own_v, other_v, own_f, other_f, mat_momentum, mat_weights)


def exchange(a, axis, mask):
    return lax.ppermute(a, axis, [(i, i ^ mask) for i in range(lax.axis_size(axis))])


def local(grads, errors, warm_start, vec_grads, owners, mat_momentum, mat_weights, vec_momentum, vec_weights):
    reps, groups = lax.axis_size("rep"), lax.axis_size("grp")
    count = float(reps * groups)
    blocks = reps // 2
    bits = blocks.bit_length() - 1
    matrices, rows, cols = grads.shape[1:]
    rank = warm_start.shape[1]
    streams = 2 if (cols // blocks) % 256 == 0 else 1
    rep = lax.axis_index("rep")
    core, spot = rep % 2, rep // 2
    device = rep * groups + lax.axis_index("grp")

    items = owners.shape[0]
    slots, head = mat_momentum.shape[:2]
    earlier = jnp.arange(items)[None, :] < jnp.arange(items)[:, None]
    same = owners[None, :] == owners[:, None]
    slot = jnp.sum((earlier & same).astype(jnp.int32), axis=1)
    match = (owners[None, :] == device) & (slot[None, :] == jnp.arange(slots)[:, None])
    head_items = matrices * (rows // head)
    mat_match = match[:, :head_items]
    chosen = jnp.max(jnp.where(mat_match, jnp.arange(head_items)[None, :], -1), axis=1)
    place = jnp.concatenate([jnp.stack([core, spot]), chosen]).astype(jnp.int32)

    def z_sum(a):
        mask = 1
        while mask < groups:
            a = a + exchange(a, "grp", mask)
            mask *= 2
        return a

    def plane_sum(a):
        for bit in range(bits):
            a = a + exchange(a, "rep", 2 << bit)
        return a

    sent = [outgoing(place, grads, errors, blocks, streams, s) for s in range(streams)]
    received = [exchange(a, "rep", 1) for a in sent]
    vec_own = lax.dynamic_index_in_dim(vec_grads[0], core, 0, keepdims=False)
    vec_out = lax.dynamic_index_in_dim(vec_grads[0], 1 - core, 0, keepdims=False)
    vec_pair = vec_own + exchange(vec_out, "rep", 1)

    factor = None
    kept = []
    for s in range(streams):
        order = list(range(bits)) if s == 0 else list(range(bits))[::-1]
        send, keep, term = pair(
            place, grads, errors, received[s], warm_start, blocks, streams, s, order[0]
        )
        factor = term if factor is None else factor + term
        kept.append((order, keep, exchange(send, "rep", 2 << order[0])))
    packed = jnp.concatenate([factor, vec_pair.reshape(rank, cols // rank)], axis=1)
    packed = plane_sum(z_sum(packed))
    parts = []
    for order, keep, arrived in kept:
        left = sorted(order[1:])
        for bit in order[1:]:
            where = left.index(bit)
            left.remove(bit)
            shape = keep.shape
            view = (-1, 2, 1 << where) + shape[1:]
            a, b = keep.reshape(view), arrived.reshape(view)
            goes = a[:, 1] + b[:, 1]
            keep = (a[:, 0] + b[:, 0]).reshape((-1,) + shape[1:])
            arrived = exchange(goes.reshape((-1,) + shape[1:]), "rep", 2 << bit)
        parts += [keep[0], arrived[0]]

    width = cols // blocks
    kept_sum, v = whole_call(
        functools.partial(project_kernel, streams=streams, count=count),
        [(rows, width), (rank, width)], "project", 12 * rank * rows * width, packed, *parts,
    )
    (first_root,) = whole_call(
        functools.partial(first_root_kernel, rows=rows, count=count),
        [(rank, rank)], "root1", 24 * 12 * rank**3, packed,
    )
    v = z_sum(v)
    (u,) = whole_call(
        functools.partial(lift_kernel, count=count), [(rank, rows)], "lift", 12 * rank * rows * width, v, kept_sum,
    )
    u = plane_sum(z_sum(u))
    (v,) = whole_call(
        functools.partial(lower_kernel, count=count), [(rank, width)], "lower", 12 * rank * rows * width, u, kept_sum,
    )
    (own_f,) = whole_call(
        second_root_kernel, [packed.shape], "root2", 24 * 12 * rank**3, first_root, u,
    )
    v = z_sum(v)[None]
    for bit in range(bits):
        v = jnp.concatenate([v, exchange(v, "rep", 2 << bit)], axis=0)
    other_v = exchange(v, "rep", 1)
    other_f = exchange(own_f, "rep", 1)
    new_errors, mat_momentum_out, mat_weights_out = final(
        place, grads, errors, v, other_v, own_f, other_f, mat_momentum, mat_weights
    )

    vec_own = packed[:, rows:].reshape(1, cols) / count
    vec_other = exchange(vec_own, "rep", 1)
    vec_avg = jnp.where(core == 0, jnp.concatenate([vec_own, vec_other]), jnp.concatenate([vec_other, vec_own]))
    vec_match = match[:, head_items:]
    has_vec = jnp.any(vec_match, axis=1)[:, None]
    picked = sum(jnp.where(vec_match[:, i : i + 1], vec_avg[i : i + 1], 0.0) for i in range(items - head_items))
    vec_moment = 0.9 * vec_momentum + picked
    vec_momentum_out = jnp.where(has_vec, vec_moment, vec_momentum)
    vec_weights_out = jnp.where(has_vec, vec_weights - 0.5 * vec_moment, vec_weights)
    return (new_errors, mat_momentum_out, mat_weights_out, vec_momentum_out, vec_weights_out)


def solution(mesh):
    both = ("rep", "grp")
    return jax.shard_map(
        local,
        mesh=mesh,
        in_specs=(
            P(both, None, None, None),
            P(both, None, None, None),
            P(),
            P(both, None, None),
            P(),
            P(both, None, None),
            P(both, None, None),
            P(both, None),
            P(both, None),
        ),
        out_specs=(
            P(both, None, None, None),
            P(both, None, None),
            P(both, None, None),
            P(both, None),
            P(both, None),
        ),
        check_vma=False,
    )
```

time: 588 us -> 119 us (0.20)
  waiting for transfers between devices: 458 us -> 37.5 us
  matrix products: 61.9 us -> 0 us
  blocking collectives: 41.5 us -> 0 us
  starting transfers between devices: 0.34 us -> 38.7 us
  Pallas kernels: 0 us -> 32.4 us
  between operations: 14.5 us -> 0.91 us
    psum x4 -> x0, waiting for transfers between devices: 458 us -> none  [the longest x3 335 us: replicas_total(): return lax.psum(partial_term, ('rep', 'grp'))]
    dot_general x81 -> x0, matrix products: 61.9 us -> none  [the longest x2 13.4 us: local(): jnp.einsum('mks,mkd->msd', p_hat, combined, precision=high)]
    psum x1 -> x0, blocking collectives: 41.5 us -> none  [local(): vec_sum = lax.psum(vec_grads[0], ('rep', 'grp'))]
    ppermute x0 -> x24, starting transfers between devices: none -> 38.7 us  [exchange(): lax.ppermute(a, axis, [(i, i ^ mask) for i in range(lax.axis_size(axis))])]
    ppermute x0 -> x24, waiting for transfers between devices: none -> 37.5 us  [exchange(): lax.ppermute(a, axis, [(i, i ^ mask) for i in range(lax.axis_size(axis))])]
    pallas_call x0 -> x10, Pallas kernels: none -> 32.4 us  [the longest x5 10.4 us: whole_call(): pl.pallas_call(kernel, out_shape=[jax.ShapeDtypeStruct(s, f32) for s in s...]
    broadcast_in_dim x1, other arithmetic: 6.5 us -> 0.01 us  [local(): v = z_sum(v)[None]]
  transfers between devices with their start and end apart: 4 -> 24, of which waited for: 4 -> 15; matrix products, arithmetic and copies ran while one was open for 0% -> 3% of each run, Pallas kernels for 0% -> 17%
where the time goes in v1:
time: 119 us
  starting transfers between devices  38.7 us (33%)
  waiting for transfers between devices  37.5 us (32%)
  Pallas kernels  32.4 us (27%)
  other arithmetic  4.8 us (4%)
  local copies, waits for them, and re-layouts  4.41 us (4%)
    ppermute x24, starting transfers between devices, exchange(): lax.ppermute(a, axis, [(i, i ^ mask) for i in range(lax.axis_size(axis))])  38.7 us
    ppermute x24, waiting for transfers between devices, exchange(): lax.ppermute(a, axis, [(i, i ^ mask) for i in range(lax.axis_size(axis))])  37.5 us
    pallas_call x5, Pallas kernels, whole_call(): pl.pallas_call(kernel, out_shape=[jax.ShapeDtypeStruct(s, f32) for s in s...  10.4 us
    pallas_call x1, Pallas kernels, final(): pl.pallas_call(functools.partial(final_kernel, head=head), grid_spec=pltp...  8.43 us
    pallas_call x2, Pallas kernels, pair(): pl.pallas_call(functools.partial(pair_kernel, half=half), grid_spec=pltpu...  8.06 us
    pallas_call x2, Pallas kernels, outgoing(): pl.pallas_call(outgoing_kernel, grid_spec=pltpu.PrefetchScalarGridSpec(nu...  5.57 us
    unnamed x16, local copies, waits for them, and re-layouts  4.22 us
  transfers between devices with their start and end apart: 24, of which 15 were waited for; matrix products, arithmetic and copies ran while one was open for 3% of the time, Pallas kernels for 17%

profile of v1, /device:TPU:0, one launch (start us, length us, event | category | flops | bytes accessed | tf_op | source)
XLA Modules:
  0.0 118.7 jit_solution(13788323626329751494)
XLA Ops:
  0.6 0.9 convert_reduce_fusion
  1.6 0.7 broadcast_compare_fusion
  2.2 0.1 fusion.5
  2.3 0.1 pad_add_fusion.place
  2.4 1.7 %copy-done = bf16[1,2,320,2048]{3,2,1,0:T(8,128)(2,1)S(1)} copy-done((bf16[1,2,320,2048]{3,2,1,0:T(8,128)(2,1)S(1)}, bf16[1,2,320,2048]{3,2,1,0:T(8,128)(2,1)}, u32[]{:S(2)}) %copy-start) | copy-done | bytes 2621464
  4.2 2.8 %outgoing0.1 = f32[4,320,256]{2,1,0:T(8,128)S(1)} custom-call(s32[4]{0:T(128)S(1)} %pad_add_fusion.place, bf16[1,2,320,2048]{3,2,1,0:T(8,128)(2,1)S(1)} %copy-done, f32[1,2,320,2048]{3,2,1,0:T(8,128)} %e_ref.9), custom_call_target="tpu_custom_call" | custom-call | flops 327680 | bytes 3276800 | tf_op jit(solution)/shard_map/outgoing0/pallas_call | solution.py:51
  7.0 0.5 collective-permute-start
  7.5 2.8 %outgoing1.1 = f32[4,320,256]{2,1,0:T(8,128)S(1)} custom-call(s32[4]{0:T(128)S(1)} %pad_add_fusion.place, bf16[1,2,320,2048]{3,2,1,0:T(8,128)(2,1)S(1)} %copy-done, f32[1,2,320,2048]{3,2,1,0:T(8,128)} %e_ref.9), custom_call_target="tpu_custom_call" | custom-call | flops 327680 | bytes 3276800 | tf_op jit(solution)/shard_map/outgoing1/pallas_call | solution.py:51
  10.3 0.1 collective-permute-start.1
  10.4 4.0 %pair0.1 = (f32[2,320,256]{2,1,0:T(8,128)S(1)}, f32[2,320,256]{2,1,0:T(8,128)S(1)}, f32[32,320]{1,0:T(8,128)S(1)}) custom-call(s32[4]{0:T(128)S(1)} %pad_add_fusion.place, bf16[1,2,320,2048]{3,2,1,0:T(8,128)(2,1)S(1)} %copy-done, f32[1,2,320,2048]{3,2,1,0:T(8,128)} %e_ref.9, f32[4,320,256]{2,1,0:T(8,128)S(1)} %collective-permute-done.r_ref, ...), custom_call_target="tpu_custom_call" | custom-call | flops 125829120 | bytes 4587520 | tf_op jit(solution)/shard_map/pair0/pallas_call | solution.py:106
  14.5 3.0 %collective-permute-start.7 = (f32[2,320,256]{2,1,0:T(8,128)S(1)}, f32[2,320,256]{2,1,0:T(8,128)}, u32[]{:S(2)}, u32[]{:S(2)}) collective-permute-start(f32[2,320,256]{2,1,0:T(8,128)S(1)} %get-tuple-element.19), channel_id=1, source_target_pairs={{0,8},{4,12},{8,0},{12,4},{16,24},{20,28},{24,16},{28,20},{1,9},{5... | collective-permute-start | bytes 1966088 | tf_op jit(solution)/shard_map/ppermute | solution.py:289
  17.5 4.0 %pair1.1 = (f32[2,320,256]{2,1,0:T(8,128)S(1)}, f32[2,320,256]{2,1,0:T(8,128)S(1)}, f32[32,320]{1,0:T(8,128)S(1)}) custom-call(s32[4]{0:T(128)S(1)} %pad_add_fusion.place, bf16[1,2,320,2048]{3,2,1,0:T(8,128)(2,1)S(1)} %copy-done, f32[1,2,320,2048]{3,2,1,0:T(8,128)} %e_ref.9, f32[4,320,256]{2,1,0:T(8,128)S(1)} %collective-permute-done.1.r_ref, ...), custom_call_target="tpu_custom_call" | custom-call | flops 125829120 | bytes 4587520 | tf_op jit(solution)/shard_map/pair1/pallas_call | solution.py:106
  21.5 1.6 %collective-permute-start.9 = (f32[2,320,256]{2,1,0:T(8,128)S(1)}, f32[2,320,256]{2,1,0:T(8,128)S(1)}, u32[]{:S(2)}, u32[]{:S(2)}) collective-permute-start(f32[2,320,256]{2,1,0:T(8,128)S(1)} %get-tuple-element.21), channel_id=1, source_target_pairs={{0,16},{4,20},{8,24},{12,28},{16,0},{20,4},{24,8},{28,12},{1,17},{... | collective-permute-start | bytes 1966088 | tf_op jit(solution)/shard_map/ppermute | solution.py:289
  23.1 0.1 collective-permute-start.2
  23.2 1.2 collective-permute-done.2
  24.4 0.1 reshape.114
  24.4 0.1 pad_maximum_fusion.2
  24.5 1.6 %collective-permute-start.3 = (f32[32,384]{1,0:T(8,128)S(1)}, f32[32,384]{1,0:T(8,128)S(1)}, u32[]{:S(2)}, u32[]{:S(2)}) collective-permute-start(f32[32,384]{1,0:T(8,128)S(1)} %pad_maximum_fusion.2), channel_id=1, source_target_pairs={{0,1},{1,0},{2,3},{3,2},{4,5},{5,4},{6,7},{7,6},{8,9},{9,8},{10,11... | collective-permute-start | bytes 147464 | tf_op jit(solution)/shard_map/ppermute | solution.py:289
  26.1 6.4 %collective-permute-done.7 = f32[2,320,256]{2,1,0:T(8,128)} collective-permute-done((f32[2,320,256]{2,1,0:T(8,128)S(1)}, f32[2,320,256]{2,1,0:T(8,128)}, u32[]{:S(2)}, u32[]{:S(2)}) %collective-permute-start.7) | collective-permute-done | bytes 655392 | tf_op jit(solution)/shard_map/ppermute | solution.py:289
  32.5 1.2 fusion.2
  33.6 1.8 %collective-permute-start.8 = (f32[1,320,256]{2,1,0:T(8,128)S(1)}, f32[1,320,256]{2,1,0:T(8,128)S(1)}, u32[]{:S(2)}, u32[]{:S(2)}) collective-permute-start(f32[1,320,256]{2,1,0:T(8,128)S(1)} %get-tuple-element.31), channel_id=1, source_target_pairs={{0,16},{4,20},{8,24},{12,28},{16,0},{20,4},{24,8},{28,12},{1,17},{... | collective-permute-start | bytes 983048 | tf_op jit(solution)/shard_map/ppermute | solution.py:289
  35.5 3.7 %collective-permute-done.9 = f32[2,320,256]{2,1,0:T(8,128)S(1)} collective-permute-done((f32[2,320,256]{2,1,0:T(8,128)S(1)}, f32[2,320,256]{2,1,0:T(8,128)S(1)}, u32[]{:S(2)}, u32[]{:S(2)}) %collective-permute-start.9) | collective-permute-done | bytes 655392 | tf_op jit(solution)/shard_map/ppermute | solution.py:289
  39.2 0.1 fusion
  39.3 0.1 collective-permute-start.10
  39.4 0.1 fusion.7
  39.5 3.1 %collective-permute-start.4 = (f32[32,384]{1,0:T(8,128)S(1)}, f32[32,384]{1,0:T(8,128)S(1)}, u32[]{:S(2)}, u32[]{:S(2)}) collective-permute-start(f32[32,384]{1,0:T(8,128)S(1)} %fusion.7), channel_id=1, source_target_pairs={{0,2},{1,3},{2,0},{3,1},{4,6},{5,7},{6,4},{7,5},{8,10},{9,11},{10,... | collective-permute-start | bytes 147464 | tf_op jit(solution)/shard_map/ppermute | solution.py:289
  42.6 2.1 %collective-permute-done.4 = f32[32,384]{1,0:T(8,128)S(1)} collective-permute-done((f32[32,384]{1,0:T(8,128)S(1)}, f32[32,384]{1,0:T(8,128)S(1)}, u32[]{:S(2)}, u32[]{:S(2)}) %collective-permute-start.4) | collective-permute-done | bytes 49184 | tf_op jit(solution)/shard_map/ppermute | solution.py:289
  44.6 1.9 %collective-permute-start.5 = (f32[32,384]{1,0:T(8,128)S(1)}, f32[32,384]{1,0:T(8,128)S(1)}, u32[]{:S(2)}, u32[]{:S(2)}) collective-permute-start(f32[32,384]{1,0:T(8,128)S(1)} %add.119), channel_id=1, source_target_pairs={{0,8},{4,12},{8,0},{12,4},{16,24},{20,28},{24,16},{28,20},{1,9},{5... | collective-permute-start | bytes 147464 | tf_op jit(solution)/shard_map/ppermute | solution.py:289
  46.5 2.3 %collective-permute-done.5 = f32[32,384]{1,0:T(8,128)S(1)} collective-permute-done((f32[32,384]{1,0:T(8,128)S(1)}, f32[32,384]{1,0:T(8,128)S(1)}, u32[]{:S(2)}, u32[]{:S(2)}) %collective-permute-start.5) | collective-permute-done | bytes 49184 | tf_op jit(solution)/shard_map/ppermute | solution.py:289
  48.8 1.9 %collective-permute-start.6 = (f32[32,384]{1,0:T(8,128)S(1)}, f32[32,384]{1,0:T(8,128)S(1)}, u32[]{:S(2)}, u32[]{:S(2)}) collective-permute-start(f32[32,384]{1,0:T(8,128)S(1)} %add.120), channel_id=1, source_target_pairs={{0,16},{4,20},{8,24},{12,28},{16,0},{20,4},{24,8},{28,12},{1,17},{... | collective-permute-start | bytes 147464 | tf_op jit(solution)/shard_map/ppermute | solution.py:289
  50.7 2.2 %collective-permute-done.6 = f32[32,384]{1,0:T(8,128)S(1)} collective-permute-done((f32[32,384]{1,0:T(8,128)S(1)}, f32[32,384]{1,0:T(8,128)S(1)}, u32[]{:S(2)}, u32[]{:S(2)}) %collective-permute-start.6) | collective-permute-done | bytes 49184 | tf_op jit(solution)/shard_map/ppermute | solution.py:289
  53.0 0.5 project.1
  53.5 2.0 %collective-permute-start.11 = (f32[32,512]{1,0:T(8,128)S(1)}, f32[32,512]{1,0:T(8,128)S(1)}, u32[]{:S(2)}, u32[]{:S(2)}) collective-permute-start(f32[32,512]{1,0:T(8,128)S(1)} %get-tuple-element.22), channel_id=1, source_target_pairs={{0,1},{1,0},{2,3},{3,2},{4,5},{5,4},{6,7},{7,6},{8,9},{9,8},{10,11... | collective-permute-start | bytes 196616 | tf_op jit(solution)/shard_map/ppermute | solution.py:289
  55.5 2.4 %collective-permute-done.11 = f32[32,512]{1,0:T(8,128)S(1)} collective-permute-done((f32[32,512]{1,0:T(8,128)S(1)}, f32[32,512]{1,0:T(8,128)S(1)}, u32[]{:S(2)}, u32[]{:S(2)}) %collective-permute-start.11) | collective-permute-done | bytes 65568 | tf_op jit(solution)/shard_map/ppermute | solution.py:289
  57.8 3.0 %collective-permute-start.12 = (f32[32,512]{1,0:T(8,128)S(1)}, f32[32,512]{1,0:T(8,128)S(1)}, u32[]{:S(2)}, u32[]{:S(2)}) collective-permute-start(f32[32,512]{1,0:T(8,128)S(1)} %add.130), channel_id=1, source_target_pairs={{0,2},{1,3},{2,0},{3,1},{4,6},{5,7},{6,4},{7,5},{8,10},{9,11},{10,... | collective-permute-start | bytes 196616 | tf_op jit(solution)/shard_map/ppermute | solution.py:289
  60.9 2.2 %collective-permute-done.12 = f32[32,512]{1,0:T(8,128)S(1)} collective-permute-done((f32[32,512]{1,0:T(8,128)S(1)}, f32[32,512]{1,0:T(8,128)S(1)}, u32[]{:S(2)}, u32[]{:S(2)}) %collective-permute-start.12) | collective-permute-done | bytes 65568 | tf_op jit(solution)/shard_map/ppermute | solution.py:289
  63.2 0.7 lift.1
  63.9 2.5 %collective-permute-start.13 = (f32[32,320]{1,0:T(8,128)S(1)}, f32[32,320]{1,0:T(8,128)S(1)}, u32[]{:S(2)}, u32[]{:S(2)}) collective-permute-start(f32[32,320]{1,0:T(8,128)S(1)} %lift.1), channel_id=1, source_target_pairs={{0,1},{1,0},{2,3},{3,2},{4,5},{5,4},{6,7},{7,6},{8,9},{9,8},{10,11... | collective-permute-start | bytes 122888 | tf_op jit(solution)/shard_map/ppermute | solution.py:289
  66.3 2.1 %collective-permute-done.13 = f32[32,320]{1,0:T(8,128)S(1)} collective-permute-done((f32[32,320]{1,0:T(8,128)S(1)}, f32[32,320]{1,0:T(8,128)S(1)}, u32[]{:S(2)}, u32[]{:S(2)}) %collective-permute-start.13) | collective-permute-done | bytes 40992 | tf_op jit(solution)/shard_map/ppermute | solution.py:289
  68.4 3.6 %collective-permute-start.14 = (f32[32,320]{1,0:T(8,128)S(1)}, f32[32,320]{1,0:T(8,128)S(1)}, u32[]{:S(2)}, u32[]{:S(2)}) collective-permute-start(f32[32,320]{1,0:T(8,128)S(1)} %add.132), channel_id=1, source_target_pairs={{0,2},{1,3},{2,0},{3,1},{4,6},{5,7},{6,4},{7,5},{8,10},{9,11},{10,... | collective-permute-start | bytes 122888 | tf_op jit(solution)/shard_map/ppermute | solution.py:289
  72.0 2.1 %collective-permute-done.14 = f32[32,320]{1,0:T(8,128)S(1)} collective-permute-done((f32[32,320]{1,0:T(8,128)S(1)}, f32[32,320]{1,0:T(8,128)S(1)}, u32[]{:S(2)}, u32[]{:S(2)}) %collective-permute-start.14) | collective-permute-done | bytes 40992 | tf_op jit(solution)/shard_map/ppermute | solution.py:289
  74.1 1.5 %collective-permute-start.15 = (f32[32,320]{1,0:T(8,128)S(1)}, f32[32,320]{1,0:T(8,128)S(1)}, u32[]{:S(2)}, u32[]{:S(2)}) collective-permute-start(f32[32,320]{1,0:T(8,128)S(1)} %add.133), channel_id=1, source_target_pairs={{0,8},{4,12},{8,0},{12,4},{16,24},{20,28},{24,16},{28,20},{1,9},{5... | collective-permute-start | bytes 122888 | tf_op jit(solution)/shard_map/ppermute | solution.py:289
  75.6 2.6 %collective-permute-done.15 = f32[32,320]{1,0:T(8,128)S(1)} collective-permute-done((f32[32,320]{1,0:T(8,128)S(1)}, f32[32,320]{1,0:T(8,128)S(1)}, u32[]{:S(2)}, u32[]{:S(2)}) %collective-permute-start.15) | collective-permute-done | bytes 40992 | tf_op jit(solution)/shard_map/ppermute | solution.py:289
  78.3 1.6 %collective-permute-start.16 = (f32[32,320]{1,0:T(8,128)S(1)}, f32[32,320]{1,0:T(8,128)S(1)}, u32[]{:S(2)}, u32[]{:S(2)}) collective-permute-start(f32[32,320]{1,0:T(8,128)S(1)} %add.134), channel_id=1, source_target_pairs={{0,16},{4,20},{8,24},{12,28},{16,0},{20,4},{24,8},{28,12},{1,17},{... | collective-permute-start | bytes 122888 | tf_op jit(solution)/shard_map/ppermute | solution.py:289
  79.8 0.1 slice_multiply_fusion
  79.9 0.1 div.21
  80.0 2.4 %collective-permute-done.16 = f32[32,320]{1,0:T(8,128)S(1)} collective-permute-done((f32[32,320]{1,0:T(8,128)S(1)}, f32[32,320]{1,0:T(8,128)S(1)}, u32[]{:S(2)}, u32[]{:S(2)}) %collective-permute-start.16) | collective-permute-done | bytes 40992 | tf_op jit(solution)/shard_map/ppermute | solution.py:289
  82.4 0.5 lower.1
  82.9 2.1 %collective-permute-start.17 = (f32[32,512]{1,0:T(8,128)S(1)}, f32[32,512]{1,0:T(8,128)S(1)}, u32[]{:S(2)}, u32[]{:S(2)}) collective-permute-start(f32[32,512]{1,0:T(8,128)S(1)} %lower.1), channel_id=1, source_target_pairs={{0,1},{1,0},{2,3},{3,2},{4,5},{5,4},{6,7},{7,6},{8,9},{9,8},{10,11... | collective-permute-start | bytes 196616 | tf_op jit(solution)/shard_map/ppermute | solution.py:289
  85.0 4.0 %root1.1.a_ref = f32[32,32]{1,0:T(8,128)S(1)} custom-call(f32[32,384]{1,0:T(8,128)S(1)} %add.121.refs_0_.x_ref), custom_call_target="tpu_custom_call" | custom-call | flops 9437184 | bytes 49152 | tf_op jit(solution)/shard_map/root1/pallas_call | solution.py:136
  89.0 3.0 %collective-permute-start.18 = (f32[32,512]{1,0:T(8,128)S(1)}, f32[32,512]{1,0:T(8,128)S(1)}, u32[]{:S(2)}, u32[]{:S(2)}) collective-permute-start(f32[32,512]{1,0:T(8,128)S(1)} %add.136), channel_id=1, source_target_pairs={{0,2},{1,3},{2,0},{3,1},{4,6},{5,7},{6,4},{7,5},{8,10},{9,11},{10,... | collective-permute-start | bytes 196616 | tf_op jit(solution)/shard_map/ppermute | solution.py:289
  92.1 2.6 %collective-permute-done.18 = f32[32,512]{1,0:T(8,128)S(1)} collective-permute-done((f32[32,512]{1,0:T(8,128)S(1)}, f32[32,512]{1,0:T(8,128)S(1)}, u32[]{:S(2)}, u32[]{:S(2)}) %collective-permute-start.18) | collective-permute-done | bytes 65568 | tf_op jit(solution)/shard_map/ppermute | solution.py:289
  94.6 1.5 %collective-permute-start.19 = (f32[1,32,512]{2,1,0:T(8,128)S(1)}, f32[1,32,512]{2,1,0:T(8,128)S(1)}, u32[]{:S(2)}, u32[]{:S(2)}) collective-permute-start(f32[1,32,512]{2,1,0:T(8,128)S(1)} %add_bitcast_fusion), channel_id=1, source_target_pairs={{0,8},{4,12},{8,0},{12,4},{16,24},{20,28},{24,16},{28,20},{1,9},{5... | collective-permute-start | bytes 196616 | tf_op jit(solution)/shard_map/ppermute | solution.py:289
  96.2 2.8 %collective-permute-done.19 = f32[1,32,512]{2,1,0:T(8,128)S(1)} collective-permute-done((f32[1,32,512]{2,1,0:T(8,128)S(1)}, f32[1,32,512]{2,1,0:T(8,128)S(1)}, u32[]{:S(2)}, u32[]{:S(2)}) %collective-permute-start.19) | collective-permute-done | bytes 65568 | tf_op jit(solution)/shard_map/ppermute | solution.py:289
  99.0 1.6 %collective-permute-start.20 = (f32[2,32,512]{2,1,0:T(8,128)S(1)}, f32[2,32,512]{2,1,0:T(8,128)S(1)}, u32[]{:S(2)}, u32[]{:S(2)}) collective-permute-start(f32[2,32,512]{2,1,0:T(8,128)S(1)} %pad_maximum_fusion.1), channel_id=1, source_target_pairs={{0,16},{4,20},{8,24},{12,28},{16,0},{20,4},{24,8},{28,12},{1,17},{... | collective-permute-start | bytes 393224 | tf_op jit(solution)/shard_map/ppermute | solution.py:289
  100.6 0.7 subtract_select_fusion
  101.3 4.7 %root2.1.f0_ref = f32[32,384]{1,0:T(8,128)S(1)} custom-call(f32[32,32]{1,0:T(8,128)S(1)} %root1.1.a_ref, f32[32,320]{1,0:T(8,128)S(1)} %add.135.u_ref), custom_call_target="tpu_custom_call" | custom-call | flops 9437184 | bytes 45056 | tf_op jit(solution)/shard_map/root2/pallas_call | solution.py:136
  106.0 0.1 collective-permute-start.22
  106.1 0.5 collective-permute-start.21
  106.6 0.7 broadcast_select_fusion
  107.3 0.5 collective-permute-done.21.v1_ref
  107.8 1.2 %copy-done.3 = f32[2,64,2048]{2,1,0:T(8,128)S(1)} copy-done((f32[2,64,2048]{2,1,0:T(8,128)S(1)}, f32[2,64,2048]{2,1,0:T(8,128)}, u32[]{:S(2)}) %copy-start.3) | copy-done | bytes 1048600
  109.0 1.2 %copy-done.4 = f32[2,64,2048]{2,1,0:T(8,128)S(1)} copy-done((f32[2,64,2048]{2,1,0:T(8,128)S(1)}, f32[2,64,2048]{2,1,0:T(8,128)}, u32[]{:S(2)}) %copy-start.4) | copy-done | bytes 1048600
  110.3 8.4 %final.1 = (f32[1,2,320,2048]{3,2,1,0:T(8,128)}, f32[2,64,2048]{2,1,0:T(8,128)}, f32[2,64,2048]{2,1,0:T(8,128)}) custom-call(s32[4]{0:T(128)S(1)} %pad_add_fusion.place, bf16[1,2,320,2048]{3,2,1,0:T(8,128)(2,1)S(1)} %copy-done.1, f32[1,2,320,2048]{3,2,1,0:T(8,128)} %e_ref.9, f32[4,32,512]{2,1,0:T(8,128)S(1)} %pad_maximum_fusion.v0_ref, ...), custom_call_target="tpu_custom_call" | custom-call | flops 503316480 | bytes 18000000 | tf_op jit(solution)/shard_map/final/pallas_call | solution.py:256
  (44 shorter events, 0.3 us)
Async XLA Ops:
  2.4 1.7 %copy-start = (bf16[1,2,320,2048]{3,2,1,0:T(8,128)(2,1)S(1)}, bf16[1,2,320,2048]{3,2,1,0:T(8,128)(2,1)}, u32[]{:S(2)}) copy-start(bf16[1,2,320,2048]{3,2,1,0:T(8,128)(2,1)} %g_ref.9) | copy-start | bytes 7864324
  7.0 3.5 %copy-start.2 = (f32[2,32,2048]{2,1,0:T(8,128)S(1)}, f32[2,32,2048]{2,1,0:T(8,128)}, u32[]{:S(2)}) copy-start(f32[2,32,2048]{2,1,0:T(8,128)} %w_ref.3) | copy-start | bytes 1572868
  7.0 3.4 %collective-permute-start = (f32[4,320,256]{2,1,0:T(8,128)S(1)}, f32[4,320,256]{2,1,0:T(8,128)S(1)}, u32[]{:S(2)}, u32[]{:S(2)}) collective-permute-start(f32[4,320,256]{2,1,0:T(8,128)S(1)} %outgoing0.1), channel_id=1, source_target_pairs={{0,4},{4,0},{8,12},{12,8},{16,20},{20,16},{24,28},{28,24},{1,5},{5... | collective-permute-start | bytes 3932168 | tf_op jit(solution)/shard_map/ppermute | solution.py:289
  10.3 7.2 %collective-permute-start.1 = (f32[4,320,256]{2,1,0:T(8,128)S(1)}, f32[4,320,256]{2,1,0:T(8,128)S(1)}, u32[]{:S(2)}, u32[]{:S(2)}) collective-permute-start(f32[4,320,256]{2,1,0:T(8,128)S(1)} %outgoing1.1), channel_id=1, source_target_pairs={{0,4},{4,0},{8,12},{12,8},{16,20},{20,16},{24,28},{28,24},{1,5},{5... | collective-permute-start | bytes 3932168 | tf_op jit(solution)/shard_map/ppermute | solution.py:289
  14.4 8.6 %copy-start.6 = (f32[1,2,2048]{2,1,0:T(2,128)S(1)}, f32[1,2,2048]{2,1,0:T(2,128)}, u32[]{:S(2)}) copy-start(f32[1,2,2048]{2,1,0:T(2,128)} %param.12) | copy-start | bytes 49156
  14.5 18.0 %collective-permute-start.7 = (f32[2,320,256]{2,1,0:T(8,128)S(1)}, f32[2,320,256]{2,1,0:T(8,128)}, u32[]{:S(2)}, u32[]{:S(2)}) collective-permute-start(f32[2,320,256]{2,1,0:T(8,128)S(1)} %get-tuple-element.19), channel_id=1, source_target_pairs={{0,8},{4,12},{8,0},{12,4},{16,24},{20,28},{24,16},{28,20},{1,9},{5... | collective-permute-start | bytes 1966088 | tf_op jit(solution)/shard_map/ppermute | solution.py:289
  21.5 17.7 %collective-permute-start.9 = (f32[2,320,256]{2,1,0:T(8,128)S(1)}, f32[2,320,256]{2,1,0:T(8,128)S(1)}, u32[]{:S(2)}, u32[]{:S(2)}) collective-permute-start(f32[2,320,256]{2,1,0:T(8,128)S(1)} %get-tuple-element.21), channel_id=1, source_target_pairs={{0,16},{4,20},{8,24},{12,28},{16,0},{20,4},{24,8},{28,12},{1,17},{... | collective-permute-start | bytes 1966088 | tf_op jit(solution)/shard_map/ppermute | solution.py:289
  23.1 1.2 %collective-permute-start.2 = (f32[2048]{0:T(1024)S(1)}, f32[2048]{0:T(1024)S(1)}, u32[]{:S(2)}, u32[]{:S(2)}) collective-permute-start(f32[2048]{0:T(1024)S(1)} %bitcast.34), channel_id=1, source_target_pairs={{0,4},{4,0},{8,12},{12,8},{16,20},{20,16},{24,28},{28,24},{1,5},{5... | collective-permute-start | bytes 24584 | tf_op jit(solution)/shard_map/ppermute | solution.py:289
  24.5 14.9 %collective-permute-start.3 = (f32[32,384]{1,0:T(8,128)S(1)}, f32[32,384]{1,0:T(8,128)S(1)}, u32[]{:S(2)}, u32[]{:S(2)}) collective-permute-start(f32[32,384]{1,0:T(8,128)S(1)} %pad_maximum_fusion.2), channel_id=1, source_target_pairs={{0,1},{1,0},{2,3},{3,2},{4,5},{5,4},{6,7},{7,6},{8,9},{9,8},{10,11... | collective-permute-start | bytes 147464 | tf_op jit(solution)/shard_map/ppermute | solution.py:289
  33.6 19.3 %collective-permute-start.8 = (f32[1,320,256]{2,1,0:T(8,128)S(1)}, f32[1,320,256]{2,1,0:T(8,128)S(1)}, u32[]{:S(2)}, u32[]{:S(2)}) collective-permute-start(f32[1,320,256]{2,1,0:T(8,128)S(1)} %get-tuple-element.31), channel_id=1, source_target_pairs={{0,16},{4,20},{8,24},{12,28},{16,0},{20,4},{24,8},{28,12},{1,17},{... | collective-permute-start | bytes 983048 | tf_op jit(solution)/shard_map/ppermute | solution.py:289
  39.3 13.7 %collective-permute-start.10 = (f32[1,320,256]{2,1,0:T(8,128)S(1)}, f32[1,320,256]{2,1,0:T(8,128)S(1)}, u32[]{:S(2)}, u32[]{:S(2)}) collective-permute-start(f32[1,320,256]{2,1,0:T(8,128)S(1)} %get-tuple-element.29), channel_id=1, source_target_pairs={{0,8},{4,12},{8,0},{12,4},{16,24},{20,28},{24,16},{28,20},{1,9},{5... | collective-permute-start | bytes 983048 | tf_op jit(solution)/shard_map/ppermute | solution.py:289
  39.5 5.2 %collective-permute-start.4 = (f32[32,384]{1,0:T(8,128)S(1)}, f32[32,384]{1,0:T(8,128)S(1)}, u32[]{:S(2)}, u32[]{:S(2)}) collective-permute-start(f32[32,384]{1,0:T(8,128)S(1)} %fusion.7), channel_id=1, source_target_pairs={{0,2},{1,3},{2,0},{3,1},{4,6},{5,7},{6,4},{7,5},{8,10},{9,11},{10,... | collective-permute-start | bytes 147464 | tf_op jit(solution)/shard_map/ppermute | solution.py:289
  44.6 4.2 %collective-permute-start.5 = (f32[32,384]{1,0:T(8,128)S(1)}, f32[32,384]{1,0:T(8,128)S(1)}, u32[]{:S(2)}, u32[]{:S(2)}) collective-permute-start(f32[32,384]{1,0:T(8,128)S(1)} %add.119), channel_id=1, source_target_pairs={{0,8},{4,12},{8,0},{12,4},{16,24},{20,28},{24,16},{28,20},{1,9},{5... | collective-permute-start | bytes 147464 | tf_op jit(solution)/shard_map/ppermute | solution.py:289
  48.8 4.2 %collective-permute-start.6 = (f32[32,384]{1,0:T(8,128)S(1)}, f32[32,384]{1,0:T(8,128)S(1)}, u32[]{:S(2)}, u32[]{:S(2)}) collective-permute-start(f32[32,384]{1,0:T(8,128)S(1)} %add.120), channel_id=1, source_target_pairs={{0,16},{4,20},{8,24},{12,28},{16,0},{20,4},{24,8},{28,12},{1,17},{... | collective-permute-start | bytes 147464 | tf_op jit(solution)/shard_map/ppermute | solution.py:289
  53.5 4.3 %collective-permute-start.11 = (f32[32,512]{1,0:T(8,128)S(1)}, f32[32,512]{1,0:T(8,128)S(1)}, u32[]{:S(2)}, u32[]{:S(2)}) collective-permute-start(f32[32,512]{1,0:T(8,128)S(1)} %get-tuple-element.22), channel_id=1, source_target_pairs={{0,1},{1,0},{2,3},{3,2},{4,5},{5,4},{6,7},{7,6},{8,9},{9,8},{10,11... | collective-permute-start | bytes 196616 | tf_op jit(solution)/shard_map/ppermute | solution.py:289
  57.8 5.3 %collective-permute-start.12 = (f32[32,512]{1,0:T(8,128)S(1)}, f32[32,512]{1,0:T(8,128)S(1)}, u32[]{:S(2)}, u32[]{:S(2)}) collective-permute-start(f32[32,512]{1,0:T(8,128)S(1)} %add.130), channel_id=1, source_target_pairs={{0,2},{1,3},{2,0},{3,1},{4,6},{5,7},{6,4},{7,5},{8,10},{9,11},{10,... | collective-permute-start | bytes 196616 | tf_op jit(solution)/shard_map/ppermute | solution.py:289
  63.1 37.4 %copy-start.5 = (f32[2,2048]{1,0:T(2,128)S(1)}, f32[2,2048]{1,0:T(2,128)}, u32[]{:S(2)}) copy-start(f32[2,2048]{1,0:T(2,128)} %param.16) | copy-start | bytes 49156
  63.2 37.4 %copy-start.7 = (f32[2,2048]{1,0:T(2,128)S(1)}, f32[2,2048]{1,0:T(2,128)}, u32[]{:S(2)}) copy-start(f32[2,2048]{1,0:T(2,128)} %param.17) | copy-start | bytes 49156
  63.9 4.5 %collective-permute-start.13 = (f32[32,320]{1,0:T(8,128)S(1)}, f32[32,320]{1,0:T(8,128)S(1)}, u32[]{:S(2)}, u32[]{:S(2)}) collective-permute-start(f32[32,320]{1,0:T(8,128)S(1)} %lift.1), channel_id=1, source_target_pairs={{0,1},{1,0},{2,3},{3,2},{4,5},{5,4},{6,7},{7,6},{8,9},{9,8},{10,11... | collective-permute-start | bytes 122888 | tf_op jit(solution)/shard_map/ppermute | solution.py:289
  68.4 5.7 %collective-permute-start.14 = (f32[32,320]{1,0:T(8,128)S(1)}, f32[32,320]{1,0:T(8,128)S(1)}, u32[]{:S(2)}, u32[]{:S(2)}) collective-permute-start(f32[32,320]{1,0:T(8,128)S(1)} %add.132), channel_id=1, source_target_pairs={{0,2},{1,3},{2,0},{3,1},{4,6},{5,7},{6,4},{7,5},{8,10},{9,11},{10,... | collective-permute-start | bytes 122888 | tf_op jit(solution)/shard_map/ppermute | solution.py:289
  74.1 4.2 %collective-permute-start.15 = (f32[32,320]{1,0:T(8,128)S(1)}, f32[32,320]{1,0:T(8,128)S(1)}, u32[]{:S(2)}, u32[]{:S(2)}) collective-permute-start(f32[32,320]{1,0:T(8,128)S(1)} %add.133), channel_id=1, source_target_pairs={{0,8},{4,12},{8,0},{12,4},{16,24},{20,28},{24,16},{28,20},{1,9},{5... | collective-permute-start | bytes 122888 | tf_op jit(solution)/shard_map/ppermute | solution.py:289
  78.2 29.6 %copy-start.1 = (bf16[1,2,320,2048]{3,2,1,0:T(8,128)(2,1)S(1)}, bf16[1,2,320,2048]{3,2,1,0:T(8,128)(2,1)}, u32[]{:S(2)}) copy-start(bf16[1,2,320,2048]{3,2,1,0:T(8,128)(2,1)} %g_ref.9) | copy-start | bytes 7864324
  78.3 4.2 %collective-permute-start.16 = (f32[32,320]{1,0:T(8,128)S(1)}, f32[32,320]{1,0:T(8,128)S(1)}, u32[]{:S(2)}, u32[]{:S(2)}) collective-permute-start(f32[32,320]{1,0:T(8,128)S(1)} %add.134), channel_id=1, source_target_pairs={{0,16},{4,20},{8,24},{12,28},{16,0},{20,4},{24,8},{28,12},{1,17},{... | collective-permute-start | bytes 122888 | tf_op jit(solution)/shard_map/ppermute | solution.py:289
  80.0 12.0 %collective-permute-start.23 = (f32[1,2048]{1,0:T(1,128)S(1)}, f32[1,2048]{1,0:T(1,128)S(1)}, u32[]{:S(2)}, u32[]{:S(2)}) collective-permute-start(f32[1,2048]{1,0:T(1,128)S(1)} %div.21), channel_id=1, source_target_pairs={{0,4},{4,0},{8,12},{12,8},{16,20},{20,16},{24,28},{28,24},{1,5},{5... | collective-permute-start | bytes 24584 | tf_op jit(solution)/shard_map/ppermute | solution.py:289
  82.9 6.1 %collective-permute-start.17 = (f32[32,512]{1,0:T(8,128)S(1)}, f32[32,512]{1,0:T(8,128)S(1)}, u32[]{:S(2)}, u32[]{:S(2)}) collective-permute-start(f32[32,512]{1,0:T(8,128)S(1)} %lower.1), channel_id=1, source_target_pairs={{0,1},{1,0},{2,3},{3,2},{4,5},{5,4},{6,7},{7,6},{8,9},{9,8},{10,11... | collective-permute-start | bytes 196616 | tf_op jit(solution)/shard_map/ppermute | solution.py:289
  89.0 5.6 %collective-permute-start.18 = (f32[32,512]{1,0:T(8,128)S(1)}, f32[32,512]{1,0:T(8,128)S(1)}, u32[]{:S(2)}, u32[]{:S(2)}) collective-permute-start(f32[32,512]{1,0:T(8,128)S(1)} %add.136), channel_id=1, source_target_pairs={{0,2},{1,3},{2,0},{3,1},{4,6},{5,7},{6,4},{7,5},{8,10},{9,11},{10,... | collective-permute-start | bytes 196616 | tf_op jit(solution)/shard_map/ppermute | solution.py:289
  94.6 4.3 %collective-permute-start.19 = (f32[1,32,512]{2,1,0:T(8,128)S(1)}, f32[1,32,512]{2,1,0:T(8,128)S(1)}, u32[]{:S(2)}, u32[]{:S(2)}) collective-permute-start(f32[1,32,512]{2,1,0:T(8,128)S(1)} %add_bitcast_fusion), channel_id=1, source_target_pairs={{0,8},{4,12},{8,0},{12,4},{16,24},{20,28},{24,16},{28,20},{1,9},{5... | collective-permute-start | bytes 196616 | tf_op jit(solution)/shard_map/ppermute | solution.py:289
  99.0 7.1 %collective-permute-start.20 = (f32[2,32,512]{2,1,0:T(8,128)S(1)}, f32[2,32,512]{2,1,0:T(8,128)S(1)}, u32[]{:S(2)}, u32[]{:S(2)}) collective-permute-start(f32[2,32,512]{2,1,0:T(8,128)S(1)} %pad_maximum_fusion.1), channel_id=1, source_target_pairs={{0,16},{4,20},{8,24},{12,28},{16,0},{20,4},{24,8},{28,12},{1,17},{... | collective-permute-start | bytes 393224 | tf_op jit(solution)/shard_map/ppermute | solution.py:289
  106.0 1.3 %collective-permute-start.22 = (f32[32,384]{1,0:T(8,128)S(1)}, f32[32,384]{1,0:T(8,128)S(1)}, u32[]{:S(2)}, u32[]{:S(2)}) collective-permute-start(f32[32,384]{1,0:T(8,128)S(1)} %root2.1.f0_ref), channel_id=1, source_target_pairs={{0,4},{4,0},{8,12},{12,8},{16,20},{20,16},{24,28},{28,24},{1,5},{5... | collective-permute-start | bytes 147464 | tf_op jit(solution)/shard_map/ppermute | solution.py:289
  106.1 1.7 %collective-permute-start.21 = (f32[4,32,512]{2,1,0:T(8,128)S(1)}, f32[4,32,512]{2,1,0:T(8,128)S(1)}, u32[]{:S(2)}, u32[]{:S(2)}) collective-permute-start(f32[4,32,512]{2,1,0:T(8,128)S(1)} %pad_maximum_fusion.v0_ref), channel_id=1, source_target_pairs={{0,4},{4,0},{8,12},{12,8},{16,20},{20,16},{24,28},{28,24},{1,5},{5... | collective-permute-start | bytes 786440 | tf_op jit(solution)/shard_map/ppermute | solution.py:289
  107.8 1.2 %copy-start.3 = (f32[2,64,2048]{2,1,0:T(8,128)S(1)}, f32[2,64,2048]{2,1,0:T(8,128)}, u32[]{:S(2)}) copy-start(f32[2,64,2048]{2,1,0:T(8,128)} %mm_ref.1) | copy-start | bytes 3145732
  109.0 1.2 %copy-start.4 = (f32[2,64,2048]{2,1,0:T(8,128)S(1)}, f32[2,64,2048]{2,1,0:T(8,128)}, u32[]{:S(2)}) copy-start(f32[2,64,2048]{2,1,0:T(8,128)} %mw_ref.1) | copy-start | bytes 3145732

commit v2 on v0

v2 whole, which is shorter than its diff:
```python
import functools

import jax
import jax.numpy as jnp
from jax import lax
from jax.experimental import pallas as pl
from jax.experimental.pallas import tpu as pltpu
from jax.sharding import PartitionSpec as P

ROOT_ITERS = 12
LANES = 128
f32 = jnp.float32
NN = ((1,), (0,))
NT = ((1,), (1,))
TN = ((0,), (0,))
ANY = pl.BlockSpec(memory_space=pl.ANY)
VMEM = pl.BlockSpec(memory_space=pltpu.VMEM)
SMEM = pl.BlockSpec(memory_space=pltpu.SMEM)


def dot(a, b, dims=NN):
    return lax.dot_general(
        a, b, (dims, ((), ())), precision=lax.Precision.HIGHEST, preferred_element_type=f32
    )


def split3(a):
    high = a.astype(jnp.bfloat16)
    rest = a - high.astype(f32)
    middle = rest.astype(jnp.bfloat16)
    low = (rest - middle.astype(f32)).astype(jnp.bfloat16)
    return high, middle, low


def lanes(n):
    return -(-n // LANES) * LANES


def in_hbm(a):
    return pltpu.with_memory_space_constraint(a, pltpu.HBM)


def in_vmem(a):
    return pltpu.with_memory_space_constraint(a, pltpu.VMEM)


def call(kernel, name, in_specs, out_specs, out_shape, operands, mib=8, flops=0, nbytes=0, scratch=(), aliases={}):
    return pl.pallas_call(
        kernel,
        in_specs=in_specs,
        out_specs=out_specs,
        out_shape=out_shape,
        scratch_shapes=scratch,
        input_output_aliases=aliases,
        compiler_params=pltpu.CompilerParams(vmem_limit_bytes=mib << 20),
        cost_estimate=pl.CostEstimate(flops=flops, bytes_accessed=nbytes, transcendentals=0),
        name=name,
    )(*operands)


def small_call(kernel, name, shapes, *operands):
    return call(
        kernel,
        name,
        [VMEM] * len(operands),
        [VMEM] * len(shapes),
        [jax.ShapeDtypeStruct(s, f32) for s in shapes],
        operands,
        flops=12_000_000,
        nbytes=4 * sum(o.size for o in operands),
    )


def combine_kernel(place, g_hbm, e_hbm, *refs, own, blocks, streams):
    outs, (g, e, sem) = refs[:streams], refs[streams:]
    width = g.shape[2]
    m = place[0] if own else 1 - place[0]

    def copies(i):
        s, p = divmod(i, blocks)
        start = pl.multiple_of(((place[1] ^ p) * streams + s) * width, width)
        where = pl.ds(start, width)
        return (
            pltpu.make_async_copy(g_hbm.at[0, m, :, where], g.at[i], sem.at[i, 0]),
            pltpu.make_async_copy(e_hbm.at[0, m, :, where], e.at[i], sem.at[i, 1]),
        )

    for i in range(blocks * streams):
        for copy in copies(i):
            copy.start()
    for i in range(blocks * streams):
        for copy in copies(i):
            copy.wait()
        s, p = divmod(i, blocks)
        outs[s][p] = g[i].astype(f32) + e[i]


def combine(place, grads, errors, own, blocks, streams):
    rows, cols = grads.shape[2:]
    chunks = blocks * streams
    width = cols // chunks
    return call(
        functools.partial(combine_kernel, own=own, blocks=blocks, streams=streams),
        "own" if own else "outgoing",
        [SMEM, ANY, ANY],
        [VMEM] * streams,
        [pltpu.VMEM((blocks, rows, width), f32)] * streams,
        (place, grads, errors),
        mib=10,
        flops=rows * cols,
        nbytes=rows * cols * 10,
        scratch=[
            pltpu.VMEM((chunks, rows, width), grads.dtype),
            pltpu.VMEM((chunks, rows, width), f32),
            pltpu.SemaphoreType.DMA((chunks, 2)),
        ],
    )


def factor_kernel(place, w_hbm, vec_hbm, *refs, streams):
    combined = (refs[:streams], refs[streams : 2 * streams])
    outs, (w, vec, sem) = refs[2 * streams : 2 * streams + 2], refs[2 * streams + 2 :]
    blocks, rows, width = combined[0][0].shape
    rank = w.shape[1]
    loads = (
        pltpu.make_async_copy(w_hbm, w, sem.at[0]),
        pltpu.make_async_copy(vec_hbm.at[0], vec, sem.at[1]),
    )
    for load in loads:
        load.start()
    for load in loads:
        load.wait()
    for k in range(2):
        m = place[0] if k == 0 else 1 - place[0]
        terms = jnp.zeros((rows, 3 * rank), f32)
        for s in range(streams):
            for p in range(blocks):
                start = pl.multiple_of(((place[1] ^ p) * streams + s) * width, width)
                w_high, w_middle, w_low = split3(w[m, :, pl.ds(start, width)])
                zero = jnp.zeros_like(w_low)
                high, middle, low = split3(combined[k][s][p])
                for part, factors in (
                    (high, (w_high, w_middle, w_low)),
                    (middle, (w_high, w_middle, zero)),
                    (low, (w_high, zero, zero)),
                ):
                    terms += lax.dot_general(
                        part, jnp.concatenate(factors, axis=0), (NT, ((), ())), preferred_element_type=f32
                    )
        out = outs[k]
        out[...] = jnp.zeros(out.shape, f32)
        out[:, :rows] = (terms[:, :rank] + terms[:, rank : 2 * rank] + terms[:, 2 * rank :]).T
        mine = jnp.where(m == 0, vec[0:1, :], vec[1:2, :])
        for i in range(vec.shape[1] // LANES):
            out[i : i + 1, out.shape[1] - LANES :] = mine[:, i * LANES : (i + 1) * LANES]


def first_factors(place, own_c, other_c, warm_start, vec_grads):
    streams = len(own_c)
    rows = own_c[0].shape[1]
    rank = warm_start.shape[1]
    shape = jax.ShapeDtypeStruct((rank, lanes(rows) + LANES), f32)
    return call(
        functools.partial(factor_kernel, streams=streams),
        "factor",
        [SMEM, ANY, ANY] + [VMEM] * (2 * streams),
        [VMEM] * 2,
        [shape] * 2,
        (place, warm_start, vec_grads, *own_c, *other_c),
        mib=12,
        flops=36 * rank * rows * warm_start.shape[2],
        nbytes=8 * rows * warm_start.shape[2],
        scratch=[
            pltpu.VMEM(warm_start.shape, f32),
            pltpu.VMEM(vec_grads.shape[1:], f32),
            pltpu.SemaphoreType.DMA((2,)),
        ],
    )


def kept_blocks(order, blocks, stage):
    return [p for p in range(blocks) if not any(p >> bit & 1 for bit in order[:stage])]


def fold_kernel(*refs, picks):
    ins, out = refs[:-1], refs[-1]
    for i, pick in enumerate(picks):
        out[i] = sum(ref[at] for ref, at in zip(ins, pick))


def fold(terms, order, blocks, stage):
    goes = [p for p in kept_blocks(order, blocks, stage) if p >> order[stage] & 1]
    picks = [
        (p, p, *(kept_blocks(order, blocks, t + 1).index(p) for t in range(len(terms) - 2))) for p in goes
    ]
    shape = (len(goes),) + terms[0].shape[1:]
    return call(
        functools.partial(fold_kernel, picks=picks),
        f"fold{stage}",
        [VMEM] * len(terms),
        VMEM,
        pltpu.VMEM(shape, f32),
        terms,
        nbytes=4 * len(terms) * shape[0] * shape[1] * shape[2],
    )


def project_kernel(*refs, streams, per, count):
    x_ref, parts, (s_ref, v_ref) = refs[0], refs[1 : 1 + per * streams], refs[1 + per * streams :]
    rows = s_ref.shape[0]
    width = s_ref.shape[1] // streams
    factor = x_ref[:, :rows] / count
    for s in range(streams):
        block = sum(part[0] for part in parts[s * per : (s + 1) * per])
        where = slice(s * width, (s + 1) * width)
        s_ref[:, where] = block
        v_ref[:, where] = dot(factor, block) / count


def lift_kernel(v_ref, s_ref, u_ref, *, count):
    u_ref[...] = dot(v_ref[...], s_ref[...], NT) / count


def lower_kernel(u_ref, s_ref, v_ref, *, count):
    v_ref[...] = dot(u_ref[...], s_ref[...]) / count


def identity(rank):
    return (
        lax.broadcasted_iota(jnp.int32, (rank, rank), 0)
        == lax.broadcasted_iota(jnp.int32, (rank, rank), 1)
    ).astype(f32)


def sweeps(left, right, first, last):
    eye = identity(left.shape[0])
    for sweep in range(first, last):
        middle = 1.5 * eye - 0.5 * (left if sweep == 0 else dot(right, left))
        right = middle if sweep == 0 else dot(middle, right)
        if sweep + 1 < ROOT_ITERS:
            left = dot(left, middle)
    return left, right


def root_begin(gram, state):
    spread = jnp.sqrt(jnp.sum(gram * gram, keepdims=True))
    left, right = sweeps(gram / spread, None, 0, ROOT_ITERS // 2)
    state[0], state[1] = left, right
    state[2] = jnp.broadcast_to(spread, gram.shape)


def root_end(state):
    _, right = sweeps(state[0], state[1], ROOT_ITERS // 2, ROOT_ITERS)
    return right / jnp.sqrt(state[2])


def first_begin_kernel(x_ref, state, *, rows, count):
    factor = x_ref[:, :rows] / count
    root_begin(dot(factor, factor, NT), state)


def first_end_kernel(state, a_ref):
    a_ref[...] = root_end(state)


def second_begin_kernel(a_ref, u_ref, state):
    a, u = a_ref[...], u_ref[...]
    root_begin(dot(a, dot(dot(u, u, NT), a), TN), state)


def second_end_kernel(state, a_ref, u_ref, f_ref):
    u = u_ref[...]
    rank, rows = u.shape
    both = dot(a_ref[...], root_end(state))
    f_ref[...] = jnp.zeros(f_ref.shape, f32)
    f_ref[:, :rows] = dot(both, u, TN)
    f_ref[:, rows : rows + rank] = both


def gains_kernel(place, chosen, own_ref, other_ref, mv_ref, wv_ref, mo_ref, wo_ref, vec, *, count, first):
    for i in range(mv_ref.shape[1] // LANES):
        at = slice(i * LANES, (i + 1) * LANES)
        for k, ref in enumerate((own_ref, other_ref)):
            vec[k : k + 1, at] = ref[i : i + 1, ref.shape[1] - LANES :] / count
    for slot in range(mv_ref.shape[0]):
        item = chosen[slot]
        row = jnp.where(item - first == place[0], vec[0:1, :], vec[1:2, :])
        old, weight = mv_ref[slot : slot + 1, :], wv_ref[slot : slot + 1, :]
        new = 0.9 * old + row
        mo_ref[slot : slot + 1, :] = jnp.where(item >= first, new, old)
        wo_ref[slot : slot + 1, :] = jnp.where(item >= first, weight - 0.5 * new, weight)


def gains(place, chosen, own, other, vec_momentum, vec_weights, count, first):
    return call(
        functools.partial(gains_kernel, count=count, first=first),
        "gains",
        [SMEM, SMEM] + [VMEM] * 4,
        [VMEM] * 2,
        [jax.ShapeDtypeStruct(vec_momentum.shape, f32)] * 2,
        (place, chosen, own, other, vec_momentum, vec_weights),
        flops=10 * vec_momentum.size,
        nbytes=16 * vec_momentum.size,
        scratch=[pltpu.VMEM((2, vec_momentum.shape[1]), f32)],
    )


def finish_kernel(place, chosen, v0_ref, v1_ref, f0_ref, f1_ref, *refs, positions, streams, head, later):
    combined = (refs[:streams], refs[streams : 2 * streams])
    mm_hbm, mw_hbm = refs[2 * streams : 2 * streams + 2]
    refs = refs[2 * streams + 2 + later :]
    n_hbm, mo_hbm, wo_hbm, errors, approx, moment, weight, sem, bank_sem = refs
    rank, width = v0_ref.shape[1:]
    rows = errors.shape[2]
    narrow = width // streams

    def columns(p):
        return pl.ds(pl.multiple_of((place[1] ^ p) * width, width), width)

    loads = []
    for k, p in enumerate(positions):
        loads.append(
            (
                pltpu.make_async_copy(mm_hbm.at[:, :, columns(p)], moment.at[k], bank_sem.at[k, 0]),
                pltpu.make_async_copy(mw_hbm.at[:, :, columns(p)], weight.at[k], bank_sem.at[k, 1]),
            )
        )
        for load in loads[-1]:
            load.start()
    left, both = [], []
    for f_ref in (f0_ref, f1_ref):
        high, middle, low = split3(f_ref[:, :rows].T)
        left.append(jnp.concatenate([high, high, middle, high, low, middle], axis=1))
        both.append(f_ref[:, rows : rows + rank])
    stores = []
    for k, p in enumerate(positions):
        for i, v_ref in enumerate((v0_ref, v1_ref)):
            m = place[0] if i == 0 else 1 - place[0]
            high, middle, low = split3(dot(both[i], v_ref[k], TN))
            right = jnp.concatenate([high, middle, high, low, high, middle], axis=0)
            product = jnp.dot(left[i], right, preferred_element_type=f32)
            approx[k, pl.ds(pl.multiple_of(m * rows, rows), rows), :] = product
            for s in range(streams):
                at = slice(s * narrow, (s + 1) * narrow)
                errors[k, i, :, at] = combined[i][s][p] - product[:, at]
            stores.append(
                pltpu.make_async_copy(errors.at[k, i], n_hbm.at[0, m, :, columns(p)], sem.at[k, i])
            )
            stores[-1].start()
        for load in loads[k]:
            load.wait()
        for slot in range(moment.shape[1]):
            item = chosen[slot]

            @pl.when((item >= 0) & (item < approx.shape[1] // head))
            def _():
                block = approx[k, pl.ds(pl.multiple_of(item * head, head), head), :]
                new = 0.9 * moment[k, slot] + block
                moment[k, slot] = new
                weight[k, slot] = weight[k, slot] - 0.5 * new

        for i, (ref, hbm) in enumerate(((moment, mo_hbm), (weight, wo_hbm))):
            stores.append(
                pltpu.make_async_copy(ref.at[k], hbm.at[:, :, columns(p)], bank_sem.at[len(positions) + k, i])
            )
            stores[-1].start()
    for store in stores:
        store.wait()


def finish(positions, outs, place, chosen, own_v, other_v, own_f, other_f, own_c, other_c, shapes, mat_momentum, mat_weights):
    n, rank, width = own_v.shape
    streams = len(own_c)
    matrices, rows, cols = shapes[0][1:]
    slots, head = mat_momentum.shape[:2]
    later = len(outs)
    inputs = 6 + 2 * streams + 2
    return call(
        functools.partial(finish_kernel, positions=positions, streams=streams, head=head, later=later),
        f"finish{positions[0]}",
        [SMEM, SMEM] + [VMEM] * (4 + 2 * streams) + [ANY] * (2 + later),
        [ANY] * 3,
        [pltpu.HBM(s, f32) for s in shapes],
        (place, chosen, own_v, other_v, own_f, other_f, *own_c, *other_c, mat_momentum, mat_weights, *outs),
        mib=4 + 8 * n,
        flops=2 * n * matrices * rows * width * 6 * rank,
        nbytes=4 * n * width * (matrices * rows + 4 * slots * head),
        scratch=[
            pltpu.VMEM((n, matrices, rows, width), f32),
            pltpu.VMEM((n, matrices * rows, width), f32),
            pltpu.VMEM((n, slots, head, width), f32),
            pltpu.VMEM((n, slots, head, width), f32),
            pltpu.SemaphoreType.DMA((n, matrices)),
            pltpu.SemaphoreType.DMA((2 * n, 2)),
        ],
        aliases={inputs + i: i for i in range(later)},
    )


def exchange(a, axis, mask):
    return lax.ppermute(a, axis, [(i, i ^ mask) for i in range(lax.axis_size(axis))])


def hop(a, axis, mask, work=None, *operands):
    if work is None:
        return a + exchange(a, axis, mask)
    a, *operands = lax.optimization_barrier((a, *operands))
    arrived = exchange(a, axis, mask)
    done = work(*operands)
    arrived, *done = lax.optimization_barrier((arrived, *done))
    return a + arrived, *done


def local(grads, errors, warm_start, vec_grads, owners, mat_momentum, mat_weights, vec_momentum, vec_weights):
    reps, groups = lax.axis_size("rep"), lax.axis_size("grp")
    count = float(reps * groups)
    blocks = reps // 2
    bits = blocks.bit_length() - 1
    z_masks = [1 << i for i in range(groups.bit_length() - 1)]
    matrices, rows, cols = grads.shape[1:]
    rank = warm_start.shape[1]
    width = cols // blocks
    streams = 2 if width % 256 == 0 else 1
    rep = lax.axis_index("rep")
    core, spot = rep % 2, rep // 2
    device = rep * groups + lax.axis_index("grp")
    place = jnp.stack([core, spot]).astype(jnp.int32)

    items = owners.shape[0]
    slots, head = mat_momentum.shape[:2]
    earlier = jnp.arange(items)[None, :] < jnp.arange(items)[:, None]
    same = owners[None, :] == owners[:, None]
    slot = jnp.sum((earlier & same).astype(jnp.int32), axis=1)
    match = (owners[None, :] == device) & (slot[None, :] == jnp.arange(slots)[:, None])
    head_items = matrices * (rows // head)
    chosen = jnp.max(jnp.where(match, jnp.arange(items)[None, :], -1), axis=1).astype(jnp.int32)

    grads, errors, warm_start, vec_grads = map(in_hbm, (grads, errors, warm_start, vec_grads))
    mat_momentum, mat_weights = map(in_hbm, (mat_momentum, mat_weights))

    other_c = combine(place, grads, errors, False, blocks, streams)
    arrived_c = [in_vmem(exchange(a, "rep", 1)) for a in other_c]
    own_c = combine(place, grads, errors, True, blocks, streams)

    orders = [list(range(bits)), list(range(bits))[::-1]][:streams]
    parts = [[own_c[s], arrived_c[s]] for s in range(streams)]
    goes = [fold(parts[s], orders[s], blocks, 0) for s in range(streams)]
    firsts = [exchange(goes[s], "rep", 2 << orders[s][0]) for s in range(streams)]

    tied = lax.optimization_barrier((place, *goes))
    own_p, other_p = first_factors(tied[0], own_c, other_c, warm_start, vec_grads)
    packed = own_p + exchange(other_p, "rep", 1)
    for mask in z_masks:
        packed = hop(packed, "grp", mask)
    packed = hop(packed, "rep", 2)
    *firsts, packed = lax.optimization_barrier((*firsts, packed))
    for bit in range(1, bits):
        packed = hop(packed, "rep", 2 << bit)
    for stage in range(bits):
        for s in range(streams):
            if stage == 0:
                arrived = firsts[s]
            else:
                arrived = exchange(fold(parts[s], orders[s], blocks, stage), "rep", 2 << orders[s][stage])
            parts[s].append(in_vmem(arrived))

    kept_sum, v = small_call(
        functools.partial(project_kernel, streams=streams, per=len(parts[0]), count=count),
        "project", [(rows, width), (rank, width)], packed, *sum(parts, []),
    )
    square = (rank, rank)
    state = (3, rank, rank)
    v, first_state = hop(
        v, "grp", z_masks[0],
        lambda x: small_call(
            functools.partial(first_begin_kernel, rows=rows, count=count), "root1a", [state], x
        ), packed,
    )
    v, first_root = hop(
        v, "grp", z_masks[1], lambda x: small_call(first_end_kernel, "root1b", [square], x), first_state
    )
    for mask in z_masks[2:]:
        v = hop(v, "grp", mask)
    (u,) = small_call(functools.partial(lift_kernel, count=count), "lift", [(rank, rows)], v, kept_sum)
    for mask in z_masks[:-1]:
        u = hop(u, "grp", mask)
    u, vec_momentum_out, vec_weights_out = hop(
        u, "grp", z_masks[-1],
        lambda x, y: gains(place, chosen, x, y, vec_momentum, vec_weights, count, head_items),
        packed, exchange(packed, "rep", 1),
    )
    for bit in range(bits):
        u = hop(u, "rep", 2 << bit)
    (v,) = small_call(functools.partial(lower_kernel, count=count), "lower", [(rank, width)], u, kept_sum)
    v, second_state = hop(
        v, "grp", z_masks[0], lambda *x: small_call(second_begin_kernel, "root2a", [state], *x), first_root, u
    )
    v, own_f = hop(
        v, "grp", z_masks[1],
        lambda *x: small_call(second_end_kernel, "root2b", [(rank, lanes(rows + rank))], *x),
        second_state, first_root, u,
    )
    for mask in z_masks[2:]:
        v = hop(v, "grp", mask)
    other_f = exchange(own_f, "rep", 1)

    shapes = [errors.shape, mat_momentum.shape, mat_weights.shape]
    outs = ()
    v = v[None]
    fresh, positions = v, [0]
    for bit in range(bits + 1):
        other_v = exchange(fresh, "rep", 1)
        if bit < bits:
            arrived = exchange(v, "rep", 2 << bit)
        outs = finish(
            positions, outs, place, chosen, fresh, other_v, own_f, other_f, own_c, other_c, shapes,
            mat_momentum, mat_weights,
        )
        if bit < bits:
            arrived, *outs = lax.optimization_barrier((arrived, *outs))
            v = jnp.concatenate([v, arrived], axis=0)
            fresh, positions = arrived, list(range(1 << bit, 2 << bit))
    new_errors, mat_momentum_out, mat_weights_out = outs
    return (new_errors, mat_momentum_out, mat_weights_out, vec_momentum_out, vec_weights_out)


def solution(mesh):
    both = ("rep", "grp")
    return jax.shard_map(
        local,
        mesh=mesh,
        in_specs=(
            P(both, None, None, None),
            P(both, None, None, None),
            P(),
            P(both, None, None),
            P(),
            P(both, None, None),
            P(both, None, None),
            P(both, None),
            P(both, None),
        ),
        out_specs=(
            P(both, None, None, None),
            P(both, None, None),
            P(both, None, None),
            P(both, None),
            P(both, None),
        ),
        check_vma=False,
    )
```

time: 588 us -> 98.2 us (0.17)
  waiting for transfers between devices: 458 us -> 30.9 us
  matrix products: 61.9 us -> 0 us
  blocking collectives: 41.5 us -> 0 us
  Pallas kernels: 0 us -> 33.1 us
  starting transfers between devices: 0.34 us -> 32.5 us
  between operations: 14.5 us -> 0.95 us
  other arithmetic: 7.02 us -> 0.52 us
    psum x4 -> x0, waiting for transfers between devices: 458 us -> none  [the longest x3 335 us: replicas_total(): return lax.psum(partial_term, ('rep', 'grp'))]
    dot_general x81 -> x0, matrix products: 61.9 us -> none  [the longest x2 13.4 us: local(): jnp.einsum('mks,mkd->msd', p_hat, combined, precision=high)]
    psum x1 -> x0, blocking collectives: 41.5 us -> none  [local(): vec_sum = lax.psum(vec_grads[0], ('rep', 'grp'))]
    pallas_call x0 -> x18, Pallas kernels: none -> 33.1 us  [call(): pl.pallas_call(kernel, in_specs=in_specs, out_specs=out_specs, out_shape=...]
    ppermute x0 -> x26, starting transfers between devices: none -> 32.5 us  [exchange(): lax.ppermute(a, axis, [(i, i ^ mask) for i in range(lax.axis_size(axis))])]
    ppermute x0 -> x26, waiting for transfers between devices: none -> 30.9 us  [exchange(): lax.ppermute(a, axis, [(i, i ^ mask) for i in range(lax.axis_size(axis))])]
    broadcast_in_dim x1, other arithmetic: 6.5 us -> 0.01 us  [local(): v = v[None]]
  transfers between devices with their start and end apart: 4 -> 26, of which waited for: 4 -> 16; matrix products, arithmetic and copies ran while one was open for 0% -> 0% of each run, Pallas kernels for 0% -> 25%
where the time goes in v2:
time: 98.2 us; the launch traced here: 98 us
  Pallas kernels  33.1 us (34%)
  starting transfers between devices  32.5 us (33%)
  waiting for transfers between devices  30.9 us (31%)
    pallas_call x18, Pallas kernels, call(): pl.pallas_call(kernel, in_specs=in_specs, out_specs=out_specs, out_shape=...  33.1 us
    ppermute x26, starting transfers between devices, exchange(): lax.ppermute(a, axis, [(i, i ^ mask) for i in range(lax.axis_size(axis))])  32.5 us
    ppermute x26, waiting for transfers between devices, exchange(): lax.ppermute(a, axis, [(i, i ^ mask) for i in range(lax.axis_size(axis))])  30.9 us
  transfers between devices with their start and end apart: 26, of which 16 were waited for; matrix products, arithmetic and copies ran while one was open for 0% of the time, Pallas kernels for 25%

profile of v2, /device:TPU:0, one launch (start us, length us, event | category | flops | bytes accessed | tf_op | source)
XLA Modules:
  0.0 98.0 jit_solution(10008521959181087862)
XLA Ops:
  0.7 0.1 pad_add_fusion.place
  0.7 2.9 %outgoing.1 = (f32[4,320,256]{2,1,0:T(8,128)S(1)}, f32[4,320,256]{2,1,0:T(8,128)S(1)}) custom-call(s32[2]{0:T(128)S(1)} %pad_add_fusion.place, bf16[1,2,320,2048]{3,2,1,0:T(8,128)(2,1)} %g_hbm.3, f32[1,2,320,2048]{3,2,1,0:T(8,128)} %e_hbm.3), custom_call_target="tpu_custom_call" | custom-call | flops 655360 | bytes 6553600 | tf_op jit(solution)/shard_map/outgoing/pallas_call | solution.py:48
  3.6 0.0 copy-start
  3.6 0.5 collective-permute-start.2
  4.2 0.1 collective-permute-start
  4.2 2.9 %own.1 = (f32[4,320,256]{2,1,0:T(8,128)S(1)}, f32[4,320,256]{2,1,0:T(8,128)S(1)}) custom-call(s32[2]{0:T(128)S(1)} %pad_add_fusion.place, bf16[1,2,320,2048]{3,2,1,0:T(8,128)(2,1)} %g_hbm.3, f32[1,2,320,2048]{3,2,1,0:T(8,128)} %e_hbm.3), custom_call_target="tpu_custom_call" | custom-call | flops 655360 | bytes 6553600 | tf_op jit(solution)/shard_map/own/pallas_call | solution.py:48
  7.1 0.1 fold0.3
  7.2 3.0 %collective-permute-start.3 = (f32[2,320,256]{2,1,0:T(8,128)S(1)}, f32[2,320,256]{2,1,0:T(8,128)S(1)}, u32[]{:S(2)}, u32[]{:S(2)}) collective-permute-start(f32[2,320,256]{2,1,0:T(8,128)S(1)} %fold0.3), channel_id=1, source_target_pairs={{0,16},{4,20},{8,24},{12,28},{16,0},{20,4},{24,8},{28,12},{1,17},{... | collective-permute-start | bytes 1966088 | tf_op jit(solution)/shard_map/ppermute | solution.py:401
  10.2 0.1 fold0.2
  10.3 1.6 %collective-permute-start.1 = (f32[2,320,256]{2,1,0:T(8,128)S(1)}, f32[2,320,256]{2,1,0:T(8,128)S(1)}, u32[]{:S(2)}, u32[]{:S(2)}) collective-permute-start(f32[2,320,256]{2,1,0:T(8,128)S(1)} %fold0.2), channel_id=1, source_target_pairs={{0,8},{4,12},{8,0},{12,4},{16,24},{20,28},{24,16},{28,20},{1,9},{5... | collective-permute-start | bytes 1966088 | tf_op jit(solution)/shard_map/ppermute | solution.py:401
  11.9 4.1 %factor.1 = (f32[32,512]{1,0:T(8,128)S(1)}, f32[32,512]{1,0:T(8,128)S(1)}) custom-call(s32[2]{0:T(128)S(1)} %pad_add_fusion.place, f32[2,32,2048]{2,1,0:T(8,128)} %w_hbm.1, f32[1,2,2048]{2,1,0:T(2,128)} %vec_hbm.1, f32[4,320,256]{2,1,0:T(8,128)S(1)} %get-tuple-element.61.refs_0_.refs_1_, f32[4,320,256]{2,1,0:T(8,128)S(1)} %get-tuple-element.63.refs_0_.refs_1_.refs_5_, ...), custom_call_target="tpu_custom_call" | custom-call | flops 754974720 | bytes 5242880 | tf_op jit(solution)/shard_map/factor/pallas_call | solution.py:48
  16.0 0.1 collective-permute-start.4
  16.1 1.2 %collective-permute-done.4 = f32[32,512]{1,0:T(8,128)S(1)} collective-permute-done((f32[32,512]{1,0:T(8,128)S(1)}, f32[32,512]{1,0:T(8,128)S(1)}, u32[]{:S(2)}, u32[]{:S(2)}) %collective-permute-start.4) | collective-permute-done | bytes 65568 | tf_op jit(solution)/shard_map/ppermute | solution.py:401
  17.3 1.6 %collective-permute-start.5 = (f32[32,512]{1,0:T(8,128)S(1)}, f32[32,512]{1,0:T(8,128)S(1)}, u32[]{:S(2)}, u32[]{:S(2)}) collective-permute-start(f32[32,512]{1,0:T(8,128)S(1)} %add.49), channel_id=1, source_target_pairs={{0,1},{1,0},{2,3},{3,2},{4,5},{5,4},{6,7},{7,6},{8,9},{9,8},{10,11... | collective-permute-start | bytes 196616 | tf_op jit(solution)/shard_map/ppermute | solution.py:401
  19.0 2.7 %collective-permute-done.5 = f32[32,512]{1,0:T(8,128)S(1)} collective-permute-done((f32[32,512]{1,0:T(8,128)S(1)}, f32[32,512]{1,0:T(8,128)S(1)}, u32[]{:S(2)}, u32[]{:S(2)}) %collective-permute-start.5) | collective-permute-done | bytes 65568 | tf_op jit(solution)/shard_map/ppermute | solution.py:401
  21.7 2.7 %collective-permute-start.6 = (f32[32,512]{1,0:T(8,128)S(1)}, f32[32,512]{1,0:T(8,128)S(1)}, u32[]{:S(2)}, u32[]{:S(2)}) collective-permute-start(f32[32,512]{1,0:T(8,128)S(1)} %add.50), channel_id=1, source_target_pairs={{0,2},{1,3},{2,0},{3,1},{4,6},{5,7},{6,4},{7,5},{8,10},{9,11},{10,... | collective-permute-start | bytes 196616 | tf_op jit(solution)/shard_map/ppermute | solution.py:401
  24.3 2.6 %collective-permute-done.6 = f32[32,512]{1,0:T(8,128)S(1)} collective-permute-done((f32[32,512]{1,0:T(8,128)S(1)}, f32[32,512]{1,0:T(8,128)S(1)}, u32[]{:S(2)}, u32[]{:S(2)}) %collective-permute-start.6) | collective-permute-done | bytes 65568 | tf_op jit(solution)/shard_map/ppermute | solution.py:401
  27.0 0.6 collective-permute-start.7
  27.6 4.1 %collective-permute-done.7 = f32[32,512]{1,0:T(8,128)S(1)} collective-permute-done((f32[32,512]{1,0:T(8,128)S(1)}, f32[32,512]{1,0:T(8,128)S(1)}, u32[]{:S(2)}, u32[]{:S(2)}) %collective-permute-start.7) | collective-permute-done | bytes 65568 | tf_op jit(solution)/shard_map/ppermute | solution.py:401
  31.7 0.1 fold1.3
  31.8 0.4 collective-permute-start.10
  32.1 0.1 fold1.2
  32.2 1.3 %collective-permute-start.9 = (f32[1,320,256]{2,1,0:T(8,128)S(1)}, f32[1,320,256]{2,1,0:T(8,128)S(1)}, u32[]{:S(2)}, u32[]{:S(2)}) collective-permute-start(f32[1,320,256]{2,1,0:T(8,128)S(1)} %fold1.2), channel_id=1, source_target_pairs={{0,16},{4,20},{8,24},{12,28},{16,0},{20,4},{24,8},{28,12},{1,17},{... | collective-permute-start | bytes 983048 | tf_op jit(solution)/shard_map/ppermute | solution.py:401
  33.5 0.8 collective-permute-start.8
  34.3 5.8 %collective-permute-done.8 = f32[32,512]{1,0:T(8,128)S(1)} collective-permute-done((f32[32,512]{1,0:T(8,128)S(1)}, f32[32,512]{1,0:T(8,128)S(1)}, u32[]{:S(2)}, u32[]{:S(2)}) %collective-permute-start.8) | collective-permute-done | bytes 65568 | tf_op jit(solution)/shard_map/ppermute | solution.py:401
  40.1 0.0 copy-start.6
  40.1 0.6 project.1
  40.7 0.0 copy-start.4
  40.7 1.6 %collective-permute-start.11 = (f32[32,512]{1,0:T(8,128)S(1)}, f32[32,512]{1,0:T(8,128)S(1)}, u32[]{:S(2)}, u32[]{:S(2)}) collective-permute-start(f32[32,512]{1,0:T(8,128)S(1)} %get-tuple-element.72), channel_id=1, source_target_pairs={{0,1},{1,0},{2,3},{3,2},{4,5},{5,4},{6,7},{7,6},{8,9},{9,8},{10,11... | collective-permute-start | bytes 196616 | tf_op jit(solution)/shard_map/ppermute | solution.py:401
  42.4 2.1 %root1a.1.state = f32[3,32,32]{2,1,0:T(8,128)S(1)} custom-call(f32[32,512]{1,0:T(8,128)S(1)} %add.53.refs_0_.x_ref.own_ref), custom_call_target="tpu_custom_call" | custom-call | flops 12000000 | bytes 65536 | tf_op jit(solution)/shard_map/root1a/pallas_call | solution.py:48
  44.4 0.9 collective-permute-done.11
  45.4 2.6 %collective-permute-start.12 = (f32[32,512]{1,0:T(8,128)S(1)}, f32[32,512]{1,0:T(8,128)S(1)}, u32[]{:S(2)}, u32[]{:S(2)}) collective-permute-start(f32[32,512]{1,0:T(8,128)S(1)} %add.54), channel_id=1, source_target_pairs={{0,2},{1,3},{2,0},{3,1},{4,6},{5,7},{6,4},{7,5},{8,10},{9,11},{10,... | collective-permute-start | bytes 196616 | tf_op jit(solution)/shard_map/ppermute | solution.py:401
  48.0 1.9 %root1b.1.a_ref = f32[32,32]{1,0:T(8,128)S(1)} custom-call(f32[3,32,32]{2,1,0:T(8,128)S(1)} %root1a.1.state), custom_call_target="tpu_custom_call" | custom-call | flops 12000000 | bytes 12288 | tf_op jit(solution)/shard_map/root1b/pallas_call | solution.py:48
  49.9 0.7 collective-permute-done.12
  50.6 0.7 lift.1
  51.3 1.9 %collective-permute-start.13 = (f32[32,320]{1,0:T(8,128)S(1)}, f32[32,320]{1,0:T(8,128)S(1)}, u32[]{:S(2)}, u32[]{:S(2)}) collective-permute-start(f32[32,320]{1,0:T(8,128)S(1)} %lift.1), channel_id=1, source_target_pairs={{0,1},{1,0},{2,3},{3,2},{4,5},{5,4},{6,7},{7,6},{8,9},{9,8},{10,11... | collective-permute-start | bytes 122888 | tf_op jit(solution)/shard_map/ppermute | solution.py:401
  53.3 0.2 convert_reduce_fusion
  53.5 2.0 %collective-permute-done.13 = f32[32,320]{1,0:T(8,128)S(1)} collective-permute-done((f32[32,320]{1,0:T(8,128)S(1)}, f32[32,320]{1,0:T(8,128)S(1)}, u32[]{:S(2)}, u32[]{:S(2)}) %collective-permute-start.13) | collective-permute-done | bytes 40992 | tf_op jit(solution)/shard_map/ppermute | solution.py:401
  55.5 2.8 %collective-permute-start.15 = (f32[32,320]{1,0:T(8,128)S(1)}, f32[32,320]{1,0:T(8,128)S(1)}, u32[]{:S(2)}, u32[]{:S(2)}) collective-permute-start(f32[32,320]{1,0:T(8,128)S(1)} %add.56), channel_id=1, source_target_pairs={{0,2},{1,3},{2,0},{3,1},{4,6},{5,7},{6,4},{7,5},{8,10},{9,11},{10,... | collective-permute-start | bytes 122888 | tf_op jit(solution)/shard_map/ppermute | solution.py:401
  58.4 0.1 fusion.1.chosen
  58.5 1.2 %gains.1 = (f32[2,2048]{1,0:T(2,128)}, f32[2,2048]{1,0:T(2,128)}) custom-call(s32[2]{0:T(128)S(1)} %pad_add_fusion.place, s32[2]{0:T(128)S(1)} %fusion.1.chosen, f32[32,512]{1,0:T(8,128)S(1)} %add.53.refs_0_.x_ref.own_ref, f32[32,512]{1,0:T(8,128)S(1)} %collective-permute-done.14.other_ref, f32[2,2048]{1,0:T(2,128)S(1)} %copy-done.4, f32[2,2048]{1,0:T(2,128)S(1)} %copy-done.5), custom_call_target="tpu_custom_call" | custom-call | flops 40960 | bytes 65536 | tf_op jit(solution)/shard_map/gains/pallas_call | solution.py:48
  59.7 0.9 collective-permute-done.15
  60.6 1.6 %collective-permute-start.16 = (f32[32,320]{1,0:T(8,128)S(1)}, f32[32,320]{1,0:T(8,128)S(1)}, u32[]{:S(2)}, u32[]{:S(2)}) collective-permute-start(f32[32,320]{1,0:T(8,128)S(1)} %add.57), channel_id=1, source_target_pairs={{0,8},{4,12},{8,0},{12,4},{16,24},{20,28},{24,16},{28,20},{1,9},{5... | collective-permute-start | bytes 122888 | tf_op jit(solution)/shard_map/ppermute | solution.py:401
  62.1 2.6 %collective-permute-done.16 = f32[32,320]{1,0:T(8,128)S(1)} collective-permute-done((f32[32,320]{1,0:T(8,128)S(1)}, f32[32,320]{1,0:T(8,128)S(1)}, u32[]{:S(2)}, u32[]{:S(2)}) %collective-permute-start.16) | collective-permute-done | bytes 40992 | tf_op jit(solution)/shard_map/ppermute | solution.py:401
  64.8 1.5 %collective-permute-start.17 = (f32[32,320]{1,0:T(8,128)S(1)}, f32[32,320]{1,0:T(8,128)S(1)}, u32[]{:S(2)}, u32[]{:S(2)}) collective-permute-start(f32[32,320]{1,0:T(8,128)S(1)} %add.58), channel_id=1, source_target_pairs={{0,16},{4,20},{8,24},{12,28},{16,0},{20,4},{24,8},{28,12},{1,17},{... | collective-permute-start | bytes 122888 | tf_op jit(solution)/shard_map/ppermute | solution.py:401
  66.3 2.6 %collective-permute-done.17 = f32[32,320]{1,0:T(8,128)S(1)} collective-permute-done((f32[32,320]{1,0:T(8,128)S(1)}, f32[32,320]{1,0:T(8,128)S(1)}, u32[]{:S(2)}, u32[]{:S(2)}) %collective-permute-start.17) | collective-permute-done | bytes 40992 | tf_op jit(solution)/shard_map/ppermute | solution.py:401
  68.9 0.5 lower.1
  69.4 1.9 %collective-permute-start.18 = (f32[32,512]{1,0:T(8,128)S(1)}, f32[32,512]{1,0:T(8,128)S(1)}, u32[]{:S(2)}, u32[]{:S(2)}) collective-permute-start(f32[32,512]{1,0:T(8,128)S(1)} %lower.1), channel_id=1, source_target_pairs={{0,1},{1,0},{2,3},{3,2},{4,5},{5,4},{6,7},{7,6},{8,9},{9,8},{10,11... | collective-permute-start | bytes 196616 | tf_op jit(solution)/shard_map/ppermute | solution.py:401
  71.3 2.4 %root2a.1.state = f32[3,32,32]{2,1,0:T(8,128)S(1)} custom-call(f32[32,32]{1,0:T(8,128)S(1)} %root1b.1.a_ref, f32[32,320]{1,0:T(8,128)S(1)} %add.59.u_ref), custom_call_target="tpu_custom_call" | custom-call | flops 12000000 | bytes 45056 | tf_op jit(solution)/shard_map/root2a/pallas_call | solution.py:48
  73.7 0.6 collective-permute-done.18
  74.3 2.4 %collective-permute-start.19 = (f32[32,512]{1,0:T(8,128)S(1)}, f32[32,512]{1,0:T(8,128)S(1)}, u32[]{:S(2)}, u32[]{:S(2)}) collective-permute-start(f32[32,512]{1,0:T(8,128)S(1)} %add.60), channel_id=1, source_target_pairs={{0,2},{1,3},{2,0},{3,1},{4,6},{5,7},{6,4},{7,5},{8,10},{9,11},{10,... | collective-permute-start | bytes 196616 | tf_op jit(solution)/shard_map/ppermute | solution.py:401
  76.8 2.3 %root2b.1.f0_ref = f32[32,384]{1,0:T(8,128)S(1)} custom-call(f32[3,32,32]{2,1,0:T(8,128)S(1)} %root2a.1.state, f32[32,32]{1,0:T(8,128)S(1)} %root1b.1.a_ref, f32[32,320]{1,0:T(8,128)S(1)} %add.59.u_ref), custom_call_target="tpu_custom_call" | custom-call | flops 12000000 | bytes 57344 | tf_op jit(solution)/shard_map/root2b/pallas_call | solution.py:48
  79.0 0.6 collective-permute-done.19
  79.6 0.1 collective-permute-start.21
  79.7 1.6 %collective-permute-start.20 = (f32[1,32,512]{2,1,0:T(8,128)S(1)}, f32[1,32,512]{2,1,0:T(8,128)S(1)}, u32[]{:S(2)}, u32[]{:S(2)}) collective-permute-start(f32[1,32,512]{2,1,0:T(8,128)S(1)} %add_bitcast_fusion.v0_ref), channel_id=1, source_target_pairs={{0,8},{4,12},{8,0},{12,4},{16,24},{20,28},{24,16},{28,20},{1,9},{5... | collective-permute-start | bytes 196616 | tf_op jit(solution)/shard_map/ppermute | solution.py:401
  81.2 0.2 collective-permute-start.22
  81.4 1.1 %collective-permute-done.22.f1_ref = f32[32,384]{1,0:T(8,128)S(1)} collective-permute-done((f32[32,384]{1,0:T(8,128)S(1)}, f32[32,384]{1,0:T(8,128)S(1)}, u32[]{:S(2)}, u32[]{:S(2)}) %collective-permute-start.22) | collective-permute-done | bytes 49184 | tf_op jit(solution)/shard_map/ppermute | solution.py:401
  82.5 3.4 %finish0.1 = (f32[1,2,320,2048]{3,2,1,0:T(8,128)}, f32[2,64,2048]{2,1,0:T(8,128)}, f32[2,64,2048]{2,1,0:T(8,128)}) custom-call(s32[2]{0:T(128)S(1)} %pad_add_fusion.place, s32[2]{0:T(128)S(1)} %fusion.1.chosen, f32[1,32,512]{2,1,0:T(8,128)S(1)} %add_bitcast_fusion.v0_ref, f32[1,32,512]{2,1,0:T(8,128)S(1)} %collective-permute-done.21.v1_ref, ...), custom_call_target="tpu_custom_call" | custom-call | flops 125829120 | bytes 2359296 | tf_op jit(solution)/shard_map/finish0/pallas_call | solution.py:48
  85.9 1.4 %collective-permute-start.23 = (f32[2,32,512]{2,1,0:T(8,128)S(1)}, f32[2,32,512]{2,1,0:T(8,128)S(1)}, u32[]{:S(2)}, u32[]{:S(2)}) collective-permute-start(f32[2,32,512]{2,1,0:T(8,128)S(1)} %pad_maximum_fusion), channel_id=1, source_target_pairs={{0,16},{4,20},{8,24},{12,28},{16,0},{20,4},{24,8},{28,12},{1,17},{... | collective-permute-start | bytes 393224 | tf_op jit(solution)/shard_map/ppermute | solution.py:401
  87.3 1.3 %collective-permute-done.24.v1_ref = f32[1,32,512]{2,1,0:T(8,128)S(1)} collective-permute-done((f32[1,32,512]{2,1,0:T(8,128)S(1)}, f32[1,32,512]{2,1,0:T(8,128)S(1)}, u32[]{:S(2)}, u32[]{:S(2)}) %collective-permute-start.24) | collective-permute-done | bytes 65568 | tf_op jit(solution)/shard_map/ppermute | solution.py:401
  88.6 3.4 %finish1.1 = (f32[1,2,320,2048]{3,2,1,0:T(8,128)}, f32[2,64,2048]{2,1,0:T(8,128)}, f32[2,64,2048]{2,1,0:T(8,128)}) custom-call(s32[2]{0:T(128)S(1)} %pad_add_fusion.place, s32[2]{0:T(128)S(1)} %fusion.1.chosen, f32[1,32,512]{2,1,0:T(8,128)S(1)} %collective-permute-done.20.v0_ref, ...), custom_call_target="tpu_custom_call", output_to_operand_aliasing={{0}: (12, {}), {1}: (13, {}), {2}: (14, {})} | custom-call | flops 125829120 | bytes 2359296 | tf_op jit(solution)/shard_map/finish1/pallas_call | solution.py:48
  92.0 0.2 collective-permute-start.25
  92.3 1.2 %collective-permute-done.25.v1_ref = f32[2,32,512]{2,1,0:T(8,128)S(1)} collective-permute-done((f32[2,32,512]{2,1,0:T(8,128)S(1)}, f32[2,32,512]{2,1,0:T(8,128)S(1)}, u32[]{:S(2)}, u32[]{:S(2)}) %collective-permute-start.25) | collective-permute-done | bytes 131104 | tf_op jit(solution)/shard_map/ppermute | solution.py:401
  93.4 4.5 %finish2.1 = (f32[1,2,320,2048]{3,2,1,0:T(8,128)}, f32[2,64,2048]{2,1,0:T(8,128)}, f32[2,64,2048]{2,1,0:T(8,128)}) custom-call(s32[2]{0:T(128)S(1)} %pad_add_fusion.place, s32[2]{0:T(128)S(1)} %fusion.1.chosen, f32[2,32,512]{2,1,0:T(8,128)S(1)} %collective-permute-done.23.v0_ref, ...), custom_call_target="tpu_custom_call", output_to_operand_aliasing={{0}: (12, {}), {1}: (13, {}), {2}: (14, {})} | custom-call | flops 251658240 | bytes 4718592 | tf_op jit(solution)/shard_map/finish2/pallas_call | solution.py:48
  (38 shorter events, 0.2 us)
Async XLA Ops:
  3.6 8.3 %copy-start = (f32[4,320,256]{2,1,0:T(8,128)}, f32[4,320,256]{2,1,0:T(8,128)S(1)}, u32[]{:S(2)}) copy-start(f32[4,320,256]{2,1,0:T(8,128)S(1)} %get-tuple-element.62.refs_2_) | copy-start | bytes 3932164
  3.6 8.3 %copy-start.2 = (f32[4,320,256]{2,1,0:T(8,128)}, f32[4,320,256]{2,1,0:T(8,128)S(1)}, u32[]{:S(2)}) copy-start(f32[4,320,256]{2,1,0:T(8,128)S(1)} %get-tuple-element.64.refs_3_) | copy-start | bytes 3932164
  3.6 3.5 %collective-permute-start.2 = (f32[4,320,256]{2,1,0:T(8,128)S(1)}, f32[4,320,256]{2,1,0:T(8,128)S(1)}, u32[]{:S(2)}, u32[]{:S(2)}) collective-permute-start(f32[4,320,256]{2,1,0:T(8,128)S(1)} %get-tuple-element.64.refs_3_), channel_id=1, source_target_pairs={{0,4},{4,0},{8,12},{12,8},{16,20},{20,16},{24,28},{28,24},{1,5},{5... | collective-permute-start | bytes 3932168 | tf_op jit(solution)/shard_map/ppermute | solution.py:401
  4.2 6.1 %collective-permute-start = (f32[4,320,256]{2,1,0:T(8,128)S(1)}, f32[4,320,256]{2,1,0:T(8,128)S(1)}, u32[]{:S(2)}, u32[]{:S(2)}) collective-permute-start(f32[4,320,256]{2,1,0:T(8,128)S(1)} %get-tuple-element.62.refs_2_), channel_id=1, source_target_pairs={{0,4},{4,0},{8,12},{12,8},{16,20},{20,16},{24,28},{28,24},{1,5},{5... | collective-permute-start | bytes 3932168 | tf_op jit(solution)/shard_map/ppermute | solution.py:401
  7.2 24.5 %collective-permute-start.3 = (f32[2,320,256]{2,1,0:T(8,128)S(1)}, f32[2,320,256]{2,1,0:T(8,128)S(1)}, u32[]{:S(2)}, u32[]{:S(2)}) collective-permute-start(f32[2,320,256]{2,1,0:T(8,128)S(1)} %fold0.3), channel_id=1, source_target_pairs={{0,16},{4,20},{8,24},{12,28},{16,0},{20,4},{24,8},{28,12},{1,17},{... | collective-permute-start | bytes 1966088 | tf_op jit(solution)/shard_map/ppermute | solution.py:401
  10.3 21.4 %collective-permute-start.1 = (f32[2,320,256]{2,1,0:T(8,128)S(1)}, f32[2,320,256]{2,1,0:T(8,128)S(1)}, u32[]{:S(2)}, u32[]{:S(2)}) collective-permute-start(f32[2,320,256]{2,1,0:T(8,128)S(1)} %fold0.2), channel_id=1, source_target_pairs={{0,8},{4,12},{8,0},{12,4},{16,24},{20,28},{24,16},{28,20},{1,9},{5... | collective-permute-start | bytes 1966088 | tf_op jit(solution)/shard_map/ppermute | solution.py:401
  16.0 1.3 %collective-permute-start.4 = (f32[32,512]{1,0:T(8,128)S(1)}, f32[32,512]{1,0:T(8,128)S(1)}, u32[]{:S(2)}, u32[]{:S(2)}) collective-permute-start(f32[32,512]{1,0:T(8,128)S(1)} %get-tuple-element.67), channel_id=1, source_target_pairs={{0,4},{4,0},{8,12},{12,8},{16,20},{20,16},{24,28},{28,24},{1,5},{5... | collective-permute-start | bytes 196616 | tf_op jit(solution)/shard_map/ppermute | solution.py:401
  17.3 4.3 %collective-permute-start.5 = (f32[32,512]{1,0:T(8,128)S(1)}, f32[32,512]{1,0:T(8,128)S(1)}, u32[]{:S(2)}, u32[]{:S(2)}) collective-permute-start(f32[32,512]{1,0:T(8,128)S(1)} %add.49), channel_id=1, source_target_pairs={{0,1},{1,0},{2,3},{3,2},{4,5},{5,4},{6,7},{7,6},{8,9},{9,8},{10,11... | collective-permute-start | bytes 196616 | tf_op jit(solution)/shard_map/ppermute | solution.py:401
  21.7 5.3 %collective-permute-start.6 = (f32[32,512]{1,0:T(8,128)S(1)}, f32[32,512]{1,0:T(8,128)S(1)}, u32[]{:S(2)}, u32[]{:S(2)}) collective-permute-start(f32[32,512]{1,0:T(8,128)S(1)} %add.50), channel_id=1, source_target_pairs={{0,2},{1,3},{2,0},{3,1},{4,6},{5,7},{6,4},{7,5},{8,10},{9,11},{10,... | collective-permute-start | bytes 196616 | tf_op jit(solution)/shard_map/ppermute | solution.py:401
  27.0 4.7 %collective-permute-start.7 = (f32[32,512]{1,0:T(8,128)S(1)}, f32[32,512]{1,0:T(8,128)S(1)}, u32[]{:S(2)}, u32[]{:S(2)}) collective-permute-start(f32[32,512]{1,0:T(8,128)S(1)} %add.51), channel_id=1, source_target_pairs={{0,8},{4,12},{8,0},{12,4},{16,24},{20,28},{24,16},{28,20},{1,9},{5... | collective-permute-start | bytes 196616 | tf_op jit(solution)/shard_map/ppermute | solution.py:401
  31.8 8.3 %collective-permute-start.10 = (f32[1,320,256]{2,1,0:T(8,128)S(1)}, f32[1,320,256]{2,1,0:T(8,128)S(1)}, u32[]{:S(2)}, u32[]{:S(2)}) collective-permute-start(f32[1,320,256]{2,1,0:T(8,128)S(1)} %fold1.3), channel_id=1, source_target_pairs={{0,8},{4,12},{8,0},{12,4},{16,24},{20,28},{24,16},{28,20},{1,9},{5... | collective-permute-start | bytes 983048 | tf_op jit(solution)/shard_map/ppermute | solution.py:401
  32.2 7.9 %collective-permute-start.9 = (f32[1,320,256]{2,1,0:T(8,128)S(1)}, f32[1,320,256]{2,1,0:T(8,128)S(1)}, u32[]{:S(2)}, u32[]{:S(2)}) collective-permute-start(f32[1,320,256]{2,1,0:T(8,128)S(1)} %fold1.2), channel_id=1, source_target_pairs={{0,16},{4,20},{8,24},{12,28},{16,0},{20,4},{24,8},{28,12},{1,17},{... | collective-permute-start | bytes 983048 | tf_op jit(solution)/shard_map/ppermute | solution.py:401
  33.5 6.6 %collective-permute-start.8 = (f32[32,512]{1,0:T(8,128)S(1)}, f32[32,512]{1,0:T(8,128)S(1)}, u32[]{:S(2)}, u32[]{:S(2)}) collective-permute-start(f32[32,512]{1,0:T(8,128)S(1)} %add.52), channel_id=1, source_target_pairs={{0,16},{4,20},{8,24},{12,28},{16,0},{20,4},{24,8},{28,12},{1,17},{... | collective-permute-start | bytes 196616 | tf_op jit(solution)/shard_map/ppermute | solution.py:401
  40.1 7.9 %copy-start.6 = (s32[12]{0:T(128)S(1)}, s32[12]{0:T(128)}, u32[]{:S(2)}) copy-start(s32[12]{0:T(128)} %param.13) | copy-start | bytes 148
  40.7 17.8 %copy-start.4 = (f32[2,2048]{1,0:T(2,128)S(1)}, f32[2,2048]{1,0:T(2,128)}, u32[]{:S(2)}) copy-start(f32[2,2048]{1,0:T(2,128)} %mv_ref.1) | copy-start | bytes 49156
  40.7 17.8 %copy-start.5 = (f32[2,2048]{1,0:T(2,128)S(1)}, f32[2,2048]{1,0:T(2,128)}, u32[]{:S(2)}) copy-start(f32[2,2048]{1,0:T(2,128)} %wv_ref.1) | copy-start | bytes 49156
  40.7 4.6 %collective-permute-start.11 = (f32[32,512]{1,0:T(8,128)S(1)}, f32[32,512]{1,0:T(8,128)S(1)}, u32[]{:S(2)}, u32[]{:S(2)}) collective-permute-start(f32[32,512]{1,0:T(8,128)S(1)} %get-tuple-element.72), channel_id=1, source_target_pairs={{0,1},{1,0},{2,3},{3,2},{4,5},{5,4},{6,7},{7,6},{8,9},{9,8},{10,11... | collective-permute-start | bytes 196616 | tf_op jit(solution)/shard_map/ppermute | solution.py:401
  45.4 5.2 %collective-permute-start.12 = (f32[32,512]{1,0:T(8,128)S(1)}, f32[32,512]{1,0:T(8,128)S(1)}, u32[]{:S(2)}, u32[]{:S(2)}) collective-permute-start(f32[32,512]{1,0:T(8,128)S(1)} %add.54), channel_id=1, source_target_pairs={{0,2},{1,3},{2,0},{3,1},{4,6},{5,7},{6,4},{7,5},{8,10},{9,11},{10,... | collective-permute-start | bytes 196616 | tf_op jit(solution)/shard_map/ppermute | solution.py:401
  48.0 7.5 %collective-permute-start.14 = (f32[32,512]{1,0:T(8,128)S(1)}, f32[32,512]{1,0:T(8,128)S(1)}, u32[]{:S(2)}, u32[]{:S(2)}) collective-permute-start(f32[32,512]{1,0:T(8,128)S(1)} %add.53.refs_0_.x_ref.own_ref), channel_id=1, source_target_pairs={{0,4},{4,0},{8,12},{12,8},{16,20},{20,16},{24,28},{28,24},{1,5},{5... | collective-permute-start | bytes 196616 | tf_op jit(solution)/shard_map/ppermute | solution.py:401
  50.6 31.8 %copy-start.1 = (f32[4,320,256]{2,1,0:T(8,128)S(1)}, f32[4,320,256]{2,1,0:T(8,128)}, u32[]{:S(2)}) copy-start(f32[4,320,256]{2,1,0:T(8,128)} %copy-done) | copy-start | bytes 3932164
  50.6 31.8 %copy-start.3 = (f32[4,320,256]{2,1,0:T(8,128)S(1)}, f32[4,320,256]{2,1,0:T(8,128)}, u32[]{:S(2)}) copy-start(f32[4,320,256]{2,1,0:T(8,128)} %copy-done.2) | copy-start | bytes 3932164
  51.3 4.2 %collective-permute-start.13 = (f32[32,320]{1,0:T(8,128)S(1)}, f32[32,320]{1,0:T(8,128)S(1)}, u32[]{:S(2)}, u32[]{:S(2)}) collective-permute-start(f32[32,320]{1,0:T(8,128)S(1)} %lift.1), channel_id=1, source_target_pairs={{0,1},{1,0},{2,3},{3,2},{4,5},{5,4},{6,7},{7,6},{8,9},{9,8},{10,11... | collective-permute-start | bytes 122888 | tf_op jit(solution)/shard_map/ppermute | solution.py:401
  55.5 5.1 %collective-permute-start.15 = (f32[32,320]{1,0:T(8,128)S(1)}, f32[32,320]{1,0:T(8,128)S(1)}, u32[]{:S(2)}, u32[]{:S(2)}) collective-permute-start(f32[32,320]{1,0:T(8,128)S(1)} %add.56), channel_id=1, source_target_pairs={{0,2},{1,3},{2,0},{3,1},{4,6},{5,7},{6,4},{7,5},{8,10},{9,11},{10,... | collective-permute-start | bytes 122888 | tf_op jit(solution)/shard_map/ppermute | solution.py:401
  60.6 4.2 %collective-permute-start.16 = (f32[32,320]{1,0:T(8,128)S(1)}, f32[32,320]{1,0:T(8,128)S(1)}, u32[]{:S(2)}, u32[]{:S(2)}) collective-permute-start(f32[32,320]{1,0:T(8,128)S(1)} %add.57), channel_id=1, source_target_pairs={{0,8},{4,12},{8,0},{12,4},{16,24},{20,28},{24,16},{28,20},{1,9},{5... | collective-permute-start | bytes 122888 | tf_op jit(solution)/shard_map/ppermute | solution.py:401
  64.8 4.2 %collective-permute-start.17 = (f32[32,320]{1,0:T(8,128)S(1)}, f32[32,320]{1,0:T(8,128)S(1)}, u32[]{:S(2)}, u32[]{:S(2)}) collective-permute-start(f32[32,320]{1,0:T(8,128)S(1)} %add.58), channel_id=1, source_target_pairs={{0,16},{4,20},{8,24},{12,28},{16,0},{20,4},{24,8},{28,12},{1,17},{... | collective-permute-start | bytes 122888 | tf_op jit(solution)/shard_map/ppermute | solution.py:401
  69.4 4.9 %collective-permute-start.18 = (f32[32,512]{1,0:T(8,128)S(1)}, f32[32,512]{1,0:T(8,128)S(1)}, u32[]{:S(2)}, u32[]{:S(2)}) collective-permute-start(f32[32,512]{1,0:T(8,128)S(1)} %lower.1), channel_id=1, source_target_pairs={{0,1},{1,0},{2,3},{3,2},{4,5},{5,4},{6,7},{7,6},{8,9},{9,8},{10,11... | collective-permute-start | bytes 196616 | tf_op jit(solution)/shard_map/ppermute | solution.py:401
  74.3 5.2 %collective-permute-start.19 = (f32[32,512]{1,0:T(8,128)S(1)}, f32[32,512]{1,0:T(8,128)S(1)}, u32[]{:S(2)}, u32[]{:S(2)}) collective-permute-start(f32[32,512]{1,0:T(8,128)S(1)} %add.60), channel_id=1, source_target_pairs={{0,2},{1,3},{2,0},{3,1},{4,6},{5,7},{6,4},{7,5},{8,10},{9,11},{10,... | collective-permute-start | bytes 196616 | tf_op jit(solution)/shard_map/ppermute | solution.py:401
  79.6 2.9 %collective-permute-start.21 = (f32[1,32,512]{2,1,0:T(8,128)S(1)}, f32[1,32,512]{2,1,0:T(8,128)S(1)}, u32[]{:S(2)}, u32[]{:S(2)}) collective-permute-start(f32[1,32,512]{2,1,0:T(8,128)S(1)} %add_bitcast_fusion.v0_ref), channel_id=1, source_target_pairs={{0,4},{4,0},{8,12},{12,8},{16,20},{20,16},{24,28},{28,24},{1,5},{5... | collective-permute-start | bytes 196616 | tf_op jit(solution)/shard_map/ppermute | solution.py:401
  79.7 6.2 %collective-permute-start.20 = (f32[1,32,512]{2,1,0:T(8,128)S(1)}, f32[1,32,512]{2,1,0:T(8,128)S(1)}, u32[]{:S(2)}, u32[]{:S(2)}) collective-permute-start(f32[1,32,512]{2,1,0:T(8,128)S(1)} %add_bitcast_fusion.v0_ref), channel_id=1, source_target_pairs={{0,8},{4,12},{8,0},{12,4},{16,24},{20,28},{24,16},{28,20},{1,9},{5... | collective-permute-start | bytes 196616 | tf_op jit(solution)/shard_map/ppermute | solution.py:401
  81.2 1.2 %collective-permute-start.22 = (f32[32,384]{1,0:T(8,128)S(1)}, f32[32,384]{1,0:T(8,128)S(1)}, u32[]{:S(2)}, u32[]{:S(2)}) collective-permute-start(f32[32,384]{1,0:T(8,128)S(1)} %root2b.1.f0_ref), channel_id=1, source_target_pairs={{0,4},{4,0},{8,12},{12,8},{16,20},{20,16},{24,28},{28,24},{1,5},{5... | collective-permute-start | bytes 147464 | tf_op jit(solution)/shard_map/ppermute | solution.py:401
  85.9 6.1 %collective-permute-start.23 = (f32[2,32,512]{2,1,0:T(8,128)S(1)}, f32[2,32,512]{2,1,0:T(8,128)S(1)}, u32[]{:S(2)}, u32[]{:S(2)}) collective-permute-start(f32[2,32,512]{2,1,0:T(8,128)S(1)} %pad_maximum_fusion), channel_id=1, source_target_pairs={{0,16},{4,20},{8,24},{12,28},{16,0},{20,4},{24,8},{28,12},{1,17},{... | collective-permute-start | bytes 393224 | tf_op jit(solution)/shard_map/ppermute | solution.py:401
  87.3 1.3 %collective-permute-start.24 = (f32[1,32,512]{2,1,0:T(8,128)S(1)}, f32[1,32,512]{2,1,0:T(8,128)S(1)}, u32[]{:S(2)}, u32[]{:S(2)}) collective-permute-start(f32[1,32,512]{2,1,0:T(8,128)S(1)} %collective-permute-done.20.v0_ref), channel_id=1, source_target_pairs={{0,4},{4,0},{8,12},{12,8},{16,20},{20,16},{24,28},{28,24},{1,5},{5... | collective-permute-start | bytes 196616 | tf_op jit(solution)/shard_map/ppermute | solution.py:401
  92.0 1.4 %collective-permute-start.25 = (f32[2,32,512]{2,1,0:T(8,128)S(1)}, f32[2,32,512]{2,1,0:T(8,128)S(1)}, u32[]{:S(2)}, u32[]{:S(2)}) collective-permute-start(f32[2,32,512]{2,1,0:T(8,128)S(1)} %collective-permute-done.23.v0_ref), channel_id=1, source_target_pairs={{0,4},{4,0},{8,12},{12,8},{16,20},{20,16},{24,28},{28,24},{1,5},{5... | collective-permute-start | bytes 393224 | tf_op jit(solution)/shard_map/ppermute | solution.py:401

commit v3 on v2

v3 whole, which is shorter than its diff:
```python
import functools

import jax
import jax.numpy as jnp
from jax import lax
from jax.experimental import pallas as pl
from jax.experimental.pallas import tpu as pltpu
from jax.sharding import PartitionSpec as P

ROOT_ITERS = 12
LANES = 128
f32 = jnp.float32
NN = ((1,), (0,))
NT = ((1,), (1,))
TN = ((0,), (0,))
ANY = pl.BlockSpec(memory_space=pl.ANY)
VMEM = pl.BlockSpec(memory_space=pltpu.VMEM)
SMEM = pl.BlockSpec(memory_space=pltpu.SMEM)


def dot(a, b, dims=NN):
    return lax.dot_general(
        a, b, (dims, ((), ())), precision=lax.Precision.HIGHEST, preferred_element_type=f32
    )


def split3(a):
    high = a.astype(jnp.bfloat16)
    rest = a - high.astype(f32)
    middle = rest.astype(jnp.bfloat16)
    low = (rest - middle.astype(f32)).astype(jnp.bfloat16)
    return high, middle, low


def lanes(n):
    return -(-n // LANES) * LANES


def in_hbm(a):
    return pltpu.with_memory_space_constraint(a, pltpu.HBM)


def in_vmem(a):
    return pltpu.with_memory_space_constraint(a, pltpu.VMEM)


def call(kernel, name, in_specs, out_specs, out_shape, operands, mib=8, flops=0, nbytes=0, scratch=(), aliases={}):
    return pl.pallas_call(
        kernel,
        in_specs=in_specs,
        out_specs=out_specs,
        out_shape=out_shape,
        scratch_shapes=scratch,
        input_output_aliases=aliases,
        compiler_params=pltpu.CompilerParams(vmem_limit_bytes=mib << 20),
        cost_estimate=pl.CostEstimate(flops=flops, bytes_accessed=nbytes, transcendentals=0),
        name=name,
    )(*operands)


def small_call(kernel, name, shapes, *operands):
    return call(
        kernel,
        name,
        [VMEM] * len(operands),
        [VMEM] * len(shapes),
        [jax.ShapeDtypeStruct(s, f32) for s in shapes],
        operands,
        flops=12_000_000,
        nbytes=4 * sum(o.size for o in operands),
    )


def block_columns(place, own, p, blocks, width):
    bits = blocks.bit_length() - 1
    mirrored = sum((p >> i & 1) << (bits - 1 - i) for i in range(bits))
    core = place[0] if own else 1 - place[0]
    block = place[1] ^ jnp.where(core == 0, p, mirrored)
    return pl.ds(pl.multiple_of(block * width, width), width)


def write_factor(out, place, own, w_ref, vec_ref, halves):
    half, rows, width = halves[0].shape
    rank = w_ref.shape[1]
    m = place[0] if own else 1 - place[0]
    terms = jnp.zeros((rows, 3 * rank), f32)
    for p in range(2 * half):
        w_high, w_middle, w_low = split3(w_ref[m, :, block_columns(place, own, p, 2 * half, width)])
        high, middle, _ = split3(halves[p % 2][p // 2])
        for part, pieces in (
            (high, (w_high, w_middle, w_low)),
            (middle, (w_high, w_middle, jnp.zeros_like(w_low))),
        ):
            terms += lax.dot_general(
                part, jnp.concatenate(pieces, axis=0), (NT, ((), ())), preferred_element_type=f32
            )
    out[...] = jnp.zeros(out.shape, f32)
    out[:, :rows] = (terms[:, :rank] + terms[:, rank : 2 * rank] + terms[:, 2 * rank :]).T
    mine = jnp.where(m == 0, vec_ref[0, 0:1, :], vec_ref[0, 1:2, :])
    for i in range(vec_ref.shape[2] // LANES):
        out[i : i + 1, out.shape[1] - LANES :] = mine[:, i * LANES : (i + 1) * LANES]


def factor_shape(rows, warm_start):
    return jax.ShapeDtypeStruct((warm_start.shape[1], lanes(rows) + LANES), f32)


def factor_kernel(place, w_ref, vec_ref, even, odd, out):
    write_factor(out, place, True, w_ref, vec_ref, (even, odd))


def own_factor(place, halves, warm_start, vec_grads):
    rows = halves[0].shape[1]
    return call(
        factor_kernel,
        "factor",
        [SMEM] + [VMEM] * 4,
        VMEM,
        factor_shape(rows, warm_start),
        (place, warm_start, vec_grads, *halves),
        flops=12 * rows * warm_start.size,
        nbytes=8 * rows * warm_start.shape[2],
    )


def combine_kernel(place, g_hbm, e_hbm, *refs, own):
    if own:
        w_ref, vec_ref, other_even, other_odd, *refs = refs
        even, odd, factor, g, e, sem = refs
    else:
        even, odd, g, e, sem = refs
    blocks, rows, width = g.shape
    m = place[0] if own else 1 - place[0]
    order = [*range(1, blocks, 2), *range(0, blocks, 2)]
    loads = {}
    for p in order:
        where = block_columns(place, own, p, blocks, width)
        loads[p] = (
            pltpu.make_async_copy(g_hbm.at[0, m, :, where], g.at[p], sem.at[p, 0]),
            pltpu.make_async_copy(e_hbm.at[0, m, :, where], e.at[p], sem.at[p, 1]),
        )
        for load in loads[p]:
            load.start()
    if own:
        write_factor(factor, place, False, w_ref, vec_ref, (other_even, other_odd))
    for p in order:
        for load in loads[p]:
            load.wait()
        (even, odd)[p % 2][p // 2] = g[p].astype(f32) + e[p]


def combine(place, grads, errors, blocks, factor_of=()):
    rows, cols = grads.shape[2:]
    own = bool(factor_of)
    shape = (blocks, rows, cols // blocks)
    half = pltpu.VMEM((blocks // 2,) + shape[1:], f32)
    return call(
        functools.partial(combine_kernel, own=own),
        "own" if own else "other",
        [SMEM, ANY, ANY] + [VMEM] * len(factor_of),
        [VMEM] * (3 if own else 2),
        [half, half] + ([factor_shape(rows, factor_of[0])] if own else []),
        (place, grads, errors, *factor_of),
        mib=12,
        flops=rows * cols * (200 if own else 1),
        nbytes=rows * cols * 10,
        scratch=[pltpu.VMEM(shape, grads.dtype), pltpu.VMEM(shape, f32), pltpu.SemaphoreType.DMA((blocks, 2))],
    )


def fold_kernel(*refs, picks):
    for i, pick in enumerate(picks):
        refs[-1][i] = sum(refs[k][at] for k, at in pick)


def fold(terms, after=()):
    arrays, picks = [], []
    for pairs in terms:
        pick = []
        for a, at in pairs:
            if not any(a is b for b in arrays):
                arrays.append(a)
            pick.append((next(k for k, b in enumerate(arrays) if a is b), at))
        picks.append(pick)
    shape = (len(terms),) + arrays[0].shape[1:]
    return call(
        functools.partial(fold_kernel, picks=picks),
        "fold",
        [VMEM] * len(arrays) + [ANY] * len(after),
        VMEM,
        pltpu.VMEM(shape, f32),
        (*arrays, *after),
        nbytes=4 * len(picks[0]) * shape[0] * shape[1] * shape[2],
    )


def project_kernel(x_ref, *refs, places, count):
    parts, (s_ref, v_ref) = refs[:-2], refs[-2:]
    block = sum(part[at] for part, at in zip(parts, places))
    s_ref[...] = block
    v_ref[...] = dot(x_ref[:, : block.shape[0]] / count, block) / count


def lift_kernel(v_ref, s_ref, u_ref, *, count):
    u_ref[...] = dot(v_ref[...], s_ref[...], NT) / count


def lower_kernel(u_ref, s_ref, v_ref, *, count):
    v_ref[...] = dot(u_ref[...], s_ref[...]) / count


def identity(rank):
    return (
        lax.broadcasted_iota(jnp.int32, (rank, rank), 0)
        == lax.broadcasted_iota(jnp.int32, (rank, rank), 1)
    ).astype(f32)


def sweeps(left, right, first, last):
    eye = identity(left.shape[0])
    for sweep in range(first, last):
        middle = 1.5 * eye - 0.5 * (left if sweep == 0 else dot(right, left))
        right = middle if sweep == 0 else dot(middle, right)
        if sweep + 1 < ROOT_ITERS:
            left = dot(left, middle)
    return left, right


def root_begin(gram, state):
    spread = jnp.sqrt(jnp.sum(gram * gram, keepdims=True))
    left, right = sweeps(gram / spread, None, 0, ROOT_ITERS // 2)
    state[0], state[1] = left, right
    state[2] = jnp.broadcast_to(spread, gram.shape)


def root_end(state):
    _, right = sweeps(state[0], state[1], ROOT_ITERS // 2, ROOT_ITERS)
    return right / jnp.sqrt(state[2])


def first_begin_kernel(x_ref, state, *, rows, count):
    factor = x_ref[:, :rows] / count
    root_begin(dot(factor, factor, NT), state)


def first_end_kernel(state, a_ref):
    a_ref[...] = root_end(state)


def second_begin_kernel(a_ref, u_ref, state):
    a, u = a_ref[...], u_ref[...]
    root_begin(dot(a, dot(dot(u, u, NT), a), TN), state)


def second_end_kernel(state, a_ref, u_ref, f_ref):
    u = u_ref[...]
    rank, rows = u.shape
    both = dot(a_ref[...], root_end(state))
    f_ref[...] = jnp.zeros(f_ref.shape, f32)
    f_ref[:, :rows] = dot(both, u, TN)
    f_ref[:, rows : rows + rank] = both


def gains_kernel(place, chosen, own_ref, other_ref, mv_ref, wv_ref, mo_ref, wo_ref, vec, *, count, first):
    for i in range(mv_ref.shape[1] // LANES):
        at = slice(i * LANES, (i + 1) * LANES)
        for k, ref in enumerate((own_ref, other_ref)):
            vec[k : k + 1, at] = ref[i : i + 1, ref.shape[1] - LANES :] / count
    for slot in range(mv_ref.shape[0]):
        item = chosen[slot]
        row = jnp.where(item - first == place[0], vec[0:1, :], vec[1:2, :])
        old, weight = mv_ref[slot : slot + 1, :], wv_ref[slot : slot + 1, :]
        new = 0.9 * old + row
        mo_ref[slot : slot + 1, :] = jnp.where(item >= first, new, old)
        wo_ref[slot : slot + 1, :] = jnp.where(item >= first, weight - 0.5 * new, weight)


def gains(place, chosen, own, other, vec_momentum, vec_weights, count, first):
    return call(
        functools.partial(gains_kernel, count=count, first=first),
        "gains",
        [SMEM, SMEM] + [VMEM] * 4,
        [VMEM] * 2,
        [jax.ShapeDtypeStruct(vec_momentum.shape, f32)] * 2,
        (place, chosen, own, other, vec_momentum, vec_weights),
        flops=10 * vec_momentum.size,
        nbytes=16 * vec_momentum.size,
        scratch=[pltpu.VMEM((2, vec_momentum.shape[1]), f32)],
    )


def banks_kernel(mm_hbm, mw_hbm, mm, mw, sem):
    loads = (pltpu.make_async_copy(mm_hbm, mm, sem.at[0]), pltpu.make_async_copy(mw_hbm, mw, sem.at[1]))
    for load in loads:
        load.start()
    for load in loads:
        load.wait()


def banks(mat_momentum, mat_weights):
    return call(
        banks_kernel,
        "banks",
        [ANY, ANY],
        [VMEM] * 2,
        [pltpu.VMEM(mat_momentum.shape, f32)] * 2,
        (mat_momentum, mat_weights),
        nbytes=8 * mat_momentum.size,
        scratch=[pltpu.SemaphoreType.DMA((2,))],
    )


def finish_kernel(
    place, chosen, v0_ref, v1_ref, f0_ref, f1_ref, c0_even, c0_odd, c1_even, c1_odd, mm, mw, *refs, positions, head, later
):
    if later:
        left, refs = refs[0], refs[1 + 3 :]
        n_hbm, mo_hbm, wo_hbm, errors, approx, moment, weight, sem, bank_sem = refs
    else:
        n_hbm, mo_hbm, wo_hbm, left, errors, approx, moment, weight, sem, bank_sem = refs
    rank, width = v0_ref.shape[1:]
    blocks, rows = 2 * c0_even.shape[0], c0_even.shape[1]
    per = rows // head
    stores, bank_stores = [], []
    for k, p in enumerate(positions):
        for i, (v_ref, f_ref, *c_refs) in enumerate(
            ((v0_ref, f0_ref, c0_even, c0_odd), (v1_ref, f1_ref, c1_even, c1_odd))
        ):
            if k == 0 and not later:
                high, middle, low = split3(f_ref[:, :rows].T)
                left[i] = jnp.concatenate([high, high, middle, high, low, middle], axis=1)
            m = place[0] if i == 0 else 1 - place[0]
            columns = block_columns(place, i == 0, p, blocks, width)
            high, middle, low = split3(dot(f_ref[:, rows : rows + rank], v_ref[k], TN))
            right = jnp.concatenate([high, middle, high, low, high, middle], axis=0)
            product = jnp.dot(left[i], right, preferred_element_type=f32)
            approx[k, i] = product
            errors[k, i] = c_refs[p % 2][p // 2] - product
            stores.append(pltpu.make_async_copy(errors.at[k, i], n_hbm.at[0, m, :, columns], sem.at[k, i]))
            stores[-1].start()
            for slot in range(mm.shape[0]):
                item = chosen[slot]
                taken = (item >= m * per) & (item < (m + 1) * per)
                idle = (item < 0) | (item >= 2 * per)
                copies = (
                    pltpu.make_async_copy(
                        moment.at[k, i, slot], mo_hbm.at[slot, :, columns], bank_sem.at[k, i, slot, 0]
                    ),
                    pltpu.make_async_copy(
                        weight.at[k, i, slot], wo_hbm.at[slot, :, columns], bank_sem.at[k, i, slot, 1]
                    ),
                )

                @pl.when(taken)
                def _():
                    at = pl.ds(pl.multiple_of((item - m * per) * head, head), head)
                    new = 0.9 * mm[slot, :, columns] + approx[k, i, at, :]
                    moment[k, i, slot] = new
                    weight[k, i, slot] = mw[slot, :, columns] - 0.5 * new

                writes = taken
                if i == 0:
                    writes = taken | idle

                    @pl.when(idle)
                    def _():
                        moment[k, i, slot] = mm[slot, :, columns]
                        weight[k, i, slot] = mw[slot, :, columns]

                @pl.when(writes)
                def _():
                    for copy in copies:
                        copy.start()

                bank_stores.append((writes, copies))
    for store in stores:
        store.wait()
    for writes, copies in bank_stores:

        @pl.when(writes)
        def _():
            for copy in copies:
                copy.wait()


def finish(positions, left, outs, place, chosen, own_v, other_v, own_f, other_f, own_c, other_c, shapes, mm, mw):
    n, rank, width = own_v.shape
    matrices, rows, cols = shapes[0][1:]
    slots, head = mm.shape[:2]
    later = len(outs) > 0
    inputs = 12 + len(left)
    first = [] if later else [pltpu.VMEM((2, rows, 6 * rank), jnp.bfloat16)]
    return call(
        functools.partial(finish_kernel, positions=positions, head=head, later=later),
        f"finish{positions[0]}",
        [SMEM, SMEM] + [VMEM] * (10 + len(left)) + [ANY] * len(outs),
        [ANY] * 3 + [VMEM] * len(first),
        [pltpu.HBM(s, f32) for s in shapes] + first,
        (place, chosen, own_v, other_v, own_f, other_f, *own_c, *other_c, mm, mw, *left, *outs),
        mib=4 + 8 * n,
        flops=2 * n * matrices * rows * width * 6 * rank,
        nbytes=4 * n * width * (matrices * rows + 4 * slots * head),
        scratch=[
            pltpu.VMEM((n, 2, rows, width), f32),
            pltpu.VMEM((n, 2, rows, width), f32),
            pltpu.VMEM((n, 2, slots, head, width), f32),
            pltpu.VMEM((n, 2, slots, head, width), f32),
            pltpu.SemaphoreType.DMA((n, 2)),
            pltpu.SemaphoreType.DMA((n, 2, slots, 2)),
        ],
        aliases={inputs + i: i for i in range(len(outs))},
    )


def partner(kind, step):
    planes = (lax.axis_size("rep") // 2).bit_length() - 1
    depths = lax.axis_size("grp").bit_length() - 1

    def of(rep, grp):
        if kind == "core":
            return rep ^ 1, grp
        if kind == "plane":
            return rep ^ (2 << (step if rep % 2 == 0 else planes - 1 - step)), grp
        return rep, grp ^ (1 << (step if rep % 2 == 0 else depths - 1 - step))

    return of


def exchange(a, kind, step=0):
    groups = lax.axis_size("grp")
    of = partner(kind, step)
    pairs = []
    for rep in range(lax.axis_size("rep")):
        for grp in range(groups):
            to_rep, to_grp = of(rep, grp)
            pairs.append((rep * groups + grp, to_rep * groups + to_grp))
    return lax.ppermute(a, ("rep", "grp"), pairs)


def hop(a, kind, step, work=None, *operands):
    if work is None:
        return a + exchange(a, kind, step)
    a, *operands = lax.optimization_barrier((a, *operands))
    arrived = exchange(a, kind, step)
    done = work(*operands)
    arrived, *done = lax.optimization_barrier((arrived, *done))
    return a + arrived, *done


def local(grads, errors, warm_start, vec_grads, owners, mat_momentum, mat_weights, vec_momentum, vec_weights):
    reps, groups = lax.axis_size("rep"), lax.axis_size("grp")
    count = float(reps * groups)
    blocks = reps // 2
    bits = blocks.bit_length() - 1
    depths = groups.bit_length() - 1
    matrices, rows, cols = grads.shape[1:]
    rank = warm_start.shape[1]
    width = cols // blocks
    rep = lax.axis_index("rep")
    core, spot = rep % 2, rep // 2
    device = rep * groups + lax.axis_index("grp")
    place = jnp.stack([core, spot]).astype(jnp.int32)

    items = owners.shape[0]
    slots, head = mat_momentum.shape[:2]
    earlier = jnp.arange(items)[None, :] < jnp.arange(items)[:, None]
    same = owners[None, :] == owners[:, None]
    slot = jnp.sum((earlier & same).astype(jnp.int32), axis=1)
    match = (owners[None, :] == device) & (slot[None, :] == jnp.arange(slots)[:, None])
    head_items = matrices * (rows // head)
    chosen = jnp.max(jnp.where(match, jnp.arange(items)[None, :], -1), axis=1).astype(jnp.int32)

    grads, errors = in_hbm(grads), in_hbm(errors)
    mat_momentum, mat_weights = map(in_hbm, (mat_momentum, mat_weights))

    other_c = combine(place, grads, errors, blocks)
    arrived_odd = in_vmem(exchange(other_c[1], "core"))
    arrived_even = in_vmem(exchange(other_c[0], "core"))
    *own_c, other_p = combine(place, grads, errors, blocks, (warm_start, vec_grads, *other_c))

    terms = [[(own_c[p % 2], p // 2), ((arrived_even, arrived_odd)[p % 2], p // 2)] for p in range(blocks)]

    def send(goes, stage, after=()):
        return goes, stage, exchange(fold([terms[p] for p in goes], after), "plane", stage)

    def land(goes, stage, arrived):
        arrived = in_vmem(arrived)
        for i, p in enumerate(goes):
            terms[p ^ (1 << stage)].append((arrived, i))

    odd = [p for p in range(blocks) if p & 1]
    go = fold([terms[p] for p in odd if p & 2])
    ahead = [p for p in odd if p & 2], 0, exchange(go, "plane", 0)

    rest = [p for p in odd if not p & 2]
    go_rest = fold([terms[p] for p in rest])
    pending = [(rest, 0, exchange(go_rest, "plane", 0))]

    later, *_ = lax.optimization_barrier((place, go, go_rest))
    own_p = own_factor(later, own_c, warm_start, vec_grads)
    packed = own_p + exchange(other_p, "core")
    packed = hop(packed, "plane", bits - 1)
    land(*ahead)
    for stage in range(1, bits):
        goes = [p for p in range(blocks) if p >> stage & 1 and not p & ((1 << stage) - 1)]
        if stage > 1:
            while pending:
                land(*pending.pop(0))
        pending.append(send(goes, stage, (packed,)))
    for step in range(depths):
        packed = hop(packed, "z", step)
    for step in range(bits - 2, -1, -1):
        packed = hop(packed, "plane", step)
    while pending:
        land(*pending.pop(0))

    kept_sum, v = small_call(
        functools.partial(project_kernel, places=[at for _, at in terms[0]], count=count),
        "project", [(rows, width), (rank, width)], packed, *[a for a, _ in terms[0]],
    )
    square = (rank, rank)
    state = (3, rank, rank)
    v, first_state = hop(
        v, "z", 0,
        lambda x: small_call(
            functools.partial(first_begin_kernel, rows=rows, count=count), "root1a", [state], x
        ), packed,
    )
    v, first_root = hop(v, "z", 1, lambda x: small_call(first_end_kernel, "root1b", [square], x), first_state)
    for step in range(2, depths):
        v = hop(v, "z", step)
    (u,) = small_call(functools.partial(lift_kernel, count=count), "lift", [(rank, rows)], v, kept_sum)
    for step in range(depths - 1):
        u = hop(u, "z", step)
    u, vec_momentum_out, vec_weights_out = hop(
        u, "z", depths - 1,
        lambda x, y: gains(place, chosen, x, y, vec_momentum, vec_weights, count, head_items),
        packed, exchange(packed, "core"),
    )
    u, mm, mw = hop(u, "plane", 0, banks, mat_momentum, mat_weights)
    for step in range(1, bits):
        u = hop(u, "plane", step)
    (v,) = small_call(functools.partial(lower_kernel, count=count), "lower", [(rank, width)], u, kept_sum)
    v, second_state = hop(
        v, "z", 0, lambda *x: small_call(second_begin_kernel, "root2a", [state], *x), first_root, u
    )
    early = []

    def second_end(*x):
        early.extend(small_call(second_end_kernel, "root2b", [(rank, lanes(rows + rank))], *x))
        return early

    v, own_f = hop(v, "z", 1, second_end, second_state, first_root, u)
    other_f = exchange(early[0], "core")
    for step in range(2, depths):
        v = hop(v, "z", step)

    shapes = [errors.shape, mat_momentum.shape, mat_weights.shape]
    outs, left = (), ()
    v = v[None]
    fresh, positions = v, [0]
    for step in range(bits + 1):
        other_v = exchange(fresh, "core")
        if step < bits:
            arrived = exchange(v, "plane", step)
        outs = finish(
            positions, left, outs, place, chosen, fresh, other_v, own_f, other_f, own_c, other_c, shapes, mm, mw
        )
        if not left:
            *outs, left = outs
            left = (left,)
        if step < bits:
            arrived, *outs = lax.optimization_barrier((arrived, *outs))
            v = jnp.concatenate([v, arrived], axis=0)
            fresh, positions = arrived, list(range(1 << step, 2 << step))
    new_errors, mat_momentum_out, mat_weights_out = outs
    return (new_errors, mat_momentum_out, mat_weights_out, vec_momentum_out, vec_weights_out)


def solution(mesh):
    both = ("rep", "grp")
    return jax.shard_map(
        local,
        mesh=mesh,
        in_specs=(
            P(both, None, None, None),
            P(both, None, None, None),
            P(),
            P(both, None, None),
            P(),
            P(both, None, None),
            P(both, None, None),
            P(both, None),
            P(both, None),
        ),
        out_specs=(
            P(both, None, None, None),
            P(both, None, None),
            P(both, None, None),
            P(both, None),
            P(both, None),
        ),
        check_vma=False,
    )
```

time: 98.2 us -> 91.5 us (0.932)
  waiting for transfers between devices: 30.9 us -> 27.4 us
  Pallas kernels: 33.1 us -> 30.8 us
    ppermute x26 -> x25, waiting for transfers between devices: 30.9 us -> 27.4 us  [exchange(): return lax.ppermute(a, ('rep', 'grp'), pairs)]
    pallas_call x18, Pallas kernels: 33.1 us -> 30.8 us  [call(): pl.pallas_call(kernel, in_specs=in_specs, out_specs=out_specs, out_shape=...]
    ppermute x26 -> x25, starting transfers between devices: 32.5 us -> 31.6 us  [exchange(): return lax.ppermute(a, ('rep', 'grp'), pairs)]
  transfers between devices with their start and end apart: 26 -> 25, of which waited for: 16 -> 17; matrix products, arithmetic and copies ran while one was open for 0% -> 0% of each run, Pallas kernels for 25% -> 25%
where the time goes in v3:
time: 91.5 us; the launch traced here: 91.4 us
  starting transfers between devices  31.6 us (35%)
  Pallas kernels  30.8 us (34%)
  waiting for transfers between devices  27.4 us (30%)
  between operations  0.93 us (1%)
    ppermute x25, starting transfers between devices, exchange(): return lax.ppermute(a, ('rep', 'grp'), pairs)  31.6 us
    pallas_call x18, Pallas kernels, call(): pl.pallas_call(kernel, in_specs=in_specs, out_specs=out_specs, out_shape=...  30.8 us
    ppermute x25, waiting for transfers between devices, exchange(): return lax.ppermute(a, ('rep', 'grp'), pairs)  27.4 us
  transfers between devices with their start and end apart: 25, of which 17 were waited for; matrix products, arithmetic and copies ran while one was open for 0% of the time, Pallas kernels for 25%

profile of v3, /device:TPU:0, one launch (start us, length us, event | category | flops | bytes accessed | tf_op | source)
XLA Modules:
  0.0 91.4 jit_solution(15972656622613737635)
XLA Ops:
  0.7 0.1 pad_add_fusion.place
  0.7 2.8 %other.1 = (f32[2,320,512]{2,1,0:T(8,128)S(1)}, f32[2,320,512]{2,1,0:T(8,128)S(1)}) custom-call(s32[2]{0:T(128)S(1)} %pad_add_fusion.place, bf16[1,2,320,2048]{3,2,1,0:T(8,128)(2,1)} %g_hbm.3, f32[1,2,320,2048]{3,2,1,0:T(8,128)} %e_hbm.3), custom_call_target="tpu_custom_call" | custom-call | flops 655360 | bytes 6553600 | tf_op jit(solution)/shard_map/other/pallas_call | solution.py:48
  3.5 0.0 copy-start
  3.5 0.5 collective-permute-start
  4.0 0.1 collective-permute-start.6
  4.1 3.6 %own.1 = (f32[2,320,512]{2,1,0:T(8,128)S(1)}, f32[2,320,512]{2,1,0:T(8,128)S(1)}, f32[32,512]{1,0:T(8,128)S(1)}) custom-call(s32[2]{0:T(128)S(1)} %pad_add_fusion.place, bf16[1,2,320,2048]{3,2,1,0:T(8,128)(2,1)} %g_hbm.3, f32[1,2,320,2048]{3,2,1,0:T(8,128)} %e_hbm.3, f32[2,32,2048]{2,1,0:T(8,128)S(1)} %copy-done.4, f32[1,2,2048]{2,1,0:T(2,128)S(1)} %copy-done.5, ...), custom_call_target="tpu_custom_call" | custom-call | flops 131072000 | bytes 6553600 | tf_op jit(solution)/shard_map/own/pallas_call | solution.py:48
  7.8 0.1 fold.3
  7.9 3.0 %collective-permute-start.8 = (f32[1,320,512]{2,1,0:T(8,128)S(1)}, f32[1,320,512]{2,1,0:T(8,128)S(1)}, u32[]{:S(2)}, u32[]{:S(2)}) collective-permute-start(f32[1,320,512]{2,1,0:T(8,128)S(1)} %fold.3), channel_id=1, source_target_pairs={{0,8},{1,9},{2,10},{3,11},{4,20},{5,21},{6,22},{7,23},{8,0},{9,1},... | collective-permute-start | bytes 1966088 | tf_op jit(solution)/shard_map/ppermute | solution.py:437
  10.9 0.1 fold.4
  11.0 1.5 %factor.1 = f32[32,512]{1,0:T(8,128)S(1)} custom-call(s32[2]{0:T(128)S(1)} %pad_add_fusion.place, f32[2,32,2048]{2,1,0:T(8,128)S(1)} %copy-done.4, f32[1,2,2048]{2,1,0:T(2,128)S(1)} %copy-done.5, f32[2,320,512]{2,1,0:T(8,128)S(1)} %get-tuple-element.70.even.refs_0_.c0_even, f32[2,320,512]{2,1,0:T(8,128)S(1)} %get-tuple-element.68.refs_0_.odd.c0_odd), custom_call_target="tpu_custom_call" | custom-call | flops 503316480 | bytes 5242880 | tf_op jit(solution)/shard_map/factor/pallas_call | solution.py:48
  12.5 0.0 collective-permute-done.1
  12.5 1.6 %collective-permute-start.2 = (f32[32,512]{1,0:T(8,128)S(1)}, f32[32,512]{1,0:T(8,128)S(1)}, u32[]{:S(2)}, u32[]{:S(2)}) collective-permute-start(f32[32,512]{1,0:T(8,128)S(1)} %add.49), channel_id=1, source_target_pairs={{0,16},{1,17},{2,18},{3,19},{4,12},{5,13},{6,14},{7,15},{8,24},{9,... | collective-permute-start | bytes 196616 | tf_op jit(solution)/shard_map/ppermute | solution.py:437
  14.1 0.5 collective-permute-start.7
  14.7 3.0 %collective-permute-done.2 = f32[32,512]{1,0:T(8,128)S(1)} collective-permute-done((f32[32,512]{1,0:T(8,128)S(1)}, f32[32,512]{1,0:T(8,128)S(1)}, u32[]{:S(2)}, u32[]{:S(2)}) %collective-permute-start.2) | collective-permute-done | bytes 65568 | tf_op jit(solution)/shard_map/ppermute | solution.py:437
  17.7 2.5 %collective-permute-done.8.refs_2_ = f32[1,320,512]{2,1,0:T(8,128)S(1)} collective-permute-done((f32[1,320,512]{2,1,0:T(8,128)S(1)}, f32[1,320,512]{2,1,0:T(8,128)S(1)}, u32[]{:S(2)}, u32[]{:S(2)}) %collective-permute-start.8) | collective-permute-done | bytes 655392 | tf_op jit(solution)/shard_map/ppermute | solution.py:437
  20.2 0.1 fold.5
  20.3 2.1 %collective-permute-start.9 = (f32[1,320,512]{2,1,0:T(8,128)S(1)}, f32[1,320,512]{2,1,0:T(8,128)S(1)}, u32[]{:S(2)}, u32[]{:S(2)}) collective-permute-start(f32[1,320,512]{2,1,0:T(8,128)S(1)} %fold.5), channel_id=1, source_target_pairs={{0,16},{1,17},{2,18},{3,19},{4,12},{5,13},{6,14},{7,15},{8,24},{9,... | collective-permute-start | bytes 1966088 | tf_op jit(solution)/shard_map/ppermute | solution.py:437
  22.4 1.6 %collective-permute-start.3 = (f32[32,512]{1,0:T(8,128)S(1)}, f32[32,512]{1,0:T(8,128)S(1)}, u32[]{:S(2)}, u32[]{:S(2)}) collective-permute-start(f32[32,512]{1,0:T(8,128)S(1)} %add.50.refs_3_), channel_id=1, source_target_pairs={{0,1},{1,0},{2,3},{3,2},{4,6},{5,7},{6,4},{7,5},{8,9},{9,8},{10,11... | collective-permute-start | bytes 196616 | tf_op jit(solution)/shard_map/ppermute | solution.py:437
  24.0 2.7 %collective-permute-done.3 = f32[32,512]{1,0:T(8,128)S(1)} collective-permute-done((f32[32,512]{1,0:T(8,128)S(1)}, f32[32,512]{1,0:T(8,128)S(1)}, u32[]{:S(2)}, u32[]{:S(2)}) %collective-permute-start.3) | collective-permute-done | bytes 65568 | tf_op jit(solution)/shard_map/ppermute | solution.py:437
  26.7 2.6 %collective-permute-start.4 = (f32[32,512]{1,0:T(8,128)S(1)}, f32[32,512]{1,0:T(8,128)S(1)}, u32[]{:S(2)}, u32[]{:S(2)}) collective-permute-start(f32[32,512]{1,0:T(8,128)S(1)} %add.51), channel_id=1, source_target_pairs={{0,2},{1,3},{2,0},{3,1},{4,5},{5,4},{6,7},{7,6},{8,10},{9,11},{10,... | collective-permute-start | bytes 196616 | tf_op jit(solution)/shard_map/ppermute | solution.py:437
  29.3 2.6 %collective-permute-done.4 = f32[32,512]{1,0:T(8,128)S(1)} collective-permute-done((f32[32,512]{1,0:T(8,128)S(1)}, f32[32,512]{1,0:T(8,128)S(1)}, u32[]{:S(2)}, u32[]{:S(2)}) %collective-permute-start.4) | collective-permute-done | bytes 65568 | tf_op jit(solution)/shard_map/ppermute | solution.py:437
  31.9 1.6 %collective-permute-start.5 = (f32[32,512]{1,0:T(8,128)S(1)}, f32[32,512]{1,0:T(8,128)S(1)}, u32[]{:S(2)}, u32[]{:S(2)}) collective-permute-start(f32[32,512]{1,0:T(8,128)S(1)} %add.52), channel_id=1, source_target_pairs={{0,8},{1,9},{2,10},{3,11},{4,20},{5,21},{6,22},{7,23},{8,0},{9,1},... | collective-permute-start | bytes 196616 | tf_op jit(solution)/shard_map/ppermute | solution.py:437
  33.5 2.8 %collective-permute-done.5 = f32[32,512]{1,0:T(8,128)S(1)} collective-permute-done((f32[32,512]{1,0:T(8,128)S(1)}, f32[32,512]{1,0:T(8,128)S(1)}, u32[]{:S(2)}, u32[]{:S(2)}) %collective-permute-start.5) | collective-permute-done | bytes 65568 | tf_op jit(solution)/shard_map/ppermute | solution.py:437
  36.3 0.0 copy-start.8
  36.3 0.6 project.1
  36.9 0.0 copy-start.6
  36.9 0.0 copy-start.7
  36.9 1.6 %collective-permute-start.10 = (f32[32,512]{1,0:T(8,128)S(1)}, f32[32,512]{1,0:T(8,128)S(1)}, u32[]{:S(2)}, u32[]{:S(2)}) collective-permute-start(f32[32,512]{1,0:T(8,128)S(1)} %get-tuple-element.73), channel_id=1, source_target_pairs={{0,1},{1,0},{2,3},{3,2},{4,6},{5,7},{6,4},{7,5},{8,9},{9,8},{10,11... | collective-permute-start | bytes 196616 | tf_op jit(solution)/shard_map/ppermute | solution.py:437
  38.5 2.1 %root1a.1.state = f32[3,32,32]{2,1,0:T(8,128)S(1)} custom-call(f32[32,512]{1,0:T(8,128)S(1)} %add.53.x_ref.own_ref), custom_call_target="tpu_custom_call" | custom-call | flops 12000000 | bytes 65536 | tf_op jit(solution)/shard_map/root1a/pallas_call | solution.py:48
  40.6 0.6 collective-permute-done.10
  41.3 2.8 %collective-permute-start.11 = (f32[32,512]{1,0:T(8,128)S(1)}, f32[32,512]{1,0:T(8,128)S(1)}, u32[]{:S(2)}, u32[]{:S(2)}) collective-permute-start(f32[32,512]{1,0:T(8,128)S(1)} %add.54), channel_id=1, source_target_pairs={{0,2},{1,3},{2,0},{3,1},{4,5},{5,4},{6,7},{7,6},{8,10},{9,11},{10,... | collective-permute-start | bytes 196616 | tf_op jit(solution)/shard_map/ppermute | solution.py:437
  44.1 1.9 %root1b.1.a_ref = f32[32,32]{1,0:T(8,128)S(1)} custom-call(f32[3,32,32]{2,1,0:T(8,128)S(1)} %root1a.1.state), custom_call_target="tpu_custom_call" | custom-call | flops 12000000 | bytes 12288 | tf_op jit(solution)/shard_map/root1b/pallas_call | solution.py:48
  46.0 0.5 collective-permute-done.11
  46.5 0.7 lift.1
  47.2 1.9 %collective-permute-start.12 = (f32[32,320]{1,0:T(8,128)S(1)}, f32[32,320]{1,0:T(8,128)S(1)}, u32[]{:S(2)}, u32[]{:S(2)}) collective-permute-start(f32[32,320]{1,0:T(8,128)S(1)} %lift.1), channel_id=1, source_target_pairs={{0,1},{1,0},{2,3},{3,2},{4,6},{5,7},{6,4},{7,5},{8,9},{9,8},{10,11... | collective-permute-start | bytes 122888 | tf_op jit(solution)/shard_map/ppermute | solution.py:437
  49.1 0.2 convert_reduce_fusion
  49.3 2.5 %collective-permute-done.12 = f32[32,320]{1,0:T(8,128)S(1)} collective-permute-done((f32[32,320]{1,0:T(8,128)S(1)}, f32[32,320]{1,0:T(8,128)S(1)}, u32[]{:S(2)}, u32[]{:S(2)}) %collective-permute-start.12) | collective-permute-done | bytes 40992 | tf_op jit(solution)/shard_map/ppermute | solution.py:437
  51.8 2.5 %collective-permute-start.14 = (f32[32,320]{1,0:T(8,128)S(1)}, f32[32,320]{1,0:T(8,128)S(1)}, u32[]{:S(2)}, u32[]{:S(2)}) collective-permute-start(f32[32,320]{1,0:T(8,128)S(1)} %add.56), channel_id=1, source_target_pairs={{0,2},{1,3},{2,0},{3,1},{4,5},{5,4},{6,7},{7,6},{8,10},{9,11},{10,... | collective-permute-start | bytes 122888 | tf_op jit(solution)/shard_map/ppermute | solution.py:437
  54.3 0.1 fusion.1.chosen
  54.5 1.2 %gains.1 = (f32[2,2048]{1,0:T(2,128)}, f32[2,2048]{1,0:T(2,128)}) custom-call(s32[2]{0:T(128)S(1)} %pad_add_fusion.place, s32[2]{0:T(128)S(1)} %fusion.1.chosen, f32[32,512]{1,0:T(8,128)S(1)} %add.53.x_ref.own_ref, f32[32,512]{1,0:T(8,128)S(1)} %collective-permute-done.13.other_ref, f32[2,2048]{1,0:T(2,128)S(1)} %copy-done.6, f32[2,2048]{1,0:T(2,128)S(1)} %copy-done.7), custom_call_target="tpu_custom_call" | custom-call | flops 40960 | bytes 65536 | tf_op jit(solution)/shard_map/gains/pallas_call | solution.py:48
  55.6 1.3 %collective-permute-done.14 = f32[32,320]{1,0:T(8,128)S(1)} collective-permute-done((f32[32,320]{1,0:T(8,128)S(1)}, f32[32,320]{1,0:T(8,128)S(1)}, u32[]{:S(2)}, u32[]{:S(2)}) %collective-permute-start.14) | collective-permute-done | bytes 40992 | tf_op jit(solution)/shard_map/ppermute | solution.py:437
  56.9 1.6 %collective-permute-start.15 = (f32[32,320]{1,0:T(8,128)S(1)}, f32[32,320]{1,0:T(8,128)S(1)}, u32[]{:S(2)}, u32[]{:S(2)}) collective-permute-start(f32[32,320]{1,0:T(8,128)S(1)} %add.57), channel_id=1, source_target_pairs={{0,8},{1,9},{2,10},{3,11},{4,20},{5,21},{6,22},{7,23},{8,0},{9,1},... | collective-permute-start | bytes 122888 | tf_op jit(solution)/shard_map/ppermute | solution.py:437
  58.5 1.7 %banks.1 = (f32[2,64,2048]{2,1,0:T(8,128)S(1)}, f32[2,64,2048]{2,1,0:T(8,128)S(1)}) custom-call(f32[2,64,2048]{2,1,0:T(8,128)} %mm_hbm, f32[2,64,2048]{2,1,0:T(8,128)} %mw_hbm), custom_call_target="tpu_custom_call" | custom-call | bytes 2097152 | tf_op jit(solution)/shard_map/banks/pallas_call | solution.py:48
  60.1 0.0 copy-start.1
  60.1 1.0 %collective-permute-done.15 = f32[32,320]{1,0:T(8,128)S(1)} collective-permute-done((f32[32,320]{1,0:T(8,128)S(1)}, f32[32,320]{1,0:T(8,128)S(1)}, u32[]{:S(2)}, u32[]{:S(2)}) %collective-permute-start.15) | collective-permute-done | bytes 40992 | tf_op jit(solution)/shard_map/ppermute | solution.py:437
  61.2 0.7 collective-permute-start.16
  61.9 3.5 %collective-permute-done.16 = f32[32,320]{1,0:T(8,128)S(1)} collective-permute-done((f32[32,320]{1,0:T(8,128)S(1)}, f32[32,320]{1,0:T(8,128)S(1)}, u32[]{:S(2)}, u32[]{:S(2)}) %collective-permute-start.16) | collective-permute-done | bytes 40992 | tf_op jit(solution)/shard_map/ppermute | solution.py:437
  65.3 0.5 lower.1
  65.8 1.8 %collective-permute-start.17 = (f32[32,512]{1,0:T(8,128)S(1)}, f32[32,512]{1,0:T(8,128)S(1)}, u32[]{:S(2)}, u32[]{:S(2)}) collective-permute-start(f32[32,512]{1,0:T(8,128)S(1)} %lower.1), channel_id=1, source_target_pairs={{0,1},{1,0},{2,3},{3,2},{4,6},{5,7},{6,4},{7,5},{8,9},{9,8},{10,11... | collective-permute-start | bytes 196616 | tf_op jit(solution)/shard_map/ppermute | solution.py:437
  67.6 2.4 %root2a.1.state = f32[3,32,32]{2,1,0:T(8,128)S(1)} custom-call(f32[32,32]{1,0:T(8,128)S(1)} %root1b.1.a_ref, f32[32,320]{1,0:T(8,128)S(1)} %add.59.u_ref), custom_call_target="tpu_custom_call" | custom-call | flops 12000000 | bytes 45056 | tf_op jit(solution)/shard_map/root2a/pallas_call | solution.py:48
  70.0 0.1 collective-permute-done.17
  70.1 2.8 %collective-permute-start.18 = (f32[32,512]{1,0:T(8,128)S(1)}, f32[32,512]{1,0:T(8,128)S(1)}, u32[]{:S(2)}, u32[]{:S(2)}) collective-permute-start(f32[32,512]{1,0:T(8,128)S(1)} %add.60), channel_id=1, source_target_pairs={{0,2},{1,3},{2,0},{3,1},{4,5},{5,4},{6,7},{7,6},{8,10},{9,11},{10,... | collective-permute-start | bytes 196616 | tf_op jit(solution)/shard_map/ppermute | solution.py:437
  73.0 2.3 %root2b.1.f0_ref = f32[32,384]{1,0:T(8,128)S(1)} custom-call(f32[3,32,32]{2,1,0:T(8,128)S(1)} %root2a.1.state, f32[32,32]{1,0:T(8,128)S(1)} %root1b.1.a_ref, f32[32,320]{1,0:T(8,128)S(1)} %add.59.u_ref), custom_call_target="tpu_custom_call" | custom-call | flops 12000000 | bytes 57344 | tf_op jit(solution)/shard_map/root2b/pallas_call | solution.py:48
  75.2 0.1 collective-permute-done.18
  75.4 0.1 collective-permute-start.20
  75.5 1.6 %collective-permute-start.19 = (f32[1,32,512]{2,1,0:T(8,128)S(1)}, f32[1,32,512]{2,1,0:T(8,128)S(1)}, u32[]{:S(2)}, u32[]{:S(2)}) collective-permute-start(f32[1,32,512]{2,1,0:T(8,128)S(1)} %add_bitcast_fusion.v0_ref), channel_id=1, source_target_pairs={{0,8},{1,9},{2,10},{3,11},{4,20},{5,21},{6,22},{7,23},{8,0},{9,1},... | collective-permute-start | bytes 196616 | tf_op jit(solution)/shard_map/ppermute | solution.py:437
  77.0 1.2 %collective-permute-done.21.f1_ref = f32[32,384]{1,0:T(8,128)S(1)} collective-permute-done((f32[32,384]{1,0:T(8,128)S(1)}, f32[32,384]{1,0:T(8,128)S(1)}, u32[]{:S(2)}, u32[]{:S(2)}) %collective-permute-start.21) | collective-permute-done | bytes 49184 | tf_op jit(solution)/shard_map/ppermute | solution.py:437
  78.3 2.7 %finish0.1 = (f32[1,2,320,2048]{3,2,1,0:T(8,128)}, f32[2,64,2048]{2,1,0:T(8,128)}, f32[2,64,2048]{2,1,0:T(8,128)}, bf16[2,320,192]{2,1,0:T(8,128)(2,1)S(1)}) custom-call(s32[2]{0:T(128)S(1)} %pad_add_fusion.place, s32[2]{0:T(128)S(1)} %fusion.1.chosen, f32[1,32,512]{2,1,0:T(8,128)S(1)} %add_bitcast_fusion.v0_ref, ...), custom_call_target="tpu_custom_call" | custom-call | flops 125829120 | bytes 2359296 | tf_op jit(solution)/shard_map/finish0/pallas_call | solution.py:48
  81.0 0.7 collective-permute-start.22
  81.7 1.3 %collective-permute-done.23.v1_ref = f32[1,32,512]{2,1,0:T(8,128)S(1)} collective-permute-done((f32[1,32,512]{2,1,0:T(8,128)S(1)}, f32[1,32,512]{2,1,0:T(8,128)S(1)}, u32[]{:S(2)}, u32[]{:S(2)}) %collective-permute-start.23) | collective-permute-done | bytes 65568 | tf_op jit(solution)/shard_map/ppermute | solution.py:437
  83.0 2.7 %finish1.1 = (f32[1,2,320,2048]{3,2,1,0:T(8,128)}, f32[2,64,2048]{2,1,0:T(8,128)}, f32[2,64,2048]{2,1,0:T(8,128)}) custom-call(s32[2]{0:T(128)S(1)} %pad_add_fusion.place, s32[2]{0:T(128)S(1)} %fusion.1.chosen, f32[1,32,512]{2,1,0:T(8,128)S(1)} %collective-permute-done.19.v0_ref, ...), custom_call_target="tpu_custom_call", output_to_operand_aliasing={{0}: (13, {}), {1}: (14, {}), {2}: (15, {})} | custom-call | flops 125829120 | bytes 2359296 | tf_op jit(solution)/shard_map/finish1/pallas_call | solution.py:48
  85.7 0.4 collective-permute-done.22.v0_ref
  86.1 1.3 %collective-permute-done.24.v1_ref = f32[2,32,512]{2,1,0:T(8,128)S(1)} collective-permute-done((f32[2,32,512]{2,1,0:T(8,128)S(1)}, f32[2,32,512]{2,1,0:T(8,128)S(1)}, u32[]{:S(2)}, u32[]{:S(2)}) %collective-permute-start.24) | collective-permute-done | bytes 131104 | tf_op jit(solution)/shard_map/ppermute | solution.py:437
  87.4 4.0 %finish2.1 = (f32[1,2,320,2048]{3,2,1,0:T(8,128)}, f32[2,64,2048]{2,1,0:T(8,128)}, f32[2,64,2048]{2,1,0:T(8,128)}) custom-call(s32[2]{0:T(128)S(1)} %pad_add_fusion.place, s32[2]{0:T(128)S(1)} %fusion.1.chosen, f32[2,32,512]{2,1,0:T(8,128)S(1)} %collective-permute-done.22.v0_ref, ...), custom_call_target="tpu_custom_call", output_to_operand_aliasing={{0}: (13, {}), {1}: (14, {}), {2}: (15, {})} | custom-call | flops 251658240 | bytes 4718592 | tf_op jit(solution)/shard_map/finish2/pallas_call | solution.py:48
  (40 shorter events, 0.2 us)
Async XLA Ops:
  0.7 3.4 %copy-start.4 = (f32[2,32,2048]{2,1,0:T(8,128)S(1)}, f32[2,32,2048]{2,1,0:T(8,128)}, u32[]{:S(2)}) copy-start(f32[2,32,2048]{2,1,0:T(8,128)} %w_ref.1) | copy-start | bytes 1572868
  0.7 3.4 %copy-start.5 = (f32[1,2,2048]{2,1,0:T(2,128)S(1)}, f32[1,2,2048]{2,1,0:T(2,128)}, u32[]{:S(2)}) copy-start(f32[1,2,2048]{2,1,0:T(2,128)} %vec_ref.1) | copy-start | bytes 49156
  3.5 4.3 %copy-start = (f32[2,320,512]{2,1,0:T(8,128)}, f32[2,320,512]{2,1,0:T(8,128)S(1)}, u32[]{:S(2)}) copy-start(f32[2,320,512]{2,1,0:T(8,128)S(1)} %get-tuple-element.66.refs_2_.c1_even) | copy-start | bytes 3932164
  3.5 4.3 %copy-start.2 = (f32[2,320,512]{2,1,0:T(8,128)}, f32[2,320,512]{2,1,0:T(8,128)S(1)}, u32[]{:S(2)}) copy-start(f32[2,320,512]{2,1,0:T(8,128)S(1)} %get-tuple-element.67.refs_3_.c1_odd) | copy-start | bytes 3932164
  3.5 4.3 %collective-permute-start = (f32[2,320,512]{2,1,0:T(8,128)S(1)}, f32[2,320,512]{2,1,0:T(8,128)S(1)}, u32[]{:S(2)}, u32[]{:S(2)}) collective-permute-start(f32[2,320,512]{2,1,0:T(8,128)S(1)} %get-tuple-element.67.refs_3_.c1_odd), channel_id=1, source_target_pairs={{0,4},{1,5},{2,6},{3,7},{4,0},{5,1},{6,2},{7,3},{8,12},{9,13},{10,... | collective-permute-start | bytes 3932168 | tf_op jit(solution)/shard_map/ppermute | solution.py:437
  4.0 13.6 %collective-permute-start.6 = (f32[2,320,512]{2,1,0:T(8,128)S(1)}, f32[2,320,512]{2,1,0:T(8,128)S(1)}, u32[]{:S(2)}, u32[]{:S(2)}) collective-permute-start(f32[2,320,512]{2,1,0:T(8,128)S(1)} %get-tuple-element.66.refs_2_.c1_even), channel_id=1, source_target_pairs={{0,4},{1,5},{2,6},{3,7},{4,0},{5,1},{6,2},{7,3},{8,12},{9,13},{10,... | collective-permute-start | bytes 3932168 | tf_op jit(solution)/shard_map/ppermute | solution.py:437
  7.9 12.3 %collective-permute-start.8 = (f32[1,320,512]{2,1,0:T(8,128)S(1)}, f32[1,320,512]{2,1,0:T(8,128)S(1)}, u32[]{:S(2)}, u32[]{:S(2)}) collective-permute-start(f32[1,320,512]{2,1,0:T(8,128)S(1)} %fold.3), channel_id=1, source_target_pairs={{0,8},{1,9},{2,10},{3,11},{4,20},{5,21},{6,22},{7,23},{8,0},{9,1},... | collective-permute-start | bytes 1966088 | tf_op jit(solution)/shard_map/ppermute | solution.py:437
  10.9 1.6 %collective-permute-start.1 = (f32[32,512]{1,0:T(8,128)S(1)}, f32[32,512]{1,0:T(8,128)S(1)}, u32[]{:S(2)}, u32[]{:S(2)}) collective-permute-start(f32[32,512]{1,0:T(8,128)S(1)} %get-tuple-element.71), channel_id=1, source_target_pairs={{0,4},{1,5},{2,6},{3,7},{4,0},{5,1},{6,2},{7,3},{8,12},{9,13},{10,... | collective-permute-start | bytes 196616 | tf_op jit(solution)/shard_map/ppermute | solution.py:437
  12.5 5.1 %collective-permute-start.2 = (f32[32,512]{1,0:T(8,128)S(1)}, f32[32,512]{1,0:T(8,128)S(1)}, u32[]{:S(2)}, u32[]{:S(2)}) collective-permute-start(f32[32,512]{1,0:T(8,128)S(1)} %add.49), channel_id=1, source_target_pairs={{0,16},{1,17},{2,18},{3,19},{4,12},{5,13},{6,14},{7,15},{8,24},{9,... | collective-permute-start | bytes 196616 | tf_op jit(solution)/shard_map/ppermute | solution.py:437
  14.1 22.2 %collective-permute-start.7 = (f32[1,320,512]{2,1,0:T(8,128)S(1)}, f32[1,320,512]{2,1,0:T(8,128)S(1)}, u32[]{:S(2)}, u32[]{:S(2)}) collective-permute-start(f32[1,320,512]{2,1,0:T(8,128)S(1)} %fold.4), channel_id=1, source_target_pairs={{0,8},{1,9},{2,10},{3,11},{4,20},{5,21},{6,22},{7,23},{8,0},{9,1},... | collective-permute-start | bytes 1966088 | tf_op jit(solution)/shard_map/ppermute | solution.py:437
  20.3 16.0 %collective-permute-start.9 = (f32[1,320,512]{2,1,0:T(8,128)S(1)}, f32[1,320,512]{2,1,0:T(8,128)S(1)}, u32[]{:S(2)}, u32[]{:S(2)}) collective-permute-start(f32[1,320,512]{2,1,0:T(8,128)S(1)} %fold.5), channel_id=1, source_target_pairs={{0,16},{1,17},{2,18},{3,19},{4,12},{5,13},{6,14},{7,15},{8,24},{9,... | collective-permute-start | bytes 1966088 | tf_op jit(solution)/shard_map/ppermute | solution.py:437
  22.4 4.3 %collective-permute-start.3 = (f32[32,512]{1,0:T(8,128)S(1)}, f32[32,512]{1,0:T(8,128)S(1)}, u32[]{:S(2)}, u32[]{:S(2)}) collective-permute-start(f32[32,512]{1,0:T(8,128)S(1)} %add.50.refs_3_), channel_id=1, source_target_pairs={{0,1},{1,0},{2,3},{3,2},{4,6},{5,7},{6,4},{7,5},{8,9},{9,8},{10,11... | collective-permute-start | bytes 196616 | tf_op jit(solution)/shard_map/ppermute | solution.py:437
  26.7 5.2 %collective-permute-start.4 = (f32[32,512]{1,0:T(8,128)S(1)}, f32[32,512]{1,0:T(8,128)S(1)}, u32[]{:S(2)}, u32[]{:S(2)}) collective-permute-start(f32[32,512]{1,0:T(8,128)S(1)} %add.51), channel_id=1, source_target_pairs={{0,2},{1,3},{2,0},{3,1},{4,5},{5,4},{6,7},{7,6},{8,10},{9,11},{10,... | collective-permute-start | bytes 196616 | tf_op jit(solution)/shard_map/ppermute | solution.py:437
  31.9 4.3 %collective-permute-start.5 = (f32[32,512]{1,0:T(8,128)S(1)}, f32[32,512]{1,0:T(8,128)S(1)}, u32[]{:S(2)}, u32[]{:S(2)}) collective-permute-start(f32[32,512]{1,0:T(8,128)S(1)} %add.52), channel_id=1, source_target_pairs={{0,8},{1,9},{2,10},{3,11},{4,20},{5,21},{6,22},{7,23},{8,0},{9,1},... | collective-permute-start | bytes 196616 | tf_op jit(solution)/shard_map/ppermute | solution.py:437
  36.3 7.8 %copy-start.8 = (s32[12]{0:T(128)S(1)}, s32[12]{0:T(128)}, u32[]{:S(2)}) copy-start(s32[12]{0:T(128)} %param.13) | copy-start | bytes 148
  36.9 17.6 %copy-start.6 = (f32[2,2048]{1,0:T(2,128)S(1)}, f32[2,2048]{1,0:T(2,128)}, u32[]{:S(2)}) copy-start(f32[2,2048]{1,0:T(2,128)} %mv_ref.1) | copy-start | bytes 49156
  36.9 17.6 %copy-start.7 = (f32[2,2048]{1,0:T(2,128)S(1)}, f32[2,2048]{1,0:T(2,128)}, u32[]{:S(2)}) copy-start(f32[2,2048]{1,0:T(2,128)} %wv_ref.1) | copy-start | bytes 49156
  36.9 4.3 %collective-permute-start.10 = (f32[32,512]{1,0:T(8,128)S(1)}, f32[32,512]{1,0:T(8,128)S(1)}, u32[]{:S(2)}, u32[]{:S(2)}) collective-permute-start(f32[32,512]{1,0:T(8,128)S(1)} %get-tuple-element.73), channel_id=1, source_target_pairs={{0,1},{1,0},{2,3},{3,2},{4,6},{5,7},{6,4},{7,5},{8,9},{9,8},{10,11... | collective-permute-start | bytes 196616 | tf_op jit(solution)/shard_map/ppermute | solution.py:437
  41.3 5.2 %collective-permute-start.11 = (f32[32,512]{1,0:T(8,128)S(1)}, f32[32,512]{1,0:T(8,128)S(1)}, u32[]{:S(2)}, u32[]{:S(2)}) collective-permute-start(f32[32,512]{1,0:T(8,128)S(1)} %add.54), channel_id=1, source_target_pairs={{0,2},{1,3},{2,0},{3,1},{4,5},{5,4},{6,7},{7,6},{8,10},{9,11},{10,... | collective-permute-start | bytes 196616 | tf_op jit(solution)/shard_map/ppermute | solution.py:437
  44.1 7.8 %collective-permute-start.13 = (f32[32,512]{1,0:T(8,128)S(1)}, f32[32,512]{1,0:T(8,128)S(1)}, u32[]{:S(2)}, u32[]{:S(2)}) collective-permute-start(f32[32,512]{1,0:T(8,128)S(1)} %add.53.x_ref.own_ref), channel_id=1, source_target_pairs={{0,4},{1,5},{2,6},{3,7},{4,0},{5,1},{6,2},{7,3},{8,12},{9,13},{10,... | collective-permute-start | bytes 196616 | tf_op jit(solution)/shard_map/ppermute | solution.py:437
  47.2 4.6 %collective-permute-start.12 = (f32[32,320]{1,0:T(8,128)S(1)}, f32[32,320]{1,0:T(8,128)S(1)}, u32[]{:S(2)}, u32[]{:S(2)}) collective-permute-start(f32[32,320]{1,0:T(8,128)S(1)} %lift.1), channel_id=1, source_target_pairs={{0,1},{1,0},{2,3},{3,2},{4,6},{5,7},{6,4},{7,5},{8,9},{9,8},{10,11... | collective-permute-start | bytes 122888 | tf_op jit(solution)/shard_map/ppermute | solution.py:437
  51.8 5.1 %collective-permute-start.14 = (f32[32,320]{1,0:T(8,128)S(1)}, f32[32,320]{1,0:T(8,128)S(1)}, u32[]{:S(2)}, u32[]{:S(2)}) collective-permute-start(f32[32,320]{1,0:T(8,128)S(1)} %add.56), channel_id=1, source_target_pairs={{0,2},{1,3},{2,0},{3,1},{4,5},{5,4},{6,7},{7,6},{8,10},{9,11},{10,... | collective-permute-start | bytes 122888 | tf_op jit(solution)/shard_map/ppermute | solution.py:437
  56.9 4.2 %collective-permute-start.15 = (f32[32,320]{1,0:T(8,128)S(1)}, f32[32,320]{1,0:T(8,128)S(1)}, u32[]{:S(2)}, u32[]{:S(2)}) collective-permute-start(f32[32,320]{1,0:T(8,128)S(1)} %add.57), channel_id=1, source_target_pairs={{0,8},{1,9},{2,10},{3,11},{4,20},{5,21},{6,22},{7,23},{8,0},{9,1},... | collective-permute-start | bytes 122888 | tf_op jit(solution)/shard_map/ppermute | solution.py:437
  58.5 19.8 %copy-start.3 = (f32[2,320,512]{2,1,0:T(8,128)S(1)}, f32[2,320,512]{2,1,0:T(8,128)}, u32[]{:S(2)}) copy-start(f32[2,320,512]{2,1,0:T(8,128)} %copy-done.2) | copy-start | bytes 3932164
  60.1 18.1 %copy-start.1 = (f32[2,320,512]{2,1,0:T(8,128)S(1)}, f32[2,320,512]{2,1,0:T(8,128)}, u32[]{:S(2)}) copy-start(f32[2,320,512]{2,1,0:T(8,128)} %copy-done) | copy-start | bytes 3932164
  61.2 4.2 %collective-permute-start.16 = (f32[32,320]{1,0:T(8,128)S(1)}, f32[32,320]{1,0:T(8,128)S(1)}, u32[]{:S(2)}, u32[]{:S(2)}) collective-permute-start(f32[32,320]{1,0:T(8,128)S(1)} %add.58), channel_id=1, source_target_pairs={{0,16},{1,17},{2,18},{3,19},{4,12},{5,13},{6,14},{7,15},{8,24},{9,... | collective-permute-start | bytes 122888 | tf_op jit(solution)/shard_map/ppermute | solution.py:437
  65.8 4.3 %collective-permute-start.17 = (f32[32,512]{1,0:T(8,128)S(1)}, f32[32,512]{1,0:T(8,128)S(1)}, u32[]{:S(2)}, u32[]{:S(2)}) collective-permute-start(f32[32,512]{1,0:T(8,128)S(1)} %lower.1), channel_id=1, source_target_pairs={{0,1},{1,0},{2,3},{3,2},{4,6},{5,7},{6,4},{7,5},{8,9},{9,8},{10,11... | collective-permute-start | bytes 196616 | tf_op jit(solution)/shard_map/ppermute | solution.py:437
  70.1 5.2 %collective-permute-start.18 = (f32[32,512]{1,0:T(8,128)S(1)}, f32[32,512]{1,0:T(8,128)S(1)}, u32[]{:S(2)}, u32[]{:S(2)}) collective-permute-start(f32[32,512]{1,0:T(8,128)S(1)} %add.60), channel_id=1, source_target_pairs={{0,2},{1,3},{2,0},{3,1},{4,5},{5,4},{6,7},{7,6},{8,10},{9,11},{10,... | collective-permute-start | bytes 196616 | tf_op jit(solution)/shard_map/ppermute | solution.py:437
  75.4 2.9 %collective-permute-start.20 = (f32[1,32,512]{2,1,0:T(8,128)S(1)}, f32[1,32,512]{2,1,0:T(8,128)S(1)}, u32[]{:S(2)}, u32[]{:S(2)}) collective-permute-start(f32[1,32,512]{2,1,0:T(8,128)S(1)} %add_bitcast_fusion.v0_ref), channel_id=1, source_target_pairs={{0,4},{1,5},{2,6},{3,7},{4,0},{5,1},{6,2},{7,3},{8,12},{9,13},{10,... | collective-permute-start | bytes 196616 | tf_op jit(solution)/shard_map/ppermute | solution.py:437
  75.5 5.5 %collective-permute-start.19 = (f32[1,32,512]{2,1,0:T(8,128)S(1)}, f32[1,32,512]{2,1,0:T(8,128)S(1)}, u32[]{:S(2)}, u32[]{:S(2)}) collective-permute-start(f32[1,32,512]{2,1,0:T(8,128)S(1)} %add_bitcast_fusion.v0_ref), channel_id=1, source_target_pairs={{0,8},{1,9},{2,10},{3,11},{4,20},{5,21},{6,22},{7,23},{8,0},{9,1},... | collective-permute-start | bytes 196616 | tf_op jit(solution)/shard_map/ppermute | solution.py:437
  77.0 1.2 %collective-permute-start.21 = (f32[32,384]{1,0:T(8,128)S(1)}, f32[32,384]{1,0:T(8,128)S(1)}, u32[]{:S(2)}, u32[]{:S(2)}) collective-permute-start(f32[32,384]{1,0:T(8,128)S(1)} %root2b.1.f0_ref), channel_id=1, source_target_pairs={{0,4},{1,5},{2,6},{3,7},{4,0},{5,1},{6,2},{7,3},{8,12},{9,13},{10,... | collective-permute-start | bytes 147464 | tf_op jit(solution)/shard_map/ppermute | solution.py:437
  81.0 5.0 %collective-permute-start.22 = (f32[2,32,512]{2,1,0:T(8,128)S(1)}, f32[2,32,512]{2,1,0:T(8,128)S(1)}, u32[]{:S(2)}, u32[]{:S(2)}) collective-permute-start(f32[2,32,512]{2,1,0:T(8,128)S(1)} %pad_maximum_fusion), channel_id=1, source_target_pairs={{0,16},{1,17},{2,18},{3,19},{4,12},{5,13},{6,14},{7,15},{8,24},{9,... | collective-permute-start | bytes 393224 | tf_op jit(solution)/shard_map/ppermute | solution.py:437
  81.7 1.3 %collective-permute-start.23 = (f32[1,32,512]{2,1,0:T(8,128)S(1)}, f32[1,32,512]{2,1,0:T(8,128)S(1)}, u32[]{:S(2)}, u32[]{:S(2)}) collective-permute-start(f32[1,32,512]{2,1,0:T(8,128)S(1)} %collective-permute-done.19.v0_ref), channel_id=1, source_target_pairs={{0,4},{1,5},{2,6},{3,7},{4,0},{5,1},{6,2},{7,3},{8,12},{9,13},{10,... | collective-permute-start | bytes 196616 | tf_op jit(solution)/shard_map/ppermute | solution.py:437
  86.1 1.3 %collective-permute-start.24 = (f32[2,32,512]{2,1,0:T(8,128)S(1)}, f32[2,32,512]{2,1,0:T(8,128)S(1)}, u32[]{:S(2)}, u32[]{:S(2)}) collective-permute-start(f32[2,32,512]{2,1,0:T(8,128)S(1)} %collective-permute-done.22.v0_ref), channel_id=1, source_target_pairs={{0,4},{1,5},{2,6},{3,7},{4,0},{5,1},{6,2},{7,3},{8,12},{9,13},{10,... | collective-permute-start | bytes 393224 | tf_op jit(solution)/shard_map/ppermute | solution.py:437

commit v4 on v3

--- a/solution.py
+++ b/solution.py
@@ -44,7 +44,7 @@
     return pltpu.with_memory_space_constraint(a, pltpu.VMEM)
 
 
-def call(kernel, name, in_specs, out_specs, out_shape, operands, mib=8, flops=0, nbytes=0, scratch=(), aliases={}):
+def call(kernel, name, in_specs, out_specs, out_shape, operands, mib=4, flops=0, nbytes=0, scratch=(), aliases={}):
     return pl.pallas_call(
         kernel,
         in_specs=in_specs,
@@ -73,9 +73,8 @@
 
 def block_columns(place, own, p, blocks, width):
     bits = blocks.bit_length() - 1
-    mirrored = sum((p >> i & 1) << (bits - 1 - i) for i in range(bits))
     core = place[0] if own else 1 - place[0]
-    block = place[1] ^ jnp.where(core == 0, p, mirrored)
+    block = place[1] ^ jnp.where(core == 0, p, mirror(p, bits))
     return pl.ds(pl.multiple_of(block * width, width), width)
 
 
@@ -161,7 +160,7 @@
         [VMEM] * (3 if own else 2),
         [half, half] + ([factor_shape(rows, factor_of[0])] if own else []),
         (place, grads, errors, *factor_of),
-        mib=12,
+        mib=8,
         flops=rows * cols * (200 if own else 1),
         nbytes=rows * cols * 10,
         scratch=[pltpu.VMEM(shape, grads.dtype), pltpu.VMEM(shape, f32), pltpu.SemaphoreType.DMA((blocks, 2))],
@@ -261,13 +260,21 @@
     f_ref[:, rows : rows + rank] = both
 
 
-def gains_kernel(place, chosen, own_ref, other_ref, mv_ref, wv_ref, mo_ref, wo_ref, vec, *, count, first):
+def taken_items(place, owners, slots):
+    items, before = [jnp.int32(-1)] * slots, jnp.int32(0)
+    for item in range(owners.shape[0]):
+        mine = owners[item] == place[2]
+        items = [jnp.where(mine & (before == slot), item, old) for slot, old in enumerate(items)]
+        before = before + jnp.where(mine, 1, 0)
+    return items
+
+
+def gains_kernel(place, owners, own_ref, other_ref, mv_ref, wv_ref, mo_ref, wo_ref, vec, *, count, first):
     for i in range(mv_ref.shape[1] // LANES):
         at = slice(i * LANES, (i + 1) * LANES)
         for k, ref in enumerate((own_ref, other_ref)):
             vec[k : k + 1, at] = ref[i : i + 1, ref.shape[1] - LANES :] / count
-    for slot in range(mv_ref.shape[0]):
-        item = chosen[slot]
+    for slot, item in enumerate(taken_items(place, owners, mv_ref.shape[0])):
         row = jnp.where(item - first == place[0], vec[0:1, :], vec[1:2, :])
         old, weight = mv_ref[slot : slot + 1, :], wv_ref[slot : slot + 1, :]
         new = 0.9 * old + row
@@ -275,14 +282,14 @@
         wo_ref[slot : slot + 1, :] = jnp.where(item >= first, weight - 0.5 * new, weight)
 
 
-def gains(place, chosen, own, other, vec_momentum, vec_weights, count, first):
+def gains(place, owners, own, other, vec_momentum, vec_weights, count, first):
     return call(
         functools.partial(gains_kernel, count=count, first=first),
         "gains",
         [SMEM, SMEM] + [VMEM] * 4,
         [VMEM] * 2,
         [jax.ShapeDtypeStruct(vec_momentum.shape, f32)] * 2,
-        (place, chosen, own, other, vec_momentum, vec_weights),
+        (place, owners, own, other, vec_momentum, vec_weights),
         flops=10 * vec_momentum.size,
         nbytes=16 * vec_momentum.size,
         scratch=[pltpu.VMEM((2, vec_momentum.shape[1]), f32)],
@@ -311,7 +318,7 @@
 
 
 def finish_kernel(
-    place, chosen, v0_ref, v1_ref, f0_ref, f1_ref, c0_even, c0_odd, c1_even, c1_odd, mm, mw, *refs, positions, head, later
+    place, owners, v0_ref, v1_ref, f0_ref, f1_ref, c0_even, c0_odd, c1_even, c1_odd, mm, mw, *refs, positions, head, later
 ):
     if later:
         left, refs = refs[0], refs[1 + 3 :]
@@ -321,58 +328,63 @@
     rank, width = v0_ref.shape[1:]
     blocks, rows = 2 * c0_even.shape[0], c0_even.shape[1]
     per = rows // head
-    stores, bank_stores = [], []
-    for k, p in enumerate(positions):
-        for i, (v_ref, f_ref, *c_refs) in enumerate(
-            ((v0_ref, f0_ref, c0_even, c0_odd), (v1_ref, f1_ref, c1_even, c1_odd))
-        ):
-            if k == 0 and not later:
-                high, middle, low = split3(f_ref[:, :rows].T)
-                left[i] = jnp.concatenate([high, high, middle, high, low, middle], axis=1)
-            m = place[0] if i == 0 else 1 - place[0]
-            columns = block_columns(place, i == 0, p, blocks, width)
-            high, middle, low = split3(dot(f_ref[:, rows : rows + rank], v_ref[k], TN))
-            right = jnp.concatenate([high, middle, high, low, high, middle], axis=0)
-            product = jnp.dot(left[i], right, preferred_element_type=f32)
-            approx[k, i] = product
-            errors[k, i] = c_refs[p % 2][p // 2] - product
-            stores.append(pltpu.make_async_copy(errors.at[k, i], n_hbm.at[0, m, :, columns], sem.at[k, i]))
-            stores[-1].start()
-            for slot in range(mm.shape[0]):
-                item = chosen[slot]
-                taken = (item >= m * per) & (item < (m + 1) * per)
-                idle = (item < 0) | (item >= 2 * per)
-                copies = (
-                    pltpu.make_async_copy(
-                        moment.at[k, i, slot], mo_hbm.at[slot, :, columns], bank_sem.at[k, i, slot, 0]
-                    ),
-                    pltpu.make_async_copy(
-                        weight.at[k, i, slot], wo_hbm.at[slot, :, columns], bank_sem.at[k, i, slot, 1]
-                    ),
-                )
-
-                @pl.when(taken)
+    if not later:
+        for i, f_ref in enumerate((f0_ref, f1_ref)):
+            high, middle, low = split3(f_ref[:, :rows].T)
+            left[i] = jnp.concatenate([high, high, middle, high, low, middle], axis=1)
+    units = [(k, p, i) for k, p in enumerate(positions) for i in range(2)]
+    rights = []
+    for k, p, i in units:
+        f_ref, v_ref = ((f0_ref, v0_ref), (f1_ref, v1_ref))[i]
+        high, middle, low = split3(dot(f_ref[:, rows : rows + rank], v_ref[k], TN))
+        rights.append(jnp.concatenate([high, middle, high, low, high, middle], axis=0))
+    stores = []
+    for (k, p, i), right in zip(units, rights):
+        m = place[0] if i == 0 else 1 - place[0]
+        product = jnp.dot(left[i], right, preferred_element_type=f32)
+        approx[k, i] = product
+        errors[k, i] = ((c0_even, c0_odd), (c1_even, c1_odd))[i][p % 2][p // 2] - product
+        columns = block_columns(place, i == 0, p, blocks, width)
+        stores.append(pltpu.make_async_copy(errors.at[k, i], n_hbm.at[0, m, :, columns], sem.at[k, i]))
+        stores[-1].start()
+    bank_stores = []
+    items = taken_items(place, owners, mm.shape[0])
+    for k, p, i in units:
+        m = place[0] if i == 0 else 1 - place[0]
+        columns = block_columns(place, i == 0, p, blocks, width)
+        for slot, item in enumerate(items):
+            taken = (item >= m * per) & (item < (m + 1) * per)
+            idle = (item < 0) | (item >= 2 * per)
+            copies = (
+                pltpu.make_async_copy(
+                    moment.at[k, i, slot], mo_hbm.at[slot, :, columns], bank_sem.at[k, i, slot, 0]
+                ),
+                pltpu.make_async_copy(
+                    weight.at[k, i, slot], wo_hbm.at[slot, :, columns], bank_sem.at[k, i, slot, 1]
+                ),
+            )
+
+            @pl.when(taken)
+            def _():
+                at = pl.ds(pl.multiple_of((item - m * per) * head, head), head)
+                new = 0.9 * mm[slot, :, columns] + approx[k, i, at, :]
+                moment[k, i, slot] = new
+                weight[k, i, slot] = mw[slot, :, columns] - 0.5 * new
+                for copy in copies:
+                    copy.start()
+
+            writes = taken
+            if i == 0:
+                writes = taken | idle
+
+                @pl.when(idle)
                 def _():
-                    at = pl.ds(pl.multiple_of((item - m * per) * head, head), head)
-                    new = 0.9 * mm[slot, :, columns] + approx[k, i, at, :]
-                    moment[k, i, slot] = new
-                    weight[k, i, slot] = mw[slot, :, columns] - 0.5 * new
-
-                writes = taken
-                if i == 0:
-                    writes = taken | idle
-
-                    @pl.when(idle)
-                    def _():
-                        moment[k, i, slot] = mm[slot, :, columns]
-                        weight[k, i, slot] = mw[slot, :, columns]
-
-                @pl.when(writes)
-                def _():
+                    moment[k, i, slot] = mm[slot, :, columns]
+                    weight[k, i, slot] = mw[slot, :, columns]
                     for copy in copies:
                         copy.start()
 
-                bank_stores.append((writes, copies))
+            bank_stores.append((writes, copies))
     for store in stores:
         store.wait()
     for writes, copies in bank_stores:
@@ -383,7 +395,7 @@
                 copy.wait()
 
 
-def finish(positions, left, outs, place, chosen, own_v, other_v, own_f, other_f, own_c, other_c, shapes, mm, mw):
+def finish(positions, left, outs, place, owners, own_v, other_v, own_f, other_f, own_c, other_c, shapes, mm, mw):
     n, rank, width = own_v.shape
     matrices, rows, cols = shapes[0][1:]
     slots, head = mm.shape[:2]
@@ -396,8 +408,8 @@
         [SMEM, SMEM] + [VMEM] * (10 + len(left)) + [ANY] * len(outs),
         [ANY] * 3 + [VMEM] * len(first),
         [pltpu.HBM(s, f32) for s in shapes] + first,
-        (place, chosen, own_v, other_v, own_f, other_f, *own_c, *other_c, mm, mw, *left, *outs),
-        mib=4 + 8 * n,
+        (place, owners, own_v, other_v, own_f, other_f, *own_c, *other_c, mm, mw, *left, *outs),
+        mib=4 + 5 * n,
         flops=2 * n * matrices * rows * width * 6 * rank,
         nbytes=4 * n * width * (matrices * rows + 4 * slots * head),
         scratch=[
@@ -412,6 +424,10 @@
     )
 
 
+def mirror(p, bits):
+    return sum((p >> i & 1) << (bits - 1 - i) for i in range(bits))
+
+
 def partner(kind, step):
     planes = (lax.axis_size("rep") // 2).bit_length() - 1
     depths = lax.axis_size("grp").bit_length() - 1
@@ -421,6 +437,10 @@
             return rep ^ 1, grp
         if kind == "plane":
             return rep ^ (2 << (step if rep % 2 == 0 else planes - 1 - step)), grp
+        if kind == "depth":
+            return rep, grp ^ step
+        if kind == "place":
+            return rep ^ 2 * (step if rep % 2 == 0 else mirror(step, planes)), grp
         return rep, grp ^ (1 << (step if rep % 2 == 0 else depths - 1 - step))
 
     return of
@@ -441,10 +461,11 @@
     if work is None:
         return a + exchange(a, kind, step)
     a, *operands = lax.optimization_barrier((a, *operands))
-    arrived = exchange(a, kind, step)
+    steps = step if isinstance(step, list) else [step]
+    arrived = [exchange(a, kind, each) for each in steps]
     done = work(*operands)
-    arrived, *done = lax.optimization_barrier((arrived, *done))
-    return a + arrived, *done
+    arrived, done = lax.optimization_barrier((arrived, list(done)))
+    return sum(arrived, a), *done
 
 
 def local(grads, errors, warm_start, vec_grads, owners, mat_momentum, mat_weights, vec_momentum, vec_weights):
@@ -458,17 +479,8 @@
     width = cols // blocks
     rep = lax.axis_index("rep")
     core, spot = rep % 2, rep // 2
-    device = rep * groups + lax.axis_index("grp")
-    place = jnp.stack([core, spot]).astype(jnp.int32)
-
-    items = owners.shape[0]
-    slots, head = mat_momentum.shape[:2]
-    earlier = jnp.arange(items)[None, :] < jnp.arange(items)[:, None]
-    same = owners[None, :] == owners[:, None]
-    slot = jnp.sum((earlier & same).astype(jnp.int32), axis=1)
-    match = (owners[None, :] == device) & (slot[None, :] == jnp.arange(slots)[:, None])
-    head_items = matrices * (rows // head)
-    chosen = jnp.max(jnp.where(match, jnp.arange(items)[None, :], -1), axis=1).astype(jnp.int32)
+    place = jnp.stack([core, spot, rep * groups + lax.axis_index("grp")]).astype(jnp.int32)
+    head_items = matrices * (rows // mat_momentum.shape[1])
 
     grads, errors = in_hbm(grads), in_hbm(errors)
     mat_momentum, mat_weights = map(in_hbm, (mat_momentum, mat_weights))
@@ -500,6 +512,7 @@
     own_p = own_factor(later, own_c, warm_start, vec_grads)
     packed = own_p + exchange(other_p, "core")
     packed = hop(packed, "plane", bits - 1)
+    packed = hop(packed, "z", 0)
     land(*ahead)
     for stage in range(1, bits):
         goes = [p for p in range(blocks) if p >> stage & 1 and not p & ((1 << stage) - 1)]
@@ -507,8 +520,10 @@
             while pending:
                 land(*pending.pop(0))
         pending.append(send(goes, stage, (packed,)))
-    for step in range(depths):
+    for step in range(1, depths):
         packed = hop(packed, "z", step)
+    arrived, packed = lax.optimization_barrier((pending[0][2], packed))
+    pending[0] = (*pending[0][:2], arrived)
     for step in range(bits - 2, -1, -1):
         packed = hop(packed, "plane", step)
     while pending:
@@ -520,59 +535,39 @@
     )
     square = (rank, rank)
     state = (3, rank, rank)
-    v, first_state = hop(
-        v, "z", 0,
-        lambda x: small_call(
-            functools.partial(first_begin_kernel, rows=rows, count=count), "root1a", [state], x
-        ), packed,
-    )
-    v, first_root = hop(v, "z", 1, lambda x: small_call(first_end_kernel, "root1b", [square], x), first_state)
-    for step in range(2, depths):
-        v = hop(v, "z", step)
+    def first(x):
+        (begun,) = small_call(functools.partial(first_begin_kernel, rows=rows, count=count), "root1a", [state], x)
+        return small_call(first_end_kernel, "root1b", [square], begun)
+
+    depth = list(range(1, groups))
+    v, first_root = hop(v, "depth", depth, first, packed)
     (u,) = small_call(functools.partial(lift_kernel, count=count), "lift", [(rank, rows)], v, kept_sum)
-    for step in range(depths - 1):
-        u = hop(u, "z", step)
     u, vec_momentum_out, vec_weights_out = hop(
-        u, "z", depths - 1,
-        lambda x, y: gains(place, chosen, x, y, vec_momentum, vec_weights, count, head_items),
+        u, "depth", depth,
+        lambda x, y: gains(place, owners, x, y, vec_momentum, vec_weights, count, head_items),
         packed, exchange(packed, "core"),
     )
-    u, mm, mw = hop(u, "plane", 0, banks, mat_momentum, mat_weights)
-    for step in range(1, bits):
-        u = hop(u, "plane", step)
+    u, mm, mw = hop(u, "place", list(range(1, blocks)), banks, mat_momentum, mat_weights)
     (v,) = small_call(functools.partial(lower_kernel, count=count), "lower", [(rank, width)], u, kept_sum)
-    v, second_state = hop(
-        v, "z", 0, lambda *x: small_call(second_begin_kernel, "root2a", [state], *x), first_root, u
-    )
-    early = []
-
-    def second_end(*x):
-        early.extend(small_call(second_end_kernel, "root2b", [(rank, lanes(rows + rank))], *x))
-        return early
-
-    v, own_f = hop(v, "z", 1, second_end, second_state, first_root, u)
-    other_f = exchange(early[0], "core")
-    for step in range(2, depths):
-        v = hop(v, "z", step)
-
+    def second(a, u):
+        (begun,) = small_call(second_begin_kernel, "root2a", [state], a, u)
+        return small_call(second_end_kernel, "root2b", [(rank, lanes(rows + rank))], begun, a, u)
+
+    v, own_f = hop(v, "depth", depth, second, first_root, u)
+    other_f = exchange(own_f, "core")
     shapes = [errors.shape, mat_momentum.shape, mat_weights.shape]
-    outs, left = (), ()
     v = v[None]
-    fresh, positions = v, [0]
-    for step in range(bits + 1):
-        other_v = exchange(fresh, "core")
-        if step < bits:
-            arrived = exchange(v, "plane", step)
-        outs = finish(
-            positions, left, outs, place, chosen, fresh, other_v, own_f, other_f, own_c, other_c, shapes, mm, mw
-        )
-        if not left:
-            *outs, left = outs
-            left = (left,)
-        if step < bits:
-            arrived, *outs = lax.optimization_barrier((arrived, *outs))
-            v = jnp.concatenate([v, arrived], axis=0)
-            fresh, positions = arrived, list(range(1 << step, 2 << step))
+    other_v = exchange(v, "core")
+    arrived = [exchange(v, "place", p) for p in range(1, blocks)]
+    *outs, left = finish(
+        [0], (), (), place, owners, v, other_v, own_f, other_f, own_c, other_c, shapes, mm, mw
+    )
+    *arrived, left = lax.optimization_barrier((*arrived, left))
+    v = jnp.concatenate(arrived, axis=0)
+    outs = finish(
+        list(range(1, blocks)), (left,), outs, place, owners, v, exchange(v, "core"), own_f, other_f, own_c, other_c,
+        shapes, mm, mw,
+    )
     new_errors, mat_momentum_out, mat_weights_out = outs
     return (new_errors, mat_momentum_out, mat_weights_out, vec_momentum_out, vec_weights_out)
 

time: 91.5 us -> 84.1 us (0.919)
  waiting for transfers between devices: 27.4 us -> 20.5 us
  Pallas kernels: 30.8 us -> 27.7 us
  starting transfers between devices: 31.6 us -> 34.5 us
    ppermute x25 -> x29, waiting for transfers between devices: 27.4 us -> 20.5 us  [exchange(): return lax.ppermute(a, ('rep', 'grp'), pairs)]
    pallas_call x18 -> x17, Pallas kernels: 30.8 us -> 27.7 us  [call(): pl.pallas_call(kernel, in_specs=in_specs, out_specs=out_specs, out_shape=...]
    ppermute x25 -> x29, starting transfers between devices: 31.6 us -> 34.5 us  [exchange(): return lax.ppermute(a, ('rep', 'grp'), pairs)]
  transfers between devices with their start and end apart: 25 -> 29, of which waited for: 17 -> 14; matrix products, arithmetic and copies ran while one was open for 0% -> 0% of each run, Pallas kernels for 25% -> 24%
where the time goes in v4:
time: 84.1 us; the launch traced here: 83.9 us
  starting transfers between devices  34.5 us (41%)
  Pallas kernels  27.7 us (33%)
  waiting for transfers between devices  20.5 us (24%)
  between operations  0.92 us (1%)
    ppermute x29, starting transfers between devices, exchange(): return lax.ppermute(a, ('rep', 'grp'), pairs)  34.5 us
    pallas_call x17, Pallas kernels, call(): pl.pallas_call(kernel, in_specs=in_specs, out_specs=out_specs, out_shape=...  27.7 us
    ppermute x29, waiting for transfers between devices, exchange(): return lax.ppermute(a, ('rep', 'grp'), pairs)  20.5 us
  transfers between devices with their start and end apart: 29, of which 14 were waited for; matrix products, arithmetic and copies ran while one was open for 0% of the time, Pallas kernels for 24%

profile of v4, /device:TPU:0, one launch (start us, length us, event | category | flops | bytes accessed | tf_op | source)
XLA Modules:
  0.0 83.9 jit_solution(17502013807830365940)
XLA Ops:
  0.7 0.1 pad_add_fusion.place
  0.7 2.8 %other.1 = (f32[2,320,512]{2,1,0:T(8,128)S(1)}, f32[2,320,512]{2,1,0:T(8,128)S(1)}) custom-call(s32[3]{0:T(128)S(1)} %pad_add_fusion.place, bf16[1,2,320,2048]{3,2,1,0:T(8,128)(2,1)} %g_hbm.3, f32[1,2,320,2048]{3,2,1,0:T(8,128)} %e_hbm.3), custom_call_target="tpu_custom_call" | custom-call | flops 655360 | bytes 6553600 | tf_op jit(solution)/shard_map/other/pallas_call | solution.py:48
  3.5 0.5 collective-permute-start
  4.0 0.1 collective-permute-start.7
  4.1 3.6 %own.1 = (f32[2,320,512]{2,1,0:T(8,128)S(1)}, f32[2,320,512]{2,1,0:T(8,128)S(1)}, f32[32,512]{1,0:T(8,128)S(1)}) custom-call(s32[3]{0:T(128)S(1)} %pad_add_fusion.place, bf16[1,2,320,2048]{3,2,1,0:T(8,128)(2,1)} %g_hbm.3, f32[1,2,320,2048]{3,2,1,0:T(8,128)} %e_hbm.3, f32[2,32,2048]{2,1,0:T(8,128)S(1)} %copy-done, f32[1,2,2048]{2,1,0:T(2,128)S(1)} %copy-done.1, ...), custom_call_target="tpu_custom_call" | custom-call | flops 131072000 | bytes 6553600 | tf_op jit(solution)/shard_map/own/pallas_call | solution.py:48
  7.8 0.0 collective-permute-done.refs_1_
  7.8 0.1 fold.4
  7.8 3.0 %collective-permute-start.8 = (f32[1,320,512]{2,1,0:T(8,128)S(1)}, f32[1,320,512]{2,1,0:T(8,128)S(1)}, u32[]{:S(2)}, u32[]{:S(2)}) collective-permute-start(f32[1,320,512]{2,1,0:T(8,128)S(1)} %fold.4), channel_id=1, source_target_pairs={{0,8},{1,9},{2,10},{3,11},{4,20},{5,21},{6,22},{7,23},{8,0},{9,1},... | collective-permute-start | bytes 1966088 | tf_op jit(solution)/shard_map/ppermute | solution.py:457
  10.8 0.0 collective-permute-start.2
  10.8 0.1 fold.3
  10.9 1.5 %factor.1 = f32[32,512]{1,0:T(8,128)S(1)} custom-call(s32[3]{0:T(128)S(1)} %pad_add_fusion.place, f32[2,32,2048]{2,1,0:T(8,128)S(1)} %copy-done, f32[1,2,2048]{2,1,0:T(2,128)S(1)} %copy-done.1, f32[2,320,512]{2,1,0:T(8,128)S(1)} %get-tuple-element.63.even.refs_0_.c0_even, f32[2,320,512]{2,1,0:T(8,128)S(1)} %get-tuple-element.61.refs_0_.odd.c0_odd), custom_call_target="tpu_custom_call" | custom-call | flops 503316480 | bytes 5242880 | tf_op jit(solution)/shard_map/factor/pallas_call | solution.py:48
  12.5 1.6 %collective-permute-start.3 = (f32[32,512]{1,0:T(8,128)S(1)}, f32[32,512]{1,0:T(8,128)S(1)}, u32[]{:S(2)}, u32[]{:S(2)}) collective-permute-start(f32[32,512]{1,0:T(8,128)S(1)} %add.61), channel_id=1, source_target_pairs={{0,16},{1,17},{2,18},{3,19},{4,12},{5,13},{6,14},{7,15},{8,24},{9,... | collective-permute-start | bytes 196616 | tf_op jit(solution)/shard_map/ppermute | solution.py:457
  14.1 0.5 collective-permute-start.1
  14.6 3.0 %collective-permute-done.3 = f32[32,512]{1,0:T(8,128)S(1)} collective-permute-done((f32[32,512]{1,0:T(8,128)S(1)}, f32[32,512]{1,0:T(8,128)S(1)}, u32[]{:S(2)}, u32[]{:S(2)}) %collective-permute-start.3) | collective-permute-done | bytes 65568 | tf_op jit(solution)/shard_map/ppermute | solution.py:457
  17.6 1.6 %collective-permute-start.4 = (f32[32,512]{1,0:T(8,128)S(1)}, f32[32,512]{1,0:T(8,128)S(1)}, u32[]{:S(2)}, u32[]{:S(2)}) collective-permute-start(f32[32,512]{1,0:T(8,128)S(1)} %add.62), channel_id=1, source_target_pairs={{0,1},{1,0},{2,3},{3,2},{4,6},{5,7},{6,4},{7,5},{8,9},{9,8},{10,11... | collective-permute-start | bytes 196616 | tf_op jit(solution)/shard_map/ppermute | solution.py:457
  19.2 3.0 %collective-permute-done.4 = f32[32,512]{1,0:T(8,128)S(1)} collective-permute-done((f32[32,512]{1,0:T(8,128)S(1)}, f32[32,512]{1,0:T(8,128)S(1)}, u32[]{:S(2)}, u32[]{:S(2)}) %collective-permute-start.4) | collective-permute-done | bytes 65568 | tf_op jit(solution)/shard_map/ppermute | solution.py:457
  22.2 0.0 collective-permute-done.8.refs_2_
  22.2 0.1 fold.5
  22.3 1.6 %collective-permute-start.9 = (f32[1,320,512]{2,1,0:T(8,128)S(1)}, f32[1,320,512]{2,1,0:T(8,128)S(1)}, u32[]{:S(2)}, u32[]{:S(2)}) collective-permute-start(f32[1,320,512]{2,1,0:T(8,128)S(1)} %fold.5), channel_id=1, source_target_pairs={{0,16},{1,17},{2,18},{3,19},{4,12},{5,13},{6,14},{7,15},{8,24},{9,... | collective-permute-start | bytes 1966088 | tf_op jit(solution)/shard_map/ppermute | solution.py:457
  23.9 2.3 %collective-permute-start.5 = (f32[32,512]{1,0:T(8,128)S(1)}, f32[32,512]{1,0:T(8,128)S(1)}, u32[]{:S(2)}, u32[]{:S(2)}) collective-permute-start(f32[32,512]{1,0:T(8,128)S(1)} %add.63.refs_3_), channel_id=1, source_target_pairs={{0,2},{1,3},{2,0},{3,1},{4,5},{5,4},{6,7},{7,6},{8,10},{9,11},{10,... | collective-permute-start | bytes 196616 | tf_op jit(solution)/shard_map/ppermute | solution.py:457
  26.2 2.9 %collective-permute-done.5 = f32[32,512]{1,0:T(8,128)S(1)} collective-permute-done((f32[32,512]{1,0:T(8,128)S(1)}, f32[32,512]{1,0:T(8,128)S(1)}, u32[]{:S(2)}, u32[]{:S(2)}) %collective-permute-start.5) | collective-permute-done | bytes 65568 | tf_op jit(solution)/shard_map/ppermute | solution.py:457
  29.1 1.7 %collective-permute-done.1.refs_2_ = f32[1,320,512]{2,1,0:T(8,128)S(1)} collective-permute-done((f32[1,320,512]{2,1,0:T(8,128)S(1)}, f32[1,320,512]{2,1,0:T(8,128)S(1)}, u32[]{:S(2)}, u32[]{:S(2)}) %collective-permute-start.1) | collective-permute-done | bytes 655392 | tf_op jit(solution)/shard_map/ppermute | solution.py:457
  30.8 2.5 %collective-permute-start.6 = (f32[32,512]{1,0:T(8,128)S(1)}, f32[32,512]{1,0:T(8,128)S(1)}, u32[]{:S(2)}, u32[]{:S(2)}) collective-permute-start(f32[32,512]{1,0:T(8,128)S(1)} %add.64), channel_id=1, source_target_pairs={{0,8},{1,9},{2,10},{3,11},{4,20},{5,21},{6,22},{7,23},{8,0},{9,1},... | collective-permute-start | bytes 196616 | tf_op jit(solution)/shard_map/ppermute | solution.py:457
  33.3 2.2 %collective-permute-done.6 = f32[32,512]{1,0:T(8,128)S(1)} collective-permute-done((f32[32,512]{1,0:T(8,128)S(1)}, f32[32,512]{1,0:T(8,128)S(1)}, u32[]{:S(2)}, u32[]{:S(2)}) %collective-permute-start.6) | collective-permute-done | bytes 65568 | tf_op jit(solution)/shard_map/ppermute | solution.py:457
  35.5 0.0 copy-start.2
  35.6 0.0 copy-start.3
  35.6 0.0 copy-start.4
  35.6 0.6 project.1
  36.2 3.5 %collective-permute-start.12 = (f32[32,512]{1,0:T(8,128)S(1)}, f32[32,512]{1,0:T(8,128)S(1)}, u32[]{:S(2)}, u32[]{:S(2)}) collective-permute-start(f32[32,512]{1,0:T(8,128)S(1)} %get-tuple-element.68), channel_id=1, source_target_pairs={{0,3},{1,2},{2,1},{3,0},{4,7},{5,6},{6,5},{7,4},{8,11},{9,10},{10,... | collective-permute-start | bytes 196616 | tf_op jit(solution)/shard_map/ppermute | solution.py:457
  39.7 0.0 collective-permute-start.11
  39.7 0.9 %collective-permute-start.10 = (f32[32,512]{1,0:T(8,128)S(1)}, f32[32,512]{1,0:T(8,128)S(1)}, u32[]{:S(2)}, u32[]{:S(2)}) collective-permute-start(f32[32,512]{1,0:T(8,128)S(1)} %get-tuple-element.68), channel_id=1, source_target_pairs={{0,1},{1,0},{2,3},{3,2},{4,5},{5,4},{6,7},{7,6},{8,9},{9,8},{10,11... | collective-permute-start | bytes 196616 | tf_op jit(solution)/shard_map/ppermute | solution.py:457
  40.6 2.1 %root1a.1.state = f32[3,32,32]{2,1,0:T(8,128)S(1)} custom-call(f32[32,512]{1,0:T(8,128)S(1)} %add.65.x_ref.own_ref), custom_call_target="tpu_custom_call" | custom-call | flops 12000000 | bytes 65536 | tf_op jit(solution)/shard_map/root1a/pallas_call | solution.py:48
  42.7 1.9 %root1b.1.a_ref = f32[32,32]{1,0:T(8,128)S(1)} custom-call(f32[3,32,32]{2,1,0:T(8,128)S(1)} %root1a.1.state), custom_call_target="tpu_custom_call" | custom-call | flops 12000000 | bytes 12288 | tf_op jit(solution)/shard_map/root1b/pallas_call | solution.py:48
  44.6 0.6 collective-permute-done.11
  45.3 0.7 lift.1
  46.0 2.9 %collective-permute-start.16 = (f32[32,320]{1,0:T(8,128)S(1)}, f32[32,320]{1,0:T(8,128)S(1)}, u32[]{:S(2)}, u32[]{:S(2)}) collective-permute-start(f32[32,320]{1,0:T(8,128)S(1)} %lift.1), channel_id=1, source_target_pairs={{0,3},{1,2},{2,1},{3,0},{4,7},{5,6},{6,5},{7,4},{8,11},{9,10},{10,... | collective-permute-start | bytes 122888 | tf_op jit(solution)/shard_map/ppermute | solution.py:457
  48.9 1.5 %collective-permute-start.14 = (f32[32,320]{1,0:T(8,128)S(1)}, f32[32,320]{1,0:T(8,128)S(1)}, u32[]{:S(2)}, u32[]{:S(2)}) collective-permute-start(f32[32,320]{1,0:T(8,128)S(1)} %lift.1), channel_id=1, source_target_pairs={{0,1},{1,0},{2,3},{3,2},{4,5},{5,4},{6,7},{7,6},{8,9},{9,8},{10,11... | collective-permute-start | bytes 122888 | tf_op jit(solution)/shard_map/ppermute | solution.py:457
  50.4 1.2 %gains.1 = (f32[2,2048]{1,0:T(2,128)}, f32[2,2048]{1,0:T(2,128)}) custom-call(s32[3]{0:T(128)S(1)} %pad_add_fusion.place, s32[12]{0:T(128)S(1)} %copy-done.4, f32[32,512]{1,0:T(8,128)S(1)} %add.65.x_ref.own_ref, f32[32,512]{1,0:T(8,128)S(1)} %collective-permute-done.13.other_ref, f32[2,2048]{1,0:T(2,128)S(1)} %copy-done.2, f32[2,2048]{1,0:T(2,128)S(1)} %copy-done.3), custom_call_target="tpu_custom_call" | custom-call | flops 40960 | bytes 65536 | tf_op jit(solution)/shard_map/gains/pallas_call | solution.py:48
  51.6 0.7 collective-permute-done.16
  52.3 1.6 %collective-permute-done.15 = f32[32,320]{1,0:T(8,128)S(1)} collective-permute-done((f32[32,320]{1,0:T(8,128)S(1)}, f32[32,320]{1,0:T(8,128)S(1)}, u32[]{:S(2)}, u32[]{:S(2)}) %collective-permute-start.15) | collective-permute-done | bytes 40992 | tf_op jit(solution)/shard_map/ppermute | solution.py:457
  54.0 0.2 collective-permute-done.14
  54.2 2.7 %collective-permute-start.19 = (f32[32,320]{1,0:T(8,128)S(1)}, f32[32,320]{1,0:T(8,128)S(1)}, u32[]{:S(2)}, u32[]{:S(2)}) collective-permute-start(f32[32,320]{1,0:T(8,128)S(1)} %add_add_fusion.2), channel_id=1, source_target_pairs={{0,24},{1,25},{2,26},{3,27},{4,28},{5,29},{6,30},{7,31},{8,16},{9,... | collective-permute-start | bytes 122888 | tf_op jit(solution)/shard_map/ppermute | solution.py:457
  56.9 0.4 collective-permute-start.18
  57.3 0.5 collective-permute-start.17
  57.8 1.6 %banks.1 = (f32[2,64,2048]{2,1,0:T(8,128)S(1)}, f32[2,64,2048]{2,1,0:T(8,128)S(1)}) custom-call(f32[2,64,2048]{2,1,0:T(8,128)} %mm_hbm, f32[2,64,2048]{2,1,0:T(8,128)} %mw_hbm), custom_call_target="tpu_custom_call" | custom-call | bytes 2097152 | tf_op jit(solution)/shard_map/banks/pallas_call | solution.py:48
  59.3 0.4 collective-permute-done.19
  59.7 1.3 %collective-permute-done.18 = f32[32,320]{1,0:T(8,128)S(1)} collective-permute-done((f32[32,320]{1,0:T(8,128)S(1)}, f32[32,320]{1,0:T(8,128)S(1)}, u32[]{:S(2)}, u32[]{:S(2)}) %collective-permute-start.18) | collective-permute-done | bytes 40992 | tf_op jit(solution)/shard_map/ppermute | solution.py:457
  61.0 0.4 collective-permute-done.17
  61.4 0.5 lower.1
  61.9 2.5 %collective-permute-start.22 = (f32[32,512]{1,0:T(8,128)S(1)}, f32[32,512]{1,0:T(8,128)S(1)}, u32[]{:S(2)}, u32[]{:S(2)}) collective-permute-start(f32[32,512]{1,0:T(8,128)S(1)} %lower.1), channel_id=1, source_target_pairs={{0,3},{1,2},{2,1},{3,0},{4,7},{5,6},{6,5},{7,4},{8,11},{9,10},{10,... | collective-permute-start | bytes 196616 | tf_op jit(solution)/shard_map/ppermute | solution.py:457
  64.4 0.0 collective-permute-start.21
  64.4 1.9 %collective-permute-start.20 = (f32[32,512]{1,0:T(8,128)S(1)}, f32[32,512]{1,0:T(8,128)S(1)}, u32[]{:S(2)}, u32[]{:S(2)}) collective-permute-start(f32[32,512]{1,0:T(8,128)S(1)} %lower.1), channel_id=1, source_target_pairs={{0,1},{1,0},{2,3},{3,2},{4,5},{5,4},{6,7},{7,6},{8,9},{9,8},{10,11... | collective-permute-start | bytes 196616 | tf_op jit(solution)/shard_map/ppermute | solution.py:457
  66.3 2.4 %root2a.1.state = f32[3,32,32]{2,1,0:T(8,128)S(1)} custom-call(f32[32,32]{1,0:T(8,128)S(1)} %root1b.1.a_ref, f32[32,320]{1,0:T(8,128)S(1)} %add_add_fusion.1.u_ref), custom_call_target="tpu_custom_call" | custom-call | flops 12000000 | bytes 45056 | tf_op jit(solution)/shard_map/root2a/pallas_call | solution.py:48
  68.7 2.3 %root2b.1.f0_ref = f32[32,384]{1,0:T(8,128)S(1)} custom-call(f32[3,32,32]{2,1,0:T(8,128)S(1)} %root2a.1.state, f32[32,32]{1,0:T(8,128)S(1)} %root1b.1.a_ref, f32[32,320]{1,0:T(8,128)S(1)} %add_add_fusion.1.u_ref), custom_call_target="tpu_custom_call" | custom-call | flops 12000000 | bytes 57344 | tf_op jit(solution)/shard_map/root2b/pallas_call | solution.py:48
  71.0 0.0 collective-permute-done.22
  71.1 0.1 collective-permute-start.26
  71.2 1.5 %collective-permute-start.25 = (f32[1,32,512]{2,1,0:T(8,128)S(1)}, f32[1,32,512]{2,1,0:T(8,128)S(1)}, u32[]{:S(2)}, u32[]{:S(2)}) collective-permute-start(f32[1,32,512]{2,1,0:T(8,128)S(1)} %add_bitcast_fusion.v0_ref), channel_id=1, source_target_pairs={{0,24},{1,25},{2,26},{3,27},{4,28},{5,29},{6,30},{7,31},{8,16},{9,... | collective-permute-start | bytes 196616 | tf_op jit(solution)/shard_map/ppermute | solution.py:457
  72.7 0.5 collective-permute-start.24
  73.2 1.6 %collective-permute-start.23 = (f32[1,32,512]{2,1,0:T(8,128)S(1)}, f32[1,32,512]{2,1,0:T(8,128)S(1)}, u32[]{:S(2)}, u32[]{:S(2)}) collective-permute-start(f32[1,32,512]{2,1,0:T(8,128)S(1)} %add_bitcast_fusion.v0_ref), channel_id=1, source_target_pairs={{0,8},{1,9},{2,10},{3,11},{4,20},{5,21},{6,22},{7,23},{8,0},{9,1},... | collective-permute-start | bytes 196616 | tf_op jit(solution)/shard_map/ppermute | solution.py:457
  74.8 1.2 %collective-permute-done.27.f1_ref = f32[32,384]{1,0:T(8,128)S(1)} collective-permute-done((f32[32,384]{1,0:T(8,128)S(1)}, f32[32,384]{1,0:T(8,128)S(1)}, u32[]{:S(2)}, u32[]{:S(2)}) %collective-permute-start.27) | collective-permute-done | bytes 49184 | tf_op jit(solution)/shard_map/ppermute | solution.py:457
  76.0 2.4 %finish0.1 = (f32[1,2,320,2048]{3,2,1,0:T(8,128)}, f32[2,64,2048]{2,1,0:T(8,128)}, f32[2,64,2048]{2,1,0:T(8,128)}, bf16[2,320,192]{2,1,0:T(8,128)(2,1)S(1)}) custom-call(s32[3]{0:T(128)S(1)} %pad_add_fusion.place, s32[12]{0:T(128)S(1)} %copy-done.4, f32[1,32,512]{2,1,0:T(8,128)S(1)} %add_bitcast_fusion.v0_ref, ...), custom_call_target="tpu_custom_call" | custom-call | flops 125829120 | bytes 2359296 | tf_op jit(solution)/shard_map/finish0/pallas_call | solution.py:48
  78.5 0.2 collective-permute-start.28
  78.8 1.3 %collective-permute-done.28.v1_ref = f32[3,32,512]{2,1,0:T(8,128)S(1)} collective-permute-done((f32[3,32,512]{2,1,0:T(8,128)S(1)}, f32[3,32,512]{2,1,0:T(8,128)S(1)}, u32[]{:S(2)}, u32[]{:S(2)}) %collective-permute-start.28) | collective-permute-done | bytes 196640 | tf_op jit(solution)/shard_map/ppermute | solution.py:457
  80.0 3.9 %finish1.1 = (f32[1,2,320,2048]{3,2,1,0:T(8,128)}, f32[2,64,2048]{2,1,0:T(8,128)}, f32[2,64,2048]{2,1,0:T(8,128)}) custom-call(s32[3]{0:T(128)S(1)} %pad_add_fusion.place, s32[12]{0:T(128)S(1)} %copy-done.4, f32[3,32,512]{2,1,0:T(8,128)S(1)} %constant_dynamic-update-slice_fusion.v0_ref, ...), custom_call_target="tpu_custom_call", output_to_operand_aliasing={{0}: (13, {}), {1}: (14, {}), {2}: (15, {})} | custom-call | flops 377487360 | bytes 7077888 | tf_op jit(solution)/shard_map/finish1/pallas_call | solution.py:48
  (34 shorter events, 0.2 us)
Async XLA Ops:
  0.7 3.4 %copy-start = (f32[2,32,2048]{2,1,0:T(8,128)S(1)}, f32[2,32,2048]{2,1,0:T(8,128)}, u32[]{:S(2)}) copy-start(f32[2,32,2048]{2,1,0:T(8,128)} %w_ref.1) | copy-start | bytes 1572868
  0.7 3.4 %copy-start.1 = (f32[1,2,2048]{2,1,0:T(2,128)S(1)}, f32[1,2,2048]{2,1,0:T(2,128)}, u32[]{:S(2)}) copy-start(f32[1,2,2048]{2,1,0:T(2,128)} %vec_ref.1) | copy-start | bytes 49156
  3.5 4.2 %collective-permute-start = (f32[2,320,512]{2,1,0:T(8,128)S(1)}, f32[2,320,512]{2,1,0:T(8,128)S(1)}, u32[]{:S(2)}, u32[]{:S(2)}) collective-permute-start(f32[2,320,512]{2,1,0:T(8,128)S(1)} %get-tuple-element.60.refs_3_.c1_odd), channel_id=1, source_target_pairs={{0,4},{1,5},{2,6},{3,7},{4,0},{5,1},{6,2},{7,3},{8,12},{9,13},{10,... | collective-permute-start | bytes 3932168 | tf_op jit(solution)/shard_map/ppermute | solution.py:457
  4.0 18.2 %collective-permute-start.7 = (f32[2,320,512]{2,1,0:T(8,128)S(1)}, f32[2,320,512]{2,1,0:T(8,128)S(1)}, u32[]{:S(2)}, u32[]{:S(2)}) collective-permute-start(f32[2,320,512]{2,1,0:T(8,128)S(1)} %get-tuple-element.59.refs_2_.c1_even), channel_id=1, source_target_pairs={{0,4},{1,5},{2,6},{3,7},{4,0},{5,1},{6,2},{7,3},{8,12},{9,13},{10,... | collective-permute-start | bytes 3932168 | tf_op jit(solution)/shard_map/ppermute | solution.py:457
  7.8 14.4 %collective-permute-start.8 = (f32[1,320,512]{2,1,0:T(8,128)S(1)}, f32[1,320,512]{2,1,0:T(8,128)S(1)}, u32[]{:S(2)}, u32[]{:S(2)}) collective-permute-start(f32[1,320,512]{2,1,0:T(8,128)S(1)} %fold.4), channel_id=1, source_target_pairs={{0,8},{1,9},{2,10},{3,11},{4,20},{5,21},{6,22},{7,23},{8,0},{9,1},... | collective-permute-start | bytes 1966088 | tf_op jit(solution)/shard_map/ppermute | solution.py:457
  10.8 1.6 %collective-permute-start.2 = (f32[32,512]{1,0:T(8,128)S(1)}, f32[32,512]{1,0:T(8,128)S(1)}, u32[]{:S(2)}, u32[]{:S(2)}) collective-permute-start(f32[32,512]{1,0:T(8,128)S(1)} %get-tuple-element.64), channel_id=1, source_target_pairs={{0,4},{1,5},{2,6},{3,7},{4,0},{5,1},{6,2},{7,3},{8,12},{9,13},{10,... | collective-permute-start | bytes 196616 | tf_op jit(solution)/shard_map/ppermute | solution.py:457
  12.5 5.1 %collective-permute-start.3 = (f32[32,512]{1,0:T(8,128)S(1)}, f32[32,512]{1,0:T(8,128)S(1)}, u32[]{:S(2)}, u32[]{:S(2)}) collective-permute-start(f32[32,512]{1,0:T(8,128)S(1)} %add.61), channel_id=1, source_target_pairs={{0,16},{1,17},{2,18},{3,19},{4,12},{5,13},{6,14},{7,15},{8,24},{9,... | collective-permute-start | bytes 196616 | tf_op jit(solution)/shard_map/ppermute | solution.py:457
  14.1 16.7 %collective-permute-start.1 = (f32[1,320,512]{2,1,0:T(8,128)S(1)}, f32[1,320,512]{2,1,0:T(8,128)S(1)}, u32[]{:S(2)}, u32[]{:S(2)}) collective-permute-start(f32[1,320,512]{2,1,0:T(8,128)S(1)} %fold.3), channel_id=1, source_target_pairs={{0,8},{1,9},{2,10},{3,11},{4,20},{5,21},{6,22},{7,23},{8,0},{9,1},... | collective-permute-start | bytes 1966088 | tf_op jit(solution)/shard_map/ppermute | solution.py:457
  17.6 4.6 %collective-permute-start.4 = (f32[32,512]{1,0:T(8,128)S(1)}, f32[32,512]{1,0:T(8,128)S(1)}, u32[]{:S(2)}, u32[]{:S(2)}) collective-permute-start(f32[32,512]{1,0:T(8,128)S(1)} %add.62), channel_id=1, source_target_pairs={{0,1},{1,0},{2,3},{3,2},{4,6},{5,7},{6,4},{7,5},{8,9},{9,8},{10,11... | collective-permute-start | bytes 196616 | tf_op jit(solution)/shard_map/ppermute | solution.py:457
  22.3 13.2 %collective-permute-start.9 = (f32[1,320,512]{2,1,0:T(8,128)S(1)}, f32[1,320,512]{2,1,0:T(8,128)S(1)}, u32[]{:S(2)}, u32[]{:S(2)}) collective-permute-start(f32[1,320,512]{2,1,0:T(8,128)S(1)} %fold.5), channel_id=1, source_target_pairs={{0,16},{1,17},{2,18},{3,19},{4,12},{5,13},{6,14},{7,15},{8,24},{9,... | collective-permute-start | bytes 1966088 | tf_op jit(solution)/shard_map/ppermute | solution.py:457
  23.9 5.2 %collective-permute-start.5 = (f32[32,512]{1,0:T(8,128)S(1)}, f32[32,512]{1,0:T(8,128)S(1)}, u32[]{:S(2)}, u32[]{:S(2)}) collective-permute-start(f32[32,512]{1,0:T(8,128)S(1)} %add.63.refs_3_), channel_id=1, source_target_pairs={{0,2},{1,3},{2,0},{3,1},{4,5},{5,4},{6,7},{7,6},{8,10},{9,11},{10,... | collective-permute-start | bytes 196616 | tf_op jit(solution)/shard_map/ppermute | solution.py:457
  30.8 4.7 %collective-permute-start.6 = (f32[32,512]{1,0:T(8,128)S(1)}, f32[32,512]{1,0:T(8,128)S(1)}, u32[]{:S(2)}, u32[]{:S(2)}) collective-permute-start(f32[32,512]{1,0:T(8,128)S(1)} %add.64), channel_id=1, source_target_pairs={{0,8},{1,9},{2,10},{3,11},{4,20},{5,21},{6,22},{7,23},{8,0},{9,1},... | collective-permute-start | bytes 196616 | tf_op jit(solution)/shard_map/ppermute | solution.py:457
  35.5 14.9 %copy-start.2 = (f32[2,2048]{1,0:T(2,128)S(1)}, f32[2,2048]{1,0:T(2,128)}, u32[]{:S(2)}) copy-start(f32[2,2048]{1,0:T(2,128)} %mv_ref.1) | copy-start | bytes 49156
  35.6 14.9 %copy-start.3 = (f32[2,2048]{1,0:T(2,128)S(1)}, f32[2,2048]{1,0:T(2,128)}, u32[]{:S(2)}) copy-start(f32[2,2048]{1,0:T(2,128)} %wv_ref.1) | copy-start | bytes 49156
  35.6 14.9 %copy-start.4 = (s32[12]{0:T(128)S(1)}, s32[12]{0:T(128)}, u32[]{:S(2)}) copy-start(s32[12]{0:T(128)} %owners.5) | copy-start | bytes 148
  36.2 8.4 %collective-permute-start.12 = (f32[32,512]{1,0:T(8,128)S(1)}, f32[32,512]{1,0:T(8,128)S(1)}, u32[]{:S(2)}, u32[]{:S(2)}) collective-permute-start(f32[32,512]{1,0:T(8,128)S(1)} %get-tuple-element.68), channel_id=1, source_target_pairs={{0,3},{1,2},{2,1},{3,0},{4,7},{5,6},{6,5},{7,4},{8,11},{9,10},{10,... | collective-permute-start | bytes 196616 | tf_op jit(solution)/shard_map/ppermute | solution.py:457
  39.7 5.5 %collective-permute-start.11 = (f32[32,512]{1,0:T(8,128)S(1)}, f32[32,512]{1,0:T(8,128)S(1)}, u32[]{:S(2)}, u32[]{:S(2)}) collective-permute-start(f32[32,512]{1,0:T(8,128)S(1)} %get-tuple-element.68), channel_id=1, source_target_pairs={{0,2},{1,3},{2,0},{3,1},{4,6},{5,7},{6,4},{7,5},{8,10},{9,11},{10,... | collective-permute-start | bytes 196616 | tf_op jit(solution)/shard_map/ppermute | solution.py:457
  39.7 5.5 %collective-permute-start.10 = (f32[32,512]{1,0:T(8,128)S(1)}, f32[32,512]{1,0:T(8,128)S(1)}, u32[]{:S(2)}, u32[]{:S(2)}) collective-permute-start(f32[32,512]{1,0:T(8,128)S(1)} %get-tuple-element.68), channel_id=1, source_target_pairs={{0,1},{1,0},{2,3},{3,2},{4,5},{5,4},{6,7},{7,6},{8,9},{9,8},{10,11... | collective-permute-start | bytes 196616 | tf_op jit(solution)/shard_map/ppermute | solution.py:457
  40.6 5.3 %collective-permute-start.13 = (f32[32,512]{1,0:T(8,128)S(1)}, f32[32,512]{1,0:T(8,128)S(1)}, u32[]{:S(2)}, u32[]{:S(2)}) collective-permute-start(f32[32,512]{1,0:T(8,128)S(1)} %add.65.x_ref.own_ref), channel_id=1, source_target_pairs={{0,4},{1,5},{2,6},{3,7},{4,0},{5,1},{6,2},{7,3},{8,12},{9,13},{10,... | collective-permute-start | bytes 196616 | tf_op jit(solution)/shard_map/ppermute | solution.py:457
  46.0 6.4 %collective-permute-start.16 = (f32[32,320]{1,0:T(8,128)S(1)}, f32[32,320]{1,0:T(8,128)S(1)}, u32[]{:S(2)}, u32[]{:S(2)}) collective-permute-start(f32[32,320]{1,0:T(8,128)S(1)} %lift.1), channel_id=1, source_target_pairs={{0,3},{1,2},{2,1},{3,0},{4,7},{5,6},{6,5},{7,4},{8,11},{9,10},{10,... | collective-permute-start | bytes 122888 | tf_op jit(solution)/shard_map/ppermute | solution.py:457
  48.9 5.0 %collective-permute-start.15 = (f32[32,320]{1,0:T(8,128)S(1)}, f32[32,320]{1,0:T(8,128)S(1)}, u32[]{:S(2)}, u32[]{:S(2)}) collective-permute-start(f32[32,320]{1,0:T(8,128)S(1)} %lift.1), channel_id=1, source_target_pairs={{0,2},{1,3},{2,0},{3,1},{4,6},{5,7},{6,4},{7,5},{8,10},{9,11},{10,... | collective-permute-start | bytes 122888 | tf_op jit(solution)/shard_map/ppermute | solution.py:457
  48.9 5.3 %collective-permute-start.14 = (f32[32,320]{1,0:T(8,128)S(1)}, f32[32,320]{1,0:T(8,128)S(1)}, u32[]{:S(2)}, u32[]{:S(2)}) collective-permute-start(f32[32,320]{1,0:T(8,128)S(1)} %lift.1), channel_id=1, source_target_pairs={{0,1},{1,0},{2,3},{3,2},{4,5},{5,4},{6,7},{7,6},{8,9},{9,8},{10,11... | collective-permute-start | bytes 122888 | tf_op jit(solution)/shard_map/ppermute | solution.py:457
  54.2 5.5 %collective-permute-start.19 = (f32[32,320]{1,0:T(8,128)S(1)}, f32[32,320]{1,0:T(8,128)S(1)}, u32[]{:S(2)}, u32[]{:S(2)}) collective-permute-start(f32[32,320]{1,0:T(8,128)S(1)} %add_add_fusion.2), channel_id=1, source_target_pairs={{0,24},{1,25},{2,26},{3,27},{4,28},{5,29},{6,30},{7,31},{8,16},{9,... | collective-permute-start | bytes 122888 | tf_op jit(solution)/shard_map/ppermute | solution.py:457
  56.9 4.1 %collective-permute-start.18 = (f32[32,320]{1,0:T(8,128)S(1)}, f32[32,320]{1,0:T(8,128)S(1)}, u32[]{:S(2)}, u32[]{:S(2)}) collective-permute-start(f32[32,320]{1,0:T(8,128)S(1)} %add_add_fusion.2), channel_id=1, source_target_pairs={{0,16},{1,17},{2,18},{3,19},{4,12},{5,13},{6,14},{7,15},{8,24},{9,... | collective-permute-start | bytes 122888 | tf_op jit(solution)/shard_map/ppermute | solution.py:457
  57.3 4.1 %collective-permute-start.17 = (f32[32,320]{1,0:T(8,128)S(1)}, f32[32,320]{1,0:T(8,128)S(1)}, u32[]{:S(2)}, u32[]{:S(2)}) collective-permute-start(f32[32,320]{1,0:T(8,128)S(1)} %add_add_fusion.2), channel_id=1, source_target_pairs={{0,8},{1,9},{2,10},{3,11},{4,20},{5,21},{6,22},{7,23},{8,0},{9,1},... | collective-permute-start | bytes 122888 | tf_op jit(solution)/shard_map/ppermute | solution.py:457
  61.9 9.2 %collective-permute-start.22 = (f32[32,512]{1,0:T(8,128)S(1)}, f32[32,512]{1,0:T(8,128)S(1)}, u32[]{:S(2)}, u32[]{:S(2)}) collective-permute-start(f32[32,512]{1,0:T(8,128)S(1)} %lower.1), channel_id=1, source_target_pairs={{0,3},{1,2},{2,1},{3,0},{4,7},{5,6},{6,5},{7,4},{8,11},{9,10},{10,... | collective-permute-start | bytes 196616 | tf_op jit(solution)/shard_map/ppermute | solution.py:457
  64.4 6.7 %collective-permute-start.21 = (f32[32,512]{1,0:T(8,128)S(1)}, f32[32,512]{1,0:T(8,128)S(1)}, u32[]{:S(2)}, u32[]{:S(2)}) collective-permute-start(f32[32,512]{1,0:T(8,128)S(1)} %lower.1), channel_id=1, source_target_pairs={{0,2},{1,3},{2,0},{3,1},{4,6},{5,7},{6,4},{7,5},{8,10},{9,11},{10,... | collective-permute-start | bytes 196616 | tf_op jit(solution)/shard_map/ppermute | solution.py:457
  64.4 6.7 %collective-permute-start.20 = (f32[32,512]{1,0:T(8,128)S(1)}, f32[32,512]{1,0:T(8,128)S(1)}, u32[]{:S(2)}, u32[]{:S(2)}) collective-permute-start(f32[32,512]{1,0:T(8,128)S(1)} %lower.1), channel_id=1, source_target_pairs={{0,1},{1,0},{2,3},{3,2},{4,5},{5,4},{6,7},{7,6},{8,9},{9,8},{10,11... | collective-permute-start | bytes 196616 | tf_op jit(solution)/shard_map/ppermute | solution.py:457
  71.1 4.9 %collective-permute-start.26 = (f32[1,32,512]{2,1,0:T(8,128)S(1)}, f32[1,32,512]{2,1,0:T(8,128)S(1)}, u32[]{:S(2)}, u32[]{:S(2)}) collective-permute-start(f32[1,32,512]{2,1,0:T(8,128)S(1)} %add_bitcast_fusion.v0_ref), channel_id=1, source_target_pairs={{0,4},{1,5},{2,6},{3,7},{4,0},{5,1},{6,2},{7,3},{8,12},{9,13},{10,... | collective-permute-start | bytes 196616 | tf_op jit(solution)/shard_map/ppermute | solution.py:457
  71.2 7.3 %collective-permute-start.25 = (f32[1,32,512]{2,1,0:T(8,128)S(1)}, f32[1,32,512]{2,1,0:T(8,128)S(1)}, u32[]{:S(2)}, u32[]{:S(2)}) collective-permute-start(f32[1,32,512]{2,1,0:T(8,128)S(1)} %add_bitcast_fusion.v0_ref), channel_id=1, source_target_pairs={{0,24},{1,25},{2,26},{3,27},{4,28},{5,29},{6,30},{7,31},{8,16},{9,... | collective-permute-start | bytes 196616 | tf_op jit(solution)/shard_map/ppermute | solution.py:457
  72.7 5.8 %collective-permute-start.24 = (f32[1,32,512]{2,1,0:T(8,128)S(1)}, f32[1,32,512]{2,1,0:T(8,128)S(1)}, u32[]{:S(2)}, u32[]{:S(2)}) collective-permute-start(f32[1,32,512]{2,1,0:T(8,128)S(1)} %add_bitcast_fusion.v0_ref), channel_id=1, source_target_pairs={{0,16},{1,17},{2,18},{3,19},{4,12},{5,13},{6,14},{7,15},{8,24},{9,... | collective-permute-start | bytes 196616 | tf_op jit(solution)/shard_map/ppermute | solution.py:457
  73.2 5.3 %collective-permute-start.23 = (f32[1,32,512]{2,1,0:T(8,128)S(1)}, f32[1,32,512]{2,1,0:T(8,128)S(1)}, u32[]{:S(2)}, u32[]{:S(2)}) collective-permute-start(f32[1,32,512]{2,1,0:T(8,128)S(1)} %add_bitcast_fusion.v0_ref), channel_id=1, source_target_pairs={{0,8},{1,9},{2,10},{3,11},{4,20},{5,21},{6,22},{7,23},{8,0},{9,1},... | collective-permute-start | bytes 196616 | tf_op jit(solution)/shard_map/ppermute | solution.py:457
  74.8 1.2 %collective-permute-start.27 = (f32[32,384]{1,0:T(8,128)S(1)}, f32[32,384]{1,0:T(8,128)S(1)}, u32[]{:S(2)}, u32[]{:S(2)}) collective-permute-start(f32[32,384]{1,0:T(8,128)S(1)} %root2b.1.f0_ref), channel_id=1, source_target_pairs={{0,4},{1,5},{2,6},{3,7},{4,0},{5,1},{6,2},{7,3},{8,12},{9,13},{10,... | collective-permute-start | bytes 147464 | tf_op jit(solution)/shard_map/ppermute | solution.py:457
  78.5 1.5 %collective-permute-start.28 = (f32[3,32,512]{2,1,0:T(8,128)S(1)}, f32[3,32,512]{2,1,0:T(8,128)S(1)}, u32[]{:S(2)}, u32[]{:S(2)}) collective-permute-start(f32[3,32,512]{2,1,0:T(8,128)S(1)} %constant_dynamic-update-slice_fusion.v0_ref), channel_id=1, source_target_pairs={{0,4},{1,5},{2,6},{3,7},{4,0},{5,1},{6,2},{7,3},{8,12},{9,13},{10,... | collective-permute-start | bytes 589832 | tf_op jit(solution)/shard_map/ppermute | solution.py:457

commit v5 on v4

--- a/solution.py
+++ b/solution.py
@@ -34,6 +34,29 @@
 
 def lanes(n):
     return -(-n // LANES) * LANES
+
+
+def pack_factor(out, u):
+    rank, rows = u.shape
+    whole, left = divmod(rows, LANES)
+    for i in range(whole):
+        out[i * rank : (i + 1) * rank, :] = u[:, i * LANES : (i + 1) * LANES]
+    if left:
+        short = rank * left // LANES
+        for i in range(LANES // left):
+            out[whole * rank : whole * rank + short, i * left : (i + 1) * left] = u[
+                i * short : (i + 1) * short, whole * LANES :
+            ]
+
+
+def unpack_factor(x, rank, rows):
+    whole, left = divmod(rows, LANES)
+    parts = [x[i * rank : (i + 1) * rank, :] for i in range(whole)]
+    if left:
+        short = rank * left // LANES
+        tail = x[whole * rank : whole * rank + short, :]
+        parts.append(jnp.concatenate([tail[:, i * left : (i + 1) * left] for i in range(LANES // left)], axis=0))
+    return jnp.concatenate(parts, axis=1)
 
 
 def in_hbm(a):
@@ -93,15 +116,16 @@
             terms += lax.dot_general(
                 part, jnp.concatenate(pieces, axis=0), (NT, ((), ())), preferred_element_type=f32
             )
-    out[...] = jnp.zeros(out.shape, f32)
-    out[:, :rows] = (terms[:, :rank] + terms[:, rank : 2 * rank] + terms[:, 2 * rank :]).T
+    pack_factor(out, (terms[:, :rank] + terms[:, rank : 2 * rank] + terms[:, 2 * rank :]).T)
+    base = rank * rows // LANES
     mine = jnp.where(m == 0, vec_ref[0, 0:1, :], vec_ref[0, 1:2, :])
     for i in range(vec_ref.shape[2] // LANES):
-        out[i : i + 1, out.shape[1] - LANES :] = mine[:, i * LANES : (i + 1) * LANES]
+        out[base + i : base + i + 1, :] = mine[:, i * LANES : (i + 1) * LANES]
 
 
 def factor_shape(rows, warm_start):
-    return jax.ShapeDtypeStruct((warm_start.shape[1], lanes(rows) + LANES), f32)
+    _, rank, cols = warm_start.shape
+    return jax.ShapeDtypeStruct(((rank * rows + cols) // LANES, LANES), f32)
 
 
 def factor_kernel(place, w_ref, vec_ref, even, odd, out):
@@ -197,15 +221,15 @@
     parts, (s_ref, v_ref) = refs[:-2], refs[-2:]
     block = sum(part[at] for part, at in zip(parts, places))
     s_ref[...] = block
-    v_ref[...] = dot(x_ref[:, : block.shape[0]] / count, block) / count
+    v_ref[...] = dot(unpack_factor(x_ref[...], v_ref.shape[0], block.shape[0]) / count, block) / count
 
 
 def lift_kernel(v_ref, s_ref, u_ref, *, count):
-    u_ref[...] = dot(v_ref[...], s_ref[...], NT) / count
+    pack_factor(u_ref, dot(v_ref[...], s_ref[...], NT) / count)
 
 
 def lower_kernel(u_ref, s_ref, v_ref, *, count):
-    v_ref[...] = dot(u_ref[...], s_ref[...]) / count
+    v_ref[...] = dot(unpack_factor(u_ref[...], v_ref.shape[0], s_ref.shape[0]), s_ref[...]) / count
 
 
 def identity(rank):
@@ -238,7 +262,7 @@
 
 
 def first_begin_kernel(x_ref, state, *, rows, count):
-    factor = x_ref[:, :rows] / count
+    factor = unpack_factor(x_ref[...], state.shape[1], rows) / count
     root_begin(dot(factor, factor, NT), state)
 
 
@@ -246,14 +270,15 @@
     a_ref[...] = root_end(state)
 
 
-def second_begin_kernel(a_ref, u_ref, state):
-    a, u = a_ref[...], u_ref[...]
+def second_begin_kernel(a_ref, u_ref, state, *, rows):
+    a = a_ref[...]
+    u = unpack_factor(u_ref[...], a.shape[0], rows)
     root_begin(dot(a, dot(dot(u, u, NT), a), TN), state)
 
 
-def second_end_kernel(state, a_ref, u_ref, f_ref):
-    u = u_ref[...]
-    rank, rows = u.shape
+def second_end_kernel(state, a_ref, u_ref, f_ref, *, rows):
+    rank = a_ref.shape[0]
+    u = unpack_factor(u_ref[...], rank, rows)
     both = dot(a_ref[...], root_end(state))
     f_ref[...] = jnp.zeros(f_ref.shape, f32)
     f_ref[:, :rows] = dot(both, u, TN)
@@ -273,7 +298,8 @@
     for i in range(mv_ref.shape[1] // LANES):
         at = slice(i * LANES, (i + 1) * LANES)
         for k, ref in enumerate((own_ref, other_ref)):
-            vec[k : k + 1, at] = ref[i : i + 1, ref.shape[1] - LANES :] / count
+            row = ref.shape[0] - mv_ref.shape[1] // LANES + i
+            vec[k : k + 1, at] = ref[row : row + 1, :] / count
     for slot, item in enumerate(taken_items(place, owners, mv_ref.shape[0])):
         row = jnp.where(item - first == place[0], vec[0:1, :], vec[1:2, :])
         old, weight = mv_ref[slot : slot + 1, :], wv_ref[slot : slot + 1, :]
@@ -511,7 +537,7 @@
     later, *_ = lax.optimization_barrier((place, go, go_rest))
     own_p = own_factor(later, own_c, warm_start, vec_grads)
     packed = own_p + exchange(other_p, "core")
-    packed = hop(packed, "plane", bits - 1)
+    packed, mm, mw = hop(packed, "plane", bits - 1, banks, mat_momentum, mat_weights)
     packed = hop(packed, "z", 0)
     land(*ahead)
     for stage in range(1, bits):
@@ -522,10 +548,12 @@
         pending.append(send(goes, stage, (packed,)))
     for step in range(1, depths):
         packed = hop(packed, "z", step)
-    arrived, packed = lax.optimization_barrier((pending[0][2], packed))
-    pending[0] = (*pending[0][:2], arrived)
-    for step in range(bits - 2, -1, -1):
+    for step in range(bits - 2, 0, -1):
         packed = hop(packed, "plane", step)
+    land(*pending.pop(0))
+    packed, keep = hop(packed, "plane", 0, lambda *x: [fold([list(zip(x, [at for _, at in terms[0]]))])],
+                       *[a for a, _ in terms[0]])
+    terms[0] = [(keep, 0)]
     while pending:
         land(*pending.pop(0))
 
@@ -535,29 +563,33 @@
     )
     square = (rank, rank)
     state = (3, rank, rank)
-    def first(x):
-        (begun,) = small_call(functools.partial(first_begin_kernel, rows=rows, count=count), "root1a", [state], x)
-        return small_call(first_end_kernel, "root1b", [square], begun)
-
     depth = list(range(1, groups))
-    v, first_root = hop(v, "depth", depth, first, packed)
-    (u,) = small_call(functools.partial(lift_kernel, count=count), "lift", [(rank, rows)], v, kept_sum)
+    v, first_state = hop(
+        v, "depth", depth,
+        lambda x: small_call(
+            functools.partial(first_begin_kernel, rows=rows, count=count), "root1a", [state], x
+        ), packed,
+    )
+    (u,) = small_call(functools.partial(lift_kernel, count=count), "lift", [(rank * rows // LANES, LANES)], v, kept_sum)
+    u, first_root = hop(u, "depth", depth, lambda x: small_call(first_end_kernel, "root1b", [square], x), first_state)
     u, vec_momentum_out, vec_weights_out = hop(
-        u, "depth", depth,
+        u, "place", list(range(1, blocks)),
         lambda x, y: gains(place, owners, x, y, vec_momentum, vec_weights, count, head_items),
         packed, exchange(packed, "core"),
     )
-    u, mm, mw = hop(u, "place", list(range(1, blocks)), banks, mat_momentum, mat_weights)
     (v,) = small_call(functools.partial(lower_kernel, count=count), "lower", [(rank, width)], u, kept_sum)
     def second(a, u):
-        (begun,) = small_call(second_begin_kernel, "root2a", [state], a, u)
-        return small_call(second_end_kernel, "root2b", [(rank, lanes(rows + rank))], begun, a, u)
+        (begun,) = small_call(functools.partial(second_begin_kernel, rows=rows), "root2a", [state], a, u)
+        return small_call(
+            functools.partial(second_end_kernel, rows=rows), "root2b", [(rank, lanes(rows + rank))], begun, a, u
+        )
 
     v, own_f = hop(v, "depth", depth, second, first_root, u)
-    other_f = exchange(own_f, "core")
+
     shapes = [errors.shape, mat_momentum.shape, mat_weights.shape]
+    swapped = exchange(jnp.concatenate([v, own_f], axis=1), "core")
+    other_v, other_f = swapped[None, :, :width], swapped[:, width:]
     v = v[None]
-    other_v = exchange(v, "core")
     arrived = [exchange(v, "place", p) for p in range(1, blocks)]
     *outs, left = finish(
         [0], (), (), place, owners, v, other_v, own_f, other_f, own_c, other_c, shapes, mm, mw

time: 84.1 us -> 82.8 us (0.985)
  waiting for transfers between devices: 20.5 us -> 18.9 us
    ppermute x29 -> x28, waiting for transfers between devices: 20.5 us -> 18.9 us  [exchange(): return lax.ppermute(a, ('rep', 'grp'), pairs)]
    pallas_call x17 -> x18, Pallas kernels: 27.7 us -> 27.9 us  [call(): pl.pallas_call(kernel, in_specs=in_specs, out_specs=out_specs, out_shape=...]
    ppermute x29 -> x28, starting transfers between devices: 34.5 us -> 34.6 us  [exchange(): return lax.ppermute(a, ('rep', 'grp'), pairs)]
  transfers between devices with their start and end apart: 29 -> 28, of which waited for: 14 -> 13; matrix products, arithmetic and copies ran while one was open for 0% -> 0% of each run, Pallas kernels for 24% -> 24%
where the time goes in v5:
time: 82.8 us; the launch traced here: 82.6 us
  starting transfers between devices  34.6 us (42%)
  Pallas kernels  27.9 us (34%)
  waiting for transfers between devices  18.9 us (23%)
  between operations  0.92 us (1%)
    ppermute x28, starting transfers between devices, exchange(): return lax.ppermute(a, ('rep', 'grp'), pairs)  34.6 us
    pallas_call x18, Pallas kernels, call(): pl.pallas_call(kernel, in_specs=in_specs, out_specs=out_specs, out_shape=...  27.9 us
    ppermute x28, waiting for transfers between devices, exchange(): return lax.ppermute(a, ('rep', 'grp'), pairs)  18.9 us
  transfers between devices with their start and end apart: 28, of which 13 were waited for; matrix products, arithmetic and copies ran while one was open for 0% of the time, Pallas kernels for 24%

profile of v5, /device:TPU:0, one launch (start us, length us, event | category | flops | bytes accessed | tf_op | source)
XLA Modules:
  0.0 82.6 jit_solution(9235850436830740766)
XLA Ops:
  0.7 0.1 pad_add_fusion.place
  0.7 2.8 %other.1 = (f32[2,320,512]{2,1,0:T(8,128)S(1)}, f32[2,320,512]{2,1,0:T(8,128)S(1)}) custom-call(s32[3]{0:T(128)S(1)} %pad_add_fusion.place, bf16[1,2,320,2048]{3,2,1,0:T(8,128)(2,1)} %g_hbm.3, f32[1,2,320,2048]{3,2,1,0:T(8,128)} %e_hbm.3), custom_call_target="tpu_custom_call" | custom-call | flops 655360 | bytes 6553600 | tf_op jit(solution)/shard_map/other/pallas_call | solution.py:71
  3.5 0.5 collective-permute-start
  4.0 0.1 collective-permute-start.5
  4.1 3.7 %own.1 = (f32[2,320,512]{2,1,0:T(8,128)S(1)}, f32[2,320,512]{2,1,0:T(8,128)S(1)}, f32[96,128]{1,0:T(8,128)S(1)}) custom-call(s32[3]{0:T(128)S(1)} %pad_add_fusion.place, bf16[1,2,320,2048]{3,2,1,0:T(8,128)(2,1)} %g_hbm.3, f32[1,2,320,2048]{3,2,1,0:T(8,128)} %e_hbm.3, f32[2,32,2048]{2,1,0:T(8,128)S(1)} %copy-done, f32[1,2,2048]{2,1,0:T(2,128)S(1)} %copy-done.1, ...), custom_call_target="tpu_custom_call" | custom-call | flops 131072000 | bytes 6553600 | tf_op jit(solution)/shard_map/own/pallas_call | solution.py:71
  7.8 0.0 collective-permute-done.refs_1_
  7.8 0.1 fold.4
  7.9 3.0 %collective-permute-start.8 = (f32[1,320,512]{2,1,0:T(8,128)S(1)}, f32[1,320,512]{2,1,0:T(8,128)S(1)}, u32[]{:S(2)}, u32[]{:S(2)}) collective-permute-start(f32[1,320,512]{2,1,0:T(8,128)S(1)} %fold.4), channel_id=1, source_target_pairs={{0,8},{1,9},{2,10},{3,11},{4,20},{5,21},{6,22},{7,23},{8,0},{9,1},... | collective-permute-start | bytes 1966088 | tf_op jit(solution)/shard_map/ppermute | solution.py:483
  10.9 0.1 fold.5
  10.9 1.6 %factor.1 = f32[96,128]{1,0:T(8,128)S(1)} custom-call(s32[3]{0:T(128)S(1)} %pad_add_fusion.place, f32[2,32,2048]{2,1,0:T(8,128)S(1)} %copy-done, f32[1,2,2048]{2,1,0:T(2,128)S(1)} %copy-done.1, f32[2,320,512]{2,1,0:T(8,128)S(1)} %get-tuple-element.80.even.refs_0_.c0_even, f32[2,320,512]{2,1,0:T(8,128)S(1)} %get-tuple-element.69.refs_0_.odd.c0_odd), custom_call_target="tpu_custom_call" | custom-call | flops 503316480 | bytes 5242880 | tf_op jit(solution)/shard_map/factor/pallas_call | solution.py:71
  12.5 0.0 collective-permute-done.1
  12.6 1.6 %collective-permute-start.2 = (f32[96,128]{1,0:T(8,128)S(1)}, f32[96,128]{1,0:T(8,128)S(1)}, u32[]{:S(2)}, u32[]{:S(2)}) collective-permute-start(f32[96,128]{1,0:T(8,128)S(1)} %add.61), channel_id=1, source_target_pairs={{0,16},{1,17},{2,18},{3,19},{4,12},{5,13},{6,14},{7,15},{8,24},{9,... | collective-permute-start | bytes 147464 | tf_op jit(solution)/shard_map/ppermute | solution.py:483
  14.2 0.5 collective-permute-start.6
  14.7 1.6 %banks.1 = (f32[2,64,2048]{2,1,0:T(8,128)S(1)}, f32[2,64,2048]{2,1,0:T(8,128)S(1)}) custom-call(f32[2,64,2048]{2,1,0:T(8,128)} %mm_hbm, f32[2,64,2048]{2,1,0:T(8,128)} %mw_hbm), custom_call_target="tpu_custom_call" | custom-call | bytes 2097152 | tf_op jit(solution)/shard_map/banks/pallas_call | solution.py:71
  16.3 1.1 %collective-permute-done.2 = f32[96,128]{1,0:T(8,128)S(1)} collective-permute-done((f32[96,128]{1,0:T(8,128)S(1)}, f32[96,128]{1,0:T(8,128)S(1)}, u32[]{:S(2)}, u32[]{:S(2)}) %collective-permute-start.2) | collective-permute-done | bytes 49184 | tf_op jit(solution)/shard_map/ppermute | solution.py:483
  17.3 1.6 %collective-permute-start.3 = (f32[96,128]{1,0:T(8,128)S(1)}, f32[96,128]{1,0:T(8,128)S(1)}, u32[]{:S(2)}, u32[]{:S(2)}) collective-permute-start(f32[96,128]{1,0:T(8,128)S(1)} %add.62), channel_id=1, source_target_pairs={{0,1},{1,0},{2,3},{3,2},{4,6},{5,7},{6,4},{7,5},{8,9},{9,8},{10,11... | collective-permute-start | bytes 147464 | tf_op jit(solution)/shard_map/ppermute | solution.py:483
  19.0 2.6 %collective-permute-done.3 = f32[96,128]{1,0:T(8,128)S(1)} collective-permute-done((f32[96,128]{1,0:T(8,128)S(1)}, f32[96,128]{1,0:T(8,128)S(1)}, u32[]{:S(2)}, u32[]{:S(2)}) %collective-permute-start.3) | collective-permute-done | bytes 49184 | tf_op jit(solution)/shard_map/ppermute | solution.py:483
  21.6 0.0 collective-permute-done.8.refs_2_
  21.6 0.1 fold.7
  21.7 1.6 %collective-permute-start.9 = (f32[1,320,512]{2,1,0:T(8,128)S(1)}, f32[1,320,512]{2,1,0:T(8,128)S(1)}, u32[]{:S(2)}, u32[]{:S(2)}) collective-permute-start(f32[1,320,512]{2,1,0:T(8,128)S(1)} %fold.7), channel_id=1, source_target_pairs={{0,16},{1,17},{2,18},{3,19},{4,12},{5,13},{6,14},{7,15},{8,24},{9,... | collective-permute-start | bytes 1966088 | tf_op jit(solution)/shard_map/ppermute | solution.py:483
  23.3 2.5 %collective-permute-start.4 = (f32[96,128]{1,0:T(8,128)S(1)}, f32[96,128]{1,0:T(8,128)S(1)}, u32[]{:S(2)}, u32[]{:S(2)}) collective-permute-start(f32[96,128]{1,0:T(8,128)S(1)} %add.63.refs_3_), channel_id=1, source_target_pairs={{0,2},{1,3},{2,0},{3,1},{4,5},{5,4},{6,7},{7,6},{8,10},{9,11},{10,... | collective-permute-start | bytes 147464 | tf_op jit(solution)/shard_map/ppermute | solution.py:483
  25.8 2.5 %collective-permute-done.4 = f32[96,128]{1,0:T(8,128)S(1)} collective-permute-done((f32[96,128]{1,0:T(8,128)S(1)}, f32[96,128]{1,0:T(8,128)S(1)}, u32[]{:S(2)}, u32[]{:S(2)}) %collective-permute-start.4) | collective-permute-done | bytes 49184 | tf_op jit(solution)/shard_map/ppermute | solution.py:483
  28.3 2.6 %collective-permute-done.6.refs_2_ = f32[1,320,512]{2,1,0:T(8,128)S(1)} collective-permute-done((f32[1,320,512]{2,1,0:T(8,128)S(1)}, f32[1,320,512]{2,1,0:T(8,128)S(1)}, u32[]{:S(2)}, u32[]{:S(2)}) %collective-permute-start.6) | collective-permute-done | bytes 655392 | tf_op jit(solution)/shard_map/ppermute | solution.py:483
  30.9 2.5 %collective-permute-start.7 = (f32[96,128]{1,0:T(8,128)S(1)}, f32[96,128]{1,0:T(8,128)S(1)}, u32[]{:S(2)}, u32[]{:S(2)}) collective-permute-start(f32[96,128]{1,0:T(8,128)S(1)} %add.64), channel_id=1, source_target_pairs={{0,8},{1,9},{2,10},{3,11},{4,20},{5,21},{6,22},{7,23},{8,0},{9,1},... | collective-permute-start | bytes 147464 | tf_op jit(solution)/shard_map/ppermute | solution.py:483
  33.4 0.1 fold.6.refs_0_
  33.5 2.0 %collective-permute-done.7 = f32[96,128]{1,0:T(8,128)S(1)} collective-permute-done((f32[96,128]{1,0:T(8,128)S(1)}, f32[96,128]{1,0:T(8,128)S(1)}, u32[]{:S(2)}, u32[]{:S(2)}) %collective-permute-start.7) | collective-permute-done | bytes 49184 | tf_op jit(solution)/shard_map/ppermute | solution.py:483
  35.5 0.0 copy-start.3
  35.5 0.0 copy-start.4
  35.5 0.5 project.1
  36.1 3.2 %collective-permute-start.12 = (f32[32,512]{1,0:T(8,128)S(1)}, f32[32,512]{1,0:T(8,128)S(1)}, u32[]{:S(2)}, u32[]{:S(2)}) collective-permute-start(f32[32,512]{1,0:T(8,128)S(1)} %get-tuple-element.86), channel_id=1, source_target_pairs={{0,3},{1,2},{2,1},{3,0},{4,7},{5,6},{6,5},{7,4},{8,11},{9,10},{10,... | collective-permute-start | bytes 196616 | tf_op jit(solution)/shard_map/ppermute | solution.py:483
  39.3 1.2 %collective-permute-start.10 = (f32[32,512]{1,0:T(8,128)S(1)}, f32[32,512]{1,0:T(8,128)S(1)}, u32[]{:S(2)}, u32[]{:S(2)}) collective-permute-start(f32[32,512]{1,0:T(8,128)S(1)} %get-tuple-element.86), channel_id=1, source_target_pairs={{0,1},{1,0},{2,3},{3,2},{4,5},{5,4},{6,7},{7,6},{8,9},{9,8},{10,11... | collective-permute-start | bytes 196616 | tf_op jit(solution)/shard_map/ppermute | solution.py:483
  40.5 2.1 %root1a.1.state = f32[3,32,32]{2,1,0:T(8,128)S(1)} custom-call(f32[96,128]{1,0:T(8,128)S(1)} %add.65.x_ref.own_ref), custom_call_target="tpu_custom_call" | custom-call | flops 12000000 | bytes 49152 | tf_op jit(solution)/shard_map/root1a/pallas_call | solution.py:71
  42.6 0.0 collective-permute-done.12
  42.6 2.3 %collective-permute-done.11 = f32[32,512]{1,0:T(8,128)S(1)} collective-permute-done((f32[32,512]{1,0:T(8,128)S(1)}, f32[32,512]{1,0:T(8,128)S(1)}, u32[]{:S(2)}, u32[]{:S(2)}) %collective-permute-start.11) | collective-permute-done | bytes 65568 | tf_op jit(solution)/shard_map/ppermute | solution.py:483
  44.9 0.7 lift.1
  45.6 2.3 %collective-permute-start.15 = (f32[80,128]{1,0:T(8,128)S(1)}, f32[80,128]{1,0:T(8,128)S(1)}, u32[]{:S(2)}, u32[]{:S(2)}) collective-permute-start(f32[80,128]{1,0:T(8,128)S(1)} %lift.1), channel_id=1, source_target_pairs={{0,3},{1,2},{2,1},{3,0},{4,7},{5,6},{6,5},{7,4},{8,11},{9,10},{10,... | collective-permute-start | bytes 122888 | tf_op jit(solution)/shard_map/ppermute | solution.py:483
  47.9 2.2 %collective-permute-start.13 = (f32[80,128]{1,0:T(8,128)S(1)}, f32[80,128]{1,0:T(8,128)S(1)}, u32[]{:S(2)}, u32[]{:S(2)}) collective-permute-start(f32[80,128]{1,0:T(8,128)S(1)} %lift.1), channel_id=1, source_target_pairs={{0,1},{1,0},{2,3},{3,2},{4,5},{5,4},{6,7},{7,6},{8,9},{9,8},{10,11... | collective-permute-start | bytes 122888 | tf_op jit(solution)/shard_map/ppermute | solution.py:483
  50.1 1.9 %root1b.1.a_ref = f32[32,32]{1,0:T(8,128)S(1)} custom-call(f32[3,32,32]{2,1,0:T(8,128)S(1)} %root1a.1.state), custom_call_target="tpu_custom_call" | custom-call | flops 12000000 | bytes 12288 | tf_op jit(solution)/shard_map/root1b/pallas_call | solution.py:71
  52.0 0.0 collective-permute-done.15
  52.0 0.8 %collective-permute-done.14 = f32[80,128]{1,0:T(8,128)S(1)} collective-permute-done((f32[80,128]{1,0:T(8,128)S(1)}, f32[80,128]{1,0:T(8,128)S(1)}, u32[]{:S(2)}, u32[]{:S(2)}) %collective-permute-start.14) | collective-permute-done | bytes 40992 | tf_op jit(solution)/shard_map/ppermute | solution.py:483
  52.8 3.0 %collective-permute-start.19 = (f32[80,128]{1,0:T(8,128)S(1)}, f32[80,128]{1,0:T(8,128)S(1)}, u32[]{:S(2)}, u32[]{:S(2)}) collective-permute-start(f32[80,128]{1,0:T(8,128)S(1)} %add_add_fusion.3), channel_id=1, source_target_pairs={{0,24},{1,25},{2,26},{3,27},{4,28},{5,29},{6,30},{7,31},{8,16},{9,... | collective-permute-start | bytes 122888 | tf_op jit(solution)/shard_map/ppermute | solution.py:483
  55.9 0.3 collective-permute-start.18
  56.2 0.3 collective-permute-start.17
  56.5 1.2 %gains.1 = (f32[2,2048]{1,0:T(2,128)}, f32[2,2048]{1,0:T(2,128)}) custom-call(s32[3]{0:T(128)S(1)} %pad_add_fusion.place, s32[12]{0:T(128)S(1)} %copy-done.4, f32[96,128]{1,0:T(8,128)S(1)} %add.65.x_ref.own_ref, f32[96,128]{1,0:T(8,128)S(1)} %collective-permute-done.16.other_ref, f32[2,2048]{1,0:T(2,128)S(1)} %copy-done.2, f32[2,2048]{1,0:T(2,128)S(1)} %copy-done.3), custom_call_target="tpu_custom_call" | custom-call | flops 40960 | bytes 65536 | tf_op jit(solution)/shard_map/gains/pallas_call | solution.py:71
  57.7 0.5 collective-permute-done.19
  58.2 1.7 %collective-permute-done.18 = f32[80,128]{1,0:T(8,128)S(1)} collective-permute-done((f32[80,128]{1,0:T(8,128)S(1)}, f32[80,128]{1,0:T(8,128)S(1)}, u32[]{:S(2)}, u32[]{:S(2)}) %collective-permute-start.18) | collective-permute-done | bytes 40992 | tf_op jit(solution)/shard_map/ppermute | solution.py:483
  59.9 0.3 collective-permute-done.17
  60.2 0.5 lower.1
  60.7 1.9 %collective-permute-start.22 = (f32[32,512]{1,0:T(8,128)S(1)}, f32[32,512]{1,0:T(8,128)S(1)}, u32[]{:S(2)}, u32[]{:S(2)}) collective-permute-start(f32[32,512]{1,0:T(8,128)S(1)} %lower.1), channel_id=1, source_target_pairs={{0,3},{1,2},{2,1},{3,0},{4,7},{5,6},{6,5},{7,4},{8,11},{9,10},{10,... | collective-permute-start | bytes 196616 | tf_op jit(solution)/shard_map/ppermute | solution.py:483
  62.6 0.7 collective-permute-start.21
  63.3 1.8 %collective-permute-start.20 = (f32[32,512]{1,0:T(8,128)S(1)}, f32[32,512]{1,0:T(8,128)S(1)}, u32[]{:S(2)}, u32[]{:S(2)}) collective-permute-start(f32[32,512]{1,0:T(8,128)S(1)} %lower.1), channel_id=1, source_target_pairs={{0,1},{1,0},{2,3},{3,2},{4,5},{5,4},{6,7},{7,6},{8,9},{9,8},{10,11... | collective-permute-start | bytes 196616 | tf_op jit(solution)/shard_map/ppermute | solution.py:483
  65.1 2.4 %root2a.1.state = f32[3,32,32]{2,1,0:T(8,128)S(1)} custom-call(f32[32,32]{1,0:T(8,128)S(1)} %root1b.1.a_ref, f32[80,128]{1,0:T(8,128)S(1)} %add_add_fusion.2.u_ref), custom_call_target="tpu_custom_call" | custom-call | flops 12000000 | bytes 45056 | tf_op jit(solution)/shard_map/root2a/pallas_call | solution.py:71
  67.6 2.3 %root2b.1.f0_ref = f32[32,384]{1,0:T(8,128)S(1)} custom-call(f32[3,32,32]{2,1,0:T(8,128)S(1)} %root2a.1.state, f32[32,32]{1,0:T(8,128)S(1)} %root1b.1.a_ref, f32[80,128]{1,0:T(8,128)S(1)} %add_add_fusion.2.u_ref), custom_call_target="tpu_custom_call" | custom-call | flops 12000000 | bytes 57344 | tf_op jit(solution)/shard_map/root2b/pallas_call | solution.py:71
  69.9 0.0 collective-permute-done.22
  70.0 0.1 collective-permute-start.26
  70.0 1.2 %collective-permute-start.25 = (f32[1,32,512]{2,1,0:T(8,128)S(1)}, f32[1,32,512]{2,1,0:T(8,128)S(1)}, u32[]{:S(2)}, u32[]{:S(2)}) collective-permute-start(f32[1,32,512]{2,1,0:T(8,128)S(1)} %bitcast.6), channel_id=1, source_target_pairs={{0,24},{1,25},{2,26},{3,27},{4,28},{5,29},{6,30},{7,31},{8,16},{9,... | collective-permute-start | bytes 196616 | tf_op jit(solution)/shard_map/ppermute | solution.py:483
  71.3 0.6 collective-permute-start.24
  71.9 1.7 %collective-permute-start.23 = (f32[1,32,512]{2,1,0:T(8,128)S(1)}, f32[1,32,512]{2,1,0:T(8,128)S(1)}, u32[]{:S(2)}, u32[]{:S(2)}) collective-permute-start(f32[1,32,512]{2,1,0:T(8,128)S(1)} %bitcast.8), channel_id=1, source_target_pairs={{0,8},{1,9},{2,10},{3,11},{4,20},{5,21},{6,22},{7,23},{8,0},{9,1},... | collective-permute-start | bytes 196616 | tf_op jit(solution)/shard_map/ppermute | solution.py:483
  73.7 2.4 %finish0.1 = (f32[1,2,320,2048]{3,2,1,0:T(8,128)}, f32[2,64,2048]{2,1,0:T(8,128)}, f32[2,64,2048]{2,1,0:T(8,128)}, bf16[2,320,192]{2,1,0:T(8,128)(2,1)S(1)}) custom-call(s32[3]{0:T(128)S(1)} %pad_add_fusion.place, s32[12]{0:T(128)S(1)} %copy-done.4, f32[1,32,512]{2,1,0:T(8,128)S(1)} %bitcast.9, f32[1,32,512]{2,1,0:T(8,128)S(1)} %slice_bitcast_fusion.v1_ref, ...), custom_call_target="tpu_custom_call" | custom-call | flops 125829120 | bytes 2359296 | tf_op jit(solution)/shard_map/finish0/pallas_call | solution.py:71
  76.1 0.4 collective-permute-done.24
  76.5 0.6 collective-permute-done.23
  77.2 0.1 collective-permute-start.27
  77.2 1.4 %collective-permute-done.27.v1_ref = f32[3,32,512]{2,1,0:T(8,128)S(1)} collective-permute-done((f32[3,32,512]{2,1,0:T(8,128)S(1)}, f32[3,32,512]{2,1,0:T(8,128)S(1)}, u32[]{:S(2)}, u32[]{:S(2)}) %collective-permute-start.27) | collective-permute-done | bytes 196640 | tf_op jit(solution)/shard_map/ppermute | solution.py:483
  78.7 3.9 %finish1.1 = (f32[1,2,320,2048]{3,2,1,0:T(8,128)}, f32[2,64,2048]{2,1,0:T(8,128)}, f32[2,64,2048]{2,1,0:T(8,128)}) custom-call(s32[3]{0:T(128)S(1)} %pad_add_fusion.place, s32[12]{0:T(128)S(1)} %copy-done.4, f32[3,32,512]{2,1,0:T(8,128)S(1)} %constant_dynamic-update-slice_fusion.v0_ref, ...), custom_call_target="tpu_custom_call", output_to_operand_aliasing={{0}: (13, {}), {1}: (14, {}), {2}: (15, {})} | custom-call | flops 377487360 | bytes 7077888 | tf_op jit(solution)/shard_map/finish1/pallas_call | solution.py:71
  (36 shorter events, 0.2 us)
Async XLA Ops:
  0.7 3.4 %copy-start = (f32[2,32,2048]{2,1,0:T(8,128)S(1)}, f32[2,32,2048]{2,1,0:T(8,128)}, u32[]{:S(2)}) copy-start(f32[2,32,2048]{2,1,0:T(8,128)} %w_ref.1) | copy-start | bytes 1572868
  0.7 3.4 %copy-start.1 = (f32[1,2,2048]{2,1,0:T(2,128)S(1)}, f32[1,2,2048]{2,1,0:T(2,128)}, u32[]{:S(2)}) copy-start(f32[1,2,2048]{2,1,0:T(2,128)} %vec_ref.1) | copy-start | bytes 49156
  3.5 4.3 %collective-permute-start = (f32[2,320,512]{2,1,0:T(8,128)S(1)}, f32[2,320,512]{2,1,0:T(8,128)S(1)}, u32[]{:S(2)}, u32[]{:S(2)}) collective-permute-start(f32[2,320,512]{2,1,0:T(8,128)S(1)} %get-tuple-element.68.refs_3_.c1_odd), channel_id=1, source_target_pairs={{0,4},{1,5},{2,6},{3,7},{4,0},{5,1},{6,2},{7,3},{8,12},{9,13},{10,... | collective-permute-start | bytes 3932168 | tf_op jit(solution)/shard_map/ppermute | solution.py:483
  4.0 17.6 %collective-permute-start.5 = (f32[2,320,512]{2,1,0:T(8,128)S(1)}, f32[2,320,512]{2,1,0:T(8,128)S(1)}, u32[]{:S(2)}, u32[]{:S(2)}) collective-permute-start(f32[2,320,512]{2,1,0:T(8,128)S(1)} %get-tuple-element.67.refs_2_.c1_even), channel_id=1, source_target_pairs={{0,4},{1,5},{2,6},{3,7},{4,0},{5,1},{6,2},{7,3},{8,12},{9,13},{10,... | collective-permute-start | bytes 3932168 | tf_op jit(solution)/shard_map/ppermute | solution.py:483
  7.9 13.7 %collective-permute-start.8 = (f32[1,320,512]{2,1,0:T(8,128)S(1)}, f32[1,320,512]{2,1,0:T(8,128)S(1)}, u32[]{:S(2)}, u32[]{:S(2)}) collective-permute-start(f32[1,320,512]{2,1,0:T(8,128)S(1)} %fold.4), channel_id=1, source_target_pairs={{0,8},{1,9},{2,10},{3,11},{4,20},{5,21},{6,22},{7,23},{8,0},{9,1},... | collective-permute-start | bytes 1966088 | tf_op jit(solution)/shard_map/ppermute | solution.py:483
  10.9 1.7 %collective-permute-start.1 = (f32[96,128]{1,0:T(8,128)S(1)}, f32[96,128]{1,0:T(8,128)S(1)}, u32[]{:S(2)}, u32[]{:S(2)}) collective-permute-start(f32[96,128]{1,0:T(8,128)S(1)} %get-tuple-element.72), channel_id=1, source_target_pairs={{0,4},{1,5},{2,6},{3,7},{4,0},{5,1},{6,2},{7,3},{8,12},{9,13},{10,... | collective-permute-start | bytes 147464 | tf_op jit(solution)/shard_map/ppermute | solution.py:483
  12.6 4.7 %collective-permute-start.2 = (f32[96,128]{1,0:T(8,128)S(1)}, f32[96,128]{1,0:T(8,128)S(1)}, u32[]{:S(2)}, u32[]{:S(2)}) collective-permute-start(f32[96,128]{1,0:T(8,128)S(1)} %add.61), channel_id=1, source_target_pairs={{0,16},{1,17},{2,18},{3,19},{4,12},{5,13},{6,14},{7,15},{8,24},{9,... | collective-permute-start | bytes 147464 | tf_op jit(solution)/shard_map/ppermute | solution.py:483
  14.2 16.8 %collective-permute-start.6 = (f32[1,320,512]{2,1,0:T(8,128)S(1)}, f32[1,320,512]{2,1,0:T(8,128)S(1)}, u32[]{:S(2)}, u32[]{:S(2)}) collective-permute-start(f32[1,320,512]{2,1,0:T(8,128)S(1)} %fold.5), channel_id=1, source_target_pairs={{0,8},{1,9},{2,10},{3,11},{4,20},{5,21},{6,22},{7,23},{8,0},{9,1},... | collective-permute-start | bytes 1966088 | tf_op jit(solution)/shard_map/ppermute | solution.py:483
  17.3 4.3 %collective-permute-start.3 = (f32[96,128]{1,0:T(8,128)S(1)}, f32[96,128]{1,0:T(8,128)S(1)}, u32[]{:S(2)}, u32[]{:S(2)}) collective-permute-start(f32[96,128]{1,0:T(8,128)S(1)} %add.62), channel_id=1, source_target_pairs={{0,1},{1,0},{2,3},{3,2},{4,6},{5,7},{6,4},{7,5},{8,9},{9,8},{10,11... | collective-permute-start | bytes 147464 | tf_op jit(solution)/shard_map/ppermute | solution.py:483
  21.7 13.8 %collective-permute-start.9 = (f32[1,320,512]{2,1,0:T(8,128)S(1)}, f32[1,320,512]{2,1,0:T(8,128)S(1)}, u32[]{:S(2)}, u32[]{:S(2)}) collective-permute-start(f32[1,320,512]{2,1,0:T(8,128)S(1)} %fold.7), channel_id=1, source_target_pairs={{0,16},{1,17},{2,18},{3,19},{4,12},{5,13},{6,14},{7,15},{8,24},{9,... | collective-permute-start | bytes 1966088 | tf_op jit(solution)/shard_map/ppermute | solution.py:483
  23.3 5.0 %collective-permute-start.4 = (f32[96,128]{1,0:T(8,128)S(1)}, f32[96,128]{1,0:T(8,128)S(1)}, u32[]{:S(2)}, u32[]{:S(2)}) collective-permute-start(f32[96,128]{1,0:T(8,128)S(1)} %add.63.refs_3_), channel_id=1, source_target_pairs={{0,2},{1,3},{2,0},{3,1},{4,5},{5,4},{6,7},{7,6},{8,10},{9,11},{10,... | collective-permute-start | bytes 147464 | tf_op jit(solution)/shard_map/ppermute | solution.py:483
  30.9 4.5 %collective-permute-start.7 = (f32[96,128]{1,0:T(8,128)S(1)}, f32[96,128]{1,0:T(8,128)S(1)}, u32[]{:S(2)}, u32[]{:S(2)}) collective-permute-start(f32[96,128]{1,0:T(8,128)S(1)} %add.64), channel_id=1, source_target_pairs={{0,8},{1,9},{2,10},{3,11},{4,20},{5,21},{6,22},{7,23},{8,0},{9,1},... | collective-permute-start | bytes 147464 | tf_op jit(solution)/shard_map/ppermute | solution.py:483
  35.5 21.0 %copy-start.2 = (f32[2,2048]{1,0:T(2,128)S(1)}, f32[2,2048]{1,0:T(2,128)}, u32[]{:S(2)}) copy-start(f32[2,2048]{1,0:T(2,128)} %mv_ref.1) | copy-start | bytes 49156
  35.5 21.0 %copy-start.3 = (f32[2,2048]{1,0:T(2,128)S(1)}, f32[2,2048]{1,0:T(2,128)}, u32[]{:S(2)}) copy-start(f32[2,2048]{1,0:T(2,128)} %wv_ref.1) | copy-start | bytes 49156
  35.5 21.0 %copy-start.4 = (s32[12]{0:T(128)S(1)}, s32[12]{0:T(128)}, u32[]{:S(2)}) copy-start(s32[12]{0:T(128)} %owners.5) | copy-start | bytes 148
  36.1 6.5 %collective-permute-start.12 = (f32[32,512]{1,0:T(8,128)S(1)}, f32[32,512]{1,0:T(8,128)S(1)}, u32[]{:S(2)}, u32[]{:S(2)}) collective-permute-start(f32[32,512]{1,0:T(8,128)S(1)} %get-tuple-element.86), channel_id=1, source_target_pairs={{0,3},{1,2},{2,1},{3,0},{4,7},{5,6},{6,5},{7,4},{8,11},{9,10},{10,... | collective-permute-start | bytes 196616 | tf_op jit(solution)/shard_map/ppermute | solution.py:483
  39.3 5.6 %collective-permute-start.11 = (f32[32,512]{1,0:T(8,128)S(1)}, f32[32,512]{1,0:T(8,128)S(1)}, u32[]{:S(2)}, u32[]{:S(2)}) collective-permute-start(f32[32,512]{1,0:T(8,128)S(1)} %get-tuple-element.86), channel_id=1, source_target_pairs={{0,2},{1,3},{2,0},{3,1},{4,6},{5,7},{6,4},{7,5},{8,10},{9,11},{10,... | collective-permute-start | bytes 196616 | tf_op jit(solution)/shard_map/ppermute | solution.py:483
  39.3 5.6 %collective-permute-start.10 = (f32[32,512]{1,0:T(8,128)S(1)}, f32[32,512]{1,0:T(8,128)S(1)}, u32[]{:S(2)}, u32[]{:S(2)}) collective-permute-start(f32[32,512]{1,0:T(8,128)S(1)} %get-tuple-element.86), channel_id=1, source_target_pairs={{0,1},{1,0},{2,3},{3,2},{4,5},{5,4},{6,7},{7,6},{8,9},{9,8},{10,11... | collective-permute-start | bytes 196616 | tf_op jit(solution)/shard_map/ppermute | solution.py:483
  45.6 6.4 %collective-permute-start.15 = (f32[80,128]{1,0:T(8,128)S(1)}, f32[80,128]{1,0:T(8,128)S(1)}, u32[]{:S(2)}, u32[]{:S(2)}) collective-permute-start(f32[80,128]{1,0:T(8,128)S(1)} %lift.1), channel_id=1, source_target_pairs={{0,3},{1,2},{2,1},{3,0},{4,7},{5,6},{6,5},{7,4},{8,11},{9,10},{10,... | collective-permute-start | bytes 122888 | tf_op jit(solution)/shard_map/ppermute | solution.py:483
  47.9 4.9 %collective-permute-start.14 = (f32[80,128]{1,0:T(8,128)S(1)}, f32[80,128]{1,0:T(8,128)S(1)}, u32[]{:S(2)}, u32[]{:S(2)}) collective-permute-start(f32[80,128]{1,0:T(8,128)S(1)} %lift.1), channel_id=1, source_target_pairs={{0,2},{1,3},{2,0},{3,1},{4,6},{5,7},{6,4},{7,5},{8,10},{9,11},{10,... | collective-permute-start | bytes 122888 | tf_op jit(solution)/shard_map/ppermute | solution.py:483
  47.9 4.9 %collective-permute-start.13 = (f32[80,128]{1,0:T(8,128)S(1)}, f32[80,128]{1,0:T(8,128)S(1)}, u32[]{:S(2)}, u32[]{:S(2)}) collective-permute-start(f32[80,128]{1,0:T(8,128)S(1)} %lift.1), channel_id=1, source_target_pairs={{0,1},{1,0},{2,3},{3,2},{4,5},{5,4},{6,7},{7,6},{8,9},{9,8},{10,11... | collective-permute-start | bytes 122888 | tf_op jit(solution)/shard_map/ppermute | solution.py:483
  50.1 2.8 %collective-permute-start.16 = (f32[96,128]{1,0:T(8,128)S(1)}, f32[96,128]{1,0:T(8,128)S(1)}, u32[]{:S(2)}, u32[]{:S(2)}) collective-permute-start(f32[96,128]{1,0:T(8,128)S(1)} %add.65.x_ref.own_ref), channel_id=1, source_target_pairs={{0,4},{1,5},{2,6},{3,7},{4,0},{5,1},{6,2},{7,3},{8,12},{9,13},{10,... | collective-permute-start | bytes 147464 | tf_op jit(solution)/shard_map/ppermute | solution.py:483
  52.8 5.4 %collective-permute-start.19 = (f32[80,128]{1,0:T(8,128)S(1)}, f32[80,128]{1,0:T(8,128)S(1)}, u32[]{:S(2)}, u32[]{:S(2)}) collective-permute-start(f32[80,128]{1,0:T(8,128)S(1)} %add_add_fusion.3), channel_id=1, source_target_pairs={{0,24},{1,25},{2,26},{3,27},{4,28},{5,29},{6,30},{7,31},{8,16},{9,... | collective-permute-start | bytes 122888 | tf_op jit(solution)/shard_map/ppermute | solution.py:483
  55.9 4.0 %collective-permute-start.18 = (f32[80,128]{1,0:T(8,128)S(1)}, f32[80,128]{1,0:T(8,128)S(1)}, u32[]{:S(2)}, u32[]{:S(2)}) collective-permute-start(f32[80,128]{1,0:T(8,128)S(1)} %add_add_fusion.3), channel_id=1, source_target_pairs={{0,16},{1,17},{2,18},{3,19},{4,12},{5,13},{6,14},{7,15},{8,24},{9,... | collective-permute-start | bytes 122888 | tf_op jit(solution)/shard_map/ppermute | solution.py:483
  56.2 4.0 %collective-permute-start.17 = (f32[80,128]{1,0:T(8,128)S(1)}, f32[80,128]{1,0:T(8,128)S(1)}, u32[]{:S(2)}, u32[]{:S(2)}) collective-permute-start(f32[80,128]{1,0:T(8,128)S(1)} %add_add_fusion.3), channel_id=1, source_target_pairs={{0,8},{1,9},{2,10},{3,11},{4,20},{5,21},{6,22},{7,23},{8,0},{9,1},... | collective-permute-start | bytes 122888 | tf_op jit(solution)/shard_map/ppermute | solution.py:483
  60.7 9.2 %collective-permute-start.22 = (f32[32,512]{1,0:T(8,128)S(1)}, f32[32,512]{1,0:T(8,128)S(1)}, u32[]{:S(2)}, u32[]{:S(2)}) collective-permute-start(f32[32,512]{1,0:T(8,128)S(1)} %lower.1), channel_id=1, source_target_pairs={{0,3},{1,2},{2,1},{3,0},{4,7},{5,6},{6,5},{7,4},{8,11},{9,10},{10,... | collective-permute-start | bytes 196616 | tf_op jit(solution)/shard_map/ppermute | solution.py:483
  62.6 7.3 %collective-permute-start.21 = (f32[32,512]{1,0:T(8,128)S(1)}, f32[32,512]{1,0:T(8,128)S(1)}, u32[]{:S(2)}, u32[]{:S(2)}) collective-permute-start(f32[32,512]{1,0:T(8,128)S(1)} %lower.1), channel_id=1, source_target_pairs={{0,2},{1,3},{2,0},{3,1},{4,6},{5,7},{6,4},{7,5},{8,10},{9,11},{10,... | collective-permute-start | bytes 196616 | tf_op jit(solution)/shard_map/ppermute | solution.py:483
  63.3 6.6 %collective-permute-start.20 = (f32[32,512]{1,0:T(8,128)S(1)}, f32[32,512]{1,0:T(8,128)S(1)}, u32[]{:S(2)}, u32[]{:S(2)}) collective-permute-start(f32[32,512]{1,0:T(8,128)S(1)} %lower.1), channel_id=1, source_target_pairs={{0,1},{1,0},{2,3},{3,2},{4,5},{5,4},{6,7},{7,6},{8,9},{9,8},{10,11... | collective-permute-start | bytes 196616 | tf_op jit(solution)/shard_map/ppermute | solution.py:483
  70.0 3.7 %collective-permute-start.26 = (f32[32,896]{1,0:T(8,128)S(1)}, f32[32,896]{1,0:T(8,128)S(1)}, u32[]{:S(2)}, u32[]{:S(2)}) collective-permute-start(f32[32,896]{1,0:T(8,128)S(1)} %pad_maximum_fusion), channel_id=1, source_target_pairs={{0,4},{1,5},{2,6},{3,7},{4,0},{5,1},{6,2},{7,3},{8,12},{9,13},{10,... | collective-permute-start | bytes 344072 | tf_op jit(solution)/shard_map/ppermute | solution.py:483
  70.0 6.1 %collective-permute-start.25 = (f32[1,32,512]{2,1,0:T(8,128)S(1)}, f32[1,32,512]{2,1,0:T(8,128)S(1)}, u32[]{:S(2)}, u32[]{:S(2)}) collective-permute-start(f32[1,32,512]{2,1,0:T(8,128)S(1)} %bitcast.6), channel_id=1, source_target_pairs={{0,24},{1,25},{2,26},{3,27},{4,28},{5,29},{6,30},{7,31},{8,16},{9,... | collective-permute-start | bytes 196616 | tf_op jit(solution)/shard_map/ppermute | solution.py:483
  71.3 5.2 %collective-permute-start.24 = (f32[1,32,512]{2,1,0:T(8,128)S(1)}, f32[1,32,512]{2,1,0:T(8,128)S(1)}, u32[]{:S(2)}, u32[]{:S(2)}) collective-permute-start(f32[1,32,512]{2,1,0:T(8,128)S(1)} %bitcast.7), channel_id=1, source_target_pairs={{0,16},{1,17},{2,18},{3,19},{4,12},{5,13},{6,14},{7,15},{8,24},{9,... | collective-permute-start | bytes 196616 | tf_op jit(solution)/shard_map/ppermute | solution.py:483
  71.9 5.2 %collective-permute-start.23 = (f32[1,32,512]{2,1,0:T(8,128)S(1)}, f32[1,32,512]{2,1,0:T(8,128)S(1)}, u32[]{:S(2)}, u32[]{:S(2)}) collective-permute-start(f32[1,32,512]{2,1,0:T(8,128)S(1)} %bitcast.8), channel_id=1, source_target_pairs={{0,8},{1,9},{2,10},{3,11},{4,20},{5,21},{6,22},{7,23},{8,0},{9,1},... | collective-permute-start | bytes 196616 | tf_op jit(solution)/shard_map/ppermute | solution.py:483
  77.2 1.5 %collective-permute-start.27 = (f32[3,32,512]{2,1,0:T(8,128)S(1)}, f32[3,32,512]{2,1,0:T(8,128)S(1)}, u32[]{:S(2)}, u32[]{:S(2)}) collective-permute-start(f32[3,32,512]{2,1,0:T(8,128)S(1)} %constant_dynamic-update-slice_fusion.v0_ref), channel_id=1, source_target_pairs={{0,4},{1,5},{2,6},{3,7},{4,0},{5,1},{6,2},{7,3},{8,12},{9,13},{10,... | collective-permute-start | bytes 589832 | tf_op jit(solution)/shard_map/ppermute | solution.py:483

commit v6 on v5

--- a/solution.py
+++ b/solution.py
@@ -67,7 +67,7 @@
     return pltpu.with_memory_space_constraint(a, pltpu.VMEM)
 
 
-def call(kernel, name, in_specs, out_specs, out_shape, operands, mib=4, flops=0, nbytes=0, scratch=(), aliases={}):
+def call(kernel, name, in_specs, out_specs, out_shape, operands, mib=4, flops=1, nbytes=1, scratch=(), aliases={}):
     return pl.pallas_call(
         kernel,
         in_specs=in_specs,
@@ -101,24 +101,29 @@
     return pl.ds(pl.multiple_of(block * width, width), width)
 
 
-def write_factor(out, place, own, w_ref, vec_ref, halves):
-    half, rows, width = halves[0].shape
+def part_of_factor(place, own, w_ref, part, places, blocks):
+    _, rows, width = part.shape
     rank = w_ref.shape[1]
     m = place[0] if own else 1 - place[0]
     terms = jnp.zeros((rows, 3 * rank), f32)
-    for p in range(2 * half):
-        w_high, w_middle, w_low = split3(w_ref[m, :, block_columns(place, own, p, 2 * half, width)])
-        high, middle, _ = split3(halves[p % 2][p // 2])
-        for part, pieces in (
+    for i, p in enumerate(places):
+        w_high, w_middle, w_low = split3(w_ref[m, :, block_columns(place, own, p, blocks, width)])
+        high, middle, _ = split3(part[i])
+        for piece, pieces in (
             (high, (w_high, w_middle, w_low)),
             (middle, (w_high, w_middle, jnp.zeros_like(w_low))),
         ):
             terms += lax.dot_general(
-                part, jnp.concatenate(pieces, axis=0), (NT, ((), ())), preferred_element_type=f32
+                piece, jnp.concatenate(pieces, axis=0), (NT, ((), ())), preferred_element_type=f32
             )
-    pack_factor(out, (terms[:, :rank] + terms[:, rank : 2 * rank] + terms[:, 2 * rank :]).T)
+    return (terms[:, :rank] + terms[:, rank : 2 * rank] + terms[:, 2 * rank :]).T
+
+
+def write_factor(out, place, own, factor, vec_ref):
+    rank, rows = factor.shape
+    pack_factor(out, factor)
     base = rank * rows // LANES
-    mine = jnp.where(m == 0, vec_ref[0, 0:1, :], vec_ref[0, 1:2, :])
+    mine = jnp.where((place[0] if own else 1 - place[0]) == 0, vec_ref[0, 0:1, :], vec_ref[0, 1:2, :])
     for i in range(vec_ref.shape[2] // LANES):
         out[base + i : base + i + 1, :] = mine[:, i * LANES : (i + 1) * LANES]
 
@@ -128,67 +133,87 @@
     return jax.ShapeDtypeStruct(((rank * rows + cols) // LANES, LANES), f32)
 
 
-def factor_kernel(place, w_ref, vec_ref, even, odd, out):
-    write_factor(out, place, True, w_ref, vec_ref, (even, odd))
-
-
-def own_factor(place, halves, warm_start, vec_grads):
-    rows = halves[0].shape[1]
+def factor_kernel(place, w_ref, vec_ref, part, before, out, *, places, blocks):
+    factor = before[...] + part_of_factor(place, True, w_ref, part, places, blocks)
+    write_factor(out, place, True, factor, vec_ref)
+
+
+def own_factor(place, part, places, before, warm_start, vec_grads, blocks):
     return call(
-        factor_kernel,
+        functools.partial(factor_kernel, places=places, blocks=blocks),
         "factor",
         [SMEM] + [VMEM] * 4,
         VMEM,
-        factor_shape(rows, warm_start),
-        (place, warm_start, vec_grads, *halves),
-        flops=12 * rows * warm_start.size,
-        nbytes=8 * rows * warm_start.shape[2],
-    )
-
-
-def combine_kernel(place, g_hbm, e_hbm, *refs, own):
-    if own:
-        w_ref, vec_ref, other_even, other_odd, *refs = refs
-        even, odd, factor, g, e, sem = refs
-    else:
-        even, odd, g, e, sem = refs
-    blocks, rows, width = g.shape
+        factor_shape(part.shape[1], warm_start),
+        (place, warm_start, vec_grads, part, before),
+    )
+
+
+def combine_kernel(place, g_hbm, e_hbm, *refs, own, groups, blocks, sides):
+    refs = list(refs)
+    if sides:
+        w_ref, vec_ref = refs.pop(0), refs.pop(0)
+    ins = [[refs.pop(0) for _ in spots] for _, spots, _ in sides]
+    outs = [refs.pop(0) for _ in groups]
+    factors = [refs.pop(0) for _ in sides]
+    g, e, sem = refs
     m = place[0] if own else 1 - place[0]
-    order = [*range(1, blocks, 2), *range(0, blocks, 2)]
-    loads = {}
-    for p in order:
-        where = block_columns(place, own, p, blocks, width)
-        loads[p] = (
-            pltpu.make_async_copy(g_hbm.at[0, m, :, where], g.at[p], sem.at[p, 0]),
-            pltpu.make_async_copy(e_hbm.at[0, m, :, where], e.at[p], sem.at[p, 1]),
+    loads = []
+    for i, p in enumerate(sum(groups, [])):
+        where = block_columns(place, own, p, blocks, g.shape[2])
+        loads.append(
+            (
+                pltpu.make_async_copy(g_hbm.at[0, m, :, where], g.at[i], sem.at[i, 0]),
+                pltpu.make_async_copy(e_hbm.at[0, m, :, where], e.at[i], sem.at[i, 1]),
+            )
         )
-        for load in loads[p]:
+        for load in loads[-1]:
             load.start()
-    if own:
-        write_factor(factor, place, False, w_ref, vec_ref, (other_even, other_odd))
-    for p in order:
-        for load in loads[p]:
-            load.wait()
-        (even, odd)[p % 2][p // 2] = g[p].astype(f32) + e[p]
-
-
-def combine(place, grads, errors, blocks, factor_of=()):
+    for (whose, spots, whole), parts, factor in zip(sides, ins, factors):
+        value = sum(part_of_factor(place, whose, w_ref, part, at, blocks) for part, at in zip(parts, spots))
+        if whole:
+            write_factor(factor, place, whose, value, vec_ref)
+        else:
+            factor[...] = value
+    i = 0
+    for out in outs:
+        for at in range(out.shape[0]):
+            for load in loads[i]:
+                load.wait()
+            out[at] = g[i].astype(f32) + e[i]
+            i += 1
+
+
+def combine(place, grads, errors, own, groups, blocks, sides=(), extra=()):
     rows, cols = grads.shape[2:]
-    own = bool(factor_of)
-    shape = (blocks, rows, cols // blocks)
-    half = pltpu.VMEM((blocks // 2,) + shape[1:], f32)
+    width = cols // blocks
+    shape = (sum(map(len, groups)), rows, width)
+    shapes = [
+        factor_shape(rows, extra[0]) if whole else jax.ShapeDtypeStruct((extra[0].shape[1], rows), f32)
+        for _, _, whole in sides
+    ]
     return call(
-        functools.partial(combine_kernel, own=own),
-        "own" if own else "other",
-        [SMEM, ANY, ANY] + [VMEM] * len(factor_of),
-        [VMEM] * (3 if own else 2),
-        [half, half] + ([factor_shape(rows, factor_of[0])] if own else []),
-        (place, grads, errors, *factor_of),
+        functools.partial(combine_kernel, own=own, groups=groups, blocks=blocks, sides=sides),
+        ("own" if own else "other") + str(len(sides)),
+        [SMEM, ANY, ANY] + [VMEM] * len(extra),
+        [VMEM] * (len(groups) + len(sides)),
+        [pltpu.VMEM((len(group), rows, width), f32) for group in groups] + shapes,
+        (place, grads, errors, *extra),
         mib=8,
-        flops=rows * cols * (200 if own else 1),
-        nbytes=rows * cols * 10,
-        scratch=[pltpu.VMEM(shape, grads.dtype), pltpu.VMEM(shape, f32), pltpu.SemaphoreType.DMA((blocks, 2))],
-    )
+        scratch=[
+            pltpu.VMEM(shape, grads.dtype), pltpu.VMEM(shape, f32), pltpu.SemaphoreType.DMA((shape[0], 2))
+        ],
+    )
+
+
+def parted(blocks):
+    front = [p for p in range(blocks) if p & 3 == 3]
+    return front, [p for p in range(blocks) if p & 3 == 1] + list(range(0, blocks, 2))
+
+
+def within(p, blocks):
+    front, back = parted(blocks)
+    return (0, front.index(p)) if p in front else (1, back.index(p))
 
 
 def fold_kernel(*refs, picks):
@@ -344,7 +369,7 @@
 
 
 def finish_kernel(
-    place, owners, v0_ref, v1_ref, f0_ref, f1_ref, c0_even, c0_odd, c1_even, c1_odd, mm, mw, *refs, positions, head, later
+    place, owners, v0_ref, v1_ref, f0_ref, f1_ref, c0_front, c0_back, c1_front, c1_back, mm, mw, *refs, positions, head, later
 ):
     if later:
         left, refs = refs[0], refs[1 + 3 :]
@@ -352,7 +377,7 @@
     else:
         n_hbm, mo_hbm, wo_hbm, left, errors, approx, moment, weight, sem, bank_sem = refs
     rank, width = v0_ref.shape[1:]
-    blocks, rows = 2 * c0_even.shape[0], c0_even.shape[1]
+    blocks, rows = c0_front.shape[0] + c0_back.shape[0], c0_front.shape[1]
     per = rows // head
     if not later:
         for i, f_ref in enumerate((f0_ref, f1_ref)):
@@ -369,7 +394,8 @@
         m = place[0] if i == 0 else 1 - place[0]
         product = jnp.dot(left[i], right, preferred_element_type=f32)
         approx[k, i] = product
-        errors[k, i] = ((c0_even, c0_odd), (c1_even, c1_odd))[i][p % 2][p // 2] - product
+        part, at = within(p, blocks)
+        errors[k, i] = ((c0_front, c0_back), (c1_front, c1_back))[i][part][at] - product
         columns = block_columns(place, i == 0, p, blocks, width)
         stores.append(pltpu.make_async_copy(errors.at[k, i], n_hbm.at[0, m, :, columns], sem.at[k, i]))
         stores[-1].start()
@@ -511,12 +537,22 @@
     grads, errors = in_hbm(grads), in_hbm(errors)
     mat_momentum, mat_weights = map(in_hbm, (mat_momentum, mat_weights))
 
-    other_c = combine(place, grads, errors, blocks)
-    arrived_odd = in_vmem(exchange(other_c[1], "core"))
-    arrived_even = in_vmem(exchange(other_c[0], "core"))
-    *own_c, other_p = combine(place, grads, errors, blocks, (warm_start, vec_grads, *other_c))
-
-    terms = [[(own_c[p % 2], p // 2), ((arrived_even, arrived_odd)[p % 2], p // 2)] for p in range(blocks)]
+    front, back = parted(blocks)
+    other_front, other_back = combine(place, grads, errors, False, [front, back], blocks)
+    arrived_front = in_vmem(exchange(other_front, "core"))
+    (own_front,) = combine(place, grads, errors, True, [front], blocks)
+    go = fold([[(own_front, i), (arrived_front, i)] for i in range(len(front))])
+    ahead = front, 0, exchange(go, "plane", 0)
+    later, go, leaves = lax.optimization_barrier((place, go, other_back))
+    arrived_back = in_vmem(exchange(leaves, "core"))
+    own_back, other_p, own_part = combine(
+        later, grads, errors, True, [back], blocks, ((False, (front, back), True), (True, (front,), False)),
+        (warm_start, vec_grads, other_front, other_back, own_front),
+    )
+    own_c, other_c = (own_front, own_back), (other_front, other_back)
+
+    arrived_c = arrived_front, arrived_back
+    terms = [[(c[part], at) for c in (own_c, arrived_c)] for part, at in (within(p, blocks) for p in range(blocks))]
 
     def send(goes, stage, after=()):
         return goes, stage, exchange(fold([terms[p] for p in goes], after), "plane", stage)
@@ -526,27 +562,24 @@
         for i, p in enumerate(goes):
             terms[p ^ (1 << stage)].append((arrived, i))
 
-    odd = [p for p in range(blocks) if p & 1]
-    go = fold([terms[p] for p in odd if p & 2])
-    ahead = [p for p in odd if p & 2], 0, exchange(go, "plane", 0)
-
-    rest = [p for p in odd if not p & 2]
-    go_rest = fold([terms[p] for p in rest])
-    pending = [(rest, 0, exchange(go_rest, "plane", 0))]
-
-    later, *_ = lax.optimization_barrier((place, go, go_rest))
-    own_p = own_factor(later, own_c, warm_start, vec_grads)
+    rest = [p for p in range(blocks) if p & 3 == 1]
+    pending = [send(rest, 0)]
+
+    own_p = own_factor(later, own_back, back, own_part, warm_start, vec_grads, blocks)
     packed = own_p + exchange(other_p, "core")
-    packed, mm, mw = hop(packed, "plane", bits - 1, banks, mat_momentum, mat_weights)
-    packed = hop(packed, "z", 0)
     land(*ahead)
-    for stage in range(1, bits):
+    goes = [p for p in range(blocks) if p & 3 == 2]
+    packed, mm, mw, go = hop(
+        packed, "plane", bits - 1,
+        lambda *x: [*banks(*x), fold([terms[p] for p in goes])], mat_momentum, mat_weights,
+    )
+    pending.append((goes, 1, exchange(go, "plane", 1)))
+    for stage in range(2, bits):
+        while pending:
+            land(*pending.pop(0))
         goes = [p for p in range(blocks) if p >> stage & 1 and not p & ((1 << stage) - 1)]
-        if stage > 1:
-            while pending:
-                land(*pending.pop(0))
         pending.append(send(goes, stage, (packed,)))
-    for step in range(1, depths):
+    for step in range(depths):
         packed = hop(packed, "z", step)
     for step in range(bits - 2, 0, -1):
         packed = hop(packed, "plane", step)

time: 82.8 us -> 81.3 us (0.982)
  Pallas kernels: 27.9 us -> 29.6 us
  waiting for transfers between devices: 18.9 us -> 17.2 us
  starting transfers between devices: 34.6 us -> 33.1 us
    ppermute x28, waiting for transfers between devices: 18.9 us -> 17.2 us  [exchange(): return lax.ppermute(a, ('rep', 'grp'), pairs)]
    pallas_call x18 -> x19, Pallas kernels: 27.9 us -> 29.6 us  [call(): pl.pallas_call(kernel, in_specs=in_specs, out_specs=out_specs, out_shape=...]
    ppermute x28, starting transfers between devices: 34.6 us -> 33.1 us  [exchange(): return lax.ppermute(a, ('rep', 'grp'), pairs)]
  transfers between devices with their start and end apart: 28 -> 28, of which waited for: 13 -> 12; matrix products, arithmetic and copies ran while one was open for 0% -> 0% of each run, Pallas kernels for 24% -> 26%
where the time goes in v6:
time: 81.3 us; the launch traced here: 81.1 us
  starting transfers between devices  33.1 us (41%)
  Pallas kernels  29.6 us (36%)
  waiting for transfers between devices  17.2 us (21%)
  between operations  0.96 us (1%)
    ppermute x28, starting transfers between devices, exchange(): return lax.ppermute(a, ('rep', 'grp'), pairs)  33.1 us
    pallas_call x19, Pallas kernels, call(): pl.pallas_call(kernel, in_specs=in_specs, out_specs=out_specs, out_shape=...  29.6 us
    ppermute x28, waiting for transfers between devices, exchange(): return lax.ppermute(a, ('rep', 'grp'), pairs)  17.2 us
  transfers between devices with their start and end apart: 28, of which 12 were waited for; matrix products, arithmetic and copies ran while one was open for 0% of the time, Pallas kernels for 26%

profile of v6, /device:TPU:0, one launch (start us, length us, event | category | flops | bytes accessed | tf_op | source)
XLA Modules:
  0.0 81.1 jit_solution(2620236859090771471)
XLA Ops:
  0.7 0.1 pad_add_fusion.place
  0.7 2.8 %other0.1 = (f32[1,320,512]{2,1,0:T(8,128)S(1)}, f32[3,320,512]{2,1,0:T(8,128)S(1)}) custom-call(s32[3]{0:T(128)S(1)} %pad_add_fusion.place, bf16[1,2,320,2048]{3,2,1,0:T(8,128)(2,1)} %g_hbm.5, f32[1,2,320,2048]{3,2,1,0:T(8,128)} %e_hbm.5), custom_call_target="tpu_custom_call" | custom-call | flops 1 | bytes 1 | tf_op jit(solution)/shard_map/other0/pallas_call | solution.py:71
  3.5 0.0 copy-start
  3.5 0.0 copy-start.1
  3.5 0.5 collective-permute-start
  4.0 1.8 %own0.1.refs_0_.refs_4_.c0_front = f32[1,320,512]{2,1,0:T(8,128)S(1)} custom-call(s32[3]{0:T(128)S(1)} %pad_add_fusion.place, bf16[1,2,320,2048]{3,2,1,0:T(8,128)(2,1)} %g_hbm.5, f32[1,2,320,2048]{3,2,1,0:T(8,128)} %e_hbm.5), custom_call_target="tpu_custom_call" | custom-call | flops 1 | bytes 1 | tf_op jit(solution)/shard_map/own0/pallas_call | solution.py:71
  5.9 0.1 fold.4
  6.0 0.3 collective-permute-start.3
  6.3 2.7 %collective-permute-start.4 = (f32[1,320,512]{2,1,0:T(8,128)S(1)}, f32[1,320,512]{2,1,0:T(8,128)S(1)}, u32[]{:S(2)}, u32[]{:S(2)}) collective-permute-start(f32[1,320,512]{2,1,0:T(8,128)S(1)} %fold.4), channel_id=1, source_target_pairs={{0,8},{1,9},{2,10},{3,11},{4,20},{5,21},{6,22},{7,23},{8,0},{9,1},... | collective-permute-start | bytes 1966088 | tf_op jit(solution)/shard_map/ppermute | solution.py:509
  9.0 3.7 %own2.1 = (f32[3,320,512]{2,1,0:T(8,128)S(1)}, f32[96,128]{1,0:T(8,128)S(1)}, f32[32,320]{1,0:T(8,128)S(1)}) custom-call(s32[3]{0:T(128)S(1)} %pad_add_fusion.place, bf16[1,2,320,2048]{3,2,1,0:T(8,128)(2,1)} %g_hbm.5, f32[1,2,320,2048]{3,2,1,0:T(8,128)} %e_hbm.5, f32[2,32,2048]{2,1,0:T(8,128)S(1)} %copy-done, f32[1,2,2048]{2,1,0:T(2,128)S(1)} %copy-done.1, ...), custom_call_target="tpu_custom_call" | custom-call | flops 1 | bytes 1 | tf_op jit(solution)/shard_map/own2/pallas_call | solution.py:71
  12.7 0.1 collective-permute-start.1
  12.8 1.4 %factor.1 = f32[96,128]{1,0:T(8,128)S(1)} custom-call(s32[3]{0:T(128)S(1)} %pad_add_fusion.place, f32[2,32,2048]{2,1,0:T(8,128)S(1)} %copy-done, f32[1,2,2048]{2,1,0:T(2,128)S(1)} %copy-done.1, f32[3,320,512]{2,1,0:T(8,128)S(1)} %get-tuple-element.83.part.refs_0_.c0_back, f32[32,320]{1,0:T(8,128)S(1)} %get-tuple-element.73.before), custom_call_target="tpu_custom_call" | custom-call | flops 1 | bytes 1 | tf_op jit(solution)/shard_map/factor/pallas_call | solution.py:71
  14.3 0.0 collective-permute-done.1
  14.3 0.1 fold.6
  14.4 1.6 %collective-permute-start.7 = (f32[1,320,512]{2,1,0:T(8,128)S(1)}, f32[1,320,512]{2,1,0:T(8,128)S(1)}, u32[]{:S(2)}, u32[]{:S(2)}) collective-permute-start(f32[1,320,512]{2,1,0:T(8,128)S(1)} %fold.6), channel_id=1, source_target_pairs={{0,8},{1,9},{2,10},{3,11},{4,20},{5,21},{6,22},{7,23},{8,0},{9,1},... | collective-permute-start | bytes 1966088 | tf_op jit(solution)/shard_map/ppermute | solution.py:509
  16.0 0.6 collective-permute-start.2
  16.5 1.6 %banks.1 = (f32[2,64,2048]{2,1,0:T(8,128)S(1)}, f32[2,64,2048]{2,1,0:T(8,128)S(1)}) custom-call(f32[2,64,2048]{2,1,0:T(8,128)} %mm_hbm, f32[2,64,2048]{2,1,0:T(8,128)} %mw_hbm), custom_call_target="tpu_custom_call" | custom-call | flops 1 | bytes 2097152 | tf_op jit(solution)/shard_map/banks/pallas_call | solution.py:71
  18.1 0.1 fold.5
  18.2 2.4 %collective-permute-done.2 = f32[96,128]{1,0:T(8,128)S(1)} collective-permute-done((f32[96,128]{1,0:T(8,128)S(1)}, f32[96,128]{1,0:T(8,128)S(1)}, u32[]{:S(2)}, u32[]{:S(2)}) %collective-permute-start.2) | collective-permute-done | bytes 49184 | tf_op jit(solution)/shard_map/ppermute | solution.py:509
  20.6 0.5 collective-permute-start.9
  21.1 1.6 %collective-permute-start.5 = (f32[96,128]{1,0:T(8,128)S(1)}, f32[96,128]{1,0:T(8,128)S(1)}, u32[]{:S(2)}, u32[]{:S(2)}) collective-permute-start(f32[96,128]{1,0:T(8,128)S(1)} %add.62), channel_id=1, source_target_pairs={{0,1},{1,0},{2,3},{3,2},{4,6},{5,7},{6,4},{7,5},{8,9},{9,8},{10,11... | collective-permute-start | bytes 147464 | tf_op jit(solution)/shard_map/ppermute | solution.py:509
  22.7 2.5 %collective-permute-done.5 = f32[96,128]{1,0:T(8,128)S(1)} collective-permute-done((f32[96,128]{1,0:T(8,128)S(1)}, f32[96,128]{1,0:T(8,128)S(1)}, u32[]{:S(2)}, u32[]{:S(2)}) %collective-permute-start.5) | collective-permute-done | bytes 49184 | tf_op jit(solution)/shard_map/ppermute | solution.py:509
  25.2 2.6 %collective-permute-start.6 = (f32[96,128]{1,0:T(8,128)S(1)}, f32[96,128]{1,0:T(8,128)S(1)}, u32[]{:S(2)}, u32[]{:S(2)}) collective-permute-start(f32[96,128]{1,0:T(8,128)S(1)} %add.63), channel_id=1, source_target_pairs={{0,2},{1,3},{2,0},{3,1},{4,5},{5,4},{6,7},{7,6},{8,10},{9,11},{10,... | collective-permute-start | bytes 147464 | tf_op jit(solution)/shard_map/ppermute | solution.py:509
  27.9 2.4 %collective-permute-done.6 = f32[96,128]{1,0:T(8,128)S(1)} collective-permute-done((f32[96,128]{1,0:T(8,128)S(1)}, f32[96,128]{1,0:T(8,128)S(1)}, u32[]{:S(2)}, u32[]{:S(2)}) %collective-permute-start.6) | collective-permute-done | bytes 49184 | tf_op jit(solution)/shard_map/ppermute | solution.py:509
  30.3 1.6 %collective-permute-start.8 = (f32[96,128]{1,0:T(8,128)S(1)}, f32[96,128]{1,0:T(8,128)S(1)}, u32[]{:S(2)}, u32[]{:S(2)}) collective-permute-start(f32[96,128]{1,0:T(8,128)S(1)} %add.64), channel_id=1, source_target_pairs={{0,8},{1,9},{2,10},{3,11},{4,20},{5,21},{6,22},{7,23},{8,0},{9,1},... | collective-permute-start | bytes 147464 | tf_op jit(solution)/shard_map/ppermute | solution.py:509
  31.9 0.1 fold.7.refs_0_
  32.0 0.0 copy-start.2
  32.1 2.4 %collective-permute-done.8 = f32[96,128]{1,0:T(8,128)S(1)} collective-permute-done((f32[96,128]{1,0:T(8,128)S(1)}, f32[96,128]{1,0:T(8,128)S(1)}, u32[]{:S(2)}, u32[]{:S(2)}) %collective-permute-start.8) | collective-permute-done | bytes 49184 | tf_op jit(solution)/shard_map/ppermute | solution.py:509
  34.5 0.5 project.1
  35.0 4.1 %collective-permute-start.12 = (f32[32,512]{1,0:T(8,128)S(1)}, f32[32,512]{1,0:T(8,128)S(1)}, u32[]{:S(2)}, u32[]{:S(2)}) collective-permute-start(f32[32,512]{1,0:T(8,128)S(1)} %get-tuple-element.90), channel_id=1, source_target_pairs={{0,3},{1,2},{2,1},{3,0},{4,7},{5,6},{6,5},{7,4},{8,11},{9,10},{10,... | collective-permute-start | bytes 196616 | tf_op jit(solution)/shard_map/ppermute | solution.py:509
  39.1 0.6 collective-permute-start.10
  39.7 2.1 %root1a.1.state = f32[3,32,32]{2,1,0:T(8,128)S(1)} custom-call(f32[96,128]{1,0:T(8,128)S(1)} %add.65.x_ref.own_ref), custom_call_target="tpu_custom_call" | custom-call | flops 12000000 | bytes 49152 | tf_op jit(solution)/shard_map/root1a/pallas_call | solution.py:71
  41.8 0.0 collective-permute-done.12
  41.8 2.4 %collective-permute-done.11 = f32[32,512]{1,0:T(8,128)S(1)} collective-permute-done((f32[32,512]{1,0:T(8,128)S(1)}, f32[32,512]{1,0:T(8,128)S(1)}, u32[]{:S(2)}, u32[]{:S(2)}) %collective-permute-start.11) | collective-permute-done | bytes 65568 | tf_op jit(solution)/shard_map/ppermute | solution.py:509
  44.3 0.7 lift.1
  45.0 1.7 %collective-permute-start.15 = (f32[80,128]{1,0:T(8,128)S(1)}, f32[80,128]{1,0:T(8,128)S(1)}, u32[]{:S(2)}, u32[]{:S(2)}) collective-permute-start(f32[80,128]{1,0:T(8,128)S(1)} %lift.1), channel_id=1, source_target_pairs={{0,3},{1,2},{2,1},{3,0},{4,7},{5,6},{6,5},{7,4},{8,11},{9,10},{10,... | collective-permute-start | bytes 122888 | tf_op jit(solution)/shard_map/ppermute | solution.py:509
  46.6 0.5 collective-permute-start.14
  47.1 2.3 %collective-permute-start.13 = (f32[80,128]{1,0:T(8,128)S(1)}, f32[80,128]{1,0:T(8,128)S(1)}, u32[]{:S(2)}, u32[]{:S(2)}) collective-permute-start(f32[80,128]{1,0:T(8,128)S(1)} %lift.1), channel_id=1, source_target_pairs={{0,1},{1,0},{2,3},{3,2},{4,5},{5,4},{6,7},{7,6},{8,9},{9,8},{10,11... | collective-permute-start | bytes 122888 | tf_op jit(solution)/shard_map/ppermute | solution.py:509
  49.4 1.9 %root1b.1.a_ref = f32[32,32]{1,0:T(8,128)S(1)} custom-call(f32[3,32,32]{2,1,0:T(8,128)S(1)} %root1a.1.state), custom_call_target="tpu_custom_call" | custom-call | flops 12000000 | bytes 12288 | tf_op jit(solution)/shard_map/root1b/pallas_call | solution.py:71
  51.3 0.3 collective-permute-done.14
  51.6 0.2 collective-permute-done.13
  51.9 2.2 %collective-permute-start.19 = (f32[80,128]{1,0:T(8,128)S(1)}, f32[80,128]{1,0:T(8,128)S(1)}, u32[]{:S(2)}, u32[]{:S(2)}) collective-permute-start(f32[80,128]{1,0:T(8,128)S(1)} %add_add_fusion.3), channel_id=1, source_target_pairs={{0,24},{1,25},{2,26},{3,27},{4,28},{5,29},{6,30},{7,31},{8,16},{9,... | collective-permute-start | bytes 122888 | tf_op jit(solution)/shard_map/ppermute | solution.py:509
  54.1 0.9 %collective-permute-start.18 = (f32[80,128]{1,0:T(8,128)S(1)}, f32[80,128]{1,0:T(8,128)S(1)}, u32[]{:S(2)}, u32[]{:S(2)}) collective-permute-start(f32[80,128]{1,0:T(8,128)S(1)} %add_add_fusion.3), channel_id=1, source_target_pairs={{0,16},{1,17},{2,18},{3,19},{4,12},{5,13},{6,14},{7,15},{8,24},{9,... | collective-permute-start | bytes 122888 | tf_op jit(solution)/shard_map/ppermute | solution.py:509
  54.9 0.5 collective-permute-start.17
  55.4 1.2 %gains.1 = (f32[2,2048]{1,0:T(2,128)}, f32[2,2048]{1,0:T(2,128)}) custom-call(s32[3]{0:T(128)S(1)} %pad_add_fusion.place, s32[12]{0:T(128)S(1)} %copy-done.4, f32[96,128]{1,0:T(8,128)S(1)} %add.65.x_ref.own_ref, f32[96,128]{1,0:T(8,128)S(1)} %collective-permute-done.16.other_ref, f32[2,2048]{1,0:T(2,128)S(1)} %copy-done.2, f32[2,2048]{1,0:T(2,128)S(1)} %copy-done.3), custom_call_target="tpu_custom_call" | custom-call | flops 40960 | bytes 65536 | tf_op jit(solution)/shard_map/gains/pallas_call | solution.py:71
  56.6 0.3 collective-permute-done.19
  56.9 1.2 %collective-permute-done.18 = f32[80,128]{1,0:T(8,128)S(1)} collective-permute-done((f32[80,128]{1,0:T(8,128)S(1)}, f32[80,128]{1,0:T(8,128)S(1)}, u32[]{:S(2)}, u32[]{:S(2)}) %collective-permute-start.18) | collective-permute-done | bytes 40992 | tf_op jit(solution)/shard_map/ppermute | solution.py:509
  58.1 0.9 %collective-permute-done.17 = f32[80,128]{1,0:T(8,128)S(1)} collective-permute-done((f32[80,128]{1,0:T(8,128)S(1)}, f32[80,128]{1,0:T(8,128)S(1)}, u32[]{:S(2)}, u32[]{:S(2)}) %collective-permute-start.17) | collective-permute-done | bytes 40992 | tf_op jit(solution)/shard_map/ppermute | solution.py:509
  59.0 0.5 lower.1
  59.4 2.4 %collective-permute-start.22 = (f32[32,512]{1,0:T(8,128)S(1)}, f32[32,512]{1,0:T(8,128)S(1)}, u32[]{:S(2)}, u32[]{:S(2)}) collective-permute-start(f32[32,512]{1,0:T(8,128)S(1)} %lower.1), channel_id=1, source_target_pairs={{0,3},{1,2},{2,1},{3,0},{4,7},{5,6},{6,5},{7,4},{8,11},{9,10},{10,... | collective-permute-start | bytes 196616 | tf_op jit(solution)/shard_map/ppermute | solution.py:509
  61.8 0.7 collective-permute-start.21
  62.5 1.3 %collective-permute-start.20 = (f32[32,512]{1,0:T(8,128)S(1)}, f32[32,512]{1,0:T(8,128)S(1)}, u32[]{:S(2)}, u32[]{:S(2)}) collective-permute-start(f32[32,512]{1,0:T(8,128)S(1)} %lower.1), channel_id=1, source_target_pairs={{0,1},{1,0},{2,3},{3,2},{4,5},{5,4},{6,7},{7,6},{8,9},{9,8},{10,11... | collective-permute-start | bytes 196616 | tf_op jit(solution)/shard_map/ppermute | solution.py:509
  63.9 2.4 %root2a.1.state = f32[3,32,32]{2,1,0:T(8,128)S(1)} custom-call(f32[32,32]{1,0:T(8,128)S(1)} %root1b.1.a_ref, f32[80,128]{1,0:T(8,128)S(1)} %add_add_fusion.2.u_ref), custom_call_target="tpu_custom_call" | custom-call | flops 12000000 | bytes 45056 | tf_op jit(solution)/shard_map/root2a/pallas_call | solution.py:71
  66.3 2.3 %root2b.1.f0_ref = f32[32,384]{1,0:T(8,128)S(1)} custom-call(f32[3,32,32]{2,1,0:T(8,128)S(1)} %root2a.1.state, f32[32,32]{1,0:T(8,128)S(1)} %root1b.1.a_ref, f32[80,128]{1,0:T(8,128)S(1)} %add_add_fusion.2.u_ref), custom_call_target="tpu_custom_call" | custom-call | flops 12000000 | bytes 57344 | tf_op jit(solution)/shard_map/root2b/pallas_call | solution.py:71
  68.6 0.0 collective-permute-done.22
  68.7 0.1 collective-permute-start.26
  68.8 1.5 %collective-permute-start.25 = (f32[1,32,512]{2,1,0:T(8,128)S(1)}, f32[1,32,512]{2,1,0:T(8,128)S(1)}, u32[]{:S(2)}, u32[]{:S(2)}) collective-permute-start(f32[1,32,512]{2,1,0:T(8,128)S(1)} %bitcast.6), channel_id=1, source_target_pairs={{0,24},{1,25},{2,26},{3,27},{4,28},{5,29},{6,30},{7,31},{8,16},{9,... | collective-permute-start | bytes 196616 | tf_op jit(solution)/shard_map/ppermute | solution.py:509
  70.3 0.5 collective-permute-start.24
  70.8 1.6 %collective-permute-start.23 = (f32[1,32,512]{2,1,0:T(8,128)S(1)}, f32[1,32,512]{2,1,0:T(8,128)S(1)}, u32[]{:S(2)}, u32[]{:S(2)}) collective-permute-start(f32[1,32,512]{2,1,0:T(8,128)S(1)} %bitcast.8), channel_id=1, source_target_pairs={{0,8},{1,9},{2,10},{3,11},{4,20},{5,21},{6,22},{7,23},{8,0},{9,1},... | collective-permute-start | bytes 196616 | tf_op jit(solution)/shard_map/ppermute | solution.py:509
  72.4 2.4 %finish0.1 = (f32[1,2,320,2048]{3,2,1,0:T(8,128)}, f32[2,64,2048]{2,1,0:T(8,128)}, f32[2,64,2048]{2,1,0:T(8,128)}, bf16[2,320,192]{2,1,0:T(8,128)(2,1)S(1)}) custom-call(s32[3]{0:T(128)S(1)} %pad_add_fusion.place, s32[12]{0:T(128)S(1)} %copy-done.4, f32[1,32,512]{2,1,0:T(8,128)S(1)} %bitcast.9, f32[1,32,512]{2,1,0:T(8,128)S(1)} %slice_bitcast_fusion.v1_ref, ...), custom_call_target="tpu_custom_call" | custom-call | flops 125829120 | bytes 2359296 | tf_op jit(solution)/shard_map/finish0/pallas_call | solution.py:71
  74.8 0.8 collective-permute-done.24
  75.6 0.2 collective-permute-start.27
  75.8 1.3 %collective-permute-done.27.v1_ref = f32[3,32,512]{2,1,0:T(8,128)S(1)} collective-permute-done((f32[3,32,512]{2,1,0:T(8,128)S(1)}, f32[3,32,512]{2,1,0:T(8,128)S(1)}, u32[]{:S(2)}, u32[]{:S(2)}) %collective-permute-start.27) | collective-permute-done | bytes 196640 | tf_op jit(solution)/shard_map/ppermute | solution.py:509
  77.2 3.9 %finish1.1 = (f32[1,2,320,2048]{3,2,1,0:T(8,128)}, f32[2,64,2048]{2,1,0:T(8,128)}, f32[2,64,2048]{2,1,0:T(8,128)}) custom-call(s32[3]{0:T(128)S(1)} %pad_add_fusion.place, s32[12]{0:T(128)S(1)} %copy-done.4, f32[3,32,512]{2,1,0:T(8,128)S(1)} %constant_dynamic-update-slice_fusion.v0_ref, ...), custom_call_target="tpu_custom_call", output_to_operand_aliasing={{0}: (13, {}), {1}: (14, {}), {2}: (15, {})} | custom-call | flops 377487360 | bytes 7077888 | tf_op jit(solution)/shard_map/finish1/pallas_call | solution.py:71
  (37 shorter events, 0.2 us)
Async XLA Ops:
  3.5 5.5 %copy-start = (f32[2,32,2048]{2,1,0:T(8,128)S(1)}, f32[2,32,2048]{2,1,0:T(8,128)}, u32[]{:S(2)}) copy-start(f32[2,32,2048]{2,1,0:T(8,128)} %w_ref.1) | copy-start | bytes 1572868
  3.5 5.5 %copy-start.1 = (f32[1,2,2048]{2,1,0:T(2,128)S(1)}, f32[1,2,2048]{2,1,0:T(2,128)}, u32[]{:S(2)}) copy-start(f32[1,2,2048]{2,1,0:T(2,128)} %vec_ref.1) | copy-start | bytes 49156
  3.5 2.3 %collective-permute-start = (f32[1,320,512]{2,1,0:T(8,128)S(1)}, f32[1,320,512]{2,1,0:T(8,128)S(1)}, u32[]{:S(2)}, u32[]{:S(2)}) collective-permute-start(f32[1,320,512]{2,1,0:T(8,128)S(1)} %get-tuple-element.69.refs_2_.c1_front), channel_id=1, source_target_pairs={{0,4},{1,5},{2,6},{3,7},{4,0},{5,1},{6,2},{7,3},{8,12},{9,13},{10,... | collective-permute-start | bytes 1966088 | tf_op jit(solution)/shard_map/ppermute | solution.py:509
  6.0 8.4 %collective-permute-start.3 = (f32[3,320,512]{2,1,0:T(8,128)S(1)}, f32[3,320,512]{2,1,0:T(8,128)S(1)}, u32[]{:S(2)}, u32[]{:S(2)}) collective-permute-start(f32[3,320,512]{2,1,0:T(8,128)S(1)} %get-tuple-element.80.refs_3_.c1_back), channel_id=1, source_target_pairs={{0,4},{1,5},{2,6},{3,7},{4,0},{5,1},{6,2},{7,3},{8,12},{9,13},{10,... | collective-permute-start | bytes 5898248 | tf_op jit(solution)/shard_map/ppermute | solution.py:509
  6.3 11.8 %collective-permute-start.4 = (f32[1,320,512]{2,1,0:T(8,128)S(1)}, f32[1,320,512]{2,1,0:T(8,128)S(1)}, u32[]{:S(2)}, u32[]{:S(2)}) collective-permute-start(f32[1,320,512]{2,1,0:T(8,128)S(1)} %fold.4), channel_id=1, source_target_pairs={{0,8},{1,9},{2,10},{3,11},{4,20},{5,21},{6,22},{7,23},{8,0},{9,1},... | collective-permute-start | bytes 1966088 | tf_op jit(solution)/shard_map/ppermute | solution.py:509
  12.7 1.5 %collective-permute-start.1 = (f32[96,128]{1,0:T(8,128)S(1)}, f32[96,128]{1,0:T(8,128)S(1)}, u32[]{:S(2)}, u32[]{:S(2)}) collective-permute-start(f32[96,128]{1,0:T(8,128)S(1)} %get-tuple-element.74), channel_id=1, source_target_pairs={{0,4},{1,5},{2,6},{3,7},{4,0},{5,1},{6,2},{7,3},{8,12},{9,13},{10,... | collective-permute-start | bytes 147464 | tf_op jit(solution)/shard_map/ppermute | solution.py:509
  14.4 15.9 %collective-permute-start.7 = (f32[1,320,512]{2,1,0:T(8,128)S(1)}, f32[1,320,512]{2,1,0:T(8,128)S(1)}, u32[]{:S(2)}, u32[]{:S(2)}) collective-permute-start(f32[1,320,512]{2,1,0:T(8,128)S(1)} %fold.6), channel_id=1, source_target_pairs={{0,8},{1,9},{2,10},{3,11},{4,20},{5,21},{6,22},{7,23},{8,0},{9,1},... | collective-permute-start | bytes 1966088 | tf_op jit(solution)/shard_map/ppermute | solution.py:509
  16.0 4.7 %collective-permute-start.2 = (f32[96,128]{1,0:T(8,128)S(1)}, f32[96,128]{1,0:T(8,128)S(1)}, u32[]{:S(2)}, u32[]{:S(2)}) collective-permute-start(f32[96,128]{1,0:T(8,128)S(1)} %add.61), channel_id=1, source_target_pairs={{0,16},{1,17},{2,18},{3,19},{4,12},{5,13},{6,14},{7,15},{8,24},{9,... | collective-permute-start | bytes 147464 | tf_op jit(solution)/shard_map/ppermute | solution.py:509
  20.6 13.8 %collective-permute-start.9 = (f32[1,320,512]{2,1,0:T(8,128)S(1)}, f32[1,320,512]{2,1,0:T(8,128)S(1)}, u32[]{:S(2)}, u32[]{:S(2)}) collective-permute-start(f32[1,320,512]{2,1,0:T(8,128)S(1)} %fold.5), channel_id=1, source_target_pairs={{0,16},{1,17},{2,18},{3,19},{4,12},{5,13},{6,14},{7,15},{8,24},{9,... | collective-permute-start | bytes 1966088 | tf_op jit(solution)/shard_map/ppermute | solution.py:509
  21.1 4.1 %collective-permute-start.5 = (f32[96,128]{1,0:T(8,128)S(1)}, f32[96,128]{1,0:T(8,128)S(1)}, u32[]{:S(2)}, u32[]{:S(2)}) collective-permute-start(f32[96,128]{1,0:T(8,128)S(1)} %add.62), channel_id=1, source_target_pairs={{0,1},{1,0},{2,3},{3,2},{4,6},{5,7},{6,4},{7,5},{8,9},{9,8},{10,11... | collective-permute-start | bytes 147464 | tf_op jit(solution)/shard_map/ppermute | solution.py:509
  25.2 5.0 %collective-permute-start.6 = (f32[96,128]{1,0:T(8,128)S(1)}, f32[96,128]{1,0:T(8,128)S(1)}, u32[]{:S(2)}, u32[]{:S(2)}) collective-permute-start(f32[96,128]{1,0:T(8,128)S(1)} %add.63), channel_id=1, source_target_pairs={{0,2},{1,3},{2,0},{3,1},{4,5},{5,4},{6,7},{7,6},{8,10},{9,11},{10,... | collective-permute-start | bytes 147464 | tf_op jit(solution)/shard_map/ppermute | solution.py:509
  30.3 4.2 %collective-permute-start.8 = (f32[96,128]{1,0:T(8,128)S(1)}, f32[96,128]{1,0:T(8,128)S(1)}, u32[]{:S(2)}, u32[]{:S(2)}) collective-permute-start(f32[96,128]{1,0:T(8,128)S(1)} %add.64), channel_id=1, source_target_pairs={{0,8},{1,9},{2,10},{3,11},{4,20},{5,21},{6,22},{7,23},{8,0},{9,1},... | collective-permute-start | bytes 147464 | tf_op jit(solution)/shard_map/ppermute | solution.py:509
  32.0 23.4 %copy-start.2 = (f32[2,2048]{1,0:T(2,128)S(1)}, f32[2,2048]{1,0:T(2,128)}, u32[]{:S(2)}) copy-start(f32[2,2048]{1,0:T(2,128)} %mv_ref.1) | copy-start | bytes 49156
  32.0 23.4 %copy-start.3 = (f32[2,2048]{1,0:T(2,128)S(1)}, f32[2,2048]{1,0:T(2,128)}, u32[]{:S(2)}) copy-start(f32[2,2048]{1,0:T(2,128)} %wv_ref.1) | copy-start | bytes 49156
  32.0 23.4 %copy-start.4 = (s32[12]{0:T(128)S(1)}, s32[12]{0:T(128)}, u32[]{:S(2)}) copy-start(s32[12]{0:T(128)} %owners.5) | copy-start | bytes 148
  35.0 6.8 %collective-permute-start.12 = (f32[32,512]{1,0:T(8,128)S(1)}, f32[32,512]{1,0:T(8,128)S(1)}, u32[]{:S(2)}, u32[]{:S(2)}) collective-permute-start(f32[32,512]{1,0:T(8,128)S(1)} %get-tuple-element.90), channel_id=1, source_target_pairs={{0,3},{1,2},{2,1},{3,0},{4,7},{5,6},{6,5},{7,4},{8,11},{9,10},{10,... | collective-permute-start | bytes 196616 | tf_op jit(solution)/shard_map/ppermute | solution.py:509
  39.1 5.2 %collective-permute-start.11 = (f32[32,512]{1,0:T(8,128)S(1)}, f32[32,512]{1,0:T(8,128)S(1)}, u32[]{:S(2)}, u32[]{:S(2)}) collective-permute-start(f32[32,512]{1,0:T(8,128)S(1)} %get-tuple-element.90), channel_id=1, source_target_pairs={{0,2},{1,3},{2,0},{3,1},{4,6},{5,7},{6,4},{7,5},{8,10},{9,11},{10,... | collective-permute-start | bytes 196616 | tf_op jit(solution)/shard_map/ppermute | solution.py:509
  39.1 5.2 %collective-permute-start.10 = (f32[32,512]{1,0:T(8,128)S(1)}, f32[32,512]{1,0:T(8,128)S(1)}, u32[]{:S(2)}, u32[]{:S(2)}) collective-permute-start(f32[32,512]{1,0:T(8,128)S(1)} %get-tuple-element.90), channel_id=1, source_target_pairs={{0,1},{1,0},{2,3},{3,2},{4,5},{5,4},{6,7},{7,6},{8,9},{9,8},{10,11... | collective-permute-start | bytes 196616 | tf_op jit(solution)/shard_map/ppermute | solution.py:509
  45.0 6.4 %collective-permute-start.15 = (f32[80,128]{1,0:T(8,128)S(1)}, f32[80,128]{1,0:T(8,128)S(1)}, u32[]{:S(2)}, u32[]{:S(2)}) collective-permute-start(f32[80,128]{1,0:T(8,128)S(1)} %lift.1), channel_id=1, source_target_pairs={{0,3},{1,2},{2,1},{3,0},{4,7},{5,6},{6,5},{7,4},{8,11},{9,10},{10,... | collective-permute-start | bytes 122888 | tf_op jit(solution)/shard_map/ppermute | solution.py:509
  46.6 5.0 %collective-permute-start.14 = (f32[80,128]{1,0:T(8,128)S(1)}, f32[80,128]{1,0:T(8,128)S(1)}, u32[]{:S(2)}, u32[]{:S(2)}) collective-permute-start(f32[80,128]{1,0:T(8,128)S(1)} %lift.1), channel_id=1, source_target_pairs={{0,2},{1,3},{2,0},{3,1},{4,6},{5,7},{6,4},{7,5},{8,10},{9,11},{10,... | collective-permute-start | bytes 122888 | tf_op jit(solution)/shard_map/ppermute | solution.py:509
  47.1 4.7 %collective-permute-start.13 = (f32[80,128]{1,0:T(8,128)S(1)}, f32[80,128]{1,0:T(8,128)S(1)}, u32[]{:S(2)}, u32[]{:S(2)}) collective-permute-start(f32[80,128]{1,0:T(8,128)S(1)} %lift.1), channel_id=1, source_target_pairs={{0,1},{1,0},{2,3},{3,2},{4,5},{5,4},{6,7},{7,6},{8,9},{9,8},{10,11... | collective-permute-start | bytes 122888 | tf_op jit(solution)/shard_map/ppermute | solution.py:509
  49.4 2.4 %collective-permute-start.16 = (f32[96,128]{1,0:T(8,128)S(1)}, f32[96,128]{1,0:T(8,128)S(1)}, u32[]{:S(2)}, u32[]{:S(2)}) collective-permute-start(f32[96,128]{1,0:T(8,128)S(1)} %add.65.x_ref.own_ref), channel_id=1, source_target_pairs={{0,4},{1,5},{2,6},{3,7},{4,0},{5,1},{6,2},{7,3},{8,12},{9,13},{10,... | collective-permute-start | bytes 147464 | tf_op jit(solution)/shard_map/ppermute | solution.py:509
  51.9 5.1 %collective-permute-start.19 = (f32[80,128]{1,0:T(8,128)S(1)}, f32[80,128]{1,0:T(8,128)S(1)}, u32[]{:S(2)}, u32[]{:S(2)}) collective-permute-start(f32[80,128]{1,0:T(8,128)S(1)} %add_add_fusion.3), channel_id=1, source_target_pairs={{0,24},{1,25},{2,26},{3,27},{4,28},{5,29},{6,30},{7,31},{8,16},{9,... | collective-permute-start | bytes 122888 | tf_op jit(solution)/shard_map/ppermute | solution.py:509
  54.1 4.0 %collective-permute-start.18 = (f32[80,128]{1,0:T(8,128)S(1)}, f32[80,128]{1,0:T(8,128)S(1)}, u32[]{:S(2)}, u32[]{:S(2)}) collective-permute-start(f32[80,128]{1,0:T(8,128)S(1)} %add_add_fusion.3), channel_id=1, source_target_pairs={{0,16},{1,17},{2,18},{3,19},{4,12},{5,13},{6,14},{7,15},{8,24},{9,... | collective-permute-start | bytes 122888 | tf_op jit(solution)/shard_map/ppermute | solution.py:509
  54.9 4.0 %collective-permute-start.17 = (f32[80,128]{1,0:T(8,128)S(1)}, f32[80,128]{1,0:T(8,128)S(1)}, u32[]{:S(2)}, u32[]{:S(2)}) collective-permute-start(f32[80,128]{1,0:T(8,128)S(1)} %add_add_fusion.3), channel_id=1, source_target_pairs={{0,8},{1,9},{2,10},{3,11},{4,20},{5,21},{6,22},{7,23},{8,0},{9,1},... | collective-permute-start | bytes 122888 | tf_op jit(solution)/shard_map/ppermute | solution.py:509
  59.4 9.2 %collective-permute-start.22 = (f32[32,512]{1,0:T(8,128)S(1)}, f32[32,512]{1,0:T(8,128)S(1)}, u32[]{:S(2)}, u32[]{:S(2)}) collective-permute-start(f32[32,512]{1,0:T(8,128)S(1)} %lower.1), channel_id=1, source_target_pairs={{0,3},{1,2},{2,1},{3,0},{4,7},{5,6},{6,5},{7,4},{8,11},{9,10},{10,... | collective-permute-start | bytes 196616 | tf_op jit(solution)/shard_map/ppermute | solution.py:509
  61.8 6.8 %collective-permute-start.21 = (f32[32,512]{1,0:T(8,128)S(1)}, f32[32,512]{1,0:T(8,128)S(1)}, u32[]{:S(2)}, u32[]{:S(2)}) collective-permute-start(f32[32,512]{1,0:T(8,128)S(1)} %lower.1), channel_id=1, source_target_pairs={{0,2},{1,3},{2,0},{3,1},{4,6},{5,7},{6,4},{7,5},{8,10},{9,11},{10,... | collective-permute-start | bytes 196616 | tf_op jit(solution)/shard_map/ppermute | solution.py:509
  62.5 6.1 %collective-permute-start.20 = (f32[32,512]{1,0:T(8,128)S(1)}, f32[32,512]{1,0:T(8,128)S(1)}, u32[]{:S(2)}, u32[]{:S(2)}) collective-permute-start(f32[32,512]{1,0:T(8,128)S(1)} %lower.1), channel_id=1, source_target_pairs={{0,1},{1,0},{2,3},{3,2},{4,5},{5,4},{6,7},{7,6},{8,9},{9,8},{10,11... | collective-permute-start | bytes 196616 | tf_op jit(solution)/shard_map/ppermute | solution.py:509
  68.7 3.6 %collective-permute-start.26 = (f32[32,896]{1,0:T(8,128)S(1)}, f32[32,896]{1,0:T(8,128)S(1)}, u32[]{:S(2)}, u32[]{:S(2)}) collective-permute-start(f32[32,896]{1,0:T(8,128)S(1)} %pad_maximum_fusion), channel_id=1, source_target_pairs={{0,4},{1,5},{2,6},{3,7},{4,0},{5,1},{6,2},{7,3},{8,12},{9,13},{10,... | collective-permute-start | bytes 344072 | tf_op jit(solution)/shard_map/ppermute | solution.py:509
  68.8 6.0 %collective-permute-start.25 = (f32[1,32,512]{2,1,0:T(8,128)S(1)}, f32[1,32,512]{2,1,0:T(8,128)S(1)}, u32[]{:S(2)}, u32[]{:S(2)}) collective-permute-start(f32[1,32,512]{2,1,0:T(8,128)S(1)} %bitcast.6), channel_id=1, source_target_pairs={{0,24},{1,25},{2,26},{3,27},{4,28},{5,29},{6,30},{7,31},{8,16},{9,... | collective-permute-start | bytes 196616 | tf_op jit(solution)/shard_map/ppermute | solution.py:509
  70.3 5.3 %collective-permute-start.24 = (f32[1,32,512]{2,1,0:T(8,128)S(1)}, f32[1,32,512]{2,1,0:T(8,128)S(1)}, u32[]{:S(2)}, u32[]{:S(2)}) collective-permute-start(f32[1,32,512]{2,1,0:T(8,128)S(1)} %bitcast.7), channel_id=1, source_target_pairs={{0,16},{1,17},{2,18},{3,19},{4,12},{5,13},{6,14},{7,15},{8,24},{9,... | collective-permute-start | bytes 196616 | tf_op jit(solution)/shard_map/ppermute | solution.py:509
  70.8 4.8 %collective-permute-start.23 = (f32[1,32,512]{2,1,0:T(8,128)S(1)}, f32[1,32,512]{2,1,0:T(8,128)S(1)}, u32[]{:S(2)}, u32[]{:S(2)}) collective-permute-start(f32[1,32,512]{2,1,0:T(8,128)S(1)} %bitcast.8), channel_id=1, source_target_pairs={{0,8},{1,9},{2,10},{3,11},{4,20},{5,21},{6,22},{7,23},{8,0},{9,1},... | collective-permute-start | bytes 196616 | tf_op jit(solution)/shard_map/ppermute | solution.py:509
  75.6 1.5 %collective-permute-start.27 = (f32[3,32,512]{2,1,0:T(8,128)S(1)}, f32[3,32,512]{2,1,0:T(8,128)S(1)}, u32[]{:S(2)}, u32[]{:S(2)}) collective-permute-start(f32[3,32,512]{2,1,0:T(8,128)S(1)} %constant_dynamic-update-slice_fusion.v0_ref), channel_id=1, source_target_pairs={{0,4},{1,5},{2,6},{3,7},{4,0},{5,1},{6,2},{7,3},{8,12},{9,13},{10,... | collective-permute-start | bytes 589832 | tf_op jit(solution)/shard_map/ppermute | solution.py:509

commit v7 on v6

--- a/solution.py
+++ b/solution.py
@@ -498,6 +498,10 @@
     return of
 
 
+def rounds(places):
+    return [1, *range(places - 1, 1, -1)]
+
+
 def exchange(a, kind, step=0):
     groups = lax.axis_size("grp")
     of = partner(kind, step)
@@ -579,8 +583,7 @@
             land(*pending.pop(0))
         goes = [p for p in range(blocks) if p >> stage & 1 and not p & ((1 << stage) - 1)]
         pending.append(send(goes, stage, (packed,)))
-    for step in range(depths):
-        packed = hop(packed, "z", step)
+    packed = packed + sum(exchange(packed, "depth", step) for step in rounds(groups))
     for step in range(bits - 2, 0, -1):
         packed = hop(packed, "plane", step)
     land(*pending.pop(0))
@@ -596,7 +599,7 @@
     )
     square = (rank, rank)
     state = (3, rank, rank)
-    depth = list(range(1, groups))
+    depth = rounds(groups)
     v, first_state = hop(
         v, "depth", depth,
         lambda x: small_call(
@@ -606,7 +609,7 @@
     (u,) = small_call(functools.partial(lift_kernel, count=count), "lift", [(rank * rows // LANES, LANES)], v, kept_sum)
     u, first_root = hop(u, "depth", depth, lambda x: small_call(first_end_kernel, "root1b", [square], x), first_state)
     u, vec_momentum_out, vec_weights_out = hop(
-        u, "place", list(range(1, blocks)),
+        u, "place", rounds(blocks),
         lambda x, y: gains(place, owners, x, y, vec_momentum, vec_weights, count, head_items),
         packed, exchange(packed, "core"),
     )
@@ -623,7 +626,8 @@
     swapped = exchange(jnp.concatenate([v, own_f], axis=1), "core")
     other_v, other_f = swapped[None, :, :width], swapped[:, width:]
     v = v[None]
-    arrived = [exchange(v, "place", p) for p in range(1, blocks)]
+    arrived = {p: exchange(v, "place", p) for p in rounds(blocks)}
+    arrived = [arrived[p] for p in range(1, blocks)]
     *outs, left = finish(
         [0], (), (), place, owners, v, other_v, own_f, other_f, own_c, other_c, shapes, mm, mw
     )

time: 81.3 us -> 80 us (0.984)
  starting transfers between devices: 33.1 us -> 30.1 us
  waiting for transfers between devices: 17.2 us -> 18.9 us
    ppermute x28 -> x29, starting transfers between devices: 33.1 us -> 30.1 us  [exchange(): return lax.ppermute(a, ('rep', 'grp'), pairs)]
    ppermute x28 -> x29, waiting for transfers between devices: 17.2 us -> 18.9 us  [exchange(): return lax.ppermute(a, ('rep', 'grp'), pairs)]
  transfers between devices with their start and end apart: 28 -> 29, of which waited for: 12 -> 12; matrix products, arithmetic and copies ran while one was open for 0% -> 0% of each run, Pallas kernels for 26% -> 27%
where the time goes in v7:
time: 80 us; the launch traced here: 79.8 us
  starting transfers between devices  30.1 us (38%)
  Pallas kernels  29.6 us (37%)
  waiting for transfers between devices  18.9 us (24%)
  between operations  0.95 us (1%)
    ppermute x29, starting transfers between devices, exchange(): return lax.ppermute(a, ('rep', 'grp'), pairs)  30.1 us
    pallas_call x19, Pallas kernels, call(): pl.pallas_call(kernel, in_specs=in_specs, out_specs=out_specs, out_shape=...  29.6 us
    ppermute x29, waiting for transfers between devices, exchange(): return lax.ppermute(a, ('rep', 'grp'), pairs)  18.9 us
  transfers between devices with their start and end apart: 29, of which 12 were waited for; matrix products, arithmetic and copies ran while one was open for 0% of the time, Pallas kernels for 27%

profile of v7, /device:TPU:0, one launch (start us, length us, event | category | flops | bytes accessed | tf_op | source)
XLA Modules:
  0.0 79.8 jit_solution(9876271639944389277)
XLA Ops:
  0.7 0.1 pad_add_fusion.place
  0.7 2.8 %other0.1 = (f32[1,320,512]{2,1,0:T(8,128)S(1)}, f32[3,320,512]{2,1,0:T(8,128)S(1)}) custom-call(s32[3]{0:T(128)S(1)} %pad_add_fusion.place, bf16[1,2,320,2048]{3,2,1,0:T(8,128)(2,1)} %g_hbm.5, f32[1,2,320,2048]{3,2,1,0:T(8,128)} %e_hbm.5), custom_call_target="tpu_custom_call" | custom-call | flops 1 | bytes 1 | tf_op jit(solution)/shard_map/other0/pallas_call | solution.py:71
  3.5 0.5 collective-permute-start
  4.0 1.8 %own0.1.refs_0_.refs_4_.c0_front = f32[1,320,512]{2,1,0:T(8,128)S(1)} custom-call(s32[3]{0:T(128)S(1)} %pad_add_fusion.place, bf16[1,2,320,2048]{3,2,1,0:T(8,128)(2,1)} %g_hbm.5, f32[1,2,320,2048]{3,2,1,0:T(8,128)} %e_hbm.5), custom_call_target="tpu_custom_call" | custom-call | flops 1 | bytes 1 | tf_op jit(solution)/shard_map/own0/pallas_call | solution.py:71
  5.9 0.1 fold.4
  6.0 0.3 collective-permute-start.3
  6.3 2.7 %collective-permute-start.4 = (f32[1,320,512]{2,1,0:T(8,128)S(1)}, f32[1,320,512]{2,1,0:T(8,128)S(1)}, u32[]{:S(2)}, u32[]{:S(2)}) collective-permute-start(f32[1,320,512]{2,1,0:T(8,128)S(1)} %fold.4), channel_id=1, source_target_pairs={{0,8},{1,9},{2,10},{3,11},{4,20},{5,21},{6,22},{7,23},{8,0},{9,1},... | collective-permute-start | bytes 1966088 | tf_op jit(solution)/shard_map/ppermute | solution.py:513
  9.0 3.7 %own2.1 = (f32[3,320,512]{2,1,0:T(8,128)S(1)}, f32[96,128]{1,0:T(8,128)S(1)}, f32[32,320]{1,0:T(8,128)S(1)}) custom-call(s32[3]{0:T(128)S(1)} %pad_add_fusion.place, bf16[1,2,320,2048]{3,2,1,0:T(8,128)(2,1)} %g_hbm.5, f32[1,2,320,2048]{3,2,1,0:T(8,128)} %e_hbm.5, f32[2,32,2048]{2,1,0:T(8,128)S(1)} %copy-done, f32[1,2,2048]{2,1,0:T(2,128)S(1)} %copy-done.1, ...), custom_call_target="tpu_custom_call" | custom-call | flops 1 | bytes 1 | tf_op jit(solution)/shard_map/own2/pallas_call | solution.py:71
  12.7 0.1 collective-permute-start.1
  12.8 1.4 %factor.1 = f32[96,128]{1,0:T(8,128)S(1)} custom-call(s32[3]{0:T(128)S(1)} %pad_add_fusion.place, f32[2,32,2048]{2,1,0:T(8,128)S(1)} %copy-done, f32[1,2,2048]{2,1,0:T(2,128)S(1)} %copy-done.1, f32[3,320,512]{2,1,0:T(8,128)S(1)} %get-tuple-element.83.part.refs_0_.c0_back, f32[32,320]{1,0:T(8,128)S(1)} %get-tuple-element.73.before), custom_call_target="tpu_custom_call" | custom-call | flops 1 | bytes 1 | tf_op jit(solution)/shard_map/factor/pallas_call | solution.py:71
  14.3 0.0 collective-permute-done.1
  14.3 0.1 fold.6
  14.4 1.6 %collective-permute-start.8 = (f32[1,320,512]{2,1,0:T(8,128)S(1)}, f32[1,320,512]{2,1,0:T(8,128)S(1)}, u32[]{:S(2)}, u32[]{:S(2)}) collective-permute-start(f32[1,320,512]{2,1,0:T(8,128)S(1)} %fold.6), channel_id=1, source_target_pairs={{0,8},{1,9},{2,10},{3,11},{4,20},{5,21},{6,22},{7,23},{8,0},{9,1},... | collective-permute-start | bytes 1966088 | tf_op jit(solution)/shard_map/ppermute | solution.py:513
  16.0 0.6 collective-permute-start.2
  16.5 1.6 %banks.1 = (f32[2,64,2048]{2,1,0:T(8,128)S(1)}, f32[2,64,2048]{2,1,0:T(8,128)S(1)}) custom-call(f32[2,64,2048]{2,1,0:T(8,128)} %mm_hbm, f32[2,64,2048]{2,1,0:T(8,128)} %mw_hbm), custom_call_target="tpu_custom_call" | custom-call | flops 1 | bytes 2097152 | tf_op jit(solution)/shard_map/banks/pallas_call | solution.py:71
  18.1 0.1 fold.5
  18.2 2.4 %collective-permute-done.2 = f32[96,128]{1,0:T(8,128)S(1)} collective-permute-done((f32[96,128]{1,0:T(8,128)S(1)}, f32[96,128]{1,0:T(8,128)S(1)}, u32[]{:S(2)}, u32[]{:S(2)}) %collective-permute-start.2) | collective-permute-done | bytes 49184 | tf_op jit(solution)/shard_map/ppermute | solution.py:513
  20.6 0.5 collective-permute-start.10
  21.1 2.6 %collective-permute-start.7 = (f32[96,128]{1,0:T(8,128)S(1)}, f32[96,128]{1,0:T(8,128)S(1)}, u32[]{:S(2)}, u32[]{:S(2)}) collective-permute-start(f32[96,128]{1,0:T(8,128)S(1)} %add.65), channel_id=1, source_target_pairs={{0,2},{1,3},{2,0},{3,1},{4,6},{5,7},{6,4},{7,5},{8,10},{9,11},{10,... | collective-permute-start | bytes 147464 | tf_op jit(solution)/shard_map/ppermute | solution.py:513
  23.7 1.3 %collective-permute-start.6 = (f32[96,128]{1,0:T(8,128)S(1)}, f32[96,128]{1,0:T(8,128)S(1)}, u32[]{:S(2)}, u32[]{:S(2)}) collective-permute-start(f32[96,128]{1,0:T(8,128)S(1)} %add.65), channel_id=1, source_target_pairs={{0,3},{1,2},{2,1},{3,0},{4,7},{5,6},{6,5},{7,4},{8,11},{9,10},{10,... | collective-permute-start | bytes 147464 | tf_op jit(solution)/shard_map/ppermute | solution.py:513
  25.1 0.2 collective-permute-start.5
  25.3 0.8 %collective-permute-done.7 = f32[96,128]{1,0:T(8,128)S(1)} collective-permute-done((f32[96,128]{1,0:T(8,128)S(1)}, f32[96,128]{1,0:T(8,128)S(1)}, u32[]{:S(2)}, u32[]{:S(2)}) %collective-permute-start.7) | collective-permute-done | bytes 49184 | tf_op jit(solution)/shard_map/ppermute | solution.py:513
  26.1 3.6 %collective-permute-done.6 = f32[96,128]{1,0:T(8,128)S(1)} collective-permute-done((f32[96,128]{1,0:T(8,128)S(1)}, f32[96,128]{1,0:T(8,128)S(1)}, u32[]{:S(2)}, u32[]{:S(2)}) %collective-permute-start.6) | collective-permute-done | bytes 49184 | tf_op jit(solution)/shard_map/ppermute | solution.py:513
  29.7 1.6 %collective-permute-start.9 = (f32[96,128]{1,0:T(8,128)S(1)}, f32[96,128]{1,0:T(8,128)S(1)}, u32[]{:S(2)}, u32[]{:S(2)}) collective-permute-start(f32[96,128]{1,0:T(8,128)S(1)} %add_add_fusion.2), channel_id=1, source_target_pairs={{0,8},{1,9},{2,10},{3,11},{4,20},{5,21},{6,22},{7,23},{8,0},{9,1},... | collective-permute-start | bytes 147464 | tf_op jit(solution)/shard_map/ppermute | solution.py:513
  31.3 0.1 fold.7.refs_0_
  31.5 0.0 copy-start.3
  31.5 2.4 %collective-permute-done.9 = f32[96,128]{1,0:T(8,128)S(1)} collective-permute-done((f32[96,128]{1,0:T(8,128)S(1)}, f32[96,128]{1,0:T(8,128)S(1)}, u32[]{:S(2)}, u32[]{:S(2)}) %collective-permute-start.9) | collective-permute-done | bytes 49184 | tf_op jit(solution)/shard_map/ppermute | solution.py:513
  33.9 0.5 project.1
  34.4 2.0 %collective-permute-start.13 = (f32[32,512]{1,0:T(8,128)S(1)}, f32[32,512]{1,0:T(8,128)S(1)}, u32[]{:S(2)}, u32[]{:S(2)}) collective-permute-start(f32[32,512]{1,0:T(8,128)S(1)} %get-tuple-element.90), channel_id=1, source_target_pairs={{0,2},{1,3},{2,0},{3,1},{4,6},{5,7},{6,4},{7,5},{8,10},{9,11},{10,... | collective-permute-start | bytes 196616 | tf_op jit(solution)/shard_map/ppermute | solution.py:513
  36.4 1.3 %collective-permute-start.12 = (f32[32,512]{1,0:T(8,128)S(1)}, f32[32,512]{1,0:T(8,128)S(1)}, u32[]{:S(2)}, u32[]{:S(2)}) collective-permute-start(f32[32,512]{1,0:T(8,128)S(1)} %get-tuple-element.90), channel_id=1, source_target_pairs={{0,3},{1,2},{2,1},{3,0},{4,7},{5,6},{6,5},{7,4},{8,11},{9,10},{10,... | collective-permute-start | bytes 196616 | tf_op jit(solution)/shard_map/ppermute | solution.py:513
  37.7 0.2 collective-permute-start.11
  38.0 2.1 %root1a.1.state = f32[3,32,32]{2,1,0:T(8,128)S(1)} custom-call(f32[96,128]{1,0:T(8,128)S(1)} %add.69.x_ref.own_ref), custom_call_target="tpu_custom_call" | custom-call | flops 12000000 | bytes 49152 | tf_op jit(solution)/shard_map/root1a/pallas_call | solution.py:71
  40.1 1.3 %collective-permute-done.13 = f32[32,512]{1,0:T(8,128)S(1)} collective-permute-done((f32[32,512]{1,0:T(8,128)S(1)}, f32[32,512]{1,0:T(8,128)S(1)}, u32[]{:S(2)}, u32[]{:S(2)}) %collective-permute-start.13) | collective-permute-done | bytes 65568 | tf_op jit(solution)/shard_map/ppermute | solution.py:513
  41.4 1.2 %collective-permute-done.12 = f32[32,512]{1,0:T(8,128)S(1)} collective-permute-done((f32[32,512]{1,0:T(8,128)S(1)}, f32[32,512]{1,0:T(8,128)S(1)}, u32[]{:S(2)}, u32[]{:S(2)}) %collective-permute-start.12) | collective-permute-done | bytes 65568 | tf_op jit(solution)/shard_map/ppermute | solution.py:513
  42.6 0.1 collective-permute-done.11
  42.8 0.7 lift.1
  43.5 2.4 %collective-permute-start.16 = (f32[80,128]{1,0:T(8,128)S(1)}, f32[80,128]{1,0:T(8,128)S(1)}, u32[]{:S(2)}, u32[]{:S(2)}) collective-permute-start(f32[80,128]{1,0:T(8,128)S(1)} %lift.1), channel_id=1, source_target_pairs={{0,2},{1,3},{2,0},{3,1},{4,6},{5,7},{6,4},{7,5},{8,10},{9,11},{10,... | collective-permute-start | bytes 122888 | tf_op jit(solution)/shard_map/ppermute | solution.py:513
  45.8 1.0 %collective-permute-start.15 = (f32[80,128]{1,0:T(8,128)S(1)}, f32[80,128]{1,0:T(8,128)S(1)}, u32[]{:S(2)}, u32[]{:S(2)}) collective-permute-start(f32[80,128]{1,0:T(8,128)S(1)} %lift.1), channel_id=1, source_target_pairs={{0,3},{1,2},{2,1},{3,0},{4,7},{5,6},{6,5},{7,4},{8,11},{9,10},{10,... | collective-permute-start | bytes 122888 | tf_op jit(solution)/shard_map/ppermute | solution.py:513
  46.9 0.2 collective-permute-start.14
  47.0 1.9 %root1b.1.a_ref = f32[32,32]{1,0:T(8,128)S(1)} custom-call(f32[3,32,32]{2,1,0:T(8,128)S(1)} %root1a.1.state), custom_call_target="tpu_custom_call" | custom-call | flops 12000000 | bytes 12288 | tf_op jit(solution)/shard_map/root1b/pallas_call | solution.py:71
  48.9 2.7 %collective-permute-done.15 = f32[80,128]{1,0:T(8,128)S(1)} collective-permute-done((f32[80,128]{1,0:T(8,128)S(1)}, f32[80,128]{1,0:T(8,128)S(1)}, u32[]{:S(2)}, u32[]{:S(2)}) %collective-permute-start.15) | collective-permute-done | bytes 40992 | tf_op jit(solution)/shard_map/ppermute | solution.py:513
  51.7 1.6 %collective-permute-start.20 = (f32[80,128]{1,0:T(8,128)S(1)}, f32[80,128]{1,0:T(8,128)S(1)}, u32[]{:S(2)}, u32[]{:S(2)}) collective-permute-start(f32[80,128]{1,0:T(8,128)S(1)} %add_add_fusion.4), channel_id=1, source_target_pairs={{0,16},{1,17},{2,18},{3,19},{4,12},{5,13},{6,14},{7,15},{8,24},{9,... | collective-permute-start | bytes 122888 | tf_op jit(solution)/shard_map/ppermute | solution.py:513
  53.2 1.3 %collective-permute-start.19 = (f32[80,128]{1,0:T(8,128)S(1)}, f32[80,128]{1,0:T(8,128)S(1)}, u32[]{:S(2)}, u32[]{:S(2)}) collective-permute-start(f32[80,128]{1,0:T(8,128)S(1)} %add_add_fusion.4), channel_id=1, source_target_pairs={{0,24},{1,25},{2,26},{3,27},{4,28},{5,29},{6,30},{7,31},{8,16},{9,... | collective-permute-start | bytes 122888 | tf_op jit(solution)/shard_map/ppermute | solution.py:513
  54.5 0.7 collective-permute-start.18
  55.2 1.2 %gains.1 = (f32[2,2048]{1,0:T(2,128)}, f32[2,2048]{1,0:T(2,128)}) custom-call(s32[3]{0:T(128)S(1)} %pad_add_fusion.place, s32[12]{0:T(128)S(1)} %copy-done.4, f32[96,128]{1,0:T(8,128)S(1)} %add.69.x_ref.own_ref, f32[96,128]{1,0:T(8,128)S(1)} %collective-permute-done.17.other_ref, f32[2,2048]{1,0:T(2,128)S(1)} %copy-done.2, f32[2,2048]{1,0:T(2,128)S(1)} %copy-done.3), custom_call_target="tpu_custom_call" | custom-call | flops 40960 | bytes 65536 | tf_op jit(solution)/shard_map/gains/pallas_call | solution.py:71
  56.4 1.7 %collective-permute-done.19 = f32[80,128]{1,0:T(8,128)S(1)} collective-permute-done((f32[80,128]{1,0:T(8,128)S(1)}, f32[80,128]{1,0:T(8,128)S(1)}, u32[]{:S(2)}, u32[]{:S(2)}) %collective-permute-start.19) | collective-permute-done | bytes 40992 | tf_op jit(solution)/shard_map/ppermute | solution.py:513
  58.1 0.4 collective-permute-done.18
  58.6 0.5 lower.1
  59.0 1.0 %collective-permute-start.23 = (f32[32,512]{1,0:T(8,128)S(1)}, f32[32,512]{1,0:T(8,128)S(1)}, u32[]{:S(2)}, u32[]{:S(2)}) collective-permute-start(f32[32,512]{1,0:T(8,128)S(1)} %lower.1), channel_id=1, source_target_pairs={{0,2},{1,3},{2,0},{3,1},{4,6},{5,7},{6,4},{7,5},{8,10},{9,11},{10,... | collective-permute-start | bytes 196616 | tf_op jit(solution)/shard_map/ppermute | solution.py:513
  60.1 1.4 %collective-permute-start.22 = (f32[32,512]{1,0:T(8,128)S(1)}, f32[32,512]{1,0:T(8,128)S(1)}, u32[]{:S(2)}, u32[]{:S(2)}) collective-permute-start(f32[32,512]{1,0:T(8,128)S(1)} %lower.1), channel_id=1, source_target_pairs={{0,3},{1,2},{2,1},{3,0},{4,7},{5,6},{6,5},{7,4},{8,11},{9,10},{10,... | collective-permute-start | bytes 196616 | tf_op jit(solution)/shard_map/ppermute | solution.py:513
  61.5 1.1 %collective-permute-start.21 = (f32[32,512]{1,0:T(8,128)S(1)}, f32[32,512]{1,0:T(8,128)S(1)}, u32[]{:S(2)}, u32[]{:S(2)}) collective-permute-start(f32[32,512]{1,0:T(8,128)S(1)} %lower.1), channel_id=1, source_target_pairs={{0,1},{1,0},{2,3},{3,2},{4,5},{5,4},{6,7},{7,6},{8,9},{9,8},{10,11... | collective-permute-start | bytes 196616 | tf_op jit(solution)/shard_map/ppermute | solution.py:513
  62.6 2.4 %root2a.1.state = f32[3,32,32]{2,1,0:T(8,128)S(1)} custom-call(f32[32,32]{1,0:T(8,128)S(1)} %root1b.1.a_ref, f32[80,128]{1,0:T(8,128)S(1)} %add_add_fusion.3.u_ref), custom_call_target="tpu_custom_call" | custom-call | flops 12000000 | bytes 45056 | tf_op jit(solution)/shard_map/root2a/pallas_call | solution.py:71
  65.0 2.3 %root2b.1.f0_ref = f32[32,384]{1,0:T(8,128)S(1)} custom-call(f32[3,32,32]{2,1,0:T(8,128)S(1)} %root2a.1.state, f32[32,32]{1,0:T(8,128)S(1)} %root1b.1.a_ref, f32[80,128]{1,0:T(8,128)S(1)} %add_add_fusion.3.u_ref), custom_call_target="tpu_custom_call" | custom-call | flops 12000000 | bytes 57344 | tf_op jit(solution)/shard_map/root2b/pallas_call | solution.py:71
  67.3 0.0 collective-permute-done.23
  67.4 0.1 collective-permute-start.27
  67.5 1.7 %collective-permute-start.26 = (f32[1,32,512]{2,1,0:T(8,128)S(1)}, f32[1,32,512]{2,1,0:T(8,128)S(1)}, u32[]{:S(2)}, u32[]{:S(2)}) collective-permute-start(f32[1,32,512]{2,1,0:T(8,128)S(1)} %bitcast.6), channel_id=1, source_target_pairs={{0,24},{1,25},{2,26},{3,27},{4,28},{5,29},{6,30},{7,31},{8,16},{9,... | collective-permute-start | bytes 196616 | tf_op jit(solution)/shard_map/ppermute | solution.py:513
  69.2 0.8 collective-permute-start.25
  70.0 1.1 %collective-permute-start.24 = (f32[1,32,512]{2,1,0:T(8,128)S(1)}, f32[1,32,512]{2,1,0:T(8,128)S(1)}, u32[]{:S(2)}, u32[]{:S(2)}) collective-permute-start(f32[1,32,512]{2,1,0:T(8,128)S(1)} %bitcast.8), channel_id=1, source_target_pairs={{0,8},{1,9},{2,10},{3,11},{4,20},{5,21},{6,22},{7,23},{8,0},{9,1},... | collective-permute-start | bytes 196616 | tf_op jit(solution)/shard_map/ppermute | solution.py:513
  71.1 2.4 %finish0.1 = (f32[1,2,320,2048]{3,2,1,0:T(8,128)}, f32[2,64,2048]{2,1,0:T(8,128)}, f32[2,64,2048]{2,1,0:T(8,128)}, bf16[2,320,192]{2,1,0:T(8,128)(2,1)S(1)}) custom-call(s32[3]{0:T(128)S(1)} %pad_add_fusion.place, s32[12]{0:T(128)S(1)} %copy-done.4, f32[1,32,512]{2,1,0:T(8,128)S(1)} %bitcast.9, f32[1,32,512]{2,1,0:T(8,128)S(1)} %slice_bitcast_fusion.v1_ref, ...), custom_call_target="tpu_custom_call" | custom-call | flops 125829120 | bytes 2359296 | tf_op jit(solution)/shard_map/finish0/pallas_call | solution.py:71
  73.5 0.8 collective-permute-done.25
  74.3 0.0 collective-permute-done.24
  74.4 0.2 collective-permute-start.28
  74.6 1.3 %collective-permute-done.28.v1_ref = f32[3,32,512]{2,1,0:T(8,128)S(1)} collective-permute-done((f32[3,32,512]{2,1,0:T(8,128)S(1)}, f32[3,32,512]{2,1,0:T(8,128)S(1)}, u32[]{:S(2)}, u32[]{:S(2)}) %collective-permute-start.28) | collective-permute-done | bytes 196640 | tf_op jit(solution)/shard_map/ppermute | solution.py:513
  75.9 3.9 %finish1.1 = (f32[1,2,320,2048]{3,2,1,0:T(8,128)}, f32[2,64,2048]{2,1,0:T(8,128)}, f32[2,64,2048]{2,1,0:T(8,128)}) custom-call(s32[3]{0:T(128)S(1)} %pad_add_fusion.place, s32[12]{0:T(128)S(1)} %copy-done.4, f32[3,32,512]{2,1,0:T(8,128)S(1)} %constant_dynamic-update-slice_fusion.v0_ref, ...), custom_call_target="tpu_custom_call", output_to_operand_aliasing={{0}: (13, {}), {1}: (14, {}), {2}: (15, {})} | custom-call | flops 377487360 | bytes 7077888 | tf_op jit(solution)/shard_map/finish1/pallas_call | solution.py:71
  (38 shorter events, 0.2 us)
Async XLA Ops:
  3.5 5.5 %copy-start = (f32[2,32,2048]{2,1,0:T(8,128)S(1)}, f32[2,32,2048]{2,1,0:T(8,128)}, u32[]{:S(2)}) copy-start(f32[2,32,2048]{2,1,0:T(8,128)} %w_ref.1) | copy-start | bytes 1572868
  3.5 5.5 %copy-start.1 = (f32[1,2,2048]{2,1,0:T(2,128)S(1)}, f32[1,2,2048]{2,1,0:T(2,128)}, u32[]{:S(2)}) copy-start(f32[1,2,2048]{2,1,0:T(2,128)} %vec_ref.1) | copy-start | bytes 49156
  3.5 2.3 %collective-permute-start = (f32[1,320,512]{2,1,0:T(8,128)S(1)}, f32[1,320,512]{2,1,0:T(8,128)S(1)}, u32[]{:S(2)}, u32[]{:S(2)}) collective-permute-start(f32[1,320,512]{2,1,0:T(8,128)S(1)} %get-tuple-element.69.refs_2_.c1_front), channel_id=1, source_target_pairs={{0,4},{1,5},{2,6},{3,7},{4,0},{5,1},{6,2},{7,3},{8,12},{9,13},{10,... | collective-permute-start | bytes 1966088 | tf_op jit(solution)/shard_map/ppermute | solution.py:513
  6.0 8.4 %collective-permute-start.3 = (f32[3,320,512]{2,1,0:T(8,128)S(1)}, f32[3,320,512]{2,1,0:T(8,128)S(1)}, u32[]{:S(2)}, u32[]{:S(2)}) collective-permute-start(f32[3,320,512]{2,1,0:T(8,128)S(1)} %get-tuple-element.80.refs_3_.c1_back), channel_id=1, source_target_pairs={{0,4},{1,5},{2,6},{3,7},{4,0},{5,1},{6,2},{7,3},{8,12},{9,13},{10,... | collective-permute-start | bytes 5898248 | tf_op jit(solution)/shard_map/ppermute | solution.py:513
  6.3 11.8 %collective-permute-start.4 = (f32[1,320,512]{2,1,0:T(8,128)S(1)}, f32[1,320,512]{2,1,0:T(8,128)S(1)}, u32[]{:S(2)}, u32[]{:S(2)}) collective-permute-start(f32[1,320,512]{2,1,0:T(8,128)S(1)} %fold.4), channel_id=1, source_target_pairs={{0,8},{1,9},{2,10},{3,11},{4,20},{5,21},{6,22},{7,23},{8,0},{9,1},... | collective-permute-start | bytes 1966088 | tf_op jit(solution)/shard_map/ppermute | solution.py:513
  12.7 1.5 %collective-permute-start.1 = (f32[96,128]{1,0:T(8,128)S(1)}, f32[96,128]{1,0:T(8,128)S(1)}, u32[]{:S(2)}, u32[]{:S(2)}) collective-permute-start(f32[96,128]{1,0:T(8,128)S(1)} %get-tuple-element.74), channel_id=1, source_target_pairs={{0,4},{1,5},{2,6},{3,7},{4,0},{5,1},{6,2},{7,3},{8,12},{9,13},{10,... | collective-permute-start | bytes 147464 | tf_op jit(solution)/shard_map/ppermute | solution.py:513
  14.4 15.3 %collective-permute-start.8 = (f32[1,320,512]{2,1,0:T(8,128)S(1)}, f32[1,320,512]{2,1,0:T(8,128)S(1)}, u32[]{:S(2)}, u32[]{:S(2)}) collective-permute-start(f32[1,320,512]{2,1,0:T(8,128)S(1)} %fold.6), channel_id=1, source_target_pairs={{0,8},{1,9},{2,10},{3,11},{4,20},{5,21},{6,22},{7,23},{8,0},{9,1},... | collective-permute-start | bytes 1966088 | tf_op jit(solution)/shard_map/ppermute | solution.py:513
  16.0 4.7 %collective-permute-start.2 = (f32[96,128]{1,0:T(8,128)S(1)}, f32[96,128]{1,0:T(8,128)S(1)}, u32[]{:S(2)}, u32[]{:S(2)}) collective-permute-start(f32[96,128]{1,0:T(8,128)S(1)} %add.64), channel_id=1, source_target_pairs={{0,16},{1,17},{2,18},{3,19},{4,12},{5,13},{6,14},{7,15},{8,24},{9,... | collective-permute-start | bytes 147464 | tf_op jit(solution)/shard_map/ppermute | solution.py:513
  20.6 13.3 %collective-permute-start.10 = (f32[1,320,512]{2,1,0:T(8,128)S(1)}, f32[1,320,512]{2,1,0:T(8,128)S(1)}, u32[]{:S(2)}, u32[]{:S(2)}) collective-permute-start(f32[1,320,512]{2,1,0:T(8,128)S(1)} %fold.5), channel_id=1, source_target_pairs={{0,16},{1,17},{2,18},{3,19},{4,12},{5,13},{6,14},{7,15},{8,24},{9,... | collective-permute-start | bytes 1966088 | tf_op jit(solution)/shard_map/ppermute | solution.py:513
  21.1 5.0 %collective-permute-start.7 = (f32[96,128]{1,0:T(8,128)S(1)}, f32[96,128]{1,0:T(8,128)S(1)}, u32[]{:S(2)}, u32[]{:S(2)}) collective-permute-start(f32[96,128]{1,0:T(8,128)S(1)} %add.65), channel_id=1, source_target_pairs={{0,2},{1,3},{2,0},{3,1},{4,6},{5,7},{6,4},{7,5},{8,10},{9,11},{10,... | collective-permute-start | bytes 147464 | tf_op jit(solution)/shard_map/ppermute | solution.py:513
  23.7 6.0 %collective-permute-start.6 = (f32[96,128]{1,0:T(8,128)S(1)}, f32[96,128]{1,0:T(8,128)S(1)}, u32[]{:S(2)}, u32[]{:S(2)}) collective-permute-start(f32[96,128]{1,0:T(8,128)S(1)} %add.65), channel_id=1, source_target_pairs={{0,3},{1,2},{2,1},{3,0},{4,7},{5,6},{6,5},{7,4},{8,11},{9,10},{10,... | collective-permute-start | bytes 147464 | tf_op jit(solution)/shard_map/ppermute | solution.py:513
  25.1 4.6 %collective-permute-start.5 = (f32[96,128]{1,0:T(8,128)S(1)}, f32[96,128]{1,0:T(8,128)S(1)}, u32[]{:S(2)}, u32[]{:S(2)}) collective-permute-start(f32[96,128]{1,0:T(8,128)S(1)} %add.65), channel_id=1, source_target_pairs={{0,1},{1,0},{2,3},{3,2},{4,5},{5,4},{6,7},{7,6},{8,9},{9,8},{10,11... | collective-permute-start | bytes 147464 | tf_op jit(solution)/shard_map/ppermute | solution.py:513
  29.7 4.2 %collective-permute-start.9 = (f32[96,128]{1,0:T(8,128)S(1)}, f32[96,128]{1,0:T(8,128)S(1)}, u32[]{:S(2)}, u32[]{:S(2)}) collective-permute-start(f32[96,128]{1,0:T(8,128)S(1)} %add_add_fusion.2), channel_id=1, source_target_pairs={{0,8},{1,9},{2,10},{3,11},{4,20},{5,21},{6,22},{7,23},{8,0},{9,1},... | collective-permute-start | bytes 147464 | tf_op jit(solution)/shard_map/ppermute | solution.py:513
  31.4 23.8 %copy-start.2 = (f32[2,2048]{1,0:T(2,128)S(1)}, f32[2,2048]{1,0:T(2,128)}, u32[]{:S(2)}) copy-start(f32[2,2048]{1,0:T(2,128)} %mv_ref.1) | copy-start | bytes 49156
  31.5 23.8 %copy-start.3 = (f32[2,2048]{1,0:T(2,128)S(1)}, f32[2,2048]{1,0:T(2,128)}, u32[]{:S(2)}) copy-start(f32[2,2048]{1,0:T(2,128)} %wv_ref.1) | copy-start | bytes 49156
  31.5 23.8 %copy-start.4 = (s32[12]{0:T(128)S(1)}, s32[12]{0:T(128)}, u32[]{:S(2)}) copy-start(s32[12]{0:T(128)} %owners.5) | copy-start | bytes 148
  34.4 7.0 %collective-permute-start.13 = (f32[32,512]{1,0:T(8,128)S(1)}, f32[32,512]{1,0:T(8,128)S(1)}, u32[]{:S(2)}, u32[]{:S(2)}) collective-permute-start(f32[32,512]{1,0:T(8,128)S(1)} %get-tuple-element.90), channel_id=1, source_target_pairs={{0,2},{1,3},{2,0},{3,1},{4,6},{5,7},{6,4},{7,5},{8,10},{9,11},{10,... | collective-permute-start | bytes 196616 | tf_op jit(solution)/shard_map/ppermute | solution.py:513
  36.4 6.2 %collective-permute-start.12 = (f32[32,512]{1,0:T(8,128)S(1)}, f32[32,512]{1,0:T(8,128)S(1)}, u32[]{:S(2)}, u32[]{:S(2)}) collective-permute-start(f32[32,512]{1,0:T(8,128)S(1)} %get-tuple-element.90), channel_id=1, source_target_pairs={{0,3},{1,2},{2,1},{3,0},{4,7},{5,6},{6,5},{7,4},{8,11},{9,10},{10,... | collective-permute-start | bytes 196616 | tf_op jit(solution)/shard_map/ppermute | solution.py:513
  37.7 5.0 %collective-permute-start.11 = (f32[32,512]{1,0:T(8,128)S(1)}, f32[32,512]{1,0:T(8,128)S(1)}, u32[]{:S(2)}, u32[]{:S(2)}) collective-permute-start(f32[32,512]{1,0:T(8,128)S(1)} %get-tuple-element.90), channel_id=1, source_target_pairs={{0,1},{1,0},{2,3},{3,2},{4,5},{5,4},{6,7},{7,6},{8,9},{9,8},{10,11... | collective-permute-start | bytes 196616 | tf_op jit(solution)/shard_map/ppermute | solution.py:513
  43.5 5.5 %collective-permute-start.16 = (f32[80,128]{1,0:T(8,128)S(1)}, f32[80,128]{1,0:T(8,128)S(1)}, u32[]{:S(2)}, u32[]{:S(2)}) collective-permute-start(f32[80,128]{1,0:T(8,128)S(1)} %lift.1), channel_id=1, source_target_pairs={{0,2},{1,3},{2,0},{3,1},{4,6},{5,7},{6,4},{7,5},{8,10},{9,11},{10,... | collective-permute-start | bytes 122888 | tf_op jit(solution)/shard_map/ppermute | solution.py:513
  45.8 5.8 %collective-permute-start.15 = (f32[80,128]{1,0:T(8,128)S(1)}, f32[80,128]{1,0:T(8,128)S(1)}, u32[]{:S(2)}, u32[]{:S(2)}) collective-permute-start(f32[80,128]{1,0:T(8,128)S(1)} %lift.1), channel_id=1, source_target_pairs={{0,3},{1,2},{2,1},{3,0},{4,7},{5,6},{6,5},{7,4},{8,11},{9,10},{10,... | collective-permute-start | bytes 122888 | tf_op jit(solution)/shard_map/ppermute | solution.py:513
  46.9 4.8 %collective-permute-start.14 = (f32[80,128]{1,0:T(8,128)S(1)}, f32[80,128]{1,0:T(8,128)S(1)}, u32[]{:S(2)}, u32[]{:S(2)}) collective-permute-start(f32[80,128]{1,0:T(8,128)S(1)} %lift.1), channel_id=1, source_target_pairs={{0,1},{1,0},{2,3},{3,2},{4,5},{5,4},{6,7},{7,6},{8,9},{9,8},{10,11... | collective-permute-start | bytes 122888 | tf_op jit(solution)/shard_map/ppermute | solution.py:513
  47.0 4.6 %collective-permute-start.17 = (f32[96,128]{1,0:T(8,128)S(1)}, f32[96,128]{1,0:T(8,128)S(1)}, u32[]{:S(2)}, u32[]{:S(2)}) collective-permute-start(f32[96,128]{1,0:T(8,128)S(1)} %add.69.x_ref.own_ref), channel_id=1, source_target_pairs={{0,4},{1,5},{2,6},{3,7},{4,0},{5,1},{6,2},{7,3},{8,12},{9,13},{10,... | collective-permute-start | bytes 147464 | tf_op jit(solution)/shard_map/ppermute | solution.py:513
  51.7 4.8 %collective-permute-start.20 = (f32[80,128]{1,0:T(8,128)S(1)}, f32[80,128]{1,0:T(8,128)S(1)}, u32[]{:S(2)}, u32[]{:S(2)}) collective-permute-start(f32[80,128]{1,0:T(8,128)S(1)} %add_add_fusion.4), channel_id=1, source_target_pairs={{0,16},{1,17},{2,18},{3,19},{4,12},{5,13},{6,14},{7,15},{8,24},{9,... | collective-permute-start | bytes 122888 | tf_op jit(solution)/shard_map/ppermute | solution.py:513
  53.2 4.9 %collective-permute-start.19 = (f32[80,128]{1,0:T(8,128)S(1)}, f32[80,128]{1,0:T(8,128)S(1)}, u32[]{:S(2)}, u32[]{:S(2)}) collective-permute-start(f32[80,128]{1,0:T(8,128)S(1)} %add_add_fusion.4), channel_id=1, source_target_pairs={{0,24},{1,25},{2,26},{3,27},{4,28},{5,29},{6,30},{7,31},{8,16},{9,... | collective-permute-start | bytes 122888 | tf_op jit(solution)/shard_map/ppermute | solution.py:513
  54.5 4.0 %collective-permute-start.18 = (f32[80,128]{1,0:T(8,128)S(1)}, f32[80,128]{1,0:T(8,128)S(1)}, u32[]{:S(2)}, u32[]{:S(2)}) collective-permute-start(f32[80,128]{1,0:T(8,128)S(1)} %add_add_fusion.4), channel_id=1, source_target_pairs={{0,8},{1,9},{2,10},{3,11},{4,20},{5,21},{6,22},{7,23},{8,0},{9,1},... | collective-permute-start | bytes 122888 | tf_op jit(solution)/shard_map/ppermute | solution.py:513
  59.0 8.3 %collective-permute-start.23 = (f32[32,512]{1,0:T(8,128)S(1)}, f32[32,512]{1,0:T(8,128)S(1)}, u32[]{:S(2)}, u32[]{:S(2)}) collective-permute-start(f32[32,512]{1,0:T(8,128)S(1)} %lower.1), channel_id=1, source_target_pairs={{0,2},{1,3},{2,0},{3,1},{4,6},{5,7},{6,4},{7,5},{8,10},{9,11},{10,... | collective-permute-start | bytes 196616 | tf_op jit(solution)/shard_map/ppermute | solution.py:513
  60.1 7.3 %collective-permute-start.22 = (f32[32,512]{1,0:T(8,128)S(1)}, f32[32,512]{1,0:T(8,128)S(1)}, u32[]{:S(2)}, u32[]{:S(2)}) collective-permute-start(f32[32,512]{1,0:T(8,128)S(1)} %lower.1), channel_id=1, source_target_pairs={{0,3},{1,2},{2,1},{3,0},{4,7},{5,6},{6,5},{7,4},{8,11},{9,10},{10,... | collective-permute-start | bytes 196616 | tf_op jit(solution)/shard_map/ppermute | solution.py:513
  61.5 5.9 %collective-permute-start.21 = (f32[32,512]{1,0:T(8,128)S(1)}, f32[32,512]{1,0:T(8,128)S(1)}, u32[]{:S(2)}, u32[]{:S(2)}) collective-permute-start(f32[32,512]{1,0:T(8,128)S(1)} %lower.1), channel_id=1, source_target_pairs={{0,1},{1,0},{2,3},{3,2},{4,5},{5,4},{6,7},{7,6},{8,9},{9,8},{10,11... | collective-permute-start | bytes 196616 | tf_op jit(solution)/shard_map/ppermute | solution.py:513
  67.4 3.6 %collective-permute-start.27 = (f32[32,896]{1,0:T(8,128)S(1)}, f32[32,896]{1,0:T(8,128)S(1)}, u32[]{:S(2)}, u32[]{:S(2)}) collective-permute-start(f32[32,896]{1,0:T(8,128)S(1)} %pad_maximum_fusion), channel_id=1, source_target_pairs={{0,4},{1,5},{2,6},{3,7},{4,0},{5,1},{6,2},{7,3},{8,12},{9,13},{10,... | collective-permute-start | bytes 344072 | tf_op jit(solution)/shard_map/ppermute | solution.py:513
  67.5 6.0 %collective-permute-start.26 = (f32[1,32,512]{2,1,0:T(8,128)S(1)}, f32[1,32,512]{2,1,0:T(8,128)S(1)}, u32[]{:S(2)}, u32[]{:S(2)}) collective-permute-start(f32[1,32,512]{2,1,0:T(8,128)S(1)} %bitcast.6), channel_id=1, source_target_pairs={{0,24},{1,25},{2,26},{3,27},{4,28},{5,29},{6,30},{7,31},{8,16},{9,... | collective-permute-start | bytes 196616 | tf_op jit(solution)/shard_map/ppermute | solution.py:513
  69.2 5.1 %collective-permute-start.25 = (f32[1,32,512]{2,1,0:T(8,128)S(1)}, f32[1,32,512]{2,1,0:T(8,128)S(1)}, u32[]{:S(2)}, u32[]{:S(2)}) collective-permute-start(f32[1,32,512]{2,1,0:T(8,128)S(1)} %bitcast.7), channel_id=1, source_target_pairs={{0,16},{1,17},{2,18},{3,19},{4,12},{5,13},{6,14},{7,15},{8,24},{9,... | collective-permute-start | bytes 196616 | tf_op jit(solution)/shard_map/ppermute | solution.py:513
  70.0 4.4 %collective-permute-start.24 = (f32[1,32,512]{2,1,0:T(8,128)S(1)}, f32[1,32,512]{2,1,0:T(8,128)S(1)}, u32[]{:S(2)}, u32[]{:S(2)}) collective-permute-start(f32[1,32,512]{2,1,0:T(8,128)S(1)} %bitcast.8), channel_id=1, source_target_pairs={{0,8},{1,9},{2,10},{3,11},{4,20},{5,21},{6,22},{7,23},{8,0},{9,1},... | collective-permute-start | bytes 196616 | tf_op jit(solution)/shard_map/ppermute | solution.py:513
  74.4 1.5 %collective-permute-start.28 = (f32[3,32,512]{2,1,0:T(8,128)S(1)}, f32[3,32,512]{2,1,0:T(8,128)S(1)}, u32[]{:S(2)}, u32[]{:S(2)}) collective-permute-start(f32[3,32,512]{2,1,0:T(8,128)S(1)} %constant_dynamic-update-slice_fusion.v0_ref), channel_id=1, source_target_pairs={{0,4},{1,5},{2,6},{3,7},{4,0},{5,1},{6,2},{7,3},{8,12},{9,13},{10,... | collective-permute-start | bytes 589832 | tf_op jit(solution)/shard_map/ppermute | solution.py:513

commit v8 on v7

--- a/solution.py
+++ b/solution.py
@@ -368,11 +368,41 @@
     )
 
 
+def turned(f_ref, v, rows):
+    rank = v.shape[0]
+    high, middle, low = split3(dot(f_ref[:, rows : rows + rank], v, TN))
+    return jnp.concatenate([high, middle, high, low, high, middle], axis=0)
+
+
+def ready_kernel(v_ref, f_ref, c_front, c_back, left, errors, approx, *, positions, blocks):
+    rows = errors.shape[1]
+    rights = [turned(f_ref, v_ref[k], rows) for k in range(len(positions))]
+    for k, p in enumerate(positions):
+        product = jnp.dot(left[0], rights[k], preferred_element_type=f32)
+        part, at = within(p, blocks)
+        approx[k] = product
+        errors[k] = (c_front, c_back)[part][at] - product
+
+
+def ready(positions, v, f, own_c, left, blocks):
+    _, rows, width = own_c[0].shape
+    shape = (len(positions), rows, width)
+    return call(
+        functools.partial(ready_kernel, positions=positions, blocks=blocks),
+        "ready",
+        [VMEM] * 5,
+        [VMEM] * 2,
+        [pltpu.VMEM(shape, f32)] * 2,
+        (v, f, *own_c, left),
+        mib=8,
+    )
+
+
 def finish_kernel(
     place, owners, v0_ref, v1_ref, f0_ref, f1_ref, c0_front, c0_back, c1_front, c1_back, mm, mw, *refs, positions, head, later
 ):
     if later:
-        left, refs = refs[0], refs[1 + 3 :]
+        left, own_errors, own_approx, refs = refs[0], refs[1], refs[2], refs[3 + 3 :]
         n_hbm, mo_hbm, wo_hbm, errors, approx, moment, weight, sem, bank_sem = refs
     else:
         n_hbm, mo_hbm, wo_hbm, left, errors, approx, moment, weight, sem, bank_sem = refs
@@ -383,25 +413,18 @@
         for i, f_ref in enumerate((f0_ref, f1_ref)):
             high, middle, low = split3(f_ref[:, :rows].T)
             left[i] = jnp.concatenate([high, high, middle, high, low, middle], axis=1)
-    units = [(k, p, i) for k, p in enumerate(positions) for i in range(2)]
-    rights = []
-    for k, p, i in units:
-        f_ref, v_ref = ((f0_ref, v0_ref), (f1_ref, v1_ref))[i]
-        high, middle, low = split3(dot(f_ref[:, rows : rows + rank], v_ref[k], TN))
-        rights.append(jnp.concatenate([high, middle, high, low, high, middle], axis=0))
-    stores = []
-    for (k, p, i), right in zip(units, rights):
+    made = [(k, p, 0) for k, p in enumerate(positions)] if later else []
+    units = [(k, p, i) for k, p in enumerate(positions) for i in range(2) if (k, p, i) not in made]
+    items = taken_items(place, owners, mm.shape[0])
+    stores, bank_stores = [], []
+
+    def store(k, p, i, source):
         m = place[0] if i == 0 else 1 - place[0]
-        product = jnp.dot(left[i], right, preferred_element_type=f32)
-        approx[k, i] = product
-        part, at = within(p, blocks)
-        errors[k, i] = ((c0_front, c0_back), (c1_front, c1_back))[i][part][at] - product
         columns = block_columns(place, i == 0, p, blocks, width)
-        stores.append(pltpu.make_async_copy(errors.at[k, i], n_hbm.at[0, m, :, columns], sem.at[k, i]))
+        stores.append(pltpu.make_async_copy(source, n_hbm.at[0, m, :, columns], sem.at[k, i]))
         stores[-1].start()
-    bank_stores = []
-    items = taken_items(place, owners, mm.shape[0])
-    for k, p, i in units:
+
+    def step(k, p, i, source):
         m = place[0] if i == 0 else 1 - place[0]
         columns = block_columns(place, i == 0, p, blocks, width)
         for slot, item in enumerate(items):
@@ -419,7 +442,7 @@
             @pl.when(taken)
             def _():
                 at = pl.ds(pl.multiple_of((item - m * per) * head, head), head)
-                new = 0.9 * mm[slot, :, columns] + approx[k, i, at, :]
+                new = 0.9 * mm[slot, :, columns] + source[at, :]
                 moment[k, i, slot] = new
                 weight[k, i, slot] = mw[slot, :, columns] - 0.5 * new
                 for copy in copies:
@@ -437,8 +460,21 @@
                         copy.start()
 
             bank_stores.append((writes, copies))
-    for store in stores:
-        store.wait()
+
+    for k, p, i in made:
+        store(k, p, i, own_errors.at[k])
+        step(k, p, i, own_approx.at[k])
+    rights = [turned((f0_ref, f1_ref)[i], (v0_ref, v1_ref)[i][k], rows) for k, p, i in units]
+    for (k, p, i), right in zip(units, rights):
+        product = jnp.dot(left[i], right, preferred_element_type=f32)
+        part, at = within(p, blocks)
+        approx[k, i] = product
+        errors[k, i] = ((c0_front, c0_back), (c1_front, c1_back))[i][part][at] - product
+        store(k, p, i, errors.at[k, i])
+    for k, p, i in units:
+        step(k, p, i, approx.at[k, i])
+    for copy in stores:
+        copy.wait()
     for writes, copies in bank_stores:
 
         @pl.when(writes)
@@ -633,10 +669,10 @@
     )
     *arrived, left = lax.optimization_barrier((*arrived, left))
     v = jnp.concatenate(arrived, axis=0)
-    outs = finish(
-        list(range(1, blocks)), (left,), outs, place, owners, v, exchange(v, "core"), own_f, other_f, own_c, other_c,
-        shapes, mm, mw,
-    )
+    other_v = exchange(v, "core")
+    others = list(range(1, blocks))
+    left = (left, *ready(others, v, own_f, own_c, left, blocks))
+    outs = finish(others, left, outs, place, owners, v, other_v, own_f, other_f, own_c, other_c, shapes, mm, mw)
     new_errors, mat_momentum_out, mat_weights_out = outs
     return (new_errors, mat_momentum_out, mat_weights_out, vec_momentum_out, vec_weights_out)
 

time: 80 us -> 79.4 us (level)
  waiting for transfers between devices: 18.9 us -> 17.9 us
    ppermute x29, waiting for transfers between devices: 18.9 us -> 17.9 us  [exchange(): return lax.ppermute(a, ('rep', 'grp'), pairs)]
    pallas_call x19 -> x20, Pallas kernels: 29.6 us -> 29.7 us  [call(): pl.pallas_call(kernel, in_specs=in_specs, out_specs=out_specs, out_shape=...]
  transfers between devices with their start and end apart: 29 -> 29, of which waited for: 12 -> 11; matrix products, arithmetic and copies ran while one was open for 0% -> 0% of each run, Pallas kernels for 27% -> 28%
where the time goes in v8:
time: 79.4 us; the launch traced here: 79.2 us
  starting transfers between devices  30.4 us (38%)
  Pallas kernels  29.7 us (37%)
  waiting for transfers between devices  17.9 us (23%)
  between operations  0.97 us (1%)
    ppermute x29, starting transfers between devices, exchange(): return lax.ppermute(a, ('rep', 'grp'), pairs)  30.4 us
    pallas_call x20, Pallas kernels, call(): pl.pallas_call(kernel, in_specs=in_specs, out_specs=out_specs, out_shape=...  29.7 us
    ppermute x29, waiting for transfers between devices, exchange(): return lax.ppermute(a, ('rep', 'grp'), pairs)  17.9 us
  transfers between devices with their start and end apart: 29, of which 11 were waited for; matrix products, arithmetic and copies ran while one was open for 0% of the time, Pallas kernels for 28%

profile of v8, /device:TPU:0, one launch (start us, length us, event | category | flops | bytes accessed | tf_op | source)
XLA Modules:
  0.0 79.2 jit_solution(6641882825481186702)
XLA Ops:
  0.7 0.1 pad_add_fusion.place
  0.7 2.8 %other0.1 = (f32[1,320,512]{2,1,0:T(8,128)S(1)}, f32[3,320,512]{2,1,0:T(8,128)S(1)}) custom-call(s32[3]{0:T(128)S(1)} %pad_add_fusion.place, bf16[1,2,320,2048]{3,2,1,0:T(8,128)(2,1)} %g_hbm.5, f32[1,2,320,2048]{3,2,1,0:T(8,128)} %e_hbm.5), custom_call_target="tpu_custom_call" | custom-call | flops 1 | bytes 1 | tf_op jit(solution)/shard_map/other0/pallas_call | solution.py:71
  3.5 0.5 collective-permute-start
  4.0 1.8 %own0.1.refs_0_.refs_4_.c0_front.c_front = f32[1,320,512]{2,1,0:T(8,128)S(1)} custom-call(s32[3]{0:T(128)S(1)} %pad_add_fusion.place, bf16[1,2,320,2048]{3,2,1,0:T(8,128)(2,1)} %g_hbm.5, f32[1,2,320,2048]{3,2,1,0:T(8,128)} %e_hbm.5), custom_call_target="tpu_custom_call" | custom-call | flops 1 | bytes 1 | tf_op jit(solution)/shard_map/own0/pallas_call | solution.py:71
  5.8 0.0 copy-start
  5.9 0.1 fold.4
  6.0 0.3 collective-permute-start.3
  6.3 2.8 %collective-permute-start.4 = (f32[1,320,512]{2,1,0:T(8,128)S(1)}, f32[1,320,512]{2,1,0:T(8,128)S(1)}, u32[]{:S(2)}, u32[]{:S(2)}) collective-permute-start(f32[1,320,512]{2,1,0:T(8,128)S(1)} %fold.4), channel_id=1, source_target_pairs={{0,8},{1,9},{2,10},{3,11},{4,20},{5,21},{6,22},{7,23},{8,0},{9,1},... | collective-permute-start | bytes 1966088 | tf_op jit(solution)/shard_map/ppermute | solution.py:549
  9.0 3.7 %own2.1 = (f32[3,320,512]{2,1,0:T(8,128)S(1)}, f32[96,128]{1,0:T(8,128)S(1)}, f32[32,320]{1,0:T(8,128)S(1)}) custom-call(s32[3]{0:T(128)S(1)} %pad_add_fusion.place, bf16[1,2,320,2048]{3,2,1,0:T(8,128)(2,1)} %g_hbm.5, f32[1,2,320,2048]{3,2,1,0:T(8,128)} %e_hbm.5, f32[2,32,2048]{2,1,0:T(8,128)S(1)} %copy-done, f32[1,2,2048]{2,1,0:T(2,128)S(1)} %copy-done.1, ...), custom_call_target="tpu_custom_call" | custom-call | flops 1 | bytes 1 | tf_op jit(solution)/shard_map/own2/pallas_call | solution.py:71
  12.8 0.1 collective-permute-start.1
  12.8 1.4 %factor.1 = f32[96,128]{1,0:T(8,128)S(1)} custom-call(s32[3]{0:T(128)S(1)} %pad_add_fusion.place, f32[2,32,2048]{2,1,0:T(8,128)S(1)} %copy-done, f32[1,2,2048]{2,1,0:T(2,128)S(1)} %copy-done.1, f32[3,320,512]{2,1,0:T(8,128)S(1)} %get-tuple-element.85.part.refs_0_.c0_back.c_back, f32[32,320]{1,0:T(8,128)S(1)} %get-tuple-element.75.before), custom_call_target="tpu_custom_call" | custom-call | flops 1 | bytes 1 | tf_op jit(solution)/shard_map/factor/pallas_call | solution.py:71
  14.3 0.0 collective-permute-done.1
  14.3 0.1 fold.6
  14.4 1.5 %collective-permute-start.8 = (f32[1,320,512]{2,1,0:T(8,128)S(1)}, f32[1,320,512]{2,1,0:T(8,128)S(1)}, u32[]{:S(2)}, u32[]{:S(2)}) collective-permute-start(f32[1,320,512]{2,1,0:T(8,128)S(1)} %fold.6), channel_id=1, source_target_pairs={{0,8},{1,9},{2,10},{3,11},{4,20},{5,21},{6,22},{7,23},{8,0},{9,1},... | collective-permute-start | bytes 1966088 | tf_op jit(solution)/shard_map/ppermute | solution.py:549
  15.9 0.9 %collective-permute-start.2 = (f32[96,128]{1,0:T(8,128)S(1)}, f32[96,128]{1,0:T(8,128)S(1)}, u32[]{:S(2)}, u32[]{:S(2)}) collective-permute-start(f32[96,128]{1,0:T(8,128)S(1)} %add.64), channel_id=1, source_target_pairs={{0,16},{1,17},{2,18},{3,19},{4,12},{5,13},{6,14},{7,15},{8,24},{9,... | collective-permute-start | bytes 147464 | tf_op jit(solution)/shard_map/ppermute | solution.py:549
  16.8 1.6 %banks.1 = (f32[2,64,2048]{2,1,0:T(8,128)S(1)}, f32[2,64,2048]{2,1,0:T(8,128)S(1)}) custom-call(f32[2,64,2048]{2,1,0:T(8,128)} %mm_hbm, f32[2,64,2048]{2,1,0:T(8,128)} %mw_hbm), custom_call_target="tpu_custom_call" | custom-call | flops 1 | bytes 2097152 | tf_op jit(solution)/shard_map/banks/pallas_call | solution.py:71
  18.4 0.1 fold.5
  18.5 2.1 %collective-permute-done.2 = f32[96,128]{1,0:T(8,128)S(1)} collective-permute-done((f32[96,128]{1,0:T(8,128)S(1)}, f32[96,128]{1,0:T(8,128)S(1)}, u32[]{:S(2)}, u32[]{:S(2)}) %collective-permute-start.2) | collective-permute-done | bytes 49184 | tf_op jit(solution)/shard_map/ppermute | solution.py:549
  20.6 0.9 %collective-permute-start.10 = (f32[1,320,512]{2,1,0:T(8,128)S(1)}, f32[1,320,512]{2,1,0:T(8,128)S(1)}, u32[]{:S(2)}, u32[]{:S(2)}) collective-permute-start(f32[1,320,512]{2,1,0:T(8,128)S(1)} %fold.5), channel_id=1, source_target_pairs={{0,16},{1,17},{2,18},{3,19},{4,12},{5,13},{6,14},{7,15},{8,24},{9,... | collective-permute-start | bytes 1966088 | tf_op jit(solution)/shard_map/ppermute | solution.py:549
  21.5 2.6 %collective-permute-start.7 = (f32[96,128]{1,0:T(8,128)S(1)}, f32[96,128]{1,0:T(8,128)S(1)}, u32[]{:S(2)}, u32[]{:S(2)}) collective-permute-start(f32[96,128]{1,0:T(8,128)S(1)} %add.65), channel_id=1, source_target_pairs={{0,2},{1,3},{2,0},{3,1},{4,6},{5,7},{6,4},{7,5},{8,10},{9,11},{10,... | collective-permute-start | bytes 147464 | tf_op jit(solution)/shard_map/ppermute | solution.py:549
  24.1 1.4 %collective-permute-start.6 = (f32[96,128]{1,0:T(8,128)S(1)}, f32[96,128]{1,0:T(8,128)S(1)}, u32[]{:S(2)}, u32[]{:S(2)}) collective-permute-start(f32[96,128]{1,0:T(8,128)S(1)} %add.65), channel_id=1, source_target_pairs={{0,3},{1,2},{2,1},{3,0},{4,7},{5,6},{6,5},{7,4},{8,11},{9,10},{10,... | collective-permute-start | bytes 147464 | tf_op jit(solution)/shard_map/ppermute | solution.py:549
  25.4 0.2 collective-permute-start.5
  25.7 1.1 %collective-permute-done.7 = f32[96,128]{1,0:T(8,128)S(1)} collective-permute-done((f32[96,128]{1,0:T(8,128)S(1)}, f32[96,128]{1,0:T(8,128)S(1)}, u32[]{:S(2)}, u32[]{:S(2)}) %collective-permute-start.7) | collective-permute-done | bytes 49184 | tf_op jit(solution)/shard_map/ppermute | solution.py:549
  26.8 3.3 %collective-permute-done.6 = f32[96,128]{1,0:T(8,128)S(1)} collective-permute-done((f32[96,128]{1,0:T(8,128)S(1)}, f32[96,128]{1,0:T(8,128)S(1)}, u32[]{:S(2)}, u32[]{:S(2)}) %collective-permute-start.6) | collective-permute-done | bytes 49184 | tf_op jit(solution)/shard_map/ppermute | solution.py:549
  30.1 1.3 %collective-permute-start.9 = (f32[96,128]{1,0:T(8,128)S(1)}, f32[96,128]{1,0:T(8,128)S(1)}, u32[]{:S(2)}, u32[]{:S(2)}) collective-permute-start(f32[96,128]{1,0:T(8,128)S(1)} %add_add_fusion.2), channel_id=1, source_target_pairs={{0,8},{1,9},{2,10},{3,11},{4,20},{5,21},{6,22},{7,23},{8,0},{9,1},... | collective-permute-start | bytes 147464 | tf_op jit(solution)/shard_map/ppermute | solution.py:549
  31.4 0.1 fold.7.refs_0_
  31.5 0.0 copy-start.4
  31.5 2.8 %collective-permute-done.9 = f32[96,128]{1,0:T(8,128)S(1)} collective-permute-done((f32[96,128]{1,0:T(8,128)S(1)}, f32[96,128]{1,0:T(8,128)S(1)}, u32[]{:S(2)}, u32[]{:S(2)}) %collective-permute-start.9) | collective-permute-done | bytes 49184 | tf_op jit(solution)/shard_map/ppermute | solution.py:549
  34.3 0.5 project.1
  34.8 1.6 %collective-permute-start.13 = (f32[32,512]{1,0:T(8,128)S(1)}, f32[32,512]{1,0:T(8,128)S(1)}, u32[]{:S(2)}, u32[]{:S(2)}) collective-permute-start(f32[32,512]{1,0:T(8,128)S(1)} %get-tuple-element.92), channel_id=1, source_target_pairs={{0,2},{1,3},{2,0},{3,1},{4,6},{5,7},{6,4},{7,5},{8,10},{9,11},{10,... | collective-permute-start | bytes 196616 | tf_op jit(solution)/shard_map/ppermute | solution.py:549
  36.4 1.3 %collective-permute-start.12 = (f32[32,512]{1,0:T(8,128)S(1)}, f32[32,512]{1,0:T(8,128)S(1)}, u32[]{:S(2)}, u32[]{:S(2)}) collective-permute-start(f32[32,512]{1,0:T(8,128)S(1)} %get-tuple-element.92), channel_id=1, source_target_pairs={{0,3},{1,2},{2,1},{3,0},{4,7},{5,6},{6,5},{7,4},{8,11},{9,10},{10,... | collective-permute-start | bytes 196616 | tf_op jit(solution)/shard_map/ppermute | solution.py:549
  37.7 0.6 collective-permute-start.11
  38.3 2.1 %root1a.1.state = f32[3,32,32]{2,1,0:T(8,128)S(1)} custom-call(f32[96,128]{1,0:T(8,128)S(1)} %add.69.x_ref.own_ref), custom_call_target="tpu_custom_call" | custom-call | flops 12000000 | bytes 49152 | tf_op jit(solution)/shard_map/root1a/pallas_call | solution.py:71
  40.4 2.3 %collective-permute-done.13 = f32[32,512]{1,0:T(8,128)S(1)} collective-permute-done((f32[32,512]{1,0:T(8,128)S(1)}, f32[32,512]{1,0:T(8,128)S(1)}, u32[]{:S(2)}, u32[]{:S(2)}) %collective-permute-start.13) | collective-permute-done | bytes 65568 | tf_op jit(solution)/shard_map/ppermute | solution.py:549
  42.8 0.3 collective-permute-done.11
  43.1 0.7 lift.1
  43.8 2.0 %collective-permute-start.16 = (f32[80,128]{1,0:T(8,128)S(1)}, f32[80,128]{1,0:T(8,128)S(1)}, u32[]{:S(2)}, u32[]{:S(2)}) collective-permute-start(f32[80,128]{1,0:T(8,128)S(1)} %lift.1), channel_id=1, source_target_pairs={{0,2},{1,3},{2,0},{3,1},{4,6},{5,7},{6,4},{7,5},{8,10},{9,11},{10,... | collective-permute-start | bytes 122888 | tf_op jit(solution)/shard_map/ppermute | solution.py:549
  45.9 1.3 %collective-permute-start.15 = (f32[80,128]{1,0:T(8,128)S(1)}, f32[80,128]{1,0:T(8,128)S(1)}, u32[]{:S(2)}, u32[]{:S(2)}) collective-permute-start(f32[80,128]{1,0:T(8,128)S(1)} %lift.1), channel_id=1, source_target_pairs={{0,3},{1,2},{2,1},{3,0},{4,7},{5,6},{6,5},{7,4},{8,11},{9,10},{10,... | collective-permute-start | bytes 122888 | tf_op jit(solution)/shard_map/ppermute | solution.py:549
  47.2 0.2 collective-permute-start.14
  47.4 1.9 %root1b.1.a_ref = f32[32,32]{1,0:T(8,128)S(1)} custom-call(f32[3,32,32]{2,1,0:T(8,128)S(1)} %root1a.1.state), custom_call_target="tpu_custom_call" | custom-call | flops 12000000 | bytes 12288 | tf_op jit(solution)/shard_map/root1b/pallas_call | solution.py:71
  49.3 2.4 %collective-permute-done.15 = f32[80,128]{1,0:T(8,128)S(1)} collective-permute-done((f32[80,128]{1,0:T(8,128)S(1)}, f32[80,128]{1,0:T(8,128)S(1)}, u32[]{:S(2)}, u32[]{:S(2)}) %collective-permute-start.15) | collective-permute-done | bytes 40992 | tf_op jit(solution)/shard_map/ppermute | solution.py:549
  51.7 1.6 %collective-permute-start.20 = (f32[80,128]{1,0:T(8,128)S(1)}, f32[80,128]{1,0:T(8,128)S(1)}, u32[]{:S(2)}, u32[]{:S(2)}) collective-permute-start(f32[80,128]{1,0:T(8,128)S(1)} %add_add_fusion.4), channel_id=1, source_target_pairs={{0,16},{1,17},{2,18},{3,19},{4,12},{5,13},{6,14},{7,15},{8,24},{9,... | collective-permute-start | bytes 122888 | tf_op jit(solution)/shard_map/ppermute | solution.py:549
  53.3 1.2 %collective-permute-start.19 = (f32[80,128]{1,0:T(8,128)S(1)}, f32[80,128]{1,0:T(8,128)S(1)}, u32[]{:S(2)}, u32[]{:S(2)}) collective-permute-start(f32[80,128]{1,0:T(8,128)S(1)} %add_add_fusion.4), channel_id=1, source_target_pairs={{0,24},{1,25},{2,26},{3,27},{4,28},{5,29},{6,30},{7,31},{8,16},{9,... | collective-permute-start | bytes 122888 | tf_op jit(solution)/shard_map/ppermute | solution.py:549
  54.5 0.7 collective-permute-start.18
  55.3 1.2 %gains.1 = (f32[2,2048]{1,0:T(2,128)}, f32[2,2048]{1,0:T(2,128)}) custom-call(s32[3]{0:T(128)S(1)} %pad_add_fusion.place, s32[12]{0:T(128)S(1)} %copy-done.4, f32[96,128]{1,0:T(8,128)S(1)} %add.69.x_ref.own_ref, f32[96,128]{1,0:T(8,128)S(1)} %collective-permute-done.17.other_ref, f32[2,2048]{1,0:T(2,128)S(1)} %copy-done.2, f32[2,2048]{1,0:T(2,128)S(1)} %copy-done.3), custom_call_target="tpu_custom_call" | custom-call | flops 40960 | bytes 65536 | tf_op jit(solution)/shard_map/gains/pallas_call | solution.py:71
  56.5 1.7 %collective-permute-done.19 = f32[80,128]{1,0:T(8,128)S(1)} collective-permute-done((f32[80,128]{1,0:T(8,128)S(1)}, f32[80,128]{1,0:T(8,128)S(1)}, u32[]{:S(2)}, u32[]{:S(2)}) %collective-permute-start.19) | collective-permute-done | bytes 40992 | tf_op jit(solution)/shard_map/ppermute | solution.py:549
  58.2 0.3 collective-permute-done.18
  58.5 0.5 lower.1
  59.0 1.0 %collective-permute-start.23 = (f32[32,512]{1,0:T(8,128)S(1)}, f32[32,512]{1,0:T(8,128)S(1)}, u32[]{:S(2)}, u32[]{:S(2)}) collective-permute-start(f32[32,512]{1,0:T(8,128)S(1)} %lower.1), channel_id=1, source_target_pairs={{0,2},{1,3},{2,0},{3,1},{4,6},{5,7},{6,4},{7,5},{8,10},{9,11},{10,... | collective-permute-start | bytes 196616 | tf_op jit(solution)/shard_map/ppermute | solution.py:549
  60.0 1.5 %collective-permute-start.22 = (f32[32,512]{1,0:T(8,128)S(1)}, f32[32,512]{1,0:T(8,128)S(1)}, u32[]{:S(2)}, u32[]{:S(2)}) collective-permute-start(f32[32,512]{1,0:T(8,128)S(1)} %lower.1), channel_id=1, source_target_pairs={{0,3},{1,2},{2,1},{3,0},{4,7},{5,6},{6,5},{7,4},{8,11},{9,10},{10,... | collective-permute-start | bytes 196616 | tf_op jit(solution)/shard_map/ppermute | solution.py:549
  61.5 1.0 %collective-permute-start.21 = (f32[32,512]{1,0:T(8,128)S(1)}, f32[32,512]{1,0:T(8,128)S(1)}, u32[]{:S(2)}, u32[]{:S(2)}) collective-permute-start(f32[32,512]{1,0:T(8,128)S(1)} %lower.1), channel_id=1, source_target_pairs={{0,1},{1,0},{2,3},{3,2},{4,5},{5,4},{6,7},{7,6},{8,9},{9,8},{10,11... | collective-permute-start | bytes 196616 | tf_op jit(solution)/shard_map/ppermute | solution.py:549
  62.5 2.4 %root2a.1.state = f32[3,32,32]{2,1,0:T(8,128)S(1)} custom-call(f32[32,32]{1,0:T(8,128)S(1)} %root1b.1.a_ref, f32[80,128]{1,0:T(8,128)S(1)} %add_add_fusion.3.u_ref), custom_call_target="tpu_custom_call" | custom-call | flops 12000000 | bytes 45056 | tf_op jit(solution)/shard_map/root2a/pallas_call | solution.py:71
  65.0 2.3 %root2b.1.f0_ref.f_ref = f32[32,384]{1,0:T(8,128)S(1)} custom-call(f32[3,32,32]{2,1,0:T(8,128)S(1)} %root2a.1.state, f32[32,32]{1,0:T(8,128)S(1)} %root1b.1.a_ref, f32[80,128]{1,0:T(8,128)S(1)} %add_add_fusion.3.u_ref), custom_call_target="tpu_custom_call" | custom-call | flops 12000000 | bytes 57344 | tf_op jit(solution)/shard_map/root2b/pallas_call | solution.py:71
  67.3 0.0 collective-permute-done.23
  67.4 0.1 collective-permute-start.27
  67.5 1.8 %collective-permute-start.26 = (f32[1,32,512]{2,1,0:T(8,128)S(1)}, f32[1,32,512]{2,1,0:T(8,128)S(1)}, u32[]{:S(2)}, u32[]{:S(2)}) collective-permute-start(f32[1,32,512]{2,1,0:T(8,128)S(1)} %bitcast.6), channel_id=1, source_target_pairs={{0,24},{1,25},{2,26},{3,27},{4,28},{5,29},{6,30},{7,31},{8,16},{9,... | collective-permute-start | bytes 196616 | tf_op jit(solution)/shard_map/ppermute | solution.py:549
  69.2 0.7 collective-permute-start.25
  70.0 1.1 %collective-permute-start.24 = (f32[1,32,512]{2,1,0:T(8,128)S(1)}, f32[1,32,512]{2,1,0:T(8,128)S(1)}, u32[]{:S(2)}, u32[]{:S(2)}) collective-permute-start(f32[1,32,512]{2,1,0:T(8,128)S(1)} %bitcast.8), channel_id=1, source_target_pairs={{0,8},{1,9},{2,10},{3,11},{4,20},{5,21},{6,22},{7,23},{8,0},{9,1},... | collective-permute-start | bytes 196616 | tf_op jit(solution)/shard_map/ppermute | solution.py:549
  71.0 2.4 %finish0.1 = (f32[1,2,320,2048]{3,2,1,0:T(8,128)}, f32[2,64,2048]{2,1,0:T(8,128)}, f32[2,64,2048]{2,1,0:T(8,128)}, bf16[2,320,192]{2,1,0:T(8,128)(2,1)S(1)}) custom-call(s32[3]{0:T(128)S(1)} %pad_add_fusion.place, s32[12]{0:T(128)S(1)} %copy-done.4, f32[1,32,512]{2,1,0:T(8,128)S(1)} %bitcast.9, f32[1,32,512]{2,1,0:T(8,128)S(1)} %slice_bitcast_fusion.v1_ref, ...), custom_call_target="tpu_custom_call" | custom-call | flops 125829120 | bytes 2359296 | tf_op jit(solution)/shard_map/finish0/pallas_call | solution.py:71
  73.5 0.8 %collective-permute-done.25 = f32[1,32,512]{2,1,0:T(8,128)S(1)} collective-permute-done((f32[1,32,512]{2,1,0:T(8,128)S(1)}, f32[1,32,512]{2,1,0:T(8,128)S(1)}, u32[]{:S(2)}, u32[]{:S(2)}) %collective-permute-start.25) | collective-permute-done | bytes 65568 | tf_op jit(solution)/shard_map/ppermute | solution.py:549
  74.4 0.2 collective-permute-start.28
  74.6 0.7 ready.1
  75.3 0.6 collective-permute-done.28.v1_ref
  75.9 3.3 %finish1.1 = (f32[1,2,320,2048]{3,2,1,0:T(8,128)}, f32[2,64,2048]{2,1,0:T(8,128)}, f32[2,64,2048]{2,1,0:T(8,128)}) custom-call(s32[3]{0:T(128)S(1)} %pad_add_fusion.place, s32[12]{0:T(128)S(1)} %copy-done.4, f32[3,32,512]{2,1,0:T(8,128)S(1)} %constant_dynamic-update-slice_fusion.v_ref.v0_ref, ...), custom_call_target="tpu_custom_call", output_to_operand_aliasing={{0}: (15, {}), {1}: (16, {}), {2}: (17, {})} | custom-call | flops 377487360 | bytes 7077888 | tf_op jit(solution)/shard_map/finish1/pallas_call | solution.py:71
  (39 shorter events, 0.2 us)
Async XLA Ops:
  3.5 2.4 %collective-permute-start = (f32[1,320,512]{2,1,0:T(8,128)S(1)}, f32[1,320,512]{2,1,0:T(8,128)S(1)}, u32[]{:S(2)}, u32[]{:S(2)}) collective-permute-start(f32[1,320,512]{2,1,0:T(8,128)S(1)} %get-tuple-element.71.refs_2_.c1_front), channel_id=1, source_target_pairs={{0,4},{1,5},{2,6},{3,7},{4,0},{5,1},{6,2},{7,3},{8,12},{9,13},{10,... | collective-permute-start | bytes 1966088 | tf_op jit(solution)/shard_map/ppermute | solution.py:549
  5.8 3.2 %copy-start = (f32[2,32,2048]{2,1,0:T(8,128)S(1)}, f32[2,32,2048]{2,1,0:T(8,128)}, u32[]{:S(2)}) copy-start(f32[2,32,2048]{2,1,0:T(8,128)} %w_ref.1) | copy-start | bytes 1572868
  5.8 3.2 %copy-start.1 = (f32[1,2,2048]{2,1,0:T(2,128)S(1)}, f32[1,2,2048]{2,1,0:T(2,128)}, u32[]{:S(2)}) copy-start(f32[1,2,2048]{2,1,0:T(2,128)} %vec_ref.1) | copy-start | bytes 49156
  6.0 8.4 %collective-permute-start.3 = (f32[3,320,512]{2,1,0:T(8,128)S(1)}, f32[3,320,512]{2,1,0:T(8,128)S(1)}, u32[]{:S(2)}, u32[]{:S(2)}) collective-permute-start(f32[3,320,512]{2,1,0:T(8,128)S(1)} %get-tuple-element.82.refs_3_.c1_back), channel_id=1, source_target_pairs={{0,4},{1,5},{2,6},{3,7},{4,0},{5,1},{6,2},{7,3},{8,12},{9,13},{10,... | collective-permute-start | bytes 5898248 | tf_op jit(solution)/shard_map/ppermute | solution.py:549
  6.3 12.2 %collective-permute-start.4 = (f32[1,320,512]{2,1,0:T(8,128)S(1)}, f32[1,320,512]{2,1,0:T(8,128)S(1)}, u32[]{:S(2)}, u32[]{:S(2)}) collective-permute-start(f32[1,320,512]{2,1,0:T(8,128)S(1)} %fold.4), channel_id=1, source_target_pairs={{0,8},{1,9},{2,10},{3,11},{4,20},{5,21},{6,22},{7,23},{8,0},{9,1},... | collective-permute-start | bytes 1966088 | tf_op jit(solution)/shard_map/ppermute | solution.py:549
  12.8 1.5 %collective-permute-start.1 = (f32[96,128]{1,0:T(8,128)S(1)}, f32[96,128]{1,0:T(8,128)S(1)}, u32[]{:S(2)}, u32[]{:S(2)}) collective-permute-start(f32[96,128]{1,0:T(8,128)S(1)} %get-tuple-element.76), channel_id=1, source_target_pairs={{0,4},{1,5},{2,6},{3,7},{4,0},{5,1},{6,2},{7,3},{8,12},{9,13},{10,... | collective-permute-start | bytes 147464 | tf_op jit(solution)/shard_map/ppermute | solution.py:549
  14.4 15.7 %collective-permute-start.8 = (f32[1,320,512]{2,1,0:T(8,128)S(1)}, f32[1,320,512]{2,1,0:T(8,128)S(1)}, u32[]{:S(2)}, u32[]{:S(2)}) collective-permute-start(f32[1,320,512]{2,1,0:T(8,128)S(1)} %fold.6), channel_id=1, source_target_pairs={{0,8},{1,9},{2,10},{3,11},{4,20},{5,21},{6,22},{7,23},{8,0},{9,1},... | collective-permute-start | bytes 1966088 | tf_op jit(solution)/shard_map/ppermute | solution.py:549
  15.9 4.7 %collective-permute-start.2 = (f32[96,128]{1,0:T(8,128)S(1)}, f32[96,128]{1,0:T(8,128)S(1)}, u32[]{:S(2)}, u32[]{:S(2)}) collective-permute-start(f32[96,128]{1,0:T(8,128)S(1)} %add.64), channel_id=1, source_target_pairs={{0,16},{1,17},{2,18},{3,19},{4,12},{5,13},{6,14},{7,15},{8,24},{9,... | collective-permute-start | bytes 147464 | tf_op jit(solution)/shard_map/ppermute | solution.py:549
  20.6 13.6 %collective-permute-start.10 = (f32[1,320,512]{2,1,0:T(8,128)S(1)}, f32[1,320,512]{2,1,0:T(8,128)S(1)}, u32[]{:S(2)}, u32[]{:S(2)}) collective-permute-start(f32[1,320,512]{2,1,0:T(8,128)S(1)} %fold.5), channel_id=1, source_target_pairs={{0,16},{1,17},{2,18},{3,19},{4,12},{5,13},{6,14},{7,15},{8,24},{9,... | collective-permute-start | bytes 1966088 | tf_op jit(solution)/shard_map/ppermute | solution.py:549
  21.5 5.3 %collective-permute-start.7 = (f32[96,128]{1,0:T(8,128)S(1)}, f32[96,128]{1,0:T(8,128)S(1)}, u32[]{:S(2)}, u32[]{:S(2)}) collective-permute-start(f32[96,128]{1,0:T(8,128)S(1)} %add.65), channel_id=1, source_target_pairs={{0,2},{1,3},{2,0},{3,1},{4,6},{5,7},{6,4},{7,5},{8,10},{9,11},{10,... | collective-permute-start | bytes 147464 | tf_op jit(solution)/shard_map/ppermute | solution.py:549
  24.1 6.0 %collective-permute-start.6 = (f32[96,128]{1,0:T(8,128)S(1)}, f32[96,128]{1,0:T(8,128)S(1)}, u32[]{:S(2)}, u32[]{:S(2)}) collective-permute-start(f32[96,128]{1,0:T(8,128)S(1)} %add.65), channel_id=1, source_target_pairs={{0,3},{1,2},{2,1},{3,0},{4,7},{5,6},{6,5},{7,4},{8,11},{9,10},{10,... | collective-permute-start | bytes 147464 | tf_op jit(solution)/shard_map/ppermute | solution.py:549
  25.4 4.6 %collective-permute-start.5 = (f32[96,128]{1,0:T(8,128)S(1)}, f32[96,128]{1,0:T(8,128)S(1)}, u32[]{:S(2)}, u32[]{:S(2)}) collective-permute-start(f32[96,128]{1,0:T(8,128)S(1)} %add.65), channel_id=1, source_target_pairs={{0,1},{1,0},{2,3},{3,2},{4,5},{5,4},{6,7},{7,6},{8,9},{9,8},{10,11... | collective-permute-start | bytes 147464 | tf_op jit(solution)/shard_map/ppermute | solution.py:549
  30.1 4.2 %collective-permute-start.9 = (f32[96,128]{1,0:T(8,128)S(1)}, f32[96,128]{1,0:T(8,128)S(1)}, u32[]{:S(2)}, u32[]{:S(2)}) collective-permute-start(f32[96,128]{1,0:T(8,128)S(1)} %add_add_fusion.2), channel_id=1, source_target_pairs={{0,8},{1,9},{2,10},{3,11},{4,20},{5,21},{6,22},{7,23},{8,0},{9,1},... | collective-permute-start | bytes 147464 | tf_op jit(solution)/shard_map/ppermute | solution.py:549
  31.5 23.8 %copy-start.2 = (f32[2,2048]{1,0:T(2,128)S(1)}, f32[2,2048]{1,0:T(2,128)}, u32[]{:S(2)}) copy-start(f32[2,2048]{1,0:T(2,128)} %mv_ref.1) | copy-start | bytes 49156
  31.5 23.8 %copy-start.3 = (f32[2,2048]{1,0:T(2,128)S(1)}, f32[2,2048]{1,0:T(2,128)}, u32[]{:S(2)}) copy-start(f32[2,2048]{1,0:T(2,128)} %wv_ref.1) | copy-start | bytes 49156
  31.5 23.8 %copy-start.4 = (s32[12]{0:T(128)S(1)}, s32[12]{0:T(128)}, u32[]{:S(2)}) copy-start(s32[12]{0:T(128)} %owners.5) | copy-start | bytes 148
  34.8 8.0 %collective-permute-start.13 = (f32[32,512]{1,0:T(8,128)S(1)}, f32[32,512]{1,0:T(8,128)S(1)}, u32[]{:S(2)}, u32[]{:S(2)}) collective-permute-start(f32[32,512]{1,0:T(8,128)S(1)} %get-tuple-element.92), channel_id=1, source_target_pairs={{0,2},{1,3},{2,0},{3,1},{4,6},{5,7},{6,4},{7,5},{8,10},{9,11},{10,... | collective-permute-start | bytes 196616 | tf_op jit(solution)/shard_map/ppermute | solution.py:549
  36.4 6.4 %collective-permute-start.12 = (f32[32,512]{1,0:T(8,128)S(1)}, f32[32,512]{1,0:T(8,128)S(1)}, u32[]{:S(2)}, u32[]{:S(2)}) collective-permute-start(f32[32,512]{1,0:T(8,128)S(1)} %get-tuple-element.92), channel_id=1, source_target_pairs={{0,3},{1,2},{2,1},{3,0},{4,7},{5,6},{6,5},{7,4},{8,11},{9,10},{10,... | collective-permute-start | bytes 196616 | tf_op jit(solution)/shard_map/ppermute | solution.py:549
  37.7 5.4 %collective-permute-start.11 = (f32[32,512]{1,0:T(8,128)S(1)}, f32[32,512]{1,0:T(8,128)S(1)}, u32[]{:S(2)}, u32[]{:S(2)}) collective-permute-start(f32[32,512]{1,0:T(8,128)S(1)} %get-tuple-element.92), channel_id=1, source_target_pairs={{0,1},{1,0},{2,3},{3,2},{4,5},{5,4},{6,7},{7,6},{8,9},{9,8},{10,11... | collective-permute-start | bytes 196616 | tf_op jit(solution)/shard_map/ppermute | solution.py:549
  43.8 5.5 %collective-permute-start.16 = (f32[80,128]{1,0:T(8,128)S(1)}, f32[80,128]{1,0:T(8,128)S(1)}, u32[]{:S(2)}, u32[]{:S(2)}) collective-permute-start(f32[80,128]{1,0:T(8,128)S(1)} %lift.1), channel_id=1, source_target_pairs={{0,2},{1,3},{2,0},{3,1},{4,6},{5,7},{6,4},{7,5},{8,10},{9,11},{10,... | collective-permute-start | bytes 122888 | tf_op jit(solution)/shard_map/ppermute | solution.py:549
  45.9 5.8 %collective-permute-start.15 = (f32[80,128]{1,0:T(8,128)S(1)}, f32[80,128]{1,0:T(8,128)S(1)}, u32[]{:S(2)}, u32[]{:S(2)}) collective-permute-start(f32[80,128]{1,0:T(8,128)S(1)} %lift.1), channel_id=1, source_target_pairs={{0,3},{1,2},{2,1},{3,0},{4,7},{5,6},{6,5},{7,4},{8,11},{9,10},{10,... | collective-permute-start | bytes 122888 | tf_op jit(solution)/shard_map/ppermute | solution.py:549
  47.2 4.5 %collective-permute-start.14 = (f32[80,128]{1,0:T(8,128)S(1)}, f32[80,128]{1,0:T(8,128)S(1)}, u32[]{:S(2)}, u32[]{:S(2)}) collective-permute-start(f32[80,128]{1,0:T(8,128)S(1)} %lift.1), channel_id=1, source_target_pairs={{0,1},{1,0},{2,3},{3,2},{4,5},{5,4},{6,7},{7,6},{8,9},{9,8},{10,11... | collective-permute-start | bytes 122888 | tf_op jit(solution)/shard_map/ppermute | solution.py:549
  47.4 4.3 %collective-permute-start.17 = (f32[96,128]{1,0:T(8,128)S(1)}, f32[96,128]{1,0:T(8,128)S(1)}, u32[]{:S(2)}, u32[]{:S(2)}) collective-permute-start(f32[96,128]{1,0:T(8,128)S(1)} %add.69.x_ref.own_ref), channel_id=1, source_target_pairs={{0,4},{1,5},{2,6},{3,7},{4,0},{5,1},{6,2},{7,3},{8,12},{9,13},{10,... | collective-permute-start | bytes 147464 | tf_op jit(solution)/shard_map/ppermute | solution.py:549
  51.7 4.8 %collective-permute-start.20 = (f32[80,128]{1,0:T(8,128)S(1)}, f32[80,128]{1,0:T(8,128)S(1)}, u32[]{:S(2)}, u32[]{:S(2)}) collective-permute-start(f32[80,128]{1,0:T(8,128)S(1)} %add_add_fusion.4), channel_id=1, source_target_pairs={{0,16},{1,17},{2,18},{3,19},{4,12},{5,13},{6,14},{7,15},{8,24},{9,... | collective-permute-start | bytes 122888 | tf_op jit(solution)/shard_map/ppermute | solution.py:549
  53.3 4.9 %collective-permute-start.19 = (f32[80,128]{1,0:T(8,128)S(1)}, f32[80,128]{1,0:T(8,128)S(1)}, u32[]{:S(2)}, u32[]{:S(2)}) collective-permute-start(f32[80,128]{1,0:T(8,128)S(1)} %add_add_fusion.4), channel_id=1, source_target_pairs={{0,24},{1,25},{2,26},{3,27},{4,28},{5,29},{6,30},{7,31},{8,16},{9,... | collective-permute-start | bytes 122888 | tf_op jit(solution)/shard_map/ppermute | solution.py:549
  54.5 4.0 %collective-permute-start.18 = (f32[80,128]{1,0:T(8,128)S(1)}, f32[80,128]{1,0:T(8,128)S(1)}, u32[]{:S(2)}, u32[]{:S(2)}) collective-permute-start(f32[80,128]{1,0:T(8,128)S(1)} %add_add_fusion.4), channel_id=1, source_target_pairs={{0,8},{1,9},{2,10},{3,11},{4,20},{5,21},{6,22},{7,23},{8,0},{9,1},... | collective-permute-start | bytes 122888 | tf_op jit(solution)/shard_map/ppermute | solution.py:549
  59.0 8.3 %collective-permute-start.23 = (f32[32,512]{1,0:T(8,128)S(1)}, f32[32,512]{1,0:T(8,128)S(1)}, u32[]{:S(2)}, u32[]{:S(2)}) collective-permute-start(f32[32,512]{1,0:T(8,128)S(1)} %lower.1), channel_id=1, source_target_pairs={{0,2},{1,3},{2,0},{3,1},{4,6},{5,7},{6,4},{7,5},{8,10},{9,11},{10,... | collective-permute-start | bytes 196616 | tf_op jit(solution)/shard_map/ppermute | solution.py:549
  60.0 7.3 %collective-permute-start.22 = (f32[32,512]{1,0:T(8,128)S(1)}, f32[32,512]{1,0:T(8,128)S(1)}, u32[]{:S(2)}, u32[]{:S(2)}) collective-permute-start(f32[32,512]{1,0:T(8,128)S(1)} %lower.1), channel_id=1, source_target_pairs={{0,3},{1,2},{2,1},{3,0},{4,7},{5,6},{6,5},{7,4},{8,11},{9,10},{10,... | collective-permute-start | bytes 196616 | tf_op jit(solution)/shard_map/ppermute | solution.py:549
  61.5 5.8 %collective-permute-start.21 = (f32[32,512]{1,0:T(8,128)S(1)}, f32[32,512]{1,0:T(8,128)S(1)}, u32[]{:S(2)}, u32[]{:S(2)}) collective-permute-start(f32[32,512]{1,0:T(8,128)S(1)} %lower.1), channel_id=1, source_target_pairs={{0,1},{1,0},{2,3},{3,2},{4,5},{5,4},{6,7},{7,6},{8,9},{9,8},{10,11... | collective-permute-start | bytes 196616 | tf_op jit(solution)/shard_map/ppermute | solution.py:549
  67.4 3.6 %collective-permute-start.27 = (f32[32,896]{1,0:T(8,128)S(1)}, f32[32,896]{1,0:T(8,128)S(1)}, u32[]{:S(2)}, u32[]{:S(2)}) collective-permute-start(f32[32,896]{1,0:T(8,128)S(1)} %pad_maximum_fusion), channel_id=1, source_target_pairs={{0,4},{1,5},{2,6},{3,7},{4,0},{5,1},{6,2},{7,3},{8,12},{9,13},{10,... | collective-permute-start | bytes 344072 | tf_op jit(solution)/shard_map/ppermute | solution.py:549
  67.5 6.0 %collective-permute-start.26 = (f32[1,32,512]{2,1,0:T(8,128)S(1)}, f32[1,32,512]{2,1,0:T(8,128)S(1)}, u32[]{:S(2)}, u32[]{:S(2)}) collective-permute-start(f32[1,32,512]{2,1,0:T(8,128)S(1)} %bitcast.6), channel_id=1, source_target_pairs={{0,24},{1,25},{2,26},{3,27},{4,28},{5,29},{6,30},{7,31},{8,16},{9,... | collective-permute-start | bytes 196616 | tf_op jit(solution)/shard_map/ppermute | solution.py:549
  69.2 5.1 %collective-permute-start.25 = (f32[1,32,512]{2,1,0:T(8,128)S(1)}, f32[1,32,512]{2,1,0:T(8,128)S(1)}, u32[]{:S(2)}, u32[]{:S(2)}) collective-permute-start(f32[1,32,512]{2,1,0:T(8,128)S(1)} %bitcast.7), channel_id=1, source_target_pairs={{0,16},{1,17},{2,18},{3,19},{4,12},{5,13},{6,14},{7,15},{8,24},{9,... | collective-permute-start | bytes 196616 | tf_op jit(solution)/shard_map/ppermute | solution.py:549
  70.0 4.4 %collective-permute-start.24 = (f32[1,32,512]{2,1,0:T(8,128)S(1)}, f32[1,32,512]{2,1,0:T(8,128)S(1)}, u32[]{:S(2)}, u32[]{:S(2)}) collective-permute-start(f32[1,32,512]{2,1,0:T(8,128)S(1)} %bitcast.8), channel_id=1, source_target_pairs={{0,8},{1,9},{2,10},{3,11},{4,20},{5,21},{6,22},{7,23},{8,0},{9,1},... | collective-permute-start | bytes 196616 | tf_op jit(solution)/shard_map/ppermute | solution.py:549
  74.4 1.5 %collective-permute-start.28 = (f32[3,32,512]{2,1,0:T(8,128)S(1)}, f32[3,32,512]{2,1,0:T(8,128)S(1)}, u32[]{:S(2)}, u32[]{:S(2)}) collective-permute-start(f32[3,32,512]{2,1,0:T(8,128)S(1)} %constant_dynamic-update-slice_fusion.v_ref.v0_ref), channel_id=1, source_target_pairs={{0,4},{1,5},{2,6},{3,7},{4,0},{5,1},{6,2},{7,3},{8,12},{9,13},{10,... | collective-permute-start | bytes 589832 | tf_op jit(solution)/shard_map/ppermute | solution.py:549

commit v9 on v8

--- a/solution.py
+++ b/solution.py
@@ -347,24 +347,48 @@
     )
 
 
-def banks_kernel(mm_hbm, mw_hbm, mm, mw, sem):
-    loads = (pltpu.make_async_copy(mm_hbm, mm, sem.at[0]), pltpu.make_async_copy(mw_hbm, mw, sem.at[1]))
+def idle(item, items):
+    return (item < 0) | (item >= items)
+
+
+def banks_kernel(place, owners, mm_hbm, mw_hbm, mm, mw, mo_hbm, wo_hbm, sem, *, items):
+    loads = (pltpu.make_async_copy(mm_hbm, mm, sem.at[0, 0]), pltpu.make_async_copy(mw_hbm, mw, sem.at[0, 1]))
     for load in loads:
         load.start()
     for load in loads:
         load.wait()
-
-
-def banks(mat_momentum, mat_weights):
+    stores = []
+    for slot, item in enumerate(taken_items(place, owners, mm.shape[0])):
+        copies = (
+            pltpu.make_async_copy(mm.at[slot], mo_hbm.at[slot], sem.at[1 + slot, 0]),
+            pltpu.make_async_copy(mw.at[slot], wo_hbm.at[slot], sem.at[1 + slot, 1]),
+        )
+        stores.append((idle(item, items), copies))
+
+        @pl.when(stores[-1][0])
+        def _():
+            for copy in copies:
+                copy.start()
+
+    for writes, copies in stores:
+
+        @pl.when(writes)
+        def _():
+            for copy in copies:
+                copy.wait()
+
+
+def banks(place, owners, mat_momentum, mat_weights, items):
+    shape = mat_momentum.shape
     return call(
-        banks_kernel,
+        functools.partial(banks_kernel, items=items),
         "banks",
-        [ANY, ANY],
-        [VMEM] * 2,
-        [pltpu.VMEM(mat_momentum.shape, f32)] * 2,
-        (mat_momentum, mat_weights),
+        [SMEM, SMEM, ANY, ANY],
+        [VMEM] * 2 + [ANY] * 2,
+        [pltpu.VMEM(shape, f32)] * 2 + [pltpu.HBM(shape, f32)] * 2,
+        (place, owners, mat_momentum, mat_weights),
         nbytes=8 * mat_momentum.size,
-        scratch=[pltpu.SemaphoreType.DMA((2,))],
+        scratch=[pltpu.SemaphoreType.DMA((1 + shape[0], 2))],
     )
 
 
@@ -374,68 +398,61 @@
     return jnp.concatenate([high, middle, high, low, high, middle], axis=0)
 
 
-def ready_kernel(v_ref, f_ref, c_front, c_back, left, errors, approx, *, positions, blocks):
-    rows = errors.shape[1]
-    rights = [turned(f_ref, v_ref[k], rows) for k in range(len(positions))]
-    for k, p in enumerate(positions):
-        product = jnp.dot(left[0], rights[k], preferred_element_type=f32)
+def left_side(f_ref, rows):
+    high, middle, low = split3(f_ref[:, :rows].T)
+    return jnp.concatenate([high, high, middle, high, low, middle], axis=1)
+
+
+def ready_kernel(v_ref, f_ref, c_front, c_back, errors, approx):
+    blocks, rows, _ = errors.shape
+    left = left_side(f_ref, rows)
+    rights = [turned(f_ref, v_ref[p], rows) for p in range(blocks)]
+    for p in range(blocks):
+        product = jnp.dot(left, rights[p], preferred_element_type=f32)
         part, at = within(p, blocks)
-        approx[k] = product
-        errors[k] = (c_front, c_back)[part][at] - product
-
-
-def ready(positions, v, f, own_c, left, blocks):
-    _, rows, width = own_c[0].shape
-    shape = (len(positions), rows, width)
+        approx[p] = product
+        errors[p] = (c_front, c_back)[part][at] - product
+
+
+def ready(v, f, own_c):
+    shape = (v.shape[0],) + own_c[0].shape[1:]
     return call(
-        functools.partial(ready_kernel, positions=positions, blocks=blocks),
+        ready_kernel,
         "ready",
-        [VMEM] * 5,
+        [VMEM] * 4,
         [VMEM] * 2,
         [pltpu.VMEM(shape, f32)] * 2,
-        (v, f, *own_c, left),
+        (v, f, *own_c),
         mib=8,
     )
 
 
 def finish_kernel(
-    place, owners, v0_ref, v1_ref, f0_ref, f1_ref, c0_front, c0_back, c1_front, c1_back, mm, mw, *refs, positions, head, later
+    place, owners, v_ref, f_ref, c_front, c_back, own_errors, own_approx, mm, mw, _, __,
+    n_hbm, mo_hbm, wo_hbm, errors, approx, moment, weight, sem, bank_sem, *, head
 ):
-    if later:
-        left, own_errors, own_approx, refs = refs[0], refs[1], refs[2], refs[3 + 3 :]
-        n_hbm, mo_hbm, wo_hbm, errors, approx, moment, weight, sem, bank_sem = refs
-    else:
-        n_hbm, mo_hbm, wo_hbm, left, errors, approx, moment, weight, sem, bank_sem = refs
-    rank, width = v0_ref.shape[1:]
-    blocks, rows = c0_front.shape[0] + c0_back.shape[0], c0_front.shape[1]
+    blocks, rows, width = errors.shape
     per = rows // head
-    if not later:
-        for i, f_ref in enumerate((f0_ref, f1_ref)):
-            high, middle, low = split3(f_ref[:, :rows].T)
-            left[i] = jnp.concatenate([high, high, middle, high, low, middle], axis=1)
-    made = [(k, p, 0) for k, p in enumerate(positions)] if later else []
-    units = [(k, p, i) for k, p in enumerate(positions) for i in range(2) if (k, p, i) not in made]
     items = taken_items(place, owners, mm.shape[0])
     stores, bank_stores = [], []
 
-    def store(k, p, i, source):
+    def store(p, i, source):
         m = place[0] if i == 0 else 1 - place[0]
         columns = block_columns(place, i == 0, p, blocks, width)
-        stores.append(pltpu.make_async_copy(source, n_hbm.at[0, m, :, columns], sem.at[k, i]))
+        stores.append(pltpu.make_async_copy(source, n_hbm.at[0, m, :, columns], sem.at[p, i]))
         stores[-1].start()
 
-    def step(k, p, i, source):
+    def step(p, i, source):
         m = place[0] if i == 0 else 1 - place[0]
         columns = block_columns(place, i == 0, p, blocks, width)
         for slot, item in enumerate(items):
             taken = (item >= m * per) & (item < (m + 1) * per)
-            idle = (item < 0) | (item >= 2 * per)
             copies = (
                 pltpu.make_async_copy(
-                    moment.at[k, i, slot], mo_hbm.at[slot, :, columns], bank_sem.at[k, i, slot, 0]
+                    moment.at[p, i, slot], mo_hbm.at[slot, :, columns], bank_sem.at[p, i, slot, 0]
                 ),
                 pltpu.make_async_copy(
-                    weight.at[k, i, slot], wo_hbm.at[slot, :, columns], bank_sem.at[k, i, slot, 1]
+                    weight.at[p, i, slot], wo_hbm.at[slot, :, columns], bank_sem.at[p, i, slot, 1]
                 ),
             )
 
@@ -443,36 +460,26 @@
             def _():
                 at = pl.ds(pl.multiple_of((item - m * per) * head, head), head)
                 new = 0.9 * mm[slot, :, columns] + source[at, :]
-                moment[k, i, slot] = new
-                weight[k, i, slot] = mw[slot, :, columns] - 0.5 * new
+                moment[p, i, slot] = new
+                weight[p, i, slot] = mw[slot, :, columns] - 0.5 * new
                 for copy in copies:
                     copy.start()
 
-            writes = taken
-            if i == 0:
-                writes = taken | idle
-
-                @pl.when(idle)
-                def _():
-                    moment[k, i, slot] = mm[slot, :, columns]
-                    weight[k, i, slot] = mw[slot, :, columns]
-                    for copy in copies:
-                        copy.start()
-
-            bank_stores.append((writes, copies))
-
-    for k, p, i in made:
-        store(k, p, i, own_errors.at[k])
-        step(k, p, i, own_approx.at[k])
-    rights = [turned((f0_ref, f1_ref)[i], (v0_ref, v1_ref)[i][k], rows) for k, p, i in units]
-    for (k, p, i), right in zip(units, rights):
-        product = jnp.dot(left[i], right, preferred_element_type=f32)
+            bank_stores.append((taken, copies))
+
+    for p in range(blocks):
+        store(p, 0, own_errors.at[p])
+        step(p, 0, own_approx.at[p])
+    left = left_side(f_ref, rows)
+    rights = [turned(f_ref, v_ref[p], rows) for p in range(blocks)]
+    for p in range(blocks):
+        product = jnp.dot(left, rights[p], preferred_element_type=f32)
         part, at = within(p, blocks)
-        approx[k, i] = product
-        errors[k, i] = ((c0_front, c0_back), (c1_front, c1_back))[i][part][at] - product
-        store(k, p, i, errors.at[k, i])
-    for k, p, i in units:
-        step(k, p, i, approx.at[k, i])
+        approx[p] = product
+        errors[p] = (c_front, c_back)[part][at] - product
+        store(p, 1, errors.at[p])
+    for p in range(blocks):
+        step(p, 1, approx.at[p])
     for copy in stores:
         copy.wait()
     for writes, copies in bank_stores:
@@ -483,32 +490,31 @@
                 copy.wait()
 
 
-def finish(positions, left, outs, place, owners, own_v, other_v, own_f, other_f, own_c, other_c, shapes, mm, mw):
-    n, rank, width = own_v.shape
-    matrices, rows, cols = shapes[0][1:]
+def finish(place, owners, v, f, other_c, made, shapes, mm, mw, mo, wo):
+    blocks, rank, width = v.shape
+    rows = other_c[0].shape[1]
     slots, head = mm.shape[:2]
-    later = len(outs) > 0
-    inputs = 12 + len(left)
-    first = [] if later else [pltpu.VMEM((2, rows, 6 * rank), jnp.bfloat16)]
+    block = pltpu.VMEM((blocks, rows, width), f32)
+    rows_of_slots = pltpu.VMEM((blocks, 2, slots, head, width), f32)
     return call(
-        functools.partial(finish_kernel, positions=positions, head=head, later=later),
-        f"finish{positions[0]}",
-        [SMEM, SMEM] + [VMEM] * (10 + len(left)) + [ANY] * len(outs),
-        [ANY] * 3 + [VMEM] * len(first),
-        [pltpu.HBM(s, f32) for s in shapes] + first,
-        (place, owners, own_v, other_v, own_f, other_f, *own_c, *other_c, mm, mw, *left, *outs),
-        mib=4 + 5 * n,
-        flops=2 * n * matrices * rows * width * 6 * rank,
-        nbytes=4 * n * width * (matrices * rows + 4 * slots * head),
+        functools.partial(finish_kernel, head=head),
+        "finish",
+        [SMEM, SMEM] + [VMEM] * 8 + [ANY] * 2,
+        [ANY] * 3,
+        [pltpu.HBM(shape, f32) for shape in shapes],
+        (place, owners, v, f, *other_c, *made, mm, mw, mo, wo),
+        mib=20,
+        flops=2 * blocks * rows * width * 6 * rank,
+        nbytes=8 * blocks * rows * width,
         scratch=[
-            pltpu.VMEM((n, 2, rows, width), f32),
-            pltpu.VMEM((n, 2, rows, width), f32),
-            pltpu.VMEM((n, 2, slots, head, width), f32),
-            pltpu.VMEM((n, 2, slots, head, width), f32),
-            pltpu.SemaphoreType.DMA((n, 2)),
-            pltpu.SemaphoreType.DMA((n, 2, slots, 2)),
+            block,
+            block,
+            rows_of_slots,
+            rows_of_slots,
+            pltpu.SemaphoreType.DMA((blocks, 2)),
+            pltpu.SemaphoreType.DMA((blocks, 2, slots, 2)),
         ],
-        aliases={inputs + i: i for i in range(len(outs))},
+        aliases={10: 1, 11: 2},
     )
 
 
@@ -603,15 +609,15 @@
             terms[p ^ (1 << stage)].append((arrived, i))
 
     rest = [p for p in range(blocks) if p & 3 == 1]
-    pending = [send(rest, 0)]
 
     own_p = own_factor(later, own_back, back, own_part, warm_start, vec_grads, blocks)
     packed = own_p + exchange(other_p, "core")
+    pending = [send(rest, 0, (packed,))]
     land(*ahead)
     goes = [p for p in range(blocks) if p & 3 == 2]
-    packed, mm, mw, go = hop(
+    packed, mm, mw, mo, wo, go = hop(
         packed, "plane", bits - 1,
-        lambda *x: [*banks(*x), fold([terms[p] for p in goes])], mat_momentum, mat_weights,
+        lambda *x: [*banks(place, owners, *x, head_items), fold([terms[p] for p in goes])], mat_momentum, mat_weights,
     )
     pending.append((goes, 1, exchange(go, "plane", 1)))
     for stage in range(2, bits):
@@ -650,29 +656,25 @@
         packed, exchange(packed, "core"),
     )
     (v,) = small_call(functools.partial(lower_kernel, count=count), "lower", [(rank, width)], u, kept_sum)
-    def second(a, u):
-        (begun,) = small_call(functools.partial(second_begin_kernel, rows=rows), "root2a", [state], a, u)
-        return small_call(
-            functools.partial(second_end_kernel, rows=rows), "root2b", [(rank, lanes(rows + rank))], begun, a, u
-        )
-
-    v, own_f = hop(v, "depth", depth, second, first_root, u)
-
-    shapes = [errors.shape, mat_momentum.shape, mat_weights.shape]
-    swapped = exchange(jnp.concatenate([v, own_f], axis=1), "core")
-    other_v, other_f = swapped[None, :, :width], swapped[:, width:]
-    v = v[None]
+    v, second_state = hop(
+        v, "depth", depth,
+        lambda *x: small_call(functools.partial(second_begin_kernel, rows=rows), "root2a", [state], *x),
+        first_root, u,
+    )
+
+    v, *tied = lax.optimization_barrier((v[None], second_state, first_root, u))
     arrived = {p: exchange(v, "place", p) for p in rounds(blocks)}
     arrived = [arrived[p] for p in range(1, blocks)]
-    *outs, left = finish(
-        [0], (), (), place, owners, v, other_v, own_f, other_f, own_c, other_c, shapes, mm, mw
-    )
-    *arrived, left = lax.optimization_barrier((*arrived, left))
-    v = jnp.concatenate(arrived, axis=0)
+    (own_f,) = small_call(
+        functools.partial(second_end_kernel, rows=rows), "root2b", [(rank, lanes(rows + rank))], *tied
+    )
+    other_f = exchange(own_f, "core")
+    arrived, own_f = lax.optimization_barrier((arrived, own_f))
+    v = jnp.concatenate([v, *arrived], axis=0)
     other_v = exchange(v, "core")
-    others = list(range(1, blocks))
-    left = (left, *ready(others, v, own_f, own_c, left, blocks))
-    outs = finish(others, left, outs, place, owners, v, other_v, own_f, other_f, own_c, other_c, shapes, mm, mw)
+    made = ready(v, own_f, own_c)
+    shapes = [errors.shape, mat_momentum.shape, mat_weights.shape]
+    outs = finish(place, owners, other_v, other_f, other_c, made, shapes, mm, mw, mo, wo)
     new_errors, mat_momentum_out, mat_weights_out = outs
     return (new_errors, mat_momentum_out, mat_weights_out, vec_momentum_out, vec_weights_out)
 

time: 79.4 us -> 79.1 us (level)
    pallas_call x20 -> x19, Pallas kernels: 29.7 us -> 29.3 us  [call(): pl.pallas_call(kernel, in_specs=in_specs, out_specs=out_specs, out_shape=...]
  transfers between devices with their start and end apart: 29 -> 29, of which waited for: 11 -> 13; matrix products, arithmetic and copies ran while one was open for 0% -> 0% of each run, Pallas kernels for 28% -> 27%
where the time goes in v9:
time: 79.1 us; the launch traced here: 78.9 us
  starting transfers between devices  30.4 us (38%)
  Pallas kernels  29.3 us (37%)
  waiting for transfers between devices  18 us (23%)
  between operations  0.91 us (1%)
    ppermute x29, starting transfers between devices, exchange(): return lax.ppermute(a, ('rep', 'grp'), pairs)  30.4 us
    pallas_call x19, Pallas kernels, call(): pl.pallas_call(kernel, in_specs=in_specs, out_specs=out_specs, out_shape=...  29.3 us
    ppermute x29, waiting for transfers between devices, exchange(): return lax.ppermute(a, ('rep', 'grp'), pairs)  18 us
  transfers between devices with their start and end apart: 29, of which 13 were waited for; matrix products, arithmetic and copies ran while one was open for 0% of the time, Pallas kernels for 27%

profile of v9, /device:TPU:0, one launch (start us, length us, event | category | flops | bytes accessed | tf_op | source)
XLA Modules:
  0.0 78.9 jit_solution(7461866257237175354)
XLA Ops:
  0.7 0.1 pad_add_fusion.place
  0.7 2.8 %other0.1 = (f32[1,320,512]{2,1,0:T(8,128)S(1)}, f32[3,320,512]{2,1,0:T(8,128)S(1)}) custom-call(s32[3]{0:T(128)S(1)} %pad_add_fusion.place, bf16[1,2,320,2048]{3,2,1,0:T(8,128)(2,1)} %g_hbm.5, f32[1,2,320,2048]{3,2,1,0:T(8,128)} %e_hbm.5), custom_call_target="tpu_custom_call" | custom-call | flops 1 | bytes 1 | tf_op jit(solution)/shard_map/other0/pallas_call | solution.py:71
  3.5 0.0 copy-start
  3.5 0.5 collective-permute-start
  4.0 1.8 %own0.1.refs_0_.refs_4_.c_front = f32[1,320,512]{2,1,0:T(8,128)S(1)} custom-call(s32[3]{0:T(128)S(1)} %pad_add_fusion.place, bf16[1,2,320,2048]{3,2,1,0:T(8,128)(2,1)} %g_hbm.5, f32[1,2,320,2048]{3,2,1,0:T(8,128)} %e_hbm.5), custom_call_target="tpu_custom_call" | custom-call | flops 1 | bytes 1 | tf_op jit(solution)/shard_map/own0/pallas_call | solution.py:71
  5.9 0.1 fold.4
  6.0 0.3 collective-permute-start.3
  6.3 2.7 %collective-permute-start.4 = (f32[1,320,512]{2,1,0:T(8,128)S(1)}, f32[1,320,512]{2,1,0:T(8,128)S(1)}, u32[]{:S(2)}, u32[]{:S(2)}) collective-permute-start(f32[1,320,512]{2,1,0:T(8,128)S(1)} %fold.4), channel_id=1, source_target_pairs={{0,8},{1,9},{2,10},{3,11},{4,20},{5,21},{6,22},{7,23},{8,0},{9,1},... | collective-permute-start | bytes 1966088 | tf_op jit(solution)/shard_map/ppermute | solution.py:555
  9.0 3.7 %own2.1 = (f32[3,320,512]{2,1,0:T(8,128)S(1)}, f32[96,128]{1,0:T(8,128)S(1)}, f32[32,320]{1,0:T(8,128)S(1)}) custom-call(s32[3]{0:T(128)S(1)} %pad_add_fusion.place, bf16[1,2,320,2048]{3,2,1,0:T(8,128)(2,1)} %g_hbm.5, f32[1,2,320,2048]{3,2,1,0:T(8,128)} %e_hbm.5, f32[2,32,2048]{2,1,0:T(8,128)S(1)} %copy-done, f32[1,2,2048]{2,1,0:T(2,128)S(1)} %copy-done.1, ...), custom_call_target="tpu_custom_call" | custom-call | flops 1 | bytes 1 | tf_op jit(solution)/shard_map/own2/pallas_call | solution.py:71
  12.7 0.1 collective-permute-start.1
  12.8 1.4 %factor.1 = f32[96,128]{1,0:T(8,128)S(1)} custom-call(s32[3]{0:T(128)S(1)} %pad_add_fusion.place, f32[2,32,2048]{2,1,0:T(8,128)S(1)} %copy-done, f32[1,2,2048]{2,1,0:T(2,128)S(1)} %copy-done.1, f32[3,320,512]{2,1,0:T(8,128)S(1)} %get-tuple-element.91.part.refs_0_.c_back, f32[32,320]{1,0:T(8,128)S(1)} %get-tuple-element.79.before), custom_call_target="tpu_custom_call" | custom-call | flops 1 | bytes 1 | tf_op jit(solution)/shard_map/factor/pallas_call | solution.py:71
  14.3 0.0 collective-permute-done.1
  14.3 0.1 fold.6
  14.4 1.6 %collective-permute-start.8 = (f32[1,320,512]{2,1,0:T(8,128)S(1)}, f32[1,320,512]{2,1,0:T(8,128)S(1)}, u32[]{:S(2)}, u32[]{:S(2)}) collective-permute-start(f32[1,320,512]{2,1,0:T(8,128)S(1)} %fold.6), channel_id=1, source_target_pairs={{0,8},{1,9},{2,10},{3,11},{4,20},{5,21},{6,22},{7,23},{8,0},{9,1},... | collective-permute-start | bytes 1966088 | tf_op jit(solution)/shard_map/ppermute | solution.py:555
  16.0 0.6 collective-permute-start.2
  16.5 3.1 %banks.1 = (f32[2,64,2048]{2,1,0:T(8,128)S(1)}, f32[2,64,2048]{2,1,0:T(8,128)S(1)}, f32[2,64,2048]{2,1,0:T(8,128)}, f32[2,64,2048]{2,1,0:T(8,128)}) custom-call(s32[3]{0:T(128)S(1)} %pad_add_fusion.place, s32[12]{0:T(128)S(1)} %copy-done.4, f32[2,64,2048]{2,1,0:T(8,128)} %mm_hbm, f32[2,64,2048]{2,1,0:T(8,128)} %mw_hbm), custom_call_target="tpu_custom_call" | custom-call | flops 1 | bytes 2097152 | tf_op jit(solution)/shard_map/banks/pallas_call | solution.py:71
  19.7 0.1 fold.5
  19.8 0.9 %collective-permute-done.2 = f32[96,128]{1,0:T(8,128)S(1)} collective-permute-done((f32[96,128]{1,0:T(8,128)S(1)}, f32[96,128]{1,0:T(8,128)S(1)}, u32[]{:S(2)}, u32[]{:S(2)}) %collective-permute-start.2) | collective-permute-done | bytes 49184 | tf_op jit(solution)/shard_map/ppermute | solution.py:555
  20.6 0.7 collective-permute-start.10
  21.3 2.9 %collective-permute-start.7 = (f32[96,128]{1,0:T(8,128)S(1)}, f32[96,128]{1,0:T(8,128)S(1)}, u32[]{:S(2)}, u32[]{:S(2)}) collective-permute-start(f32[96,128]{1,0:T(8,128)S(1)} %add.65), channel_id=1, source_target_pairs={{0,2},{1,3},{2,0},{3,1},{4,6},{5,7},{6,4},{7,5},{8,10},{9,11},{10,... | collective-permute-start | bytes 147464 | tf_op jit(solution)/shard_map/ppermute | solution.py:555
  24.3 1.4 %collective-permute-start.6 = (f32[96,128]{1,0:T(8,128)S(1)}, f32[96,128]{1,0:T(8,128)S(1)}, u32[]{:S(2)}, u32[]{:S(2)}) collective-permute-start(f32[96,128]{1,0:T(8,128)S(1)} %add.65), channel_id=1, source_target_pairs={{0,3},{1,2},{2,1},{3,0},{4,7},{5,6},{6,5},{7,4},{8,11},{9,10},{10,... | collective-permute-start | bytes 147464 | tf_op jit(solution)/shard_map/ppermute | solution.py:555
  25.6 0.2 collective-permute-start.5
  25.8 1.0 %collective-permute-done.7 = f32[96,128]{1,0:T(8,128)S(1)} collective-permute-done((f32[96,128]{1,0:T(8,128)S(1)}, f32[96,128]{1,0:T(8,128)S(1)}, u32[]{:S(2)}, u32[]{:S(2)}) %collective-permute-start.7) | collective-permute-done | bytes 49184 | tf_op jit(solution)/shard_map/ppermute | solution.py:555
  26.8 3.4 %collective-permute-done.6 = f32[96,128]{1,0:T(8,128)S(1)} collective-permute-done((f32[96,128]{1,0:T(8,128)S(1)}, f32[96,128]{1,0:T(8,128)S(1)}, u32[]{:S(2)}, u32[]{:S(2)}) %collective-permute-start.6) | collective-permute-done | bytes 49184 | tf_op jit(solution)/shard_map/ppermute | solution.py:555
  30.3 1.1 %collective-permute-start.9 = (f32[96,128]{1,0:T(8,128)S(1)}, f32[96,128]{1,0:T(8,128)S(1)}, u32[]{:S(2)}, u32[]{:S(2)}) collective-permute-start(f32[96,128]{1,0:T(8,128)S(1)} %add_add_fusion.1), channel_id=1, source_target_pairs={{0,8},{1,9},{2,10},{3,11},{4,20},{5,21},{6,22},{7,23},{8,0},{9,1},... | collective-permute-start | bytes 147464 | tf_op jit(solution)/shard_map/ppermute | solution.py:555
  31.4 0.1 fold.7.refs_0_
  31.5 2.9 %collective-permute-done.9 = f32[96,128]{1,0:T(8,128)S(1)} collective-permute-done((f32[96,128]{1,0:T(8,128)S(1)}, f32[96,128]{1,0:T(8,128)S(1)}, u32[]{:S(2)}, u32[]{:S(2)}) %collective-permute-start.9) | collective-permute-done | bytes 49184 | tf_op jit(solution)/shard_map/ppermute | solution.py:555
  34.4 0.5 project.1
  34.9 1.5 %collective-permute-start.13 = (f32[32,512]{1,0:T(8,128)S(1)}, f32[32,512]{1,0:T(8,128)S(1)}, u32[]{:S(2)}, u32[]{:S(2)}) collective-permute-start(f32[32,512]{1,0:T(8,128)S(1)} %get-tuple-element.98), channel_id=1, source_target_pairs={{0,2},{1,3},{2,0},{3,1},{4,6},{5,7},{6,4},{7,5},{8,10},{9,11},{10,... | collective-permute-start | bytes 196616 | tf_op jit(solution)/shard_map/ppermute | solution.py:555
  36.4 1.3 %collective-permute-start.12 = (f32[32,512]{1,0:T(8,128)S(1)}, f32[32,512]{1,0:T(8,128)S(1)}, u32[]{:S(2)}, u32[]{:S(2)}) collective-permute-start(f32[32,512]{1,0:T(8,128)S(1)} %get-tuple-element.98), channel_id=1, source_target_pairs={{0,3},{1,2},{2,1},{3,0},{4,7},{5,6},{6,5},{7,4},{8,11},{9,10},{10,... | collective-permute-start | bytes 196616 | tf_op jit(solution)/shard_map/ppermute | solution.py:555
  37.7 0.8 collective-permute-start.11
  38.5 2.1 %root1a.1.state = f32[3,32,32]{2,1,0:T(8,128)S(1)} custom-call(f32[96,128]{1,0:T(8,128)S(1)} %add.69.x_ref.own_ref), custom_call_target="tpu_custom_call" | custom-call | flops 12000000 | bytes 49152 | tf_op jit(solution)/shard_map/root1a/pallas_call | solution.py:71
  40.6 2.2 %collective-permute-done.13 = f32[32,512]{1,0:T(8,128)S(1)} collective-permute-done((f32[32,512]{1,0:T(8,128)S(1)}, f32[32,512]{1,0:T(8,128)S(1)}, u32[]{:S(2)}, u32[]{:S(2)}) %collective-permute-start.13) | collective-permute-done | bytes 65568 | tf_op jit(solution)/shard_map/ppermute | solution.py:555
  42.8 0.3 collective-permute-done.11
  43.1 0.7 lift.1
  43.8 2.0 %collective-permute-start.16 = (f32[80,128]{1,0:T(8,128)S(1)}, f32[80,128]{1,0:T(8,128)S(1)}, u32[]{:S(2)}, u32[]{:S(2)}) collective-permute-start(f32[80,128]{1,0:T(8,128)S(1)} %lift.1), channel_id=1, source_target_pairs={{0,2},{1,3},{2,0},{3,1},{4,6},{5,7},{6,4},{7,5},{8,10},{9,11},{10,... | collective-permute-start | bytes 122888 | tf_op jit(solution)/shard_map/ppermute | solution.py:555
  45.9 1.3 %collective-permute-start.15 = (f32[80,128]{1,0:T(8,128)S(1)}, f32[80,128]{1,0:T(8,128)S(1)}, u32[]{:S(2)}, u32[]{:S(2)}) collective-permute-start(f32[80,128]{1,0:T(8,128)S(1)} %lift.1), channel_id=1, source_target_pairs={{0,3},{1,2},{2,1},{3,0},{4,7},{5,6},{6,5},{7,4},{8,11},{9,10},{10,... | collective-permute-start | bytes 122888 | tf_op jit(solution)/shard_map/ppermute | solution.py:555
  47.2 0.2 collective-permute-start.14
  47.4 1.9 %root1b.1.a_ref = f32[32,32]{1,0:T(8,128)S(1)} custom-call(f32[3,32,32]{2,1,0:T(8,128)S(1)} %root1a.1.state), custom_call_target="tpu_custom_call" | custom-call | flops 12000000 | bytes 12288 | tf_op jit(solution)/shard_map/root1b/pallas_call | solution.py:71
  49.3 2.4 %collective-permute-done.15 = f32[80,128]{1,0:T(8,128)S(1)} collective-permute-done((f32[80,128]{1,0:T(8,128)S(1)}, f32[80,128]{1,0:T(8,128)S(1)}, u32[]{:S(2)}, u32[]{:S(2)}) %collective-permute-start.15) | collective-permute-done | bytes 40992 | tf_op jit(solution)/shard_map/ppermute | solution.py:555
  51.7 1.6 %collective-permute-start.20 = (f32[80,128]{1,0:T(8,128)S(1)}, f32[80,128]{1,0:T(8,128)S(1)}, u32[]{:S(2)}, u32[]{:S(2)}) collective-permute-start(f32[80,128]{1,0:T(8,128)S(1)} %add_add_fusion.3), channel_id=1, source_target_pairs={{0,16},{1,17},{2,18},{3,19},{4,12},{5,13},{6,14},{7,15},{8,24},{9,... | collective-permute-start | bytes 122888 | tf_op jit(solution)/shard_map/ppermute | solution.py:555
  53.3 2.0 %collective-permute-start.19 = (f32[80,128]{1,0:T(8,128)S(1)}, f32[80,128]{1,0:T(8,128)S(1)}, u32[]{:S(2)}, u32[]{:S(2)}) collective-permute-start(f32[80,128]{1,0:T(8,128)S(1)} %add_add_fusion.3), channel_id=1, source_target_pairs={{0,24},{1,25},{2,26},{3,27},{4,28},{5,29},{6,30},{7,31},{8,16},{9,... | collective-permute-start | bytes 122888 | tf_op jit(solution)/shard_map/ppermute | solution.py:555
  55.3 1.2 %gains.1 = (f32[2,2048]{1,0:T(2,128)}, f32[2,2048]{1,0:T(2,128)}) custom-call(s32[3]{0:T(128)S(1)} %pad_add_fusion.place, s32[12]{0:T(128)S(1)} %copy-done.4, f32[96,128]{1,0:T(8,128)S(1)} %add.69.x_ref.own_ref, f32[96,128]{1,0:T(8,128)S(1)} %collective-permute-done.17.other_ref, f32[2,2048]{1,0:T(2,128)S(1)} %copy-done.2, f32[2,2048]{1,0:T(2,128)S(1)} %copy-done.3), custom_call_target="tpu_custom_call" | custom-call | flops 40960 | bytes 65536 | tf_op jit(solution)/shard_map/gains/pallas_call | solution.py:71
  56.5 0.2 collective-permute-done.20
  56.6 1.6 %collective-permute-done.19 = f32[80,128]{1,0:T(8,128)S(1)} collective-permute-done((f32[80,128]{1,0:T(8,128)S(1)}, f32[80,128]{1,0:T(8,128)S(1)}, u32[]{:S(2)}, u32[]{:S(2)}) %collective-permute-start.19) | collective-permute-done | bytes 40992 | tf_op jit(solution)/shard_map/ppermute | solution.py:555
  58.2 1.1 %collective-permute-done.18 = f32[80,128]{1,0:T(8,128)S(1)} collective-permute-done((f32[80,128]{1,0:T(8,128)S(1)}, f32[80,128]{1,0:T(8,128)S(1)}, u32[]{:S(2)}, u32[]{:S(2)}) %collective-permute-start.18) | collective-permute-done | bytes 40992 | tf_op jit(solution)/shard_map/ppermute | solution.py:555
  59.3 0.5 lower.1
  59.7 1.0 %collective-permute-start.23 = (f32[32,512]{1,0:T(8,128)S(1)}, f32[32,512]{1,0:T(8,128)S(1)}, u32[]{:S(2)}, u32[]{:S(2)}) collective-permute-start(f32[32,512]{1,0:T(8,128)S(1)} %lower.1), channel_id=1, source_target_pairs={{0,2},{1,3},{2,0},{3,1},{4,6},{5,7},{6,4},{7,5},{8,10},{9,11},{10,... | collective-permute-start | bytes 196616 | tf_op jit(solution)/shard_map/ppermute | solution.py:555
  60.8 1.1 %collective-permute-start.22 = (f32[32,512]{1,0:T(8,128)S(1)}, f32[32,512]{1,0:T(8,128)S(1)}, u32[]{:S(2)}, u32[]{:S(2)}) collective-permute-start(f32[32,512]{1,0:T(8,128)S(1)} %lower.1), channel_id=1, source_target_pairs={{0,3},{1,2},{2,1},{3,0},{4,7},{5,6},{6,5},{7,4},{8,11},{9,10},{10,... | collective-permute-start | bytes 196616 | tf_op jit(solution)/shard_map/ppermute | solution.py:555
  61.9 1.4 %collective-permute-start.21 = (f32[32,512]{1,0:T(8,128)S(1)}, f32[32,512]{1,0:T(8,128)S(1)}, u32[]{:S(2)}, u32[]{:S(2)}) collective-permute-start(f32[32,512]{1,0:T(8,128)S(1)} %lower.1), channel_id=1, source_target_pairs={{0,1},{1,0},{2,3},{3,2},{4,5},{5,4},{6,7},{7,6},{8,9},{9,8},{10,11... | collective-permute-start | bytes 196616 | tf_op jit(solution)/shard_map/ppermute | solution.py:555
  63.3 2.4 %root2a.1.state = f32[3,32,32]{2,1,0:T(8,128)S(1)} custom-call(f32[32,32]{1,0:T(8,128)S(1)} %root1b.1.a_ref, f32[80,128]{1,0:T(8,128)S(1)} %add_add_fusion.2.u_ref), custom_call_target="tpu_custom_call" | custom-call | flops 12000000 | bytes 45056 | tf_op jit(solution)/shard_map/root2a/pallas_call | solution.py:71
  65.7 0.0 collective-permute-done.23
  65.7 1.1 %collective-permute-done.22 = f32[32,512]{1,0:T(8,128)S(1)} collective-permute-done((f32[32,512]{1,0:T(8,128)S(1)}, f32[32,512]{1,0:T(8,128)S(1)}, u32[]{:S(2)}, u32[]{:S(2)}) %collective-permute-start.22) | collective-permute-done | bytes 65568 | tf_op jit(solution)/shard_map/ppermute | solution.py:555
  66.9 1.5 %collective-permute-start.26 = (f32[1,32,512]{2,1,0:T(8,128)S(1)}, f32[1,32,512]{2,1,0:T(8,128)S(1)}, u32[]{:S(2)}, u32[]{:S(2)}) collective-permute-start(f32[1,32,512]{2,1,0:T(8,128)S(1)} %add_bitcast_fusion), channel_id=1, source_target_pairs={{0,24},{1,25},{2,26},{3,27},{4,28},{5,29},{6,30},{7,31},{8,16},{9,... | collective-permute-start | bytes 196616 | tf_op jit(solution)/shard_map/ppermute | solution.py:555
  68.3 1.0 %collective-permute-start.25 = (f32[1,32,512]{2,1,0:T(8,128)S(1)}, f32[1,32,512]{2,1,0:T(8,128)S(1)}, u32[]{:S(2)}, u32[]{:S(2)}) collective-permute-start(f32[1,32,512]{2,1,0:T(8,128)S(1)} %add_bitcast_fusion), channel_id=1, source_target_pairs={{0,16},{1,17},{2,18},{3,19},{4,12},{5,13},{6,14},{7,15},{8,24},{9,... | collective-permute-start | bytes 196616 | tf_op jit(solution)/shard_map/ppermute | solution.py:555
  69.4 1.1 %collective-permute-start.24 = (f32[1,32,512]{2,1,0:T(8,128)S(1)}, f32[1,32,512]{2,1,0:T(8,128)S(1)}, u32[]{:S(2)}, u32[]{:S(2)}) collective-permute-start(f32[1,32,512]{2,1,0:T(8,128)S(1)} %add_bitcast_fusion), channel_id=1, source_target_pairs={{0,8},{1,9},{2,10},{3,11},{4,20},{5,21},{6,22},{7,23},{8,0},{9,1},... | collective-permute-start | bytes 196616 | tf_op jit(solution)/shard_map/ppermute | solution.py:555
  70.4 2.3 %root2b.1.f_ref = f32[32,384]{1,0:T(8,128)S(1)} custom-call(f32[3,32,32]{2,1,0:T(8,128)S(1)} %root2a.1.state, f32[32,32]{1,0:T(8,128)S(1)} %root1b.1.a_ref, f32[80,128]{1,0:T(8,128)S(1)} %add_add_fusion.2.u_ref), custom_call_target="tpu_custom_call" | custom-call | flops 12000000 | bytes 57344 | tf_op jit(solution)/shard_map/root2b/pallas_call | solution.py:71
  72.8 0.0 collective-permute-done.25
  72.8 0.8 %collective-permute-done.24 = f32[1,32,512]{2,1,0:T(8,128)S(1)} collective-permute-done((f32[1,32,512]{2,1,0:T(8,128)S(1)}, f32[1,32,512]{2,1,0:T(8,128)S(1)}, u32[]{:S(2)}, u32[]{:S(2)}) %collective-permute-start.24) | collective-permute-done | bytes 65568 | tf_op jit(solution)/shard_map/ppermute | solution.py:555
  73.7 0.1 collective-permute-start.27
  73.7 0.5 collective-permute-start.28
  74.2 0.9 %ready.1 = (f32[4,320,512]{2,1,0:T(8,128)S(1)}, f32[4,320,512]{2,1,0:T(8,128)S(1)}) custom-call(f32[4,32,512]{2,1,0:T(8,128)S(1)} %constant_dynamic-update-slice_fusion.v_ref, f32[32,384]{1,0:T(8,128)S(1)} %root2b.1.f_ref, f32[1,320,512]{2,1,0:T(8,128)S(1)} %own0.1.refs_0_.refs_4_.c_front, f32[3,320,512]{2,1,0:T(8,128)S(1)} %get-tuple-element.91.part.refs_0_.c_back), custom_call_target="tpu_custom_call" | custom-call | flops 1 | bytes 1 | tf_op jit(solution)/shard_map/ready/pallas_call | solution.py:71
  75.1 0.2 collective-permute-done.28.f_ref
  75.3 3.6 %finish.1 = (f32[1,2,320,2048]{3,2,1,0:T(8,128)}, f32[2,64,2048]{2,1,0:T(8,128)}, f32[2,64,2048]{2,1,0:T(8,128)}) custom-call(s32[3]{0:T(128)S(1)} %pad_add_fusion.place, s32[12]{0:T(128)S(1)} %copy-done.4, f32[4,32,512]{2,1,0:T(8,128)S(1)} %collective-permute-done.27.v_ref, ...), custom_call_target="tpu_custom_call", output_to_operand_aliasing={{1}: (10, {}), {2}: (11, {})} | custom-call | flops 251658240 | bytes 5242880 | tf_op jit(solution)/shard_map/finish/pallas_call | solution.py:71
  (36 shorter events, 0.2 us)
Async XLA Ops:
  3.5 5.5 %copy-start = (f32[2,32,2048]{2,1,0:T(8,128)S(1)}, f32[2,32,2048]{2,1,0:T(8,128)}, u32[]{:S(2)}) copy-start(f32[2,32,2048]{2,1,0:T(8,128)} %w_ref.1) | copy-start | bytes 1572868
  3.5 5.5 %copy-start.1 = (f32[1,2,2048]{2,1,0:T(2,128)S(1)}, f32[1,2,2048]{2,1,0:T(2,128)}, u32[]{:S(2)}) copy-start(f32[1,2,2048]{2,1,0:T(2,128)} %vec_ref.1) | copy-start | bytes 49156
  3.5 2.3 %collective-permute-start = (f32[1,320,512]{2,1,0:T(8,128)S(1)}, f32[1,320,512]{2,1,0:T(8,128)S(1)}, u32[]{:S(2)}, u32[]{:S(2)}) collective-permute-start(f32[1,320,512]{2,1,0:T(8,128)S(1)} %get-tuple-element.75.refs_2_.c_front), channel_id=1, source_target_pairs={{0,4},{1,5},{2,6},{3,7},{4,0},{5,1},{6,2},{7,3},{8,12},{9,13},{10,... | collective-permute-start | bytes 1966088 | tf_op jit(solution)/shard_map/ppermute | solution.py:555
  6.0 8.4 %collective-permute-start.3 = (f32[3,320,512]{2,1,0:T(8,128)S(1)}, f32[3,320,512]{2,1,0:T(8,128)S(1)}, u32[]{:S(2)}, u32[]{:S(2)}) collective-permute-start(f32[3,320,512]{2,1,0:T(8,128)S(1)} %get-tuple-element.88.refs_3_.c_back), channel_id=1, source_target_pairs={{0,4},{1,5},{2,6},{3,7},{4,0},{5,1},{6,2},{7,3},{8,12},{9,13},{10,... | collective-permute-start | bytes 5898248 | tf_op jit(solution)/shard_map/ppermute | solution.py:555
  6.3 13.4 %collective-permute-start.4 = (f32[1,320,512]{2,1,0:T(8,128)S(1)}, f32[1,320,512]{2,1,0:T(8,128)S(1)}, u32[]{:S(2)}, u32[]{:S(2)}) collective-permute-start(f32[1,320,512]{2,1,0:T(8,128)S(1)} %fold.4), channel_id=1, source_target_pairs={{0,8},{1,9},{2,10},{3,11},{4,20},{5,21},{6,22},{7,23},{8,0},{9,1},... | collective-permute-start | bytes 1966088 | tf_op jit(solution)/shard_map/ppermute | solution.py:555
  12.7 1.5 %collective-permute-start.1 = (f32[96,128]{1,0:T(8,128)S(1)}, f32[96,128]{1,0:T(8,128)S(1)}, u32[]{:S(2)}, u32[]{:S(2)}) collective-permute-start(f32[96,128]{1,0:T(8,128)S(1)} %get-tuple-element.80), channel_id=1, source_target_pairs={{0,4},{1,5},{2,6},{3,7},{4,0},{5,1},{6,2},{7,3},{8,12},{9,13},{10,... | collective-permute-start | bytes 147464 | tf_op jit(solution)/shard_map/ppermute | solution.py:555
  14.3 2.3 %copy-start.4 = (s32[12]{0:T(128)S(1)}, s32[12]{0:T(128)}, u32[]{:S(2)}) copy-start(s32[12]{0:T(128)} %owners.5) | copy-start | bytes 148
  14.4 15.8 %collective-permute-start.8 = (f32[1,320,512]{2,1,0:T(8,128)S(1)}, f32[1,320,512]{2,1,0:T(8,128)S(1)}, u32[]{:S(2)}, u32[]{:S(2)}) collective-permute-start(f32[1,320,512]{2,1,0:T(8,128)S(1)} %fold.6), channel_id=1, source_target_pairs={{0,8},{1,9},{2,10},{3,11},{4,20},{5,21},{6,22},{7,23},{8,0},{9,1},... | collective-permute-start | bytes 1966088 | tf_op jit(solution)/shard_map/ppermute | solution.py:555
  16.0 4.7 %collective-permute-start.2 = (f32[96,128]{1,0:T(8,128)S(1)}, f32[96,128]{1,0:T(8,128)S(1)}, u32[]{:S(2)}, u32[]{:S(2)}) collective-permute-start(f32[96,128]{1,0:T(8,128)S(1)} %add.64.refs_2_), channel_id=1, source_target_pairs={{0,16},{1,17},{2,18},{3,19},{4,12},{5,13},{6,14},{7,15},{8,24},{9,... | collective-permute-start | bytes 147464 | tf_op jit(solution)/shard_map/ppermute | solution.py:555
  20.6 13.8 %collective-permute-start.10 = (f32[1,320,512]{2,1,0:T(8,128)S(1)}, f32[1,320,512]{2,1,0:T(8,128)S(1)}, u32[]{:S(2)}, u32[]{:S(2)}) collective-permute-start(f32[1,320,512]{2,1,0:T(8,128)S(1)} %fold.5), channel_id=1, source_target_pairs={{0,16},{1,17},{2,18},{3,19},{4,12},{5,13},{6,14},{7,15},{8,24},{9,... | collective-permute-start | bytes 1966088 | tf_op jit(solution)/shard_map/ppermute | solution.py:555
  21.3 5.5 %collective-permute-start.7 = (f32[96,128]{1,0:T(8,128)S(1)}, f32[96,128]{1,0:T(8,128)S(1)}, u32[]{:S(2)}, u32[]{:S(2)}) collective-permute-start(f32[96,128]{1,0:T(8,128)S(1)} %add.65), channel_id=1, source_target_pairs={{0,2},{1,3},{2,0},{3,1},{4,6},{5,7},{6,4},{7,5},{8,10},{9,11},{10,... | collective-permute-start | bytes 147464 | tf_op jit(solution)/shard_map/ppermute | solution.py:555
  24.3 6.0 %collective-permute-start.6 = (f32[96,128]{1,0:T(8,128)S(1)}, f32[96,128]{1,0:T(8,128)S(1)}, u32[]{:S(2)}, u32[]{:S(2)}) collective-permute-start(f32[96,128]{1,0:T(8,128)S(1)} %add.65), channel_id=1, source_target_pairs={{0,3},{1,2},{2,1},{3,0},{4,7},{5,6},{6,5},{7,4},{8,11},{9,10},{10,... | collective-permute-start | bytes 147464 | tf_op jit(solution)/shard_map/ppermute | solution.py:555
  25.6 4.6 %collective-permute-start.5 = (f32[96,128]{1,0:T(8,128)S(1)}, f32[96,128]{1,0:T(8,128)S(1)}, u32[]{:S(2)}, u32[]{:S(2)}) collective-permute-start(f32[96,128]{1,0:T(8,128)S(1)} %add.65), channel_id=1, source_target_pairs={{0,1},{1,0},{2,3},{3,2},{4,5},{5,4},{6,7},{7,6},{8,9},{9,8},{10,11... | collective-permute-start | bytes 147464 | tf_op jit(solution)/shard_map/ppermute | solution.py:555
  30.3 4.2 %collective-permute-start.9 = (f32[96,128]{1,0:T(8,128)S(1)}, f32[96,128]{1,0:T(8,128)S(1)}, u32[]{:S(2)}, u32[]{:S(2)}) collective-permute-start(f32[96,128]{1,0:T(8,128)S(1)} %add_add_fusion.1), channel_id=1, source_target_pairs={{0,8},{1,9},{2,10},{3,11},{4,20},{5,21},{6,22},{7,23},{8,0},{9,1},... | collective-permute-start | bytes 147464 | tf_op jit(solution)/shard_map/ppermute | solution.py:555
  31.5 23.8 %copy-start.2 = (f32[2,2048]{1,0:T(2,128)S(1)}, f32[2,2048]{1,0:T(2,128)}, u32[]{:S(2)}) copy-start(f32[2,2048]{1,0:T(2,128)} %mv_ref.1) | copy-start | bytes 49156
  31.5 23.8 %copy-start.3 = (f32[2,2048]{1,0:T(2,128)S(1)}, f32[2,2048]{1,0:T(2,128)}, u32[]{:S(2)}) copy-start(f32[2,2048]{1,0:T(2,128)} %wv_ref.1) | copy-start | bytes 49156
  34.9 7.8 %collective-permute-start.13 = (f32[32,512]{1,0:T(8,128)S(1)}, f32[32,512]{1,0:T(8,128)S(1)}, u32[]{:S(2)}, u32[]{:S(2)}) collective-permute-start(f32[32,512]{1,0:T(8,128)S(1)} %get-tuple-element.98), channel_id=1, source_target_pairs={{0,2},{1,3},{2,0},{3,1},{4,6},{5,7},{6,4},{7,5},{8,10},{9,11},{10,... | collective-permute-start | bytes 196616 | tf_op jit(solution)/shard_map/ppermute | solution.py:555
  36.4 6.3 %collective-permute-start.12 = (f32[32,512]{1,0:T(8,128)S(1)}, f32[32,512]{1,0:T(8,128)S(1)}, u32[]{:S(2)}, u32[]{:S(2)}) collective-permute-start(f32[32,512]{1,0:T(8,128)S(1)} %get-tuple-element.98), channel_id=1, source_target_pairs={{0,3},{1,2},{2,1},{3,0},{4,7},{5,6},{6,5},{7,4},{8,11},{9,10},{10,... | collective-permute-start | bytes 196616 | tf_op jit(solution)/shard_map/ppermute | solution.py:555
  37.7 5.4 %collective-permute-start.11 = (f32[32,512]{1,0:T(8,128)S(1)}, f32[32,512]{1,0:T(8,128)S(1)}, u32[]{:S(2)}, u32[]{:S(2)}) collective-permute-start(f32[32,512]{1,0:T(8,128)S(1)} %get-tuple-element.98), channel_id=1, source_target_pairs={{0,1},{1,0},{2,3},{3,2},{4,5},{5,4},{6,7},{7,6},{8,9},{9,8},{10,11... | collective-permute-start | bytes 196616 | tf_op jit(solution)/shard_map/ppermute | solution.py:555
  43.8 5.5 %collective-permute-start.16 = (f32[80,128]{1,0:T(8,128)S(1)}, f32[80,128]{1,0:T(8,128)S(1)}, u32[]{:S(2)}, u32[]{:S(2)}) collective-permute-start(f32[80,128]{1,0:T(8,128)S(1)} %lift.1), channel_id=1, source_target_pairs={{0,2},{1,3},{2,0},{3,1},{4,6},{5,7},{6,4},{7,5},{8,10},{9,11},{10,... | collective-permute-start | bytes 122888 | tf_op jit(solution)/shard_map/ppermute | solution.py:555
  45.9 5.8 %collective-permute-start.15 = (f32[80,128]{1,0:T(8,128)S(1)}, f32[80,128]{1,0:T(8,128)S(1)}, u32[]{:S(2)}, u32[]{:S(2)}) collective-permute-start(f32[80,128]{1,0:T(8,128)S(1)} %lift.1), channel_id=1, source_target_pairs={{0,3},{1,2},{2,1},{3,0},{4,7},{5,6},{6,5},{7,4},{8,11},{9,10},{10,... | collective-permute-start | bytes 122888 | tf_op jit(solution)/shard_map/ppermute | solution.py:555
  47.2 4.5 %collective-permute-start.14 = (f32[80,128]{1,0:T(8,128)S(1)}, f32[80,128]{1,0:T(8,128)S(1)}, u32[]{:S(2)}, u32[]{:S(2)}) collective-permute-start(f32[80,128]{1,0:T(8,128)S(1)} %lift.1), channel_id=1, source_target_pairs={{0,1},{1,0},{2,3},{3,2},{4,5},{5,4},{6,7},{7,6},{8,9},{9,8},{10,11... | collective-permute-start | bytes 122888 | tf_op jit(solution)/shard_map/ppermute | solution.py:555
  47.4 4.3 %collective-permute-start.17 = (f32[96,128]{1,0:T(8,128)S(1)}, f32[96,128]{1,0:T(8,128)S(1)}, u32[]{:S(2)}, u32[]{:S(2)}) collective-permute-start(f32[96,128]{1,0:T(8,128)S(1)} %add.69.x_ref.own_ref), channel_id=1, source_target_pairs={{0,4},{1,5},{2,6},{3,7},{4,0},{5,1},{6,2},{7,3},{8,12},{9,13},{10,... | collective-permute-start | bytes 147464 | tf_op jit(solution)/shard_map/ppermute | solution.py:555
  51.7 4.9 %collective-permute-start.20 = (f32[80,128]{1,0:T(8,128)S(1)}, f32[80,128]{1,0:T(8,128)S(1)}, u32[]{:S(2)}, u32[]{:S(2)}) collective-permute-start(f32[80,128]{1,0:T(8,128)S(1)} %add_add_fusion.3), channel_id=1, source_target_pairs={{0,16},{1,17},{2,18},{3,19},{4,12},{5,13},{6,14},{7,15},{8,24},{9,... | collective-permute-start | bytes 122888 | tf_op jit(solution)/shard_map/ppermute | solution.py:555
  53.3 4.9 %collective-permute-start.19 = (f32[80,128]{1,0:T(8,128)S(1)}, f32[80,128]{1,0:T(8,128)S(1)}, u32[]{:S(2)}, u32[]{:S(2)}) collective-permute-start(f32[80,128]{1,0:T(8,128)S(1)} %add_add_fusion.3), channel_id=1, source_target_pairs={{0,24},{1,25},{2,26},{3,27},{4,28},{5,29},{6,30},{7,31},{8,16},{9,... | collective-permute-start | bytes 122888 | tf_op jit(solution)/shard_map/ppermute | solution.py:555
  55.2 4.0 %collective-permute-start.18 = (f32[80,128]{1,0:T(8,128)S(1)}, f32[80,128]{1,0:T(8,128)S(1)}, u32[]{:S(2)}, u32[]{:S(2)}) collective-permute-start(f32[80,128]{1,0:T(8,128)S(1)} %add_add_fusion.3), channel_id=1, source_target_pairs={{0,8},{1,9},{2,10},{3,11},{4,20},{5,21},{6,22},{7,23},{8,0},{9,1},... | collective-permute-start | bytes 122888 | tf_op jit(solution)/shard_map/ppermute | solution.py:555
  59.7 6.0 %collective-permute-start.23 = (f32[32,512]{1,0:T(8,128)S(1)}, f32[32,512]{1,0:T(8,128)S(1)}, u32[]{:S(2)}, u32[]{:S(2)}) collective-permute-start(f32[32,512]{1,0:T(8,128)S(1)} %lower.1), channel_id=1, source_target_pairs={{0,2},{1,3},{2,0},{3,1},{4,6},{5,7},{6,4},{7,5},{8,10},{9,11},{10,... | collective-permute-start | bytes 196616 | tf_op jit(solution)/shard_map/ppermute | solution.py:555
  60.8 6.1 %collective-permute-start.22 = (f32[32,512]{1,0:T(8,128)S(1)}, f32[32,512]{1,0:T(8,128)S(1)}, u32[]{:S(2)}, u32[]{:S(2)}) collective-permute-start(f32[32,512]{1,0:T(8,128)S(1)} %lower.1), channel_id=1, source_target_pairs={{0,3},{1,2},{2,1},{3,0},{4,7},{5,6},{6,5},{7,4},{8,11},{9,10},{10,... | collective-permute-start | bytes 196616 | tf_op jit(solution)/shard_map/ppermute | solution.py:555
  61.9 5.0 %collective-permute-start.21 = (f32[32,512]{1,0:T(8,128)S(1)}, f32[32,512]{1,0:T(8,128)S(1)}, u32[]{:S(2)}, u32[]{:S(2)}) collective-permute-start(f32[32,512]{1,0:T(8,128)S(1)} %lower.1), channel_id=1, source_target_pairs={{0,1},{1,0},{2,3},{3,2},{4,5},{5,4},{6,7},{7,6},{8,9},{9,8},{10,11... | collective-permute-start | bytes 196616 | tf_op jit(solution)/shard_map/ppermute | solution.py:555
  66.9 5.9 %collective-permute-start.26 = (f32[1,32,512]{2,1,0:T(8,128)S(1)}, f32[1,32,512]{2,1,0:T(8,128)S(1)}, u32[]{:S(2)}, u32[]{:S(2)}) collective-permute-start(f32[1,32,512]{2,1,0:T(8,128)S(1)} %add_bitcast_fusion), channel_id=1, source_target_pairs={{0,24},{1,25},{2,26},{3,27},{4,28},{5,29},{6,30},{7,31},{8,16},{9,... | collective-permute-start | bytes 196616 | tf_op jit(solution)/shard_map/ppermute | solution.py:555
  68.3 4.5 %collective-permute-start.25 = (f32[1,32,512]{2,1,0:T(8,128)S(1)}, f32[1,32,512]{2,1,0:T(8,128)S(1)}, u32[]{:S(2)}, u32[]{:S(2)}) collective-permute-start(f32[1,32,512]{2,1,0:T(8,128)S(1)} %add_bitcast_fusion), channel_id=1, source_target_pairs={{0,16},{1,17},{2,18},{3,19},{4,12},{5,13},{6,14},{7,15},{8,24},{9,... | collective-permute-start | bytes 196616 | tf_op jit(solution)/shard_map/ppermute | solution.py:555
  69.4 4.3 %collective-permute-start.24 = (f32[1,32,512]{2,1,0:T(8,128)S(1)}, f32[1,32,512]{2,1,0:T(8,128)S(1)}, u32[]{:S(2)}, u32[]{:S(2)}) collective-permute-start(f32[1,32,512]{2,1,0:T(8,128)S(1)} %add_bitcast_fusion), channel_id=1, source_target_pairs={{0,8},{1,9},{2,10},{3,11},{4,20},{5,21},{6,22},{7,23},{8,0},{9,1},... | collective-permute-start | bytes 196616 | tf_op jit(solution)/shard_map/ppermute | solution.py:555
  73.7 1.7 %collective-permute-start.27 = (f32[4,32,512]{2,1,0:T(8,128)S(1)}, f32[4,32,512]{2,1,0:T(8,128)S(1)}, u32[]{:S(2)}, u32[]{:S(2)}) collective-permute-start(f32[4,32,512]{2,1,0:T(8,128)S(1)} %constant_dynamic-update-slice_fusion.v_ref), channel_id=1, source_target_pairs={{0,4},{1,5},{2,6},{3,7},{4,0},{5,1},{6,2},{7,3},{8,12},{9,13},{10,... | collective-permute-start | bytes 786440 | tf_op jit(solution)/shard_map/ppermute | solution.py:555
  73.7 1.6 %collective-permute-start.28 = (f32[32,384]{1,0:T(8,128)S(1)}, f32[32,384]{1,0:T(8,128)S(1)}, u32[]{:S(2)}, u32[]{:S(2)}) collective-permute-start(f32[32,384]{1,0:T(8,128)S(1)} %root2b.1.f_ref), channel_id=1, source_target_pairs={{0,4},{1,5},{2,6},{3,7},{4,0},{5,1},{6,2},{7,3},{8,12},{9,13},{10,... | collective-permute-start | bytes 147464 | tf_op jit(solution)/shard_map/ppermute | solution.py:555
